TPU v7x, 32 devices: a whole 2x2x4 slice. The times are simulated.
32 devices in a mesh: cell: 8 (over y, x, core), tm: 4 (over z).
Axes of the slice: x: 2, y: 2, z: 4, core: 2. Of those that a mesh axis runs over, the one named last changes fastest.
Arguments:
- window: float32 [8192, 8192], P('cell', 'tm'), may hold values from -0.1875 to 0.1875
- range_test: float32 [8192, 256], P('tm'), may hold values from -0.0625 to 0.0625
- co_test: float32 [256, 8192], P(None, 'cell'), may hold values from -0.0625 to 0.0625
- core_left: float32 [512, 8192], P(None, 'cell'), may hold values from -0.0625 to 0.0625
- core_right: float32 [512, 8192], P(None, 'tm'), may hold values from -0.0625 to 0.0625
Outputs:
- range_basis: float32 [8192, 256], P('cell')
- co_basis: float32 [256, 8192], P(None, 'tm')
- core: float32 [256, 256], replicated
All inputs are finite; a program needn't handle non-finite values.
Results may differ from a plain program's by a relative error of at most 0.00023.
Values sent between devices are 32-bit elements; how exact they have to be, the bound alone decides.
No kernel may reach another device: no remote copies, remote signals or barrier semaphores. Data moves between devices by JAX's collectives and lax.ppermute only.
A program may use at most 128 MiB of HBM per device.

v0:
```python
import math

import jax
import jax.numpy as jnp
from jax import lax
from jax.sharding import PartitionSpec as P


def inner_rows(left, right):
    return lax.dot_general(left, right, (((0,), (0,)), ((), ())), precision=lax.Precision.HIGHEST)


def inner_cols(left, right):
    return lax.dot_general(left, right, (((1,), (1,)), ((), ())), precision=lax.Precision.HIGHEST)


def product(left, right):
    return jnp.dot(left, right, precision=lax.Precision.HIGHEST, preferred_element_type=jnp.float32)


def per_device(window, range_test, co_test, core_left, core_right):
    rows_total = window.shape[0] * lax.axis_size("cell")
    cols_total = window.shape[1] * lax.axis_size("tm")
    range_term = product(window, range_test)
    co_term = product(co_test, window)
    left_window = product(core_left, window)
    core_term = inner_cols(left_window, core_right)
    left_fold = product(left_window, range_test)
    right_fold = inner_cols(co_term, core_right)
    sketch_z, left_total, right_total = lax.psum((core_term, left_fold, right_fold), ("cell", "tm"))
    range_full = lax.psum(range_term, "tm")
    co_full = lax.psum(co_term, "cell")
    gram_y = lax.psum(inner_rows(range_full, range_full) / rows_total, "cell")
    gram_w = lax.psum(inner_cols(co_full, co_full) / cols_total, "tm")
    lower_y = jnp.linalg.cholesky(gram_y)
    lower_w = jnp.linalg.cholesky(gram_w)
    range_basis = jax.scipy.linalg.solve_triangular(lower_y, range_full.T, lower=True).T
    co_basis = jax.scipy.linalg.solve_triangular(lower_w, co_full, lower=True)
    left_image = jax.scipy.linalg.solve_triangular(lower_y, left_total.T, lower=True).T
    right_image = jax.scipy.linalg.solve_triangular(lower_w, right_total, lower=True).T
    gram_left = inner_rows(left_image, left_image)
    gram_right = inner_rows(right_image, right_image)
    projected = inner_rows(left_image, sketch_z)
    left_solved = jax.scipy.linalg.cho_solve((jnp.linalg.cholesky(gram_left), True), projected)
    middle = product(left_solved, right_image)
    core = jax.scipy.linalg.cho_solve((jnp.linalg.cholesky(gram_right), True), middle.T).T
    core = core * math.sqrt(rows_total * cols_total)
    return (range_basis, co_basis, core)


def solution(mesh):
    return jax.shard_map(
        per_device,
        mesh=mesh,
        in_specs=(P("cell", "tm"), P("tm", None), P(None, "cell"), P(None, "cell"), P(None, "tm")),
        out_specs=(P("cell", None), P(None, "tm"), P()),
        check_vma=False,
    )
```

profile of v0, /device:TPU:0, one launch (start us, length us, event | category | flops | bytes accessed | tf_op | source)
XLA Modules:
  0.0 528.0 jit_solution(7359080283319915997)
XLA Ops:
  7.2 10.7 %fusion.62 = f32[1024,256]{1,0:T(8,128)} fusion(f32[1024,2048]{1,0:T(8,128)} %param.8, f32[2048,256]{1,0:T(8,128)} %param.9), kind=kOutput, calls=%fused_computation.138 | convolution fusion | flops 6442450944 | bytes 11534336 | tf_op jit(solution)/shard_map/dot_general | solution.py:18
  18.0 9.8 %fusion.63 = f32[256,2048]{1,0:T(8,128)S(1)} fusion(f32[256,1024]{1,0:T(8,128)S(1)} %copy-done.9, f32[1024,2048]{1,0:T(8,128)} %param.8), kind=kOutput, calls=%fused_computation.139 | convolution fusion | flops 6442450944 | bytes 11534336 | tf_op jit(solution)/shard_map/dot_general | solution.py:18
  27.8 1.3 copy-done.1
  29.1 4.5 fusion.64
  34.1 38.6 %all-reduce.8.cloned.1.call-done = f32[1024,256]{1,0:T(8,128)} async-done(((f32[1024,256]{1,0:T(8,128)}), f32[1024,256]{1,0:T(8,128)}) %all-reduce.8.cloned.1.call-update) | async-done | bytes 1048592 | tf_op jit(solution)/shard_map/psum | solution.py:31
  72.7 4.1 convolution_multiply_fusion.1
  76.8 16.3 %fusion.65 = f32[512,2048]{1,0:T(8,128)S(1)} fusion(f32[512,1024]{1,0:T(8,128)S(1)} %copy-done, f32[1024,2048]{1,0:T(8,128)} %param.8), kind=kOutput, calls=%fused_computation.141 | convolution fusion | flops 12884901888 | bytes 14680064 | tf_op jit(solution)/shard_map/dot_general | solution.py:18
  93.2 4.3 convolution_bitcast_fusion
  97.5 7.9 %fusion.66 = f32[512,512]{1,0:T(8,128)} fusion(f32[512,2048]{1,0:T(8,128)S(1)} %fusion.65, f32[512,2048]{1,0:T(8,128)S(1)} %copy-done.3), kind=kOutput, calls=%fused_computation.142 | convolution fusion | flops 6442450944 | bytes 9437184 | tf_op jit(solution)/shard_map/dot_general | solution.py:14
  105.7 33.7 %all-reduce.14.cloned.1.call-done = (f32[256,256]{0,1:T(8,128)}, f32[256,2048]{1,0:T(8,128)}) async-done(((f32[256,256]{0,1:T(8,128)}, f32[256,2048]{1,0:T(8,128)}), (f32[256,256]{0,1:T(8,128)}, f32[256,2048]{1,0:T(8,128)})) %all-reduce.14.cloned.1.call-update) | async-done | bytes 2359312 | tf_op jit(solution)/shard_map/psum | solution.py:33
  141.4 11.7 %cholesky.214 = f32[128,128]{1,0:T(8,128)S(1)} custom-call(f32[128,128]{1,0:T(8,128)S(1)} %cholesky.346), custom_call_target="Cholesky" | custom-call | tf_op jit(solution)/shard_map/jit(cholesky)/cholesky | solution.py:35
  153.2 9.8 %custom-call.39 = f32[1,128,128]{1,2,0:T(8,128)S(1)} custom-call(f32[1,128,128]{2,1,0:T(8,128)S(1)} %get-tuple-element.123), custom_call_target="InvertDiagBlocksLowerTriangular" | custom-call | tf_op jit(solution)/shard_map/jit(cholesky)/cholesky | solution.py:35
  163.5 11.7 %cholesky.231 = f32[128,128]{1,0:T(8,128)S(1)} custom-call(f32[128,128]{1,0:T(8,128)S(1)} %convolution_subtract_fusion.11), custom_call_target="Cholesky" | custom-call | tf_op jit(solution)/shard_map/jit(cholesky)/cholesky | solution.py:35
  177.3 4.0 while.10
  177.9 1.4 bitcast_dynamic-update-slice_fusion.8
  179.9 1.4 bitcast_dynamic-update-slice_fusion.8
  181.3 20.1 %custom-call.30 = f32[2,128,128]{1,2,0:T(8,128)S(1)} custom-call(f32[2,128,128]{2,1,0:T(8,128)S(1)} %get-tuple-element.20), custom_call_target="InvertDiagBlocksLowerTriangular" | custom-call | tf_op jit(solution)/shard_map/jit(_solve_triangular)/triangular_solve | solution.py:37
  201.5 4.8 convolution_multiply_fusion
  206.3 73.7 %all-reduce.12.cloned.1.call-done = (f32[512,512]{1,0:T(8,128)}, f32[256,512]{0,1:T(8,128)}, f32[256,512]{1,0:T(8,128)}) async-done(((f32[512,512]{1,0:T(8,128)}, f32[256,512]{0,1:T(8,128)}, f32[256,512]{1,0:T(8,128)}), (f32[512,512]{1,0:T(8,128)}, f32[256,512]{0,1:T(8,128)}, f32[256,512]{1,0:T(8,128)})) %all-reduce.12.cloned.1.call-update) | async-done | bytes 2097168 | tf_op jit(solution)/shard_map/psum | solution.py:30
  280.0 1.4 fusion.13
  281.4 1.5 convolution_subtract_fusion.4
  284.9 11.7 %cholesky.316 = f32[128,128]{1,0:T(8,128)S(1)} custom-call(f32[128,128]{1,0:T(8,128)S(1)} %cholesky.355), custom_call_target="Cholesky" | custom-call | tf_op jit(solution)/shard_map/jit(cholesky)/cholesky | solution.py:44
  296.6 9.8 %custom-call.44 = f32[1,128,128]{1,2,0:T(8,128)S(1)} custom-call(f32[1,128,128]{2,1,0:T(8,128)S(1)} %get-tuple-element.115), custom_call_target="InvertDiagBlocksLowerTriangular" | custom-call | tf_op jit(solution)/shard_map/jit(cholesky)/cholesky | solution.py:44
  307.5 1.1 convolution_subtract_fusion.8
  308.6 11.9 %cholesky.333 = f32[128,128]{1,0:T(8,128)S(1)} custom-call(f32[128,128]{1,0:T(8,128)S(1)} %convolution_subtract_fusion.8), custom_call_target="Cholesky" | custom-call | tf_op jit(solution)/shard_map/jit(cholesky)/cholesky | solution.py:44
  323.2 4.0 while.13
  323.8 1.4 bitcast_dynamic-update-slice_fusion.11
  325.8 1.4 bitcast_dynamic-update-slice_fusion.11
  327.2 19.7 %custom-call.33 = f32[2,128,128]{1,2,0:T(8,128)S(1)} custom-call(f32[2,128,128]{2,1,0:T(8,128)S(1)} %get-tuple-element.44), custom_call_target="InvertDiagBlocksLowerTriangular" | custom-call | tf_op jit(solution)/shard_map/jit(_cho_solve)/triangular_solve | solution.py:44
  346.9 2.3 fusion.8
  354.0 1.3 copy.14
  355.3 1.1 fusion.41
  356.4 1.1 copy.11
  358.5 11.7 %cholesky.248 = f32[128,128]{1,0:T(8,128)S(1)} custom-call(f32[128,128]{1,0:T(8,128)S(1)} %cholesky.349), custom_call_target="Cholesky" | custom-call | tf_op jit(solution)/shard_map/jit(cholesky)/cholesky | solution.py:36
  370.2 9.8 %custom-call.40 = f32[1,128,128]{1,2,0:T(8,128)S(1)} custom-call(f32[1,128,128]{2,1,0:T(8,128)S(1)} %get-tuple-element.119), custom_call_target="InvertDiagBlocksLowerTriangular" | custom-call | tf_op jit(solution)/shard_map/jit(cholesky)/cholesky | solution.py:36
  380.5 12.1 %cholesky.265 = f32[128,128]{1,0:T(8,128)S(1)} custom-call(f32[128,128]{1,0:T(8,128)S(1)} %convolution_subtract_fusion.10), custom_call_target="Cholesky" | custom-call | tf_op jit(solution)/shard_map/jit(cholesky)/cholesky | solution.py:36
  394.7 4.0 while.11
  395.3 1.4 bitcast_dynamic-update-slice_fusion.9
  397.3 1.4 bitcast_dynamic-update-slice_fusion.9
  399.4 19.7 %custom-call.31 = f32[2,128,128]{1,2,0:T(8,128)S(1)} custom-call(f32[2,128,128]{2,1,0:T(8,128)S(1)} %get-tuple-element.28), custom_call_target="InvertDiagBlocksLowerTriangular" | custom-call | tf_op jit(solution)/shard_map/jit(_solve_triangular)/triangular_solve | solution.py:38
  419.0 2.3 fusion
  421.3 1.4 fusion.15
  422.7 1.4 convolution_subtract_fusion.5
  425.2 1.3 fusion.10
  426.5 1.8 copy.12
  430.7 13.2 %cholesky.282 = f32[128,128]{1,0:T(8,128)} custom-call(f32[128,128]{1,0:T(8,128)} %cholesky.352), custom_call_target="Cholesky" | custom-call | tf_op jit(solution)/shard_map/jit(cholesky)/cholesky | solution.py:46
  443.9 1.5 select_reduce_fusion.3
  445.4 1.6 cholesky.307
  446.9 11.3 %custom-call.42 = f32[1,128,128]{1,2,0:T(8,128)} custom-call(f32[1,128,128]{2,1,0:T(8,128)} %get-tuple-element.111), custom_call_target="InvertDiagBlocksLowerTriangular" | custom-call | tf_op jit(solution)/shard_map/jit(cholesky)/cholesky | solution.py:46
  458.2 1.7 constant_dynamic-update-slice_fusion.2
  459.9 1.7 convolution_subtract_fusion.9
  461.6 13.3 %cholesky.299 = f32[128,128]{1,0:T(8,128)} custom-call(f32[128,128]{1,0:T(8,128)} %convolution_subtract_fusion.9), custom_call_target="Cholesky" | custom-call | tf_op jit(solution)/shard_map/jit(cholesky)/cholesky | solution.py:46
  474.9 1.5 select_reduce_fusion.2
  479.0 1.7 select_select_fusion.1
  481.3 7.1 %while.12 = (s32[]{:T(128)}, f32[256,256]{1,0:T(8,128)}, s32[2,2]{1,0:T(2,128)S(1)}, f32[2,128,128]{2,1,0:T(8,128)}, s32[]{:T(128)}) while((s32[]{:T(128)}, f32[256,256]{1,0:T(8,128)}, s32[2,2]{1,0:T(2,128)S(1)}, f32[2,128,128]{2,1,0:T(8,128)}, s32[]{:T(128)}) %tuple.116), condition=%wide.while_cond.3, body=%wide.while_body.3.sunk | while | flops 2 | bytes 132705 | solution.py:46
  482.0 2.9 bitcast_dynamic-update-slice_fusion.10
  485.6 2.9 bitcast_dynamic-update-slice_fusion.10
  488.4 21.1 %custom-call.32 = f32[2,128,128]{1,2,0:T(8,128)} custom-call(f32[2,128,128]{2,1,0:T(8,128)} %get-tuple-element.36), custom_call_target="InvertDiagBlocksLowerTriangular" | custom-call | tf_op jit(solution)/shard_map/jit(_cho_solve)/triangular_solve | solution.py:46
  509.5 1.8 fusion.4
  511.3 1.2 fusion.22
  512.4 1.1 convolution_subtract_fusion.7
  514.1 1.1 convolution_subtract_fusion.6
  516.4 2.3 convolution_subtract_fusion
  519.8 1.5 pad_maximum_fusion
  (111 shorter events, 29.3 us)
Async XLA Ops:
  7.2 69.7 %copy-start = (f32[512,1024]{1,0:T(8,128)S(1)}, f32[512,1024]{1,0:T(8,128)}, u32[]{:S(2)}) copy-start(f32[512,1024]{1,0:T(8,128)} %param.11) | copy-start | bytes 6291460
  7.2 10.8 %copy-start.9 = (f32[256,1024]{1,0:T(8,128)S(1)}, f32[256,1024]{1,0:T(8,128)}, u32[]{:S(2)}) copy-start(f32[256,1024]{1,0:T(8,128)} %param.10) | copy-start | bytes 3145732
  7.2 65.5 %all-reduce.8.cloned.1.call-start = ((), (), s32[]{:S(2)}) async-start(), calls=%async_computation | async-start | bytes 2097152 | tf_op jit(solution)/shard_map/psum | solution.py:31
  18.0 11.1 %copy-start.2 = (f32[512,2048]{1,0:T(8,128)S(1)}, f32[512,2048]{1,0:T(8,128)}, u32[]{:S(2)}) copy-start(f32[512,2048]{1,0:T(8,128)} %param.12) | copy-start | bytes 12582916
  27.8 1.3 copy-start.1
  33.6 105.7 %all-reduce.14.cloned.1.call-start = ((), (), s32[]{:S(2)}) async-start(), calls=%async_computation.3 | async-start | bytes 4718592 | tf_op jit(solution)/shard_map/psum | solution.py:33
  76.8 203.2 %all-reduce.12.cloned.1.call-start = ((), (), s32[]{:S(2)}) async-start(), calls=%async_computation.2 | async-start | bytes 4194304 | tf_op jit(solution)/shard_map/psum | solution.py:30
  76.8 16.4 %copy-start.5 = (f32[2048,256]{1,0:T(8,128)S(1)}, f32[2048,256]{1,0:T(8,128)}, u32[]{:S(2)}) copy-start(f32[2048,256]{1,0:T(8,128)} %param.9) | copy-start | bytes 6291460
  93.2 4.3 copy-start.3
  105.4 251.0 %all-reduce.10.cloned.1.call-start = ((), (), s32[]{:S(2)}) async-start(), calls=%async_computation.1 | async-start | bytes 524288 | tf_op jit(solution)/shard_map/psum | solution.py:34
  284.2 0.7 copy-start.10
  346.9 3.6 copy-start.12
  349.2 2.3 copy-start.4
  350.8 0.7 copy-start.7
  353.8 1.4 copy-start.13
  398.7 0.7 copy-start.8
  424.5 0.7 copy-start.6
  429.4 0.7 copy-start.11
  509.5 4.0 copy-start.14
Sparse Core Ops, SparseCore 0:
  18.1 54.5 all-reduce.7
  76.9 62.3 all-reduce.13
  145.6 134.3 all-reduce.11
  282.9 34.7 all-reduce.9
where the time goes:
time: 537 us; the launch traced here: 528 us
  other arithmetic  232 us (43%)
  waiting for transfers between devices  146 us (27%)
  matrix products  96.6 us (18%)
  local copies, waits for them, and re-layouts  32.6 us (6%)
  between operations  19.7 us (4%)
    psum x1, waiting for transfers between devices, per_device(): lax.psum((core_term, left_fold, right_fold), ('cell', 'tm'))  73.7 us
    dot_general x5, matrix products, product(): jnp.dot(left, right, precision=lax.Precision.HIGHEST, preferred_element_t...  42.8 us
    another operation x7, other arithmetic, per_device(): jnp.linalg.cholesky(gram_right)  42 us
    psum x1, waiting for transfers between devices, per_device(): range_full = lax.psum(range_term, 'tm')  38.6 us
    another operation x7, other arithmetic, per_device(): jnp.linalg.cholesky(gram_left)  34.7 us
    another operation x6, other arithmetic, per_device(): lower_w = jnp.linalg.cholesky(gram_w)  34.3 us
    another operation x6, other arithmetic, per_device(): lower_y = jnp.linalg.cholesky(gram_y)  34 us
    psum x1, waiting for transfers between devices, per_device(): gram_y = lax.psum(inner_rows(range_full, range_full) / rows_total, 'cell')  33.7 us
  transfers between devices with their start and end apart: 4, of which 3 were waited for; matrix products, arithmetic and copies ran while one was open for 34% of the time, Pallas kernels for 0%

commit v1 on v0

v1 whole, which is shorter than its diff:
```python
import math

import jax
import jax.numpy as jnp
from jax import lax
from jax.experimental import pallas as pl
from jax.experimental.pallas import tpu as pltpu
from jax.sharding import PartitionSpec as P

BASE = 64
LANES = 128
SUBLANES = 8


def contract(left, right, left_dim, right_dim, precision):
    dims = (((left_dim,), (right_dim,)), ((), ()))
    return lax.dot_general(left, right, dims, precision=precision, preferred_element_type=jnp.float32)


def high(left, right, left_dim=1, right_dim=0):
    return contract(left, right, left_dim, right_dim, lax.Precision.HIGH)


def highest(left, right, left_dim=1, right_dim=0):
    return contract(left, right, left_dim, right_dim, lax.Precision.HIGHEST)


def bits_of(axis):
    return int(math.log2(lax.axis_size(axis)))


def swap(values, axis, bit):
    return lax.ppermute(values, axis, [(i, i ^ (1 << bit)) for i in range(lax.axis_size(axis))])


def side_of(axis, bit):
    return (lax.axis_index(axis) >> bit) & 1


def halve(values, axis, bit, dim):
    extent = values.shape[dim] // 2
    side = side_of(axis, bit)
    kept = lax.dynamic_slice_in_dim(values, side * extent, extent, dim)
    sent = lax.dynamic_slice_in_dim(values, (1 - side) * extent, extent, dim)
    return kept + swap(sent, axis, bit)


def join(values, axis, bit, dim):
    other = swap(values, axis, bit)
    first = jnp.concatenate([values, other], axis=dim)
    second = jnp.concatenate([other, values], axis=dim)
    return jnp.where(side_of(axis, bit) == 0, first, second)


def reduce_pieces(values, steps, dim):
    for axis, bit in steps:
        values = halve(values, axis, bit, dim)
    return values


def gather_pieces(values, steps, dim):
    for axis, bit in reversed(steps):
        values = join(values, axis, bit, dim)
    return values


def spread_lane(values, lane):
    return jnp.broadcast_to(values[:, lane:lane + 1], values.shape)


def spread_row(values, row):
    return jnp.broadcast_to(values[row:row + 1, :], values.shape)


def factor_blocks(blocks):
    count = len(blocks)
    groups = BASE // SUBLANES
    rows = [[x[SUBLANES * g:SUBLANES * (g + 1)] for g in range(groups)] for x in blocks]
    sub = lax.broadcasted_iota(jnp.int32, (SUBLANES, LANES), 0)
    pivots = [[] for _ in blocks]
    for p in range(groups):
        cols = [{g: [spread_lane(rows[b][g], SUBLANES * p + k) for k in range(SUBLANES)] for g in range(p, groups)} for b in range(count)]
        found = [jnp.zeros((SUBLANES, LANES), jnp.float32)] * count
        for k in range(SUBLANES):
            for b in range(count):
                held = cols[b]
                pivot = spread_row(held[p][k], k)
                found[b] = jnp.where(sub == k, pivot, found[b])
                scale = 1.0 / pivot
                pivot_row = spread_row(rows[b][p], k)
                heads = [spread_row(held[p][j], k) for j in range(k + 1, SUBLANES)]
                for g in range(p, groups):
                    weight = held[g][k] * scale
                    if g == p:
                        weight = jnp.where(sub > k, weight, 0.0)
                    rows[b][g] = rows[b][g] - weight * pivot_row
                    for j in range(k + 1, SUBLANES):
                        held[g][j] = held[g][j] - weight * heads[j - k - 1]
        for b in range(count):
            pivots[b].append(found[b])
    return [jnp.concatenate([rows[b][g] * lax.rsqrt(pivots[b][g]) for g in range(groups)], axis=0) for b in range(count)]


def factor_kernel(gram_ref, inverse_ref, upper_ref):
    count, n = gram_ref.shape[0], gram_ref.shape[1]
    every = range(count)
    inverse_ref[...] = gram_ref[...]
    row_id = lax.broadcasted_iota(jnp.int32, (n, n), 0)
    col_id = lax.broadcasted_iota(jnp.int32, (n, n), 1)
    panel_col = lax.broadcasted_iota(jnp.int32, (BASE, n), 1)
    lane = lax.broadcasted_iota(jnp.int32, (BASE, LANES), 1)
    low = lax.broadcasted_iota(jnp.int32, (BASE, LANES), 0)

    def place(half, start):
        rest = [jnp.zeros((BASE, LANES), jnp.float32)] * (n // LANES - 1)
        return pltpu.roll(jnp.concatenate([jnp.where(lane < BASE, half, 0.0)] + rest, axis=1), start, 1)

    def step(t, carry):
        start = pl.multiple_of(t * BASE, BASE)
        back = jnp.where(t == 0, 0, n - start)
        panel = [inverse_ref[b, pl.ds(start, BASE), :] for b in every]
        whole = [inverse_ref[b] for b in every]
        block = [pltpu.roll(panel[b], back, 1)[:, :LANES] for b in every]
        block = [jnp.where(lane < BASE, block[b], jnp.where(lane - BASE == low, 1.0, 0.0)) for b in every]
        done = factor_blocks(block)
        inv = [pltpu.roll(done[b], LANES - BASE, 1) for b in every]
        inv_placed = [place(inv[b], start) for b in every]
        up_placed = [place(done[b], start) for b in every]
        inside = (panel_col >= start) & (panel_col < start + BASE)
        rows = [jnp.where(inside, inv_placed[b], highest(inv[b][:, :BASE], panel[b])) for b in every]
        below = [jnp.where(row_id[:, :BASE] >= start + BASE, highest(whole[b], inv_placed[b], 1, 1), 0.0) for b in every]
        spent = (row_id >= start + BASE) & (col_id >= start) & (col_id < start + BASE)
        left = [jnp.where(spent, 0.0, whole[b]) - highest(below[b], rows[b]) for b in every]
        for b in every:
            inverse_ref[b] = left[b]
        for b in every:
            inverse_ref[b, pl.ds(start, BASE), :] = rows[b]
            upper_ref[b, pl.ds(start, BASE), :] = jnp.where(inside, up_placed[b], jnp.where(panel_col >= start + BASE, rows[b], 0.0))
        return carry

    lax.fori_loop(0, n // BASE, step, 0)
    for b in every:
        inverse_ref[b] = jnp.where(row_id >= col_id, inverse_ref[b], 0.0)
        upper_ref[b] = jnp.where(row_id <= col_id, upper_ref[b], 0.0)


def factor_grams(grams):
    count, n, _ = grams.shape
    vmem = pl.BlockSpec(memory_space=pltpu.VMEM)
    return pl.pallas_call(
        factor_kernel,
        out_shape=(jax.ShapeDtypeStruct(grams.shape, jnp.float32),) * 2,
        in_specs=[vmem],
        out_specs=(vmem, vmem),
        compiler_params=pltpu.CompilerParams(vmem_limit_bytes=24 * 1024 * 1024),
        cost_estimate=pl.CostEstimate(flops=count * n * n * n * 200, bytes_accessed=count * n * n * 12, transcendentals=0),
    )(grams)


def per_device(window, range_test, co_test, core_left, core_right):
    rows_total = window.shape[0] * lax.axis_size("cell")
    cols_total = window.shape[1] * lax.axis_size("tm")
    k = range_test.shape[1]
    s_core = core_left.shape[0]
    cell_steps = [("cell", bit) for bit in range(bits_of("cell"))]
    tm_steps = [("tm", bit) for bit in range(bits_of("tm"))]
    core_steps = cell_steps[:1] + cell_steps[:0:-1] + tm_steps

    range_term = high(window, range_test)
    co_term = high(co_test, window)
    range_piece = reduce_pieces(range_term, tm_steps, 0)
    co_piece = reduce_pieces(co_term, cell_steps, 1)
    window_core = high(window, core_right, 1, 1)
    left_fold = high(core_left, range_term)
    core_term = high(core_left, window_core)
    right_fold = high(window_core, co_test, 0, 1)
    sketches = jnp.concatenate([core_term, left_fold, right_fold], axis=1)
    sketches = gather_pieces(reduce_pieces(sketches, core_steps, 0), core_steps, 0)
    sketch_z, left_total, right_total = sketches[:, :s_core], sketches[:, s_core:s_core + k], sketches[:, s_core + k:]

    grams = jnp.stack([highest(range_piece, range_piece, 0, 0) / rows_total, highest(co_piece, co_piece, 1, 1) / cols_total])
    grams = grams.reshape(-1, k)
    gram_steps = cell_steps + tm_steps
    grams = gather_pieces(reduce_pieces(grams, gram_steps, 0), gram_steps, 0).reshape(2, k, k)
    range_full = gather_pieces(range_piece, tm_steps, 0)
    co_full = gather_pieces(co_piece, cell_steps, 1)
    inverses, uppers = factor_grams(grams)
    range_basis = high(range_full, inverses[0], 1, 1)
    co_basis = high(inverses[1], co_full)

    image_grams = jnp.stack([highest(left_total, left_total, 0, 0), highest(right_total, right_total, 0, 0)])
    image_inverses, _ = factor_grams(image_grams)
    middle = highest(highest(left_total, sketch_z, 0, 0), right_total)
    middle = highest(highest(image_inverses[0], middle), image_inverses[1], 1, 1)
    left_side = highest(uppers[0], image_inverses[0], 1, 1)
    right_side = highest(image_inverses[1], uppers[1], 1, 1)
    core = highest(highest(left_side, middle), right_side) * math.sqrt(rows_total * cols_total)
    return (range_basis, co_basis, core)


def solution(mesh):
    return jax.shard_map(
        per_device,
        mesh=mesh,
        in_specs=(P("cell", "tm"), P("tm", None), P(None, "cell"), P(None, "cell"), P(None, "tm")),
        out_specs=(P("cell", None), P(None, "tm"), P()),
        check_vma=False,
    )
```

time: 537 us -> 211 us (0.39); the launches traced: 528 us -> 210 us
  other arithmetic: 232 us -> 7.48 us
  waiting for transfers between devices: 146 us -> 86.3 us
  matrix products: 96.6 us -> 46.3 us
  starting transfers between devices: 0.8 us -> 34.2 us
  Pallas kernels: 0 us -> 29.4 us
  local copies, waits for them, and re-layouts: 32.6 us -> 5.55 us
  between operations: 19.7 us -> 1.15 us
    another operation x36 -> x2, other arithmetic: 229 us -> 0.07 us  [the longest x1 0.04 us: per_device(): jnp.stack([highest(range_piece, range_piece, 0, 0) / rows_total, highest(...]
    psum x4 -> x0, waiting for transfers between devices: 146 us -> none  [the longest x1 73.7 us: per_device(): lax.psum((core_term, left_fold, right_fold), ('cell', 'tm'))]
    ppermute x0 -> x30, waiting for transfers between devices: none -> 86.3 us  [swap(): lax.ppermute(values, axis, [(i, i ^ 1 << bit) for i in range(lax.axis_siz...]
    ppermute x0 -> x30, starting transfers between devices: none -> 34.2 us  [swap(): lax.ppermute(values, axis, [(i, i ^ 1 << bit) for i in range(lax.axis_siz...]
    pallas_call x0 -> x2, Pallas kernels: none -> 29.4 us  [factor_grams(): pl.pallas_call(factor_kernel, out_shape=(jax.ShapeDtypeStruct(grams.shape...]
    another operation x32 -> x0, matrix products: 28.2 us -> none  [the longest x3 5.59 us: per_device(): co_basis = jax.scipy.linalg.solve_triangular(lower_w, co_full, lower=True)]
    dot_general x12 -> x20, matrix products: 68.4 us -> 46.3 us  [contract(): lax.dot_general(left, right, dims, precision=precision, preferred_element...]
    another operation x33 -> x0, local copies, waits for them, and re-layouts: 21.3 us -> none
  transfers between devices with their start and end apart: 4 -> 30, of which waited for: 3 -> 13; matrix products, arithmetic and copies ran while one was open for 34% -> 21% of each run, Pallas kernels for 0% -> 7%
where the time goes in v1:
time: 211 us; the launch traced here: 210 us
  waiting for transfers between devices  86.3 us (41%)
  matrix products  46.3 us (22%)
  starting transfers between devices  34.2 us (16%)
  Pallas kernels  29.4 us (14%)
  other arithmetic  7.48 us (4%)
  local copies, waits for them, and re-layouts  5.55 us (3%)
    ppermute x30, waiting for transfers between devices, swap(): lax.ppermute(values, axis, [(i, i ^ 1 << bit) for i in range(lax.axis_siz...  86.3 us
    dot_general x20, matrix products, contract(): lax.dot_general(left, right, dims, precision=precision, preferred_element...  46.3 us
    ppermute x30, starting transfers between devices, swap(): lax.ppermute(values, axis, [(i, i ^ 1 << bit) for i in range(lax.axis_siz...  34.2 us
    pallas_call x2, Pallas kernels, factor_grams(): pl.pallas_call(factor_kernel, out_shape=(jax.ShapeDtypeStruct(grams.shape...  29.4 us
    dynamic_slice x15, local copies, waits for them, and re-layouts, halve(): sent = lax.dynamic_slice_in_dim(values, (1 - side) * extent, extent, dim)  5.2 us
    add x15, other arithmetic, halve(): return kept + swap(sent, axis, bit)  4.94 us
  transfers between devices with their start and end apart: 30, of which 13 were waited for; matrix products, arithmetic and copies ran while one was open for 21% of the time, Pallas kernels for 7%

profile of v1, /device:TPU:0, one launch (start us, length us, event | category | flops | bytes accessed | tf_op | source)
XLA Modules:
  0.0 210.4 jit_solution(13425982420366639063)
XLA Ops:
  0.7 6.7 %fusion.45 = f32[1024,256]{1,0:T(8,128)S(1)} fusion(f32[1024,2048]{1,0:T(8,128)} %param.5, f32[2048,256]{1,0:T(8,128)} %param.6), kind=kOutput, calls=%fused_computation.100 | convolution fusion | flops 3221225472 | bytes 11534336 | tf_op jit(solution)/shard_map/dot_general | solution.py:17
  7.4 0.8 constant_dynamic-slice_fusion.14
  8.2 3.0 %collective-permute-start = (f32[512,256]{1,0:T(8,128)}, f32[512,256]{1,0:T(8,128)}, u32[]{:S(2)}, u32[]{:S(2)}) collective-permute-start(f32[512,256]{1,0:T(8,128)} %constant_dynamic-slice_fusion.14), channel_id=1, source_target_pairs={{0,1},{1,0},{2,3},{3,2},{4,5},{5,4},{6,7},{7,6},{8,9},{9,8},{10,11... | collective-permute-start | bytes 1572872 | tf_op jit(solution)/shard_map/ppermute | solution.py:33
  11.2 8.9 %fusion.46 = f32[256,2048]{1,0:T(8,128)} fusion(f32[256,1024]{1,0:T(8,128)} %param.7, f32[1024,2048]{1,0:T(8,128)} %param.5), kind=kOutput, calls=%fused_computation.101 | convolution fusion | flops 3221225472 | bytes 11534336 | tf_op jit(solution)/shard_map/dot_general | solution.py:17
  20.1 2.5 %constant_dynamic-slice_fusion.12 = f32[256,1024]{1,0:T(8,128)} fusion(f32[256,2048]{1,0:T(8,128)} %fusion.46, s32[]{:T(128)S(6)} %select_n.212), kind=kLoop, calls=%fused_computation.95 | loop fusion | bytes 2097156 | tf_op jit(solution)/shard_map/dynamic_slice | solution.py:44
  22.6 2.6 %convolution_bitcast_fusion.1 = f32[512,256]{0,1:T(8,128)} fusion(f32[1024,256]{1,0:T(8,128)S(1)} %fusion.45, f32[512,1024]{1,0:T(8,128)S(1)} %copy-done), kind=kOutput, calls=%fused_computation.10 | convolution fusion | flops 805306368 | bytes 3670016 | tf_op jit(solution)/shard_map/dot_general | solution.py:17
  25.2 9.9 %fusion.47 = f32[1024,512]{1,0:T(8,128)S(1)} fusion(f32[1024,2048]{1,0:T(8,128)} %param.5, f32[512,2048]{1,0:T(8,128)S(1)} %copy-done.4), kind=kOutput, calls=%fused_computation.102 | convolution fusion | flops 6442450944 | bytes 14680064 | tf_op jit(solution)/shard_map/dot_general | solution.py:17
  35.1 4.5 %convolution_bitcast_fusion = f32[512,512]{0,1:T(8,128)} fusion(f32[1024,512]{1,0:T(8,128)S(1)} %fusion.47, f32[512,1024]{1,0:T(8,128)S(1)} %copy-done), kind=kOutput, calls=%fused_computation.9 | convolution fusion | flops 1610612736 | bytes 5242880 | tf_op jit(solution)/shard_map/dot_general | solution.py:17
  39.6 1.9 fusion.48
  41.5 1.7 pad_maximum_fusion
  43.2 1.1 constant_dynamic-slice_fusion.4
  44.3 0.5 collective-permute-start.20
  44.8 1.3 dynamic-slice_add_fusion.7
  46.1 2.6 %collective-permute-start.1 = (f32[256,256]{1,0:T(8,128)S(1)}, f32[256,256]{1,0:T(8,128)S(1)}, u32[]{:S(2)}, u32[]{:S(2)}) collective-permute-start(f32[256,256]{1,0:T(8,128)S(1)} %constant_dynamic-slice_fusion.13), channel_id=1, source_target_pairs={{0,2},{1,3},{2,0},{3,1},{4,6},{5,7},{6,4},{7,5},{8,10},{9,11},{10,... | collective-permute-start | bytes 786440 | tf_op jit(solution)/shard_map/ppermute | solution.py:33
  48.8 1.4 dynamic-slice_add_fusion.1
  50.2 1.6 collective-permute-start.5
  51.7 1.4 dynamic-slice_add_fusion
  53.2 1.6 collective-permute-start.21
  54.8 5.9 %collective-permute-done.1 = f32[256,256]{1,0:T(8,128)S(1)} collective-permute-done((f32[256,256]{1,0:T(8,128)S(1)}, f32[256,256]{1,0:T(8,128)S(1)}, u32[]{:S(2)}, u32[]{:S(2)}) %collective-permute-start.1) | collective-permute-done | bytes 262176 | tf_op jit(solution)/shard_map/ppermute | solution.py:33
  60.8 0.6 fusion.7
  61.4 2.4 %collective-permute-done.5 = f32[256,512]{1,0:T(8,128)S(1)} collective-permute-done((f32[256,512]{1,0:T(8,128)S(1)}, f32[256,512]{1,0:T(8,128)S(1)}, u32[]{:S(2)}, u32[]{:S(2)}) %collective-permute-start.5) | collective-permute-done | bytes 524320 | tf_op jit(solution)/shard_map/ppermute | solution.py:33
  63.9 1.6 collective-permute-start.6
  65.5 2.2 %collective-permute-done.21 = f32[128,1024]{0,1:T(8,128)S(1)} collective-permute-done((f32[128,1024]{0,1:T(8,128)S(1)}, f32[128,1024]{0,1:T(8,128)S(1)}, u32[]{:S(2)}, u32[]{:S(2)}) %collective-permute-start.21) | collective-permute-done | bytes 524320 | tf_op jit(solution)/shard_map/ppermute | solution.py:33
  68.1 4.1 %collective-permute-done.6 = f32[256,256]{1,0:T(8,128)S(1)} collective-permute-done((f32[256,256]{1,0:T(8,128)S(1)}, f32[256,256]{1,0:T(8,128)S(1)}, u32[]{:S(2)}, u32[]{:S(2)}) %collective-permute-start.6) | collective-permute-done | bytes 262176 | tf_op jit(solution)/shard_map/ppermute | solution.py:33
  72.3 0.4 fusion.6
  72.9 6.5 %collective-permute-done.22 = f32[64,1024]{0,1:T(8,128)S(1)} collective-permute-done((f32[64,1024]{0,1:T(8,128)S(1)}, f32[64,1024]{0,1:T(8,128)S(1)}, u32[]{:S(2)}, u32[]{:S(2)}) %collective-permute-start.22) | collective-permute-done | bytes 262176 | tf_op jit(solution)/shard_map/ppermute | solution.py:33
  79.8 0.5 collective-permute-start.23
  80.4 0.6 collective-permute-start.8
  81.0 9.7 %collective-permute-done.23 = f32[32,1024]{0,1:T(8,128)S(1)} collective-permute-done((f32[32,1024]{0,1:T(8,128)S(1)}, f32[32,1024]{0,1:T(8,128)S(1)}, u32[]{:S(2)}, u32[]{:S(2)}) %collective-permute-start.23) | collective-permute-done | bytes 131104 | tf_op jit(solution)/shard_map/ppermute | solution.py:33
  91.1 2.7 %collective-permute-start.24 = (f32[16,1024]{0,1:T(8,128)S(1)}, f32[16,1024]{0,1:T(8,128)S(1)}, u32[]{:S(2)}, u32[]{:S(2)}) collective-permute-start(f32[16,1024]{0,1:T(8,128)S(1)} %constant_dynamic-slice_fusion), channel_id=1, source_target_pairs={{0,2},{1,3},{2,0},{3,1},{4,6},{5,7},{6,4},{7,5},{8,10},{9,11},{10,... | collective-permute-start | bytes 196616 | tf_op jit(solution)/shard_map/ppermute | solution.py:33
  93.8 1.6 collective-permute-start.9
  95.4 16.8 %collective-permute-done.24 = f32[16,1024]{0,1:T(8,128)S(1)} collective-permute-done((f32[16,1024]{0,1:T(8,128)S(1)}, f32[16,1024]{0,1:T(8,128)S(1)}, u32[]{:S(2)}, u32[]{:S(2)}) %collective-permute-start.24) | collective-permute-done | bytes 65568 | tf_op jit(solution)/shard_map/ppermute | solution.py:33
  112.6 2.7 %collective-permute-start.10 = (f32[32,256]{1,0:T(8,128)S(1)}, f32[32,256]{1,0:T(8,128)S(1)}, u32[]{:S(2)}, u32[]{:S(2)}) collective-permute-start(f32[32,256]{1,0:T(8,128)S(1)} %constant_dynamic-slice_fusion.6), channel_id=1, source_target_pairs={{0,1},{1,0},{2,3},{3,2},{4,5},{5,4},{6,7},{7,6},{8,9},{9,8},{10,11... | collective-permute-start | bytes 98312 | tf_op jit(solution)/shard_map/ppermute | solution.py:33
  115.5 21.4 %collective-permute-done.25 = f32[16,1024]{0,1:T(8,128)S(1)} collective-permute-done((f32[16,1024]{0,1:T(8,128)S(1)}, f32[16,1024]{0,1:T(8,128)S(1)}, u32[]{:S(2)}, u32[]{:S(2)}) %collective-permute-start.25) | collective-permute-done | bytes 65568 | tf_op jit(solution)/shard_map/ppermute | solution.py:33
  137.2 1.8 collective-permute-start.26
  139.1 2.9 %collective-permute-done.11 = f32[16,256]{1,0:T(8,128)S(1)} collective-permute-done((f32[16,256]{1,0:T(8,128)S(1)}, f32[16,256]{1,0:T(8,128)S(1)}, u32[]{:S(2)}, u32[]{:S(2)}) %collective-permute-start.11) | collective-permute-done | bytes 16416 | tf_op jit(solution)/shard_map/ppermute | solution.py:33
  142.0 1.6 collective-permute-start.17
  143.6 3.0 %collective-permute-done.12 = f32[16,256]{1,0:T(8,128)S(1)} collective-permute-done((f32[16,256]{1,0:T(8,128)S(1)}, f32[16,256]{1,0:T(8,128)S(1)}, u32[]{:S(2)}, u32[]{:S(2)}) %collective-permute-start.12) | collective-permute-done | bytes 16416 | tf_op jit(solution)/shard_map/ppermute | solution.py:33
  146.6 1.7 collective-permute-start.27
  148.3 2.2 %collective-permute-done.13 = f32[32,256]{1,0:T(8,128)S(1)} collective-permute-done((f32[32,256]{1,0:T(8,128)S(1)}, f32[32,256]{1,0:T(8,128)S(1)}, u32[]{:S(2)}, u32[]{:S(2)}) %collective-permute-start.13) | collective-permute-done | bytes 32800 | tf_op jit(solution)/shard_map/ppermute | solution.py:33
  150.5 1.6 collective-permute-start.14
  152.2 1.7 collective-permute-start.18
  154.1 0.7 collective-permute-done.14
  154.9 2.3 %collective-permute-start.15 = (f32[128,256]{1,0:T(8,128)S(1)}, f32[128,256]{1,0:T(8,128)S(1)}, u32[]{:S(2)}, u32[]{:S(2)}) collective-permute-start(f32[128,256]{1,0:T(8,128)S(1)} %maximum_select_fusion.13), channel_id=1, source_target_pairs={{0,8},{4,12},{8,0},{12,4},{16,24},{20,28},{24,16},{28,20},{1,9},{5... | collective-permute-start | bytes 393224 | tf_op jit(solution)/shard_map/ppermute | solution.py:33
  157.2 1.7 collective-permute-start.28
  158.9 8.3 %collective-permute-done.15 = f32[128,256]{1,0:T(8,128)S(1)} collective-permute-done((f32[128,256]{1,0:T(8,128)S(1)}, f32[128,256]{1,0:T(8,128)S(1)}, u32[]{:S(2)}, u32[]{:S(2)}) %collective-permute-start.15) | collective-permute-done | bytes 131104 | tf_op jit(solution)/shard_map/ppermute | solution.py:33
  167.3 1.5 collective-permute-start.3
  169.0 0.3 collective-permute-start.19
  169.4 0.4 collective-permute-start.29
  169.8 14.3 %shard_map.76 = (f32[2,256,256]{2,1,0:T(8,128)S(1)}, f32[2,256,256]{2,1,0:T(8,128)S(1)}) custom-call(f32[2,256,256]{2,1,0:T(8,128)S(1)} %bitcast.59), custom_call_target="tpu_custom_call" | custom-call | flops 6710886400 | bytes 1572864 | tf_op jit(solution)/shard_map/pallas_call | solution.py:150
  184.1 1.6 fusion.10
  185.7 2.4 %fusion = f32[256,2048]{1,0:T(8,128)} fusion(f32[256,1024]{1,0:T(8,128)S(1)} %collective-permute-done.19, f32[256,1024]{1,0:T(8,128)S(1)} %maximum_select_fusion.5, pred[]{:T(512)S(6)} %eq.12, f32[2,256,256]{2,1,0:T(8,128)S(1)} %get-tuple-element.6), kind=kOutput, calls=%fused_computation.1 | convolution fusion | flops 806879232 | bytes 4456449 | tf_op jit(solution)/shard_map/dot_general | solution.py:17
  188.1 0.2 maximum_select_fusion.2
  188.4 1.0 convolution_bitcast_fusion.2
  189.4 1.0 convolution_bitcast_fusion.3
  190.4 1.1 fusion.8
  191.6 15.1 %shard_map.77 = (f32[2,256,256]{2,1,0:T(8,128)S(1)}, f32[2,256,256]{2,1,0:T(8,128)}) custom-call(f32[2,256,256]{2,1,0:T(8,128)S(1)} %pad_maximum_fusion.2.gram_ref), custom_call_target="tpu_custom_call" | custom-call | flops 6710886400 | bytes 1572864 | tf_op jit(solution)/shard_map/pallas_call | solution.py:150
  206.7 0.4 fusion.23
  207.1 0.4 fusion.30
  207.5 0.6 fusion.18
  208.1 0.4 fusion.28
  208.5 0.4 fusion.26
  208.9 0.4 fusion.49
  209.3 1.1 convolution_multiply_fusion
  (76 shorter events, 3.3 us)
Async XLA Ops:
  0.6 21.9 %copy-start = (f32[512,1024]{1,0:T(8,128)S(1)}, f32[512,1024]{1,0:T(8,128)}, u32[]{:S(2)}) copy-start(f32[512,1024]{1,0:T(8,128)} %param.8) | copy-start | bytes 6291460
  8.2 36.6 %collective-permute-start = (f32[512,256]{1,0:T(8,128)}, f32[512,256]{1,0:T(8,128)}, u32[]{:S(2)}, u32[]{:S(2)}) collective-permute-start(f32[512,256]{1,0:T(8,128)} %constant_dynamic-slice_fusion.14), channel_id=1, source_target_pairs={{0,1},{1,0},{2,3},{3,2},{4,5},{5,4},{6,7},{7,6},{8,9},{9,8},{10,11... | collective-permute-start | bytes 1572872 | tf_op jit(solution)/shard_map/ppermute | solution.py:33
  20.1 5.1 %copy-start.4 = (f32[512,2048]{1,0:T(8,128)S(1)}, f32[512,2048]{1,0:T(8,128)}, u32[]{:S(2)}) copy-start(f32[512,2048]{1,0:T(8,128)} %param.9) | copy-start | bytes 12582916
  22.6 26.2 %collective-permute-start.4 = (f32[256,1024]{1,0:T(8,128)}, f32[256,1024]{1,0:T(8,128)}, u32[]{:S(2)}, u32[]{:S(2)}) collective-permute-start(f32[256,1024]{1,0:T(8,128)} %constant_dynamic-slice_fusion.12), channel_id=1, source_target_pairs={{0,4},{4,0},{8,12},{12,8},{16,20},{20,16},{24,28},{28,24},{1,5},{5... | collective-permute-start | bytes 3145736 | tf_op jit(solution)/shard_map/ppermute | solution.py:33
  35.1 4.5 %copy-start.3 = (f32[256,1024]{1,0:T(8,128)S(1)}, f32[256,1024]{1,0:T(8,128)}, u32[]{:S(2)}) copy-start(f32[256,1024]{1,0:T(8,128)} %param.7) | copy-start | bytes 3145732
  44.3 7.5 %collective-permute-start.20 = (f32[256,1024]{0,1:T(8,128)}, f32[256,1024]{0,1:T(8,128)}, u32[]{:S(2)}, u32[]{:S(2)}) collective-permute-start(f32[256,1024]{0,1:T(8,128)} %constant_dynamic-slice_fusion.4), channel_id=1, source_target_pairs={{0,4},{4,0},{8,12},{12,8},{16,20},{20,16},{24,28},{28,24},{1,5},{5... | collective-permute-start | bytes 3145736 | tf_op jit(solution)/shard_map/ppermute | solution.py:33
  44.8 4.0 %copy-start.2 = (f32[256,2048]{1,0:T(8,128)S(1)}, f32[256,2048]{1,0:T(8,128)}, u32[]{:S(2)}) copy-start(f32[256,2048]{1,0:T(8,128)} %fusion.46) | copy-start | bytes 6291460
  46.1 14.6 %collective-permute-start.1 = (f32[256,256]{1,0:T(8,128)S(1)}, f32[256,256]{1,0:T(8,128)S(1)}, u32[]{:S(2)}, u32[]{:S(2)}) collective-permute-start(f32[256,256]{1,0:T(8,128)S(1)} %constant_dynamic-slice_fusion.13), channel_id=1, source_target_pairs={{0,2},{1,3},{2,0},{3,1},{4,6},{5,7},{6,4},{7,5},{8,10},{9,11},{10,... | collective-permute-start | bytes 786440 | tf_op jit(solution)/shard_map/ppermute | solution.py:33
  50.2 13.6 %collective-permute-start.5 = (f32[256,512]{1,0:T(8,128)S(1)}, f32[256,512]{1,0:T(8,128)S(1)}, u32[]{:S(2)}, u32[]{:S(2)}) collective-permute-start(f32[256,512]{1,0:T(8,128)S(1)} %constant_dynamic-slice_fusion.11), channel_id=1, source_target_pairs={{0,8},{4,12},{8,0},{12,4},{16,24},{20,28},{24,16},{28,20},{1,9},{5... | collective-permute-start | bytes 1572872 | tf_op jit(solution)/shard_map/ppermute | solution.py:33
  53.2 14.5 %collective-permute-start.21 = (f32[128,1024]{0,1:T(8,128)S(1)}, f32[128,1024]{0,1:T(8,128)S(1)}, u32[]{:S(2)}, u32[]{:S(2)}) collective-permute-start(f32[128,1024]{0,1:T(8,128)S(1)} %constant_dynamic-slice_fusion.3), channel_id=1, source_target_pairs={{0,16},{4,20},{8,24},{12,28},{16,0},{20,4},{24,8},{28,12},{1,17},{... | collective-permute-start | bytes 1572872 | tf_op jit(solution)/shard_map/ppermute | solution.py:33
  63.9 8.3 %collective-permute-start.6 = (f32[256,256]{1,0:T(8,128)S(1)}, f32[256,256]{1,0:T(8,128)S(1)}, u32[]{:S(2)}, u32[]{:S(2)}) collective-permute-start(f32[256,256]{1,0:T(8,128)S(1)} %constant_dynamic-slice_fusion.10), channel_id=1, source_target_pairs={{0,16},{4,20},{8,24},{12,28},{16,0},{20,4},{24,8},{28,12},{1,17},{... | collective-permute-start | bytes 786440 | tf_op jit(solution)/shard_map/ppermute | solution.py:33
  68.0 11.4 %collective-permute-start.22 = (f32[64,1024]{0,1:T(8,128)S(1)}, f32[64,1024]{0,1:T(8,128)S(1)}, u32[]{:S(2)}, u32[]{:S(2)}) collective-permute-start(f32[64,1024]{0,1:T(8,128)S(1)} %constant_dynamic-slice_fusion.2), channel_id=1, source_target_pairs={{0,8},{4,12},{8,0},{12,4},{16,24},{20,28},{24,16},{28,20},{1,9},{5... | collective-permute-start | bytes 786440 | tf_op jit(solution)/shard_map/ppermute | solution.py:33
  72.8 7.5 %collective-permute-start.7 = (f32[256,256]{1,0:T(8,128)S(1)}, f32[256,256]{1,0:T(8,128)S(1)}, u32[]{:S(2)}, u32[]{:S(2)}) collective-permute-start(f32[256,256]{1,0:T(8,128)S(1)} %constant_dynamic-slice_fusion.9), channel_id=1, source_target_pairs={{0,4},{4,0},{8,12},{12,8},{16,20},{20,16},{24,28},{28,24},{1,5},{5... | collective-permute-start | bytes 786440 | tf_op jit(solution)/shard_map/ppermute | solution.py:33
  79.8 10.8 %collective-permute-start.23 = (f32[32,1024]{0,1:T(8,128)S(1)}, f32[32,1024]{0,1:T(8,128)S(1)}, u32[]{:S(2)}, u32[]{:S(2)}) collective-permute-start(f32[32,1024]{0,1:T(8,128)S(1)} %constant_dynamic-slice_fusion.1), channel_id=1, source_target_pairs={{0,1},{1,0},{2,3},{3,2},{4,5},{5,4},{6,7},{7,6},{8,9},{9,8},{10,11... | collective-permute-start | bytes 393224 | tf_op jit(solution)/shard_map/ppermute | solution.py:33
  80.4 13.4 %collective-permute-start.8 = (f32[128,256]{1,0:T(8,128)S(1)}, f32[128,256]{1,0:T(8,128)S(1)}, u32[]{:S(2)}, u32[]{:S(2)}) collective-permute-start(f32[128,256]{1,0:T(8,128)S(1)} %constant_dynamic-slice_fusion.8), channel_id=1, source_target_pairs={{0,8},{4,12},{8,0},{12,4},{16,24},{20,28},{24,16},{28,20},{1,9},{5... | collective-permute-start | bytes 393224 | tf_op jit(solution)/shard_map/ppermute | solution.py:33
  91.1 21.2 %collective-permute-start.24 = (f32[16,1024]{0,1:T(8,128)S(1)}, f32[16,1024]{0,1:T(8,128)S(1)}, u32[]{:S(2)}, u32[]{:S(2)}) collective-permute-start(f32[16,1024]{0,1:T(8,128)S(1)} %constant_dynamic-slice_fusion), channel_id=1, source_target_pairs={{0,2},{1,3},{2,0},{3,1},{4,6},{5,7},{6,4},{7,5},{8,10},{9,11},{10,... | collective-permute-start | bytes 196616 | tf_op jit(solution)/shard_map/ppermute | solution.py:33
  93.8 18.7 %collective-permute-start.9 = (f32[64,256]{1,0:T(8,128)S(1)}, f32[64,256]{1,0:T(8,128)S(1)}, u32[]{:S(2)}, u32[]{:S(2)}) collective-permute-start(f32[64,256]{1,0:T(8,128)S(1)} %constant_dynamic-slice_fusion.7), channel_id=1, source_target_pairs={{0,16},{4,20},{8,24},{12,28},{16,0},{20,4},{24,8},{28,12},{1,17},{... | collective-permute-start | bytes 196616 | tf_op jit(solution)/shard_map/ppermute | solution.py:33
  112.4 24.5 %collective-permute-start.25 = (f32[16,1024]{0,1:T(8,128)S(1)}, f32[16,1024]{0,1:T(8,128)S(1)}, u32[]{:S(2)}, u32[]{:S(2)}) collective-permute-start(f32[16,1024]{0,1:T(8,128)S(1)} %dynamic-slice_add_fusion.2), channel_id=1, source_target_pairs={{0,2},{1,3},{2,0},{3,1},{4,6},{5,7},{6,4},{7,5},{8,10},{9,11},{10,... | collective-permute-start | bytes 196616 | tf_op jit(solution)/shard_map/ppermute | solution.py:33
  112.6 24.5 %collective-permute-start.10 = (f32[32,256]{1,0:T(8,128)S(1)}, f32[32,256]{1,0:T(8,128)S(1)}, u32[]{:S(2)}, u32[]{:S(2)}) collective-permute-start(f32[32,256]{1,0:T(8,128)S(1)} %constant_dynamic-slice_fusion.6), channel_id=1, source_target_pairs={{0,1},{1,0},{2,3},{3,2},{4,5},{5,4},{6,7},{7,6},{8,9},{9,8},{10,11... | collective-permute-start | bytes 98312 | tf_op jit(solution)/shard_map/ppermute | solution.py:33
  137.1 4.8 %collective-permute-start.11 = (f32[16,256]{1,0:T(8,128)S(1)}, f32[16,256]{1,0:T(8,128)S(1)}, u32[]{:S(2)}, u32[]{:S(2)}) collective-permute-start(f32[16,256]{1,0:T(8,128)S(1)} %constant_dynamic-slice_fusion.5), channel_id=1, source_target_pairs={{0,2},{1,3},{2,0},{3,1},{4,6},{5,7},{6,4},{7,5},{8,10},{9,11},{10,... | collective-permute-start | bytes 49160 | tf_op jit(solution)/shard_map/ppermute | solution.py:33
  137.2 9.4 %collective-permute-start.26 = (f32[32,1024]{1,0:T(8,128)S(1)}, f32[32,1024]{1,0:T(8,128)S(1)}, u32[]{:S(2)}, u32[]{:S(2)}) collective-permute-start(f32[32,1024]{1,0:T(8,128)S(1)} %maximum_select_fusion.14), channel_id=1, source_target_pairs={{0,1},{1,0},{2,3},{3,2},{4,5},{5,4},{6,7},{7,6},{8,9},{9,8},{10,11... | collective-permute-start | bytes 393224 | tf_op jit(solution)/shard_map/ppermute | solution.py:33
  141.9 4.6 %collective-permute-start.12 = (f32[16,256]{1,0:T(8,128)S(1)}, f32[16,256]{1,0:T(8,128)S(1)}, u32[]{:S(2)}, u32[]{:S(2)}) collective-permute-start(f32[16,256]{1,0:T(8,128)S(1)} %dynamic-slice_add_fusion.14), channel_id=1, source_target_pairs={{0,2},{1,3},{2,0},{3,1},{4,6},{5,7},{6,4},{7,5},{8,10},{9,11},{10,... | collective-permute-start | bytes 49160 | tf_op jit(solution)/shard_map/ppermute | solution.py:33
  142.0 10.2 %collective-permute-start.17 = (f32[256,256]{1,0:T(8,128)S(1)}, f32[256,256]{1,0:T(8,128)S(1)}, u32[]{:S(2)}, u32[]{:S(2)}) collective-permute-start(f32[256,256]{1,0:T(8,128)S(1)} %dynamic-slice_add_fusion.9), channel_id=1, source_target_pairs={{0,16},{4,20},{8,24},{12,28},{16,0},{20,4},{24,8},{28,12},{1,17},{... | collective-permute-start | bytes 786440 | tf_op jit(solution)/shard_map/ppermute | solution.py:33
  146.6 3.9 %collective-permute-start.13 = (f32[32,256]{1,0:T(8,128)S(1)}, f32[32,256]{1,0:T(8,128)S(1)}, u32[]{:S(2)}, u32[]{:S(2)}) collective-permute-start(f32[32,256]{1,0:T(8,128)S(1)} %maximum_select_fusion.16), channel_id=1, source_target_pairs={{0,1},{1,0},{2,3},{3,2},{4,5},{5,4},{6,7},{7,6},{8,9},{9,8},{10,11... | collective-permute-start | bytes 98312 | tf_op jit(solution)/shard_map/ppermute | solution.py:33
  146.6 10.5 %collective-permute-start.27 = (f32[64,1024]{1,0:T(8,128)S(1)}, f32[64,1024]{1,0:T(8,128)S(1)}, u32[]{:S(2)}, u32[]{:S(2)}) collective-permute-start(f32[64,1024]{1,0:T(8,128)S(1)} %maximum_select_fusion.12), channel_id=1, source_target_pairs={{0,8},{4,12},{8,0},{12,4},{16,24},{20,28},{24,16},{28,20},{1,9},{5... | collective-permute-start | bytes 786440 | tf_op jit(solution)/shard_map/ppermute | solution.py:33
  150.5 4.3 %collective-permute-start.14 = (f32[64,256]{1,0:T(8,128)S(1)}, f32[64,256]{1,0:T(8,128)S(1)}, u32[]{:S(2)}, u32[]{:S(2)}) collective-permute-start(f32[64,256]{1,0:T(8,128)S(1)} %maximum_select_fusion.15), channel_id=1, source_target_pairs={{0,16},{4,20},{8,24},{12,28},{16,0},{20,4},{24,8},{28,12},{1,17},{... | collective-permute-start | bytes 196616 | tf_op jit(solution)/shard_map/ppermute | solution.py:33
  152.2 16.6 %collective-permute-start.18 = (f32[256,512]{1,0:T(8,128)S(1)}, f32[256,512]{1,0:T(8,128)S(1)}, u32[]{:S(2)}, u32[]{:S(2)}) collective-permute-start(f32[256,512]{1,0:T(8,128)S(1)} %maximum_select_fusion.9), channel_id=1, source_target_pairs={{0,8},{4,12},{8,0},{12,4},{16,24},{20,28},{24,16},{28,20},{1,9},{5... | collective-permute-start | bytes 1572872 | tf_op jit(solution)/shard_map/ppermute | solution.py:33
  153.9 13.3 %collective-permute-start.2 = (f32[256,256]{1,0:T(8,128)S(1)}, f32[256,256]{1,0:T(8,128)S(1)}, u32[]{:S(2)}, u32[]{:S(2)}) collective-permute-start(f32[256,256]{1,0:T(8,128)S(1)} %dynamic-slice_add_fusion.10), channel_id=1, source_target_pairs={{0,2},{1,3},{2,0},{3,1},{4,6},{5,7},{6,4},{7,5},{8,10},{9,11},{10,... | collective-permute-start | bytes 786440 | tf_op jit(solution)/shard_map/ppermute | solution.py:33
  154.9 12.3 %collective-permute-start.15 = (f32[128,256]{1,0:T(8,128)S(1)}, f32[128,256]{1,0:T(8,128)S(1)}, u32[]{:S(2)}, u32[]{:S(2)}) collective-permute-start(f32[128,256]{1,0:T(8,128)S(1)} %maximum_select_fusion.13), channel_id=1, source_target_pairs={{0,8},{4,12},{8,0},{12,4},{16,24},{20,28},{24,16},{28,20},{1,9},{5... | collective-permute-start | bytes 393224 | tf_op jit(solution)/shard_map/ppermute | solution.py:33
  157.2 12.1 %collective-permute-start.28 = (f32[128,1024]{1,0:T(8,128)S(1)}, f32[128,1024]{1,0:T(8,128)S(1)}, u32[]{:S(2)}, u32[]{:S(2)}) collective-permute-start(f32[128,1024]{1,0:T(8,128)S(1)} %maximum_select_fusion.10), channel_id=1, source_target_pairs={{0,16},{4,20},{8,24},{12,28},{16,0},{20,4},{24,8},{28,12},{1,17},{... | collective-permute-start | bytes 1572872 | tf_op jit(solution)/shard_map/ppermute | solution.py:33
  167.1 2.1 %collective-permute-start.16 = (f32[256,256]{1,0:T(8,128)S(1)}, f32[256,256]{1,0:T(8,128)S(1)}, u32[]{:S(2)}, u32[]{:S(2)}) collective-permute-start(f32[256,256]{1,0:T(8,128)S(1)} %maximum_select_fusion.11), channel_id=1, source_target_pairs={{0,4},{4,0},{8,12},{12,8},{16,20},{20,16},{24,28},{28,24},{1,5},{5... | collective-permute-start | bytes 786440 | tf_op jit(solution)/shard_map/ppermute | solution.py:33
  167.3 16.8 %collective-permute-start.3 = (f32[512,256]{1,0:T(8,128)S(1)}, f32[512,256]{1,0:T(8,128)S(1)}, u32[]{:S(2)}, u32[]{:S(2)}) collective-permute-start(f32[512,256]{1,0:T(8,128)S(1)} %maximum_select_fusion.7), channel_id=1, source_target_pairs={{0,1},{1,0},{2,3},{3,2},{4,5},{5,4},{6,7},{7,6},{8,9},{9,8},{10,11... | collective-permute-start | bytes 1572872 | tf_op jit(solution)/shard_map/ppermute | solution.py:33
  169.0 16.7 %collective-permute-start.19 = (f32[256,1024]{1,0:T(8,128)S(1)}, f32[256,1024]{1,0:T(8,128)S(1)}, u32[]{:S(2)}, u32[]{:S(2)}) collective-permute-start(f32[256,1024]{1,0:T(8,128)S(1)} %maximum_select_fusion.5), channel_id=1, source_target_pairs={{0,4},{4,0},{8,12},{12,8},{16,20},{20,16},{24,28},{28,24},{1,5},{5... | collective-permute-start | bytes 3145736 | tf_op jit(solution)/shard_map/ppermute | solution.py:33
  169.4 18.7 %collective-permute-start.29 = (f32[256,1024]{1,0:T(8,128)S(1)}, f32[256,1024]{1,0:T(8,128)S(1)}, u32[]{:S(2)}, u32[]{:S(2)}) collective-permute-start(f32[256,1024]{1,0:T(8,128)S(1)} %maximum_select_fusion.6), channel_id=1, source_target_pairs={{0,4},{4,0},{8,12},{12,8},{16,20},{20,16},{24,28},{28,24},{1,5},{5... | collective-permute-start | bytes 3145736 | tf_op jit(solution)/shard_map/ppermute | solution.py:33
  207.1 3.3 %copy-start.1 = (f32[512,1024]{1,0:T(8,128)S(1)}, f32[512,1024]{1,0:T(8,128)}, u32[]{:S(2)}) copy-start(f32[512,1024]{1,0:T(8,128)} %param.8) | copy-start | bytes 6291460

commit v2 on v1

--- a/solution.py
+++ b/solution.py
@@ -10,6 +10,7 @@
 BASE = 64
 LANES = 128
 SUBLANES = 8
+VMEM_BYTES = 48 * 1024 * 1024
 
 
 def contract(left, right, left_dim, right_dim, precision):
@@ -29,39 +30,212 @@
     return int(math.log2(lax.axis_size(axis)))
 
 
-def swap(values, axis, bit):
-    return lax.ppermute(values, axis, [(i, i ^ (1 << bit)) for i in range(lax.axis_size(axis))])
+def groups_of(axis, first, width):
+    bits = list(range(first, bits_of(axis)))
+    return [(axis, tuple(bits[i:i + width])) for i in range(0, len(bits), width)]
+
+
+def swap(values, axis, mask):
+    return lax.ppermute(values, axis, [(i, i ^ mask) for i in range(lax.axis_size(axis))])
 
 
 def side_of(axis, bit):
     return (lax.axis_index(axis) >> bit) & 1
 
 
-def halve(values, axis, bit, dim):
-    extent = values.shape[dim] // 2
-    side = side_of(axis, bit)
-    kept = lax.dynamic_slice_in_dim(values, side * extent, extent, dim)
-    sent = lax.dynamic_slice_in_dim(values, (1 - side) * extent, extent, dim)
-    return kept + swap(sent, axis, bit)
-
-
-def join(values, axis, bit, dim):
-    other = swap(values, axis, bit)
-    first = jnp.concatenate([values, other], axis=dim)
-    second = jnp.concatenate([other, values], axis=dim)
-    return jnp.where(side_of(axis, bit) == 0, first, second)
-
-
-def reduce_pieces(values, steps, dim):
-    for axis, bit in steps:
-        values = halve(values, axis, bit, dim)
+def place_of(axis, bits):
+    return sum(side_of(axis, bit) << i for i, bit in enumerate(bits))
+
+
+def masks_of(bits):
+    return [sum(((peer >> i) & 1) << bit for i, bit in enumerate(bits)) for peer in range(1 << len(bits))]
+
+
+def pair_sum(parts):
+    while len(parts) > 1:
+        parts = [parts[i] + parts[i + 1] for i in range(0, len(parts), 2)]
+    return parts[0]
+
+
+def scatter_sum(values, group, dim):
+    axis, bits = group
+    peers = 1 << len(bits)
+    extent = values.shape[dim] // peers
+    place = place_of(axis, bits)
+    parts = [lax.dynamic_slice_in_dim(values, (place ^ peer) * extent, extent, dim) for peer in range(peers)]
+    return pair_sum([parts[0]] + [swap(parts[peer], axis, masks_of(bits)[peer]) for peer in range(1, peers)])
+
+
+def whole_sum(values, group):
+    axis, bits = group
+    return pair_sum([values] + [swap(values, axis, mask) for mask in masks_of(bits)[1:]])
+
+
+def gather(values, group, dim):
+    axis, bits = group
+    peers = 1 << len(bits)
+    place = place_of(axis, bits)
+    parts = [values] + [swap(values, axis, mask) for mask in masks_of(bits)[1:]]
+    ordered = []
+    for slot in range(peers):
+        chosen = parts[slot]
+        for here in range(1, peers):
+            chosen = jnp.where(place == here, parts[slot ^ here], chosen)
+        ordered.append(chosen)
+    return jnp.concatenate(ordered, axis=dim)
+
+
+def total_over_chips(values):
+    for group in groups_of("cell", 1, 2):
+        values = scatter_sum(values, group, 0)
+    for group in groups_of("tm", 0, 2):
+        values = whole_sum(values, group)
+    for group in reversed(groups_of("cell", 1, 2)):
+        values = gather(values, group, 0)
     return values
 
 
-def gather_pieces(values, steps, dim):
-    for axis, bit in reversed(steps):
-        values = join(values, axis, bit, dim)
-    return values
+def split(values):
+    top = values.astype(jnp.bfloat16)
+    return top, (values - top.astype(jnp.float32)).astype(jnp.bfloat16)
+
+
+def parts_dot(left, right, left_dim=1, right_dim=0):
+    dims = (((left_dim,), (right_dim,)), ((), ()))
+    pairs = ((left[0], right[0]), (left[0], right[1]), (left[1], right[0]))
+    return sum(lax.dot_general(a, b, dims, preferred_element_type=jnp.float32) for a, b in pairs)
+
+
+def range_kernel(order_ref, window_ref, test_ref, first_ref, second_ref, top_ref, rest_ref):
+    @pl.when(pl.program_id(0) == 0)
+    def _():
+        top_ref[...], rest_ref[...] = split(test_ref[...])
+
+    tile = parts_dot(split(window_ref[...]), (top_ref[...], rest_ref[...]))
+
+    @pl.when(pl.program_id(0) == 0)
+    def _():
+        first_ref[...] = tile
+
+    @pl.when(pl.program_id(0) == 1)
+    def _():
+        second_ref[...] = tile
+
+
+def range_terms(window, range_test, order):
+    rows, depth = window.shape
+    k = range_test.shape[1]
+    tile = rows // 4
+    out = jax.ShapeDtypeStruct((tile, k), jnp.float32)
+    return pl.pallas_call(
+        range_kernel,
+        out_shape=(out, out),
+        grid_spec=pltpu.PrefetchScalarGridSpec(
+            num_scalar_prefetch=1,
+            grid=(2,),
+            in_specs=[
+                pl.BlockSpec((tile, depth), lambda i, order_ref: (order_ref[i], 0)),
+                pl.BlockSpec((depth, k), lambda i, order_ref: (0, 0)),
+            ],
+            out_specs=(pl.BlockSpec((tile, k), lambda i, order_ref: (0, 0)),) * 2,
+            scratch_shapes=[pltpu.VMEM((depth, k), jnp.bfloat16)] * 2,
+        ),
+        compiler_params=pltpu.CompilerParams(vmem_limit_bytes=VMEM_BYTES),
+        cost_estimate=pl.CostEstimate(flops=rows * depth * k * 3, bytes_accessed=rows * depth * 2, transcendentals=0),
+    )(order, window, range_test)
+
+
+def co_kernel(order_ref, window_ref, test_ref, sent_ref, kept_ref):
+    tile = parts_dot(split(test_ref[...]), split(window_ref[...]))
+
+    @pl.when(pl.program_id(0) < 2)
+    def _():
+        sent_ref[...] = tile
+
+    @pl.when(pl.program_id(0) >= 2)
+    def _():
+        kept_ref[...] = tile
+
+
+def co_terms(window, co_test, order):
+    rows, cols = window.shape
+    count = co_test.shape[0]
+    tile = cols // 4
+    out = jax.ShapeDtypeStruct((count, 2 * tile), jnp.float32)
+    return pl.pallas_call(
+        co_kernel,
+        out_shape=(out, out),
+        grid_spec=pltpu.PrefetchScalarGridSpec(
+            num_scalar_prefetch=1,
+            grid=(4,),
+            in_specs=[
+                pl.BlockSpec((rows, tile), lambda i, order_ref: (0, order_ref[i])),
+                pl.BlockSpec((count, rows), lambda i, order_ref: (0, 0)),
+            ],
+            out_specs=(
+                pl.BlockSpec((count, tile), lambda i, order_ref: (0, jnp.minimum(i, 1))),
+                pl.BlockSpec((count, tile), lambda i, order_ref: (0, jnp.maximum(i - 2, 0))),
+            ),
+        ),
+        compiler_params=pltpu.CompilerParams(vmem_limit_bytes=VMEM_BYTES),
+        cost_estimate=pl.CostEstimate(flops=rows * cols * count * 6, bytes_accessed=rows * cols * 4, transcendentals=0),
+    )(order, window, co_test)
+
+
+def core_kernel(order_ref, window_ref, right_ref, left_ref, co_ref, r0_ref, r1_ref, r2_ref, r3_ref, z_ref, lt_ref, rt_ref, top_ref, rest_ref, fold_ref):
+    step = pl.program_id(0)
+
+    @pl.when(step == 0)
+    def _():
+        top_ref[...], rest_ref[...] = split(right_ref[...])
+        z_ref[...] = jnp.zeros_like(z_ref)
+        lt_ref[...] = jnp.zeros_like(lt_ref)
+        fold_ref[...] = jnp.zeros_like(fold_ref)
+
+    image = split(parts_dot(split(window_ref[...]), (top_ref[...], rest_ref[...]), 1, 1))
+    left = split(left_ref[...])
+    z_ref[...] += parts_dot(left, image)
+    fold_ref[...] += parts_dot(split(co_ref[...]), image)
+    for i, r_ref in enumerate((r0_ref, r1_ref, r2_ref, r3_ref)):
+        @pl.when(step == i)
+        def _():
+            lt_ref[...] += parts_dot(left, split(r_ref[...]))
+
+    @pl.when(step == 3)
+    def _():
+        rt_ref[...] = fold_ref[...].T
+
+
+def core_terms(window, core_right, core_left, co_test, ranges, order):
+    rows, cols = window.shape
+    s_core, count, k = core_right.shape[0], co_test.shape[0], ranges[0].shape[1]
+    tile = rows // 4
+    return pl.pallas_call(
+        core_kernel,
+        out_shape=(
+            jax.ShapeDtypeStruct((s_core, s_core), jnp.float32),
+            jax.ShapeDtypeStruct((s_core, k), jnp.float32),
+            jax.ShapeDtypeStruct((s_core, count), jnp.float32),
+        ),
+        grid_spec=pltpu.PrefetchScalarGridSpec(
+            num_scalar_prefetch=1,
+            grid=(4,),
+            in_specs=[
+                pl.BlockSpec((tile, cols), lambda i, order_ref: (order_ref[i], 0)),
+                pl.BlockSpec((s_core, cols), lambda i, order_ref: (0, 0)),
+                pl.BlockSpec((s_core, tile), lambda i, order_ref: (0, order_ref[i])),
+                pl.BlockSpec((count, tile), lambda i, order_ref: (0, order_ref[i])),
+            ] + [pl.BlockSpec((tile, k), lambda i, order_ref: (0, 0))] * 4,
+            out_specs=(
+                pl.BlockSpec((s_core, s_core), lambda i, order_ref: (0, 0)),
+                pl.BlockSpec((s_core, k), lambda i, order_ref: (0, 0)),
+                pl.BlockSpec((s_core, count), lambda i, order_ref: (0, 0)),
+            ),
+            scratch_shapes=[pltpu.VMEM((s_core, cols), jnp.bfloat16)] * 2 + [pltpu.VMEM((count, s_core), jnp.float32)],
+        ),
+        compiler_params=pltpu.CompilerParams(vmem_limit_bytes=VMEM_BYTES),
+        cost_estimate=pl.CostEstimate(flops=rows * cols * s_core * 9, bytes_accessed=rows * cols * 4, transcendentals=0),
+    )(order, window, core_right, core_left, co_test, *ranges)
 
 
 def spread_lane(values, lane):
@@ -144,6 +318,11 @@
         upper_ref[b] = jnp.where(row_id <= col_id, upper_ref[b], 0.0)
 
 
+def factor_gram(gram):
+    inverse, upper = factor_grams(gram[None])
+    return inverse[0], upper[0]
+
+
 def factor_grams(grams):
     count, n, _ = grams.shape
     vmem = pl.BlockSpec(memory_space=pltpu.VMEM)
@@ -157,45 +336,73 @@
     )(grams)
 
 
+def reduce_rows(first, second, third, fourth, axis):
+    toward_far = swap(first, axis, 1)
+    toward_near = swap(second, axis, 1)
+    handed = swap(third + toward_far, axis, 2)
+    piece = fourth + toward_near + handed
+    for group in groups_of(axis, 2, 1):
+        piece = scatter_sum(piece, group, 0)
+    return piece
+
+
+def gather_rows(piece, axis):
+    for bit in reversed(range(bits_of(axis))):
+        piece = gather(piece, (axis, (bit,)), 0)
+    return piece
+
+
 def per_device(window, range_test, co_test, core_left, core_right):
     rows_total = window.shape[0] * lax.axis_size("cell")
     cols_total = window.shape[1] * lax.axis_size("tm")
-    k = range_test.shape[1]
-    s_core = core_left.shape[0]
-    cell_steps = [("cell", bit) for bit in range(bits_of("cell"))]
-    tm_steps = [("tm", bit) for bit in range(bits_of("tm"))]
-    core_steps = cell_steps[:1] + cell_steps[:0:-1] + tm_steps
-
-    range_term = high(window, range_test)
-    co_term = high(co_test, window)
-    range_piece = reduce_pieces(range_term, tm_steps, 0)
-    co_piece = reduce_pieces(co_term, cell_steps, 1)
-    window_core = high(window, core_right, 1, 1)
-    left_fold = high(core_left, range_term)
-    core_term = high(core_left, window_core)
-    right_fold = high(window_core, co_test, 0, 1)
-    sketches = jnp.concatenate([core_term, left_fold, right_fold], axis=1)
-    sketches = gather_pieces(reduce_pieces(sketches, core_steps, 0), core_steps, 0)
-    sketch_z, left_total, right_total = sketches[:, :s_core], sketches[:, s_core:s_core + k], sketches[:, s_core + k:]
-
-    grams = jnp.stack([highest(range_piece, range_piece, 0, 0) / rows_total, highest(co_piece, co_piece, 1, 1) / cols_total])
-    grams = grams.reshape(-1, k)
-    gram_steps = cell_steps + tm_steps
-    grams = gather_pieces(reduce_pieces(grams, gram_steps, 0), gram_steps, 0).reshape(2, k, k)
-    range_full = gather_pieces(range_piece, tm_steps, 0)
-    co_full = gather_pieces(co_piece, cell_steps, 1)
-    inverses, uppers = factor_grams(grams)
-    range_basis = high(range_full, inverses[0], 1, 1)
-    co_basis = high(inverses[1], co_full)
-
-    image_grams = jnp.stack([highest(left_total, left_total, 0, 0), highest(right_total, right_total, 0, 0)])
-    image_inverses, _ = factor_grams(image_grams)
-    middle = highest(highest(left_total, sketch_z, 0, 0), right_total)
-    middle = highest(highest(image_inverses[0], middle), image_inverses[1], 1, 1)
-    left_side = highest(uppers[0], image_inverses[0], 1, 1)
-    right_side = highest(image_inverses[1], uppers[1], 1, 1)
-    core = highest(highest(left_side, middle), right_side) * math.sqrt(rows_total * cols_total)
-    return (range_basis, co_basis, core)
+    core = side_of("cell", 0)
+    near, far = side_of("tm", 0), side_of("tm", 1)
+    cell_groups = groups_of("cell", 1, 2)
+
+    order = jnp.stack([(1 - near) * 2 + 1 - far, (1 - near) * 2 + far, near * 2 + 1 - far, near * 2 + far]).astype(jnp.int32)
+    first, second = range_terms(window, range_test, order[:2])
+    third, fourth = range_terms(window, range_test, order[2:])
+    halves = jnp.stack([(1 - core) * 2, (1 - core) * 2 + 1, core * 2, core * 2 + 1]).astype(jnp.int32)
+    co_sent, co_kept = co_terms(window, co_test, halves)
+    core_term, left_fold, right_fold = core_terms(window, core_right, core_left, co_test, (first, second, third, fourth), order)
+
+    range_piece = reduce_rows(first, second, third, fourth, "tm")
+    co_piece = co_kept + swap(co_sent, "cell", 1)
+    for group in cell_groups:
+        co_piece = scatter_sum(co_piece, group, 1)
+
+    def own(left, right):
+        return jnp.where(core == 0, left, right)
+
+    fold = own(left_fold, right_fold) + swap(own(right_fold, left_fold), "cell", 1)
+    fold = total_over_chips(fold)
+    other_fold = swap(fold, "cell", 1)
+    left_total, right_total = own(fold, other_fold), own(other_fold, fold)
+    image_inverse, _ = factor_gram(highest(fold, fold, 0, 0))
+
+    middle = high(high(left_total, core_term, 0, 0), right_total)
+    middle = scatter_sum(middle, ("cell", (0,)), 0)
+    middle = gather(total_over_chips(middle), ("cell", (0,)), 0)
+
+    gram_y = highest(range_piece, range_piece, 0, 0) / rows_total
+    gram_w = highest(co_piece, co_piece, 1, 1) / cols_total
+    gram = own(gram_y, gram_w) + swap(own(gram_w, gram_y), "cell", 1)
+    gram = total_over_chips(gram)
+    inverse, upper = factor_gram(gram)
+    other_inverse = swap(inverse, "cell", 1)
+
+    range_full = gather_rows(range_piece, "tm")
+    co_full = co_piece
+    for group in reversed(cell_groups):
+        co_full = gather(co_full, group, 1)
+    co_full = gather(co_full, ("cell", (0,)), 1)
+    range_basis = high(range_full, own(inverse, other_inverse), 1, 1)
+    co_basis = high(own(other_inverse, inverse), co_full)
+
+    flank = highest(highest(upper, image_inverse, 1, 1), image_inverse)
+    other_flank = swap(flank, "cell", 1)
+    core_out = highest(highest(own(flank, other_flank), middle), own(other_flank, flank), 1, 1)
+    return (range_basis, co_basis, core_out * math.sqrt(rows_total * cols_total))
 
 
 def solution(mesh):

time: 211 us -> 184 us (0.87)
  matrix products: 46.3 us -> 9.46 us
  waiting for transfers between devices: 86.3 us -> 52.5 us
  Pallas kernels: 29.4 us -> 58.8 us
  starting transfers between devices: 34.2 us -> 53.2 us
  local copies, waits for them, and re-layouts: 5.55 us -> 1.79 us
    dot_general x20 -> x11, matrix products: 46.3 us -> 9.46 us  [contract(): lax.dot_general(left, right, dims, precision=precision, preferred_element...]
    pallas_call x0 -> x4, Pallas kernels: none -> 34.5 us  [the longest x1 16.6 us: core_terms(): pl.pallas_call(core_kernel, out_shape=(jax.ShapeDtypeStruct((s_core, s_co...]
    ppermute x30 -> x47, waiting for transfers between devices: 86.3 us -> 52.5 us  [swap(): lax.ppermute(values, axis, [(i, i ^ mask) for i in range(lax.axis_size(ax...]
    ppermute x30 -> x47, starting transfers between devices: 34.2 us -> 53.2 us  [swap(): lax.ppermute(values, axis, [(i, i ^ mask) for i in range(lax.axis_size(ax...]
    pallas_call x2, Pallas kernels: 29.4 us -> 24.3 us  [factor_grams(): pl.pallas_call(factor_kernel, out_shape=(jax.ShapeDtypeStruct(grams.shape...]
    dynamic_slice x15 -> x5, local copies, waits for them, and re-layouts: 5.2 us -> 0.18 us  [scatter_sum(): lax.dynamic_slice_in_dim(values, (place ^ peer) * extent, extent, dim)]
    add x15 -> x13, other arithmetic: 4.94 us -> 4.77 us  [the longest x1 1.36 us: per_device(): co_piece = co_kept + swap(co_sent, 'cell', 1)]
  transfers between devices with their start and end apart: 30 -> 47, of which waited for: 13 -> 20; matrix products, arithmetic and copies ran while one was open for 21% -> 7% of each run, Pallas kernels for 7% -> 18%
where the time goes in v2:
time: 184 us
  Pallas kernels  58.8 us (32%)
  starting transfers between devices  53.2 us (29%)
  waiting for transfers between devices  52.5 us (29%)
  matrix products  9.46 us (5%)
  other arithmetic  6.6 us (4%)
    ppermute x47, starting transfers between devices, swap(): lax.ppermute(values, axis, [(i, i ^ mask) for i in range(lax.axis_size(ax...  53.2 us
    ppermute x47, waiting for transfers between devices, swap(): lax.ppermute(values, axis, [(i, i ^ mask) for i in range(lax.axis_size(ax...  52.5 us
    pallas_call x2, Pallas kernels, factor_grams(): pl.pallas_call(factor_kernel, out_shape=(jax.ShapeDtypeStruct(grams.shape...  24.3 us
    pallas_call x1, Pallas kernels, core_terms(): pl.pallas_call(core_kernel, out_shape=(jax.ShapeDtypeStruct((s_core, s_co...  16.6 us
    pallas_call x2, Pallas kernels, range_terms(): pl.pallas_call(range_kernel, out_shape=(out, out), grid_spec=pltpu.Prefet...  9.86 us
    dot_general x11, matrix products, contract(): lax.dot_general(left, right, dims, precision=precision, preferred_element...  9.46 us
    pallas_call x1, Pallas kernels, co_terms(): pl.pallas_call(co_kernel, out_shape=(out, out), grid_spec=pltpu.PrefetchS...  8.04 us
  transfers between devices with their start and end apart: 47, of which 20 were waited for; matrix products, arithmetic and copies ran while one was open for 7% of the time, Pallas kernels for 18%

profile of v2, /device:TPU:0, one launch (start us, length us, event | category | flops | bytes accessed | tf_op | source)
XLA Modules:
  0.0 183.5 jit_solution(15885931796315345044)
XLA Ops:
  0.7 1.6 copy-done
  2.3 4.6 %shard_map.76 = (f32[256,256]{1,0:T(8,128)S(1)}, f32[256,256]{1,0:T(8,128)S(1)}) custom-call(s32[2]{0:T(128)S(1)} %get-tuple-element.65.order_ref, f32[1024,2048]{1,0:T(8,128)} %window_ref.7, f32[2048,256]{1,0:T(8,128)S(1)} %copy-done), custom_call_target="tpu_custom_call" | custom-call | flops 1610612736 | bytes 4194304 | tf_op jit(solution)/shard_map/pallas_call | solution.py:130
  6.9 5.3 %shard_map.77 = (f32[256,256]{1,0:T(8,128)}, f32[256,256]{1,0:T(8,128)}) custom-call(s32[2]{0:T(128)S(1)} %get-tuple-element.66.order_ref, f32[1024,2048]{1,0:T(8,128)} %window_ref.7, f32[2048,256]{1,0:T(8,128)S(1)} %copy-done.1), custom_call_target="tpu_custom_call" | custom-call | flops 1610612736 | bytes 4194304 | tf_op jit(solution)/shard_map/pallas_call | solution.py:130
  12.3 16.6 %shard_map.80 = (f32[512,512]{1,0:T(8,128)S(1)}, f32[512,256]{1,0:T(8,128)S(1)}, f32[512,256]{1,0:T(8,128)S(1)}) custom-call(s32[4]{0:T(128)S(1)} %get-tuple-element.68.order_ref, f32[1024,2048]{1,0:T(8,128)} %window_ref.7, f32[512,2048]{1,0:T(8,128)} %right_ref.1, f32[512,1024]{1,0:T(8,128)} %left_ref.1, f32[256,1024]{1,0:T(8,128)S(1)} %copy-done.4, ...), custom_call_target="tpu_custom_call" | custom-call | flops 9663676416 | bytes 8388608 | tf_op jit(solution)/shard_map/pallas_call | solution.py:213
  28.9 0.9 broadcast_select_fusion.2
  30.3 2.6 %collective-permute-start = (f32[256,256]{1,0:T(8,128)}, f32[256,256]{1,0:T(8,128)}, u32[]{:S(2)}, u32[]{:S(2)}) collective-permute-start(f32[256,256]{1,0:T(8,128)} %get-tuple-element.16.r1_ref), channel_id=1, source_target_pairs={{0,1},{1,0},{2,3},{3,2},{4,5},{5,4},{6,7},{7,6},{8,9},{9,8},{10,11... | collective-permute-start | bytes 786440 | tf_op jit(solution)/shard_map/ppermute | solution.py:39
  32.9 8.0 %shard_map.78 = (f32[256,1024]{1,0:T(8,128)}, f32[256,1024]{1,0:T(8,128)S(1)}) custom-call(s32[4]{0:T(128)S(1)} %get-tuple-element.67.order_ref, f32[1024,2048]{1,0:T(8,128)} %window_ref.7, f32[256,1024]{1,0:T(8,128)S(1)} %copy-done.4), custom_call_target="tpu_custom_call" | custom-call | flops 3221225472 | bytes 8388608 | tf_op jit(solution)/shard_map/pallas_call | solution.py:165
  41.1 4.6 %collective-permute-done.1 = f32[256,256]{1,0:T(8,128)} collective-permute-done((f32[256,256]{1,0:T(8,128)}, f32[256,256]{1,0:T(8,128)}, u32[]{:S(2)}, u32[]{:S(2)}) %collective-permute-start.1) | collective-permute-done | bytes 262176 | tf_op jit(solution)/shard_map/ppermute | solution.py:39
  45.7 1.0 add.171
  46.7 2.8 %collective-permute-start.2 = (f32[256,256]{1,0:T(8,128)S(1)}, f32[256,256]{1,0:T(8,128)S(1)}, u32[]{:S(2)}, u32[]{:S(2)}) collective-permute-start(f32[256,256]{1,0:T(8,128)S(1)} %add.171), channel_id=1, source_target_pairs={{0,2},{1,3},{2,0},{3,1},{4,6},{5,7},{6,4},{7,5},{8,10},{9,11},{10,... | collective-permute-start | bytes 786440 | tf_op jit(solution)/shard_map/ppermute | solution.py:39
  49.5 1.1 select_add_fusion
  50.7 1.6 collective-permute-start.25
  52.3 1.5 collective-permute-start.27
  54.3 7.2 %collective-permute-done.2 = f32[256,256]{1,0:T(8,128)S(1)} collective-permute-done((f32[256,256]{1,0:T(8,128)S(1)}, f32[256,256]{1,0:T(8,128)S(1)}, u32[]{:S(2)}, u32[]{:S(2)}) %collective-permute-start.2) | collective-permute-done | bytes 262176 | tf_op jit(solution)/shard_map/ppermute | solution.py:39
  61.5 1.0 add_add_fusion.1
  62.6 3.5 %collective-permute-start.30 = (f32[128,256]{1,0:T(8,128)S(1)}, f32[128,256]{1,0:T(8,128)S(1)}, u32[]{:S(2)}, u32[]{:S(2)}) collective-permute-start(f32[128,256]{1,0:T(8,128)S(1)} %add_add_fusion.3), channel_id=1, source_target_pairs={{0,3},{1,2},{2,1},{3,0},{4,7},{5,6},{6,5},{7,4},{8,11},{9,10},{10,... | collective-permute-start | bytes 393224 | tf_op jit(solution)/shard_map/ppermute | solution.py:39
  66.1 2.0 %collective-permute-start.29 = (f32[128,256]{1,0:T(8,128)S(1)}, f32[128,256]{1,0:T(8,128)S(1)}, u32[]{:S(2)}, u32[]{:S(2)}) collective-permute-start(f32[128,256]{1,0:T(8,128)S(1)} %add_add_fusion.3), channel_id=1, source_target_pairs={{0,2},{1,3},{2,0},{3,1},{4,6},{5,7},{6,4},{7,5},{8,10},{9,11},{10,... | collective-permute-start | bytes 393224 | tf_op jit(solution)/shard_map/ppermute | solution.py:39
  68.7 7.3 %collective-permute-done.30 = f32[128,256]{1,0:T(8,128)S(1)} collective-permute-done((f32[128,256]{1,0:T(8,128)S(1)}, f32[128,256]{1,0:T(8,128)S(1)}, u32[]{:S(2)}, u32[]{:S(2)}) %collective-permute-start.30) | collective-permute-done | bytes 131104 | tf_op jit(solution)/shard_map/ppermute | solution.py:39
  76.0 11.6 %collective-permute-done.29 = f32[128,256]{1,0:T(8,128)S(1)} collective-permute-done((f32[128,256]{1,0:T(8,128)S(1)}, f32[128,256]{1,0:T(8,128)S(1)}, u32[]{:S(2)}, u32[]{:S(2)}) %collective-permute-start.29) | collective-permute-done | bytes 131104 | tf_op jit(solution)/shard_map/ppermute | solution.py:39
  87.6 1.4 collective-permute-start.33
  89.1 1.5 collective-permute-start.32
  90.6 0.6 collective-permute-start.31
  91.4 1.8 collective-permute-done.33
  93.2 1.2 collective-permute-done.32
  94.4 2.1 %collective-permute-done.31 = f32[128,256]{1,0:T(8,128)S(1)} collective-permute-done((f32[128,256]{1,0:T(8,128)S(1)}, f32[128,256]{1,0:T(8,128)S(1)}, u32[]{:S(2)}, u32[]{:S(2)}) %collective-permute-start.31) | collective-permute-done | bytes 131104 | tf_op jit(solution)/shard_map/ppermute | solution.py:39
  96.6 1.0 convolution_bitcast_fusion.gram_ref
  97.7 1.4 add.176
  99.7 1.4 collective-permute-start.8
  101.2 1.5 collective-permute-start.7
  102.7 12.6 %shard_map.81 = (f32[1,256,256]{2,1,0:T(8,128)S(1)}, f32[1,256,256]{2,1,0:T(8,128)}) custom-call(f32[1,256,256]{2,1,0:T(8,128)S(1)} %convolution_bitcast_fusion.gram_ref), custom_call_target="tpu_custom_call" | custom-call | flops 3355443200 | bytes 786432 | tf_op jit(solution)/shard_map/pallas_call | solution.py:329
  115.4 0.6 collective-permute-start.22
  116.0 1.2 collective-permute-start.21
  117.1 1.8 collective-permute-start.20
  118.9 0.6 fusion.10
  120.5 0.9 collective-permute-done.36
  121.6 1.3 collective-permute-done.9
  123.6 1.1 collective-permute-done.22
  124.7 1.2 collective-permute-start.39
  125.8 1.6 collective-permute-done.21
  127.5 2.3 %collective-permute-done.20 = f32[256,256]{1,0:T(8,128)S(1)} collective-permute-done((f32[256,256]{1,0:T(8,128)S(1)}, f32[256,256]{1,0:T(8,128)S(1)}, u32[]{:S(2)}, u32[]{:S(2)}) %collective-permute-start.20) | collective-permute-done | bytes 262176 | tf_op jit(solution)/shard_map/ppermute | solution.py:39
  129.7 2.0 %collective-permute-start.10 = (f32[64,256]{1,0:T(8,128)S(1)}, f32[64,256]{1,0:T(8,128)S(1)}, u32[]{:S(2)}, u32[]{:S(2)}) collective-permute-start(f32[64,256]{1,0:T(8,128)S(1)} %get-tuple-element.53), channel_id=1, source_target_pairs={{0,8},{4,12},{8,0},{12,4},{16,24},{20,28},{24,16},{28,20},{1,9},{5... | collective-permute-start | bytes 196616 | tf_op jit(solution)/shard_map/ppermute | solution.py:39
  131.9 3.3 %collective-permute-start.42 = (f32[32,256]{1,0:T(8,128)S(1)}, f32[32,256]{1,0:T(8,128)S(1)}, u32[]{:S(2)}, u32[]{:S(2)}) collective-permute-start(f32[32,256]{1,0:T(8,128)S(1)} %add_add_fusion.7), channel_id=1, source_target_pairs={{0,3},{1,2},{2,1},{3,0},{4,7},{5,6},{6,5},{7,4},{8,11},{9,10},{10,... | collective-permute-start | bytes 98312 | tf_op jit(solution)/shard_map/ppermute | solution.py:39
  135.2 1.2 collective-permute-start.40
  136.5 1.2 collective-permute-done.42
  137.7 3.2 %collective-permute-start.12 = (f32[64,256]{1,0:T(8,128)S(1)}, f32[64,256]{1,0:T(8,128)S(1)}, u32[]{:S(2)}, u32[]{:S(2)}) collective-permute-start(f32[64,256]{1,0:T(8,128)S(1)} %get-tuple-element.54), channel_id=1, source_target_pairs={{0,24},{4,28},{8,16},{12,20},{16,8},{20,12},{24,0},{28,4},{1,25},{... | collective-permute-start | bytes 196616 | tf_op jit(solution)/shard_map/ppermute | solution.py:39
  140.9 2.0 %collective-permute-start.11 = (f32[64,256]{1,0:T(8,128)S(1)}, f32[64,256]{1,0:T(8,128)S(1)}, u32[]{:S(2)}, u32[]{:S(2)}) collective-permute-start(f32[64,256]{1,0:T(8,128)S(1)} %get-tuple-element.55), channel_id=1, source_target_pairs={{0,16},{4,20},{8,24},{12,28},{16,0},{20,4},{24,8},{28,12},{1,17},{... | collective-permute-start | bytes 196616 | tf_op jit(solution)/shard_map/ppermute | solution.py:39
  142.9 0.9 collective-permute-start.45
  143.9 1.3 collective-permute-start.44
  145.1 3.0 %collective-permute-start.43 = (f32[32,256]{1,0:T(8,128)S(1)}, f32[32,256]{1,0:T(8,128)S(1)}, u32[]{:S(2)}, u32[]{:S(2)}) collective-permute-start(f32[32,256]{1,0:T(8,128)S(1)} %add_add_fusion.6), channel_id=1, source_target_pairs={{0,24},{4,28},{8,16},{12,20},{16,8},{20,12},{24,0},{28,4},{1,25},{... | collective-permute-start | bytes 98312 | tf_op jit(solution)/shard_map/ppermute | solution.py:39
  148.2 1.6 collective-permute-start.15
  150.1 2.6 %collective-permute-start.13 = (f32[64,256]{1,0:T(8,128)S(1)}, f32[64,256]{1,0:T(8,128)S(1)}, u32[]{:S(2)}, u32[]{:S(2)}) collective-permute-start(f32[64,256]{1,0:T(8,128)S(1)} %add_add_fusion.5), channel_id=1, source_target_pairs={{0,1},{1,0},{2,3},{3,2},{4,5},{5,4},{6,7},{7,6},{8,9},{9,8},{10,11... | collective-permute-start | bytes 196616 | tf_op jit(solution)/shard_map/ppermute | solution.py:39
  152.7 1.7 collective-permute-done.15
  154.3 1.4 collective-permute-done.14
  155.8 1.2 collective-permute-start.18
  157.0 1.3 collective-permute-start.17
  158.3 1.0 collective-permute-start.16
  159.3 0.8 collective-permute-done.18
  160.1 1.2 collective-permute-done.17
  161.2 2.2 %collective-permute-done.16 = f32[64,256]{1,0:T(8,128)S(1)} collective-permute-done((f32[64,256]{1,0:T(8,128)S(1)}, f32[64,256]{1,0:T(8,128)S(1)}, u32[]{:S(2)}, u32[]{:S(2)}) %collective-permute-start.16) | collective-permute-done | bytes 65568 | tf_op jit(solution)/shard_map/ppermute | solution.py:39
  163.5 11.7 %shard_map.79 = (f32[1,256,256]{2,1,0:T(8,128)S(1)}, f32[1,256,256]{2,1,0:T(8,128)S(1)}) custom-call(f32[1,256,256]{2,1,0:T(8,128)S(1)} %maximum_bitcast_fusion.gram_ref), custom_call_target="tpu_custom_call" | custom-call | flops 3355443200 | bytes 786432 | tf_op jit(solution)/shard_map/pallas_call | solution.py:329
  176.8 0.9 collective-permute-done.34
  178.1 1.1 convolution_multiply_fusion
  179.2 1.6 fusion.4
  181.0 2.5 %fusion = f32[256,2048]{1,0:T(8,128)} fusion(f32[256,1024]{1,0:T(8,128)S(1)} %get-tuple-element.28, f32[256,1024]{1,0:T(8,128)S(1)} %get-tuple-element.27, f32[256,256]{1,0:T(8,128)S(1)} %collective-permute-done.19, pred[]{:T(512)S(6)} %eq.16, f32[1,256,256]{2,1,0:T(8,128)S(1)} %get-tuple-element.21), kind=kOutput, calls=%fused_computation | convolution fusion | flops 805896192 | bytes 4718593 | tf_op jit(solution)/shard_map/dot_general | solution.py:18
  (91 shorter events, 7.8 us)
Async XLA Ops:
  0.7 1.6 copy-start
  2.3 4.6 %copy-start.1 = (f32[2048,256]{1,0:T(8,128)S(1)}, f32[2048,256]{1,0:T(8,128)}, u32[]{:S(2)}) copy-start(f32[2048,256]{1,0:T(8,128)} %test_ref.4) | copy-start | bytes 6291460
  6.9 5.4 %copy-start.2 = (f32[256,256]{1,0:T(8,128)}, f32[256,256]{1,0:T(8,128)S(1)}, u32[]{:S(2)}) copy-start(f32[256,256]{1,0:T(8,128)S(1)} %get-tuple-element.15.r3_ref) | copy-start | bytes 786436
  6.9 5.4 %copy-start.4 = (f32[256,1024]{1,0:T(8,128)S(1)}, f32[256,1024]{1,0:T(8,128)}, u32[]{:S(2)}) copy-start(f32[256,1024]{1,0:T(8,128)} %co_ref.1) | copy-start | bytes 3145732
  29.8 19.7 %collective-permute-start.24 = (f32[512,256]{1,0:T(8,128)}, f32[512,256]{1,0:T(8,128)}, u32[]{:S(2)}, u32[]{:S(2)}) collective-permute-start(f32[512,256]{1,0:T(8,128)} %broadcast_select_fusion.2), channel_id=1, source_target_pairs={{0,4},{4,0},{8,12},{12,8},{16,20},{20,16},{24,28},{28,24},{1,5},{5... | collective-permute-start | bytes 1572872 | tf_op jit(solution)/shard_map/ppermute | solution.py:39
  30.3 23.5 %collective-permute-start = (f32[256,256]{1,0:T(8,128)}, f32[256,256]{1,0:T(8,128)}, u32[]{:S(2)}, u32[]{:S(2)}) collective-permute-start(f32[256,256]{1,0:T(8,128)} %get-tuple-element.16.r1_ref), channel_id=1, source_target_pairs={{0,1},{1,0},{2,3},{3,2},{4,5},{5,4},{6,7},{7,6},{8,9},{9,8},{10,11... | collective-permute-start | bytes 786440 | tf_op jit(solution)/shard_map/ppermute | solution.py:39
  32.8 12.9 %collective-permute-start.1 = (f32[256,256]{1,0:T(8,128)}, f32[256,256]{1,0:T(8,128)}, u32[]{:S(2)}, u32[]{:S(2)}) collective-permute-start(f32[256,256]{1,0:T(8,128)} %get-tuple-element.18.r0_ref), channel_id=1, source_target_pairs={{0,1},{1,0},{2,3},{3,2},{4,5},{5,4},{6,7},{7,6},{8,9},{9,8},{10,11... | collective-permute-start | bytes 786440 | tf_op jit(solution)/shard_map/ppermute | solution.py:39
  40.9 56.8 %collective-permute-start.5 = (f32[256,1024]{1,0:T(8,128)}, f32[256,1024]{1,0:T(8,128)}, u32[]{:S(2)}, u32[]{:S(2)}) collective-permute-start(f32[256,1024]{1,0:T(8,128)} %get-tuple-element.20), channel_id=1, source_target_pairs={{0,4},{4,0},{8,12},{12,8},{16,20},{20,16},{24,28},{28,24},{1,5},{5... | collective-permute-start | bytes 3145736 | tf_op jit(solution)/shard_map/ppermute | solution.py:39
  41.1 20.3 %copy-start.3 = (f32[256,256]{1,0:T(8,128)S(1)}, f32[256,256]{1,0:T(8,128)}, u32[]{:S(2)}) copy-start(f32[256,256]{1,0:T(8,128)} %copy-done.2) | copy-start | bytes 786436
  46.7 14.7 %collective-permute-start.2 = (f32[256,256]{1,0:T(8,128)S(1)}, f32[256,256]{1,0:T(8,128)S(1)}, u32[]{:S(2)}, u32[]{:S(2)}) collective-permute-start(f32[256,256]{1,0:T(8,128)S(1)} %add.171), channel_id=1, source_target_pairs={{0,2},{1,3},{2,0},{3,1},{4,6},{5,7},{6,4},{7,5},{8,10},{9,11},{10,... | collective-permute-start | bytes 786440 | tf_op jit(solution)/shard_map/ppermute | solution.py:39
  50.7 11.8 %collective-permute-start.25 = (f32[128,256]{1,0:T(8,128)S(1)}, f32[128,256]{1,0:T(8,128)S(1)}, u32[]{:S(2)}, u32[]{:S(2)}) collective-permute-start(f32[128,256]{1,0:T(8,128)S(1)} %get-tuple-element.42), channel_id=1, source_target_pairs={{0,8},{4,12},{8,0},{12,4},{16,24},{20,28},{24,16},{28,20},{1,9},{5... | collective-permute-start | bytes 393224 | tf_op jit(solution)/shard_map/ppermute | solution.py:39
  52.3 10.2 %collective-permute-start.27 = (f32[128,256]{1,0:T(8,128)S(1)}, f32[128,256]{1,0:T(8,128)S(1)}, u32[]{:S(2)}, u32[]{:S(2)}) collective-permute-start(f32[128,256]{1,0:T(8,128)S(1)} %get-tuple-element.43), channel_id=1, source_target_pairs={{0,24},{4,28},{8,16},{12,20},{16,8},{20,12},{24,0},{28,4},{1,25},{... | collective-permute-start | bytes 393224 | tf_op jit(solution)/shard_map/ppermute | solution.py:39
  53.8 8.8 %collective-permute-start.26 = (f32[128,256]{1,0:T(8,128)S(1)}, f32[128,256]{1,0:T(8,128)S(1)}, u32[]{:S(2)}, u32[]{:S(2)}) collective-permute-start(f32[128,256]{1,0:T(8,128)S(1)} %get-tuple-element.44), channel_id=1, source_target_pairs={{0,16},{4,20},{8,24},{12,28},{16,0},{20,4},{24,8},{28,12},{1,17},{... | collective-permute-start | bytes 393224 | tf_op jit(solution)/shard_map/ppermute | solution.py:39
  62.5 28.7 %collective-permute-start.3 = (f32[256,256]{1,0:T(8,128)S(1)}, f32[256,256]{1,0:T(8,128)S(1)}, u32[]{:S(2)}, u32[]{:S(2)}) collective-permute-start(f32[256,256]{1,0:T(8,128)S(1)} %add_add_fusion.1), channel_id=1, source_target_pairs={{0,2},{1,3},{2,0},{3,1},{4,6},{5,7},{6,4},{7,5},{8,10},{9,11},{10,... | collective-permute-start | bytes 786440 | tf_op jit(solution)/shard_map/ppermute | solution.py:39
  62.6 13.4 %collective-permute-start.30 = (f32[128,256]{1,0:T(8,128)S(1)}, f32[128,256]{1,0:T(8,128)S(1)}, u32[]{:S(2)}, u32[]{:S(2)}) collective-permute-start(f32[128,256]{1,0:T(8,128)S(1)} %add_add_fusion.3), channel_id=1, source_target_pairs={{0,3},{1,2},{2,1},{3,0},{4,7},{5,6},{6,5},{7,4},{8,11},{9,10},{10,... | collective-permute-start | bytes 393224 | tf_op jit(solution)/shard_map/ppermute | solution.py:39
  66.1 21.5 %collective-permute-start.29 = (f32[128,256]{1,0:T(8,128)S(1)}, f32[128,256]{1,0:T(8,128)S(1)}, u32[]{:S(2)}, u32[]{:S(2)}) collective-permute-start(f32[128,256]{1,0:T(8,128)S(1)} %add_add_fusion.3), channel_id=1, source_target_pairs={{0,2},{1,3},{2,0},{3,1},{4,6},{5,7},{6,4},{7,5},{8,10},{9,11},{10,... | collective-permute-start | bytes 393224 | tf_op jit(solution)/shard_map/ppermute | solution.py:39
  68.1 19.5 %collective-permute-start.28 = (f32[128,256]{1,0:T(8,128)S(1)}, f32[128,256]{1,0:T(8,128)S(1)}, u32[]{:S(2)}, u32[]{:S(2)}) collective-permute-start(f32[128,256]{1,0:T(8,128)S(1)} %add_add_fusion.3), channel_id=1, source_target_pairs={{0,1},{1,0},{2,3},{3,2},{4,5},{5,4},{6,7},{7,6},{8,9},{9,8},{10,11... | collective-permute-start | bytes 393224 | tf_op jit(solution)/shard_map/ppermute | solution.py:39
  87.6 5.5 %collective-permute-start.33 = (f32[128,256]{1,0:T(8,128)S(1)}, f32[128,256]{1,0:T(8,128)S(1)}, u32[]{:S(2)}, u32[]{:S(2)}) collective-permute-start(f32[128,256]{1,0:T(8,128)S(1)} %add_add_fusion.2), channel_id=1, source_target_pairs={{0,8},{4,12},{8,0},{12,4},{16,24},{20,28},{24,16},{28,20},{1,9},{5... | collective-permute-start | bytes 393224 | tf_op jit(solution)/shard_map/ppermute | solution.py:39
  89.1 5.3 %collective-permute-start.32 = (f32[128,256]{1,0:T(8,128)S(1)}, f32[128,256]{1,0:T(8,128)S(1)}, u32[]{:S(2)}, u32[]{:S(2)}) collective-permute-start(f32[128,256]{1,0:T(8,128)S(1)} %add_add_fusion.2), channel_id=1, source_target_pairs={{0,16},{4,20},{8,24},{12,28},{16,0},{20,4},{24,8},{28,12},{1,17},{... | collective-permute-start | bytes 393224 | tf_op jit(solution)/shard_map/ppermute | solution.py:39
  90.6 5.9 %collective-permute-start.31 = (f32[128,256]{1,0:T(8,128)S(1)}, f32[128,256]{1,0:T(8,128)S(1)}, u32[]{:S(2)}, u32[]{:S(2)}) collective-permute-start(f32[128,256]{1,0:T(8,128)S(1)} %add_add_fusion.2), channel_id=1, source_target_pairs={{0,24},{4,28},{8,16},{12,20},{16,8},{20,12},{24,0},{28,4},{1,25},{... | collective-permute-start | bytes 393224 | tf_op jit(solution)/shard_map/ppermute | solution.py:39
  91.3 84.9 %collective-permute-start.4 = (f32[512,256]{1,0:T(8,128)S(1)}, f32[512,256]{1,0:T(8,128)S(1)}, u32[]{:S(2)}, u32[]{:S(2)}) collective-permute-start(f32[512,256]{1,0:T(8,128)S(1)} %pad_maximum_fusion.1), channel_id=1, source_target_pairs={{0,1},{1,0},{2,3},{3,2},{4,5},{5,4},{6,7},{7,6},{8,9},{9,8},{10,11... | collective-permute-start | bytes 1572872 | tf_op jit(solution)/shard_map/ppermute | solution.py:39
  96.6 22.4 %collective-permute-start.35 = (f32[512,256]{1,0:T(8,128)S(1)}, f32[512,256]{1,0:T(8,128)S(1)}, u32[]{:S(2)}, u32[]{:S(2)}) collective-permute-start(f32[512,256]{1,0:T(8,128)S(1)} %pad_maximum_fusion.2), channel_id=1, source_target_pairs={{0,4},{4,0},{8,12},{12,8},{16,20},{20,16},{24,28},{28,24},{1,5},{5... | collective-permute-start | bytes 1572872 | tf_op jit(solution)/shard_map/ppermute | solution.py:39
  99.1 16.1 %collective-permute-start.6 = (f32[256,256]{1,0:T(8,128)S(1)}, f32[256,256]{1,0:T(8,128)S(1)}, u32[]{:S(2)}, u32[]{:S(2)}) collective-permute-start(f32[256,256]{1,0:T(8,128)S(1)} %get-tuple-element.33), channel_id=1, source_target_pairs={{0,8},{4,12},{8,0},{12,4},{16,24},{20,28},{24,16},{28,20},{1,9},{5... | collective-permute-start | bytes 786440 | tf_op jit(solution)/shard_map/ppermute | solution.py:39
  99.7 15.5 %collective-permute-start.8 = (f32[256,256]{1,0:T(8,128)S(1)}, f32[256,256]{1,0:T(8,128)S(1)}, u32[]{:S(2)}, u32[]{:S(2)}) collective-permute-start(f32[256,256]{1,0:T(8,128)S(1)} %get-tuple-element.34), channel_id=1, source_target_pairs={{0,24},{4,28},{8,16},{12,20},{16,8},{20,12},{24,0},{28,4},{1,25},{... | collective-permute-start | bytes 786440 | tf_op jit(solution)/shard_map/ppermute | solution.py:39
  101.2 14.1 %collective-permute-start.7 = (f32[256,256]{1,0:T(8,128)S(1)}, f32[256,256]{1,0:T(8,128)S(1)}, u32[]{:S(2)}, u32[]{:S(2)}) collective-permute-start(f32[256,256]{1,0:T(8,128)S(1)} %get-tuple-element.35), channel_id=1, source_target_pairs={{0,16},{4,20},{8,24},{12,28},{16,0},{20,4},{24,8},{28,12},{1,17},{... | collective-permute-start | bytes 786440 | tf_op jit(solution)/shard_map/ppermute | solution.py:39
  115.4 9.3 %collective-permute-start.22 = (f32[256,256]{1,0:T(8,128)S(1)}, f32[256,256]{1,0:T(8,128)S(1)}, u32[]{:S(2)}, u32[]{:S(2)}) collective-permute-start(f32[256,256]{1,0:T(8,128)S(1)} %add_add_fusion), channel_id=1, source_target_pairs={{0,8},{4,12},{8,0},{12,4},{16,24},{20,28},{24,16},{28,20},{1,9},{5... | collective-permute-start | bytes 786440 | tf_op jit(solution)/shard_map/ppermute | solution.py:39
  116.0 11.5 %collective-permute-start.21 = (f32[256,256]{1,0:T(8,128)S(1)}, f32[256,256]{1,0:T(8,128)S(1)}, u32[]{:S(2)}, u32[]{:S(2)}) collective-permute-start(f32[256,256]{1,0:T(8,128)S(1)} %add_add_fusion), channel_id=1, source_target_pairs={{0,16},{4,20},{8,24},{12,28},{16,0},{20,4},{24,8},{28,12},{1,17},{... | collective-permute-start | bytes 786440 | tf_op jit(solution)/shard_map/ppermute | solution.py:39
  117.1 12.6 %collective-permute-start.20 = (f32[256,256]{1,0:T(8,128)S(1)}, f32[256,256]{1,0:T(8,128)S(1)}, u32[]{:S(2)}, u32[]{:S(2)}) collective-permute-start(f32[256,256]{1,0:T(8,128)S(1)} %add_add_fusion), channel_id=1, source_target_pairs={{0,24},{4,28},{8,16},{12,20},{16,8},{20,12},{24,0},{28,4},{1,25},{... | collective-permute-start | bytes 786440 | tf_op jit(solution)/shard_map/ppermute | solution.py:39
  120.0 1.4 collective-permute-start.36
  121.4 1.5 collective-permute-start.9
  123.0 8.9 %collective-permute-start.37 = (f32[32,256]{1,0:T(8,128)S(1)}, f32[32,256]{1,0:T(8,128)S(1)}, u32[]{:S(2)}, u32[]{:S(2)}) collective-permute-start(f32[32,256]{1,0:T(8,128)S(1)} %get-tuple-element.60), channel_id=1, source_target_pairs={{0,8},{4,12},{8,0},{12,4},{16,24},{20,28},{24,16},{28,20},{1,9},{5... | collective-permute-start | bytes 98312 | tf_op jit(solution)/shard_map/ppermute | solution.py:39
  124.7 7.2 %collective-permute-start.39 = (f32[32,256]{1,0:T(8,128)S(1)}, f32[32,256]{1,0:T(8,128)S(1)}, u32[]{:S(2)}, u32[]{:S(2)}) collective-permute-start(f32[32,256]{1,0:T(8,128)S(1)} %get-tuple-element.61), channel_id=1, source_target_pairs={{0,24},{4,28},{8,16},{12,20},{16,8},{20,12},{24,0},{28,4},{1,25},{... | collective-permute-start | bytes 98312 | tf_op jit(solution)/shard_map/ppermute | solution.py:39
  127.5 4.4 %collective-permute-start.38 = (f32[32,256]{1,0:T(8,128)S(1)}, f32[32,256]{1,0:T(8,128)S(1)}, u32[]{:S(2)}, u32[]{:S(2)}) collective-permute-start(f32[32,256]{1,0:T(8,128)S(1)} %get-tuple-element.62), channel_id=1, source_target_pairs={{0,16},{4,20},{8,24},{12,28},{16,0},{20,4},{24,8},{28,12},{1,17},{... | collective-permute-start | bytes 98312 | tf_op jit(solution)/shard_map/ppermute | solution.py:39
  129.7 13.2 %collective-permute-start.10 = (f32[64,256]{1,0:T(8,128)S(1)}, f32[64,256]{1,0:T(8,128)S(1)}, u32[]{:S(2)}, u32[]{:S(2)}) collective-permute-start(f32[64,256]{1,0:T(8,128)S(1)} %get-tuple-element.53), channel_id=1, source_target_pairs={{0,8},{4,12},{8,0},{12,4},{16,24},{20,28},{24,16},{28,20},{1,9},{5... | collective-permute-start | bytes 196616 | tf_op jit(solution)/shard_map/ppermute | solution.py:39
  131.9 5.8 %collective-permute-start.42 = (f32[32,256]{1,0:T(8,128)S(1)}, f32[32,256]{1,0:T(8,128)S(1)}, u32[]{:S(2)}, u32[]{:S(2)}) collective-permute-start(f32[32,256]{1,0:T(8,128)S(1)} %add_add_fusion.7), channel_id=1, source_target_pairs={{0,3},{1,2},{2,1},{3,0},{4,7},{5,6},{6,5},{7,4},{8,11},{9,10},{10,... | collective-permute-start | bytes 98312 | tf_op jit(solution)/shard_map/ppermute | solution.py:39
  135.2 5.7 %collective-permute-start.41 = (f32[32,256]{1,0:T(8,128)S(1)}, f32[32,256]{1,0:T(8,128)S(1)}, u32[]{:S(2)}, u32[]{:S(2)}) collective-permute-start(f32[32,256]{1,0:T(8,128)S(1)} %add_add_fusion.7), channel_id=1, source_target_pairs={{0,2},{1,3},{2,0},{3,1},{4,6},{5,7},{6,4},{7,5},{8,10},{9,11},{10,... | collective-permute-start | bytes 98312 | tf_op jit(solution)/shard_map/ppermute | solution.py:39
  135.2 7.7 %collective-permute-start.40 = (f32[32,256]{1,0:T(8,128)S(1)}, f32[32,256]{1,0:T(8,128)S(1)}, u32[]{:S(2)}, u32[]{:S(2)}) collective-permute-start(f32[32,256]{1,0:T(8,128)S(1)} %add_add_fusion.7), channel_id=1, source_target_pairs={{0,1},{1,0},{2,3},{3,2},{4,5},{5,4},{6,7},{7,6},{8,9},{9,8},{10,11... | collective-permute-start | bytes 98312 | tf_op jit(solution)/shard_map/ppermute | solution.py:39
  137.7 6.2 %collective-permute-start.12 = (f32[64,256]{1,0:T(8,128)S(1)}, f32[64,256]{1,0:T(8,128)S(1)}, u32[]{:S(2)}, u32[]{:S(2)}) collective-permute-start(f32[64,256]{1,0:T(8,128)S(1)} %get-tuple-element.54), channel_id=1, source_target_pairs={{0,24},{4,28},{8,16},{12,20},{16,8},{20,12},{24,0},{28,4},{1,25},{... | collective-permute-start | bytes 196616 | tf_op jit(solution)/shard_map/ppermute | solution.py:39
  140.9 4.3 %collective-permute-start.11 = (f32[64,256]{1,0:T(8,128)S(1)}, f32[64,256]{1,0:T(8,128)S(1)}, u32[]{:S(2)}, u32[]{:S(2)}) collective-permute-start(f32[64,256]{1,0:T(8,128)S(1)} %get-tuple-element.55), channel_id=1, source_target_pairs={{0,16},{4,20},{8,24},{12,28},{16,0},{20,4},{24,8},{28,12},{1,17},{... | collective-permute-start | bytes 196616 | tf_op jit(solution)/shard_map/ppermute | solution.py:39
  142.9 37.9 %collective-permute-start.23 = (f32[256,1024]{1,0:T(8,128)S(1)}, f32[256,1024]{1,0:T(8,128)S(1)}, u32[]{:S(2)}, u32[]{:S(2)}) collective-permute-start(f32[256,1024]{1,0:T(8,128)S(1)} %pad_maximum_fusion), channel_id=1, source_target_pairs={{0,4},{4,0},{8,12},{12,8},{16,20},{20,16},{24,28},{28,24},{1,5},{5... | collective-permute-start | bytes 3145736 | tf_op jit(solution)/shard_map/ppermute | solution.py:39
  142.9 5.3 %collective-permute-start.45 = (f32[32,256]{1,0:T(8,128)S(1)}, f32[32,256]{1,0:T(8,128)S(1)}, u32[]{:S(2)}, u32[]{:S(2)}) collective-permute-start(f32[32,256]{1,0:T(8,128)S(1)} %add_add_fusion.6), channel_id=1, source_target_pairs={{0,8},{4,12},{8,0},{12,4},{16,24},{20,28},{24,16},{28,20},{1,9},{5... | collective-permute-start | bytes 98312 | tf_op jit(solution)/shard_map/ppermute | solution.py:39
  143.9 5.9 %collective-permute-start.44 = (f32[32,256]{1,0:T(8,128)S(1)}, f32[32,256]{1,0:T(8,128)S(1)}, u32[]{:S(2)}, u32[]{:S(2)}) collective-permute-start(f32[32,256]{1,0:T(8,128)S(1)} %add_add_fusion.6), channel_id=1, source_target_pairs={{0,16},{4,20},{8,24},{12,28},{16,0},{20,4},{24,8},{28,12},{1,17},{... | collective-permute-start | bytes 98312 | tf_op jit(solution)/shard_map/ppermute | solution.py:39
  145.1 4.9 %collective-permute-start.43 = (f32[32,256]{1,0:T(8,128)S(1)}, f32[32,256]{1,0:T(8,128)S(1)}, u32[]{:S(2)}, u32[]{:S(2)}) collective-permute-start(f32[32,256]{1,0:T(8,128)S(1)} %add_add_fusion.6), channel_id=1, source_target_pairs={{0,24},{4,28},{8,16},{12,20},{16,8},{20,12},{24,0},{28,4},{1,25},{... | collective-permute-start | bytes 98312 | tf_op jit(solution)/shard_map/ppermute | solution.py:39
  148.2 6.1 %collective-permute-start.15 = (f32[64,256]{1,0:T(8,128)S(1)}, f32[64,256]{1,0:T(8,128)S(1)}, u32[]{:S(2)}, u32[]{:S(2)}) collective-permute-start(f32[64,256]{1,0:T(8,128)S(1)} %add_add_fusion.5), channel_id=1, source_target_pairs={{0,3},{1,2},{2,1},{3,0},{4,7},{5,6},{6,5},{7,4},{8,11},{9,10},{10,... | collective-permute-start | bytes 196616 | tf_op jit(solution)/shard_map/ppermute | solution.py:39
  149.8 6.0 %collective-permute-start.14 = (f32[64,256]{1,0:T(8,128)S(1)}, f32[64,256]{1,0:T(8,128)S(1)}, u32[]{:S(2)}, u32[]{:S(2)}) collective-permute-start(f32[64,256]{1,0:T(8,128)S(1)} %add_add_fusion.5), channel_id=1, source_target_pairs={{0,2},{1,3},{2,0},{3,1},{4,6},{5,7},{6,4},{7,5},{8,10},{9,11},{10,... | collective-permute-start | bytes 196616 | tf_op jit(solution)/shard_map/ppermute | solution.py:39
  150.1 5.7 %collective-permute-start.13 = (f32[64,256]{1,0:T(8,128)S(1)}, f32[64,256]{1,0:T(8,128)S(1)}, u32[]{:S(2)}, u32[]{:S(2)}) collective-permute-start(f32[64,256]{1,0:T(8,128)S(1)} %add_add_fusion.5), channel_id=1, source_target_pairs={{0,1},{1,0},{2,3},{3,2},{4,5},{5,4},{6,7},{7,6},{8,9},{9,8},{10,11... | collective-permute-start | bytes 196616 | tf_op jit(solution)/shard_map/ppermute | solution.py:39
  155.8 4.3 %collective-permute-start.18 = (f32[64,256]{1,0:T(8,128)S(1)}, f32[64,256]{1,0:T(8,128)S(1)}, u32[]{:S(2)}, u32[]{:S(2)}) collective-permute-start(f32[64,256]{1,0:T(8,128)S(1)} %add_add_fusion.4), channel_id=1, source_target_pairs={{0,8},{4,12},{8,0},{12,4},{16,24},{20,28},{24,16},{28,20},{1,9},{5... | collective-permute-start | bytes 196616 | tf_op jit(solution)/shard_map/ppermute | solution.py:39
  157.0 4.3 %collective-permute-start.17 = (f32[64,256]{1,0:T(8,128)S(1)}, f32[64,256]{1,0:T(8,128)S(1)}, u32[]{:S(2)}, u32[]{:S(2)}) collective-permute-start(f32[64,256]{1,0:T(8,128)S(1)} %add_add_fusion.4), channel_id=1, source_target_pairs={{0,16},{4,20},{8,24},{12,28},{16,0},{20,4},{24,8},{28,12},{1,17},{... | collective-permute-start | bytes 196616 | tf_op jit(solution)/shard_map/ppermute | solution.py:39
  158.3 5.2 %collective-permute-start.16 = (f32[64,256]{1,0:T(8,128)S(1)}, f32[64,256]{1,0:T(8,128)S(1)}, u32[]{:S(2)}, u32[]{:S(2)}) collective-permute-start(f32[64,256]{1,0:T(8,128)S(1)} %add_add_fusion.4), channel_id=1, source_target_pairs={{0,24},{4,28},{8,16},{12,20},{16,8},{20,12},{24,0},{28,4},{1,25},{... | collective-permute-start | bytes 196616 | tf_op jit(solution)/shard_map/ppermute | solution.py:39
  160.1 16.7 %collective-permute-start.46 = (f32[128,256]{1,0:T(8,128)S(1)}, f32[128,256]{1,0:T(8,128)S(1)}, u32[]{:S(2)}, u32[]{:S(2)}) collective-permute-start(f32[128,256]{1,0:T(8,128)S(1)} %pad_maximum_fusion.3), channel_id=1, source_target_pairs={{0,4},{4,0},{8,12},{12,8},{16,20},{20,16},{24,28},{28,24},{1,5},{5... | collective-permute-start | bytes 393224 | tf_op jit(solution)/shard_map/ppermute | solution.py:39
  176.1 1.6 collective-permute-start.34
  176.2 2.9 %collective-permute-start.19 = (f32[256,256]{1,0:T(8,128)S(1)}, f32[256,256]{1,0:T(8,128)S(1)}, u32[]{:S(2)}, u32[]{:S(2)}) collective-permute-start(f32[256,256]{1,0:T(8,128)S(1)} %bitcast.37), channel_id=1, source_target_pairs={{0,4},{4,0},{8,12},{12,8},{16,20},{20,16},{24,28},{28,24},{1,5},{5... | collective-permute-start | bytes 786440 | tf_op jit(solution)/shard_map/ppermute | solution.py:39

commit v3 on v1

v3 whole, which is shorter than its diff:
```python
import functools
import math

import jax
import jax.numpy as jnp
from jax import lax
from jax.experimental import pallas as pl
from jax.experimental.pallas import tpu as pltpu
from jax.sharding import PartitionSpec as P

BASE = 64
LANES = 128
SUBLANES = 8


def contract(left, right, left_dim, right_dim, precision):
    dims = (((left_dim,), (right_dim,)), ((), ()))
    return lax.dot_general(left, right, dims, precision=precision, preferred_element_type=jnp.float32)


def highest(left, right, left_dim=1, right_dim=0):
    return contract(left, right, left_dim, right_dim, lax.Precision.HIGHEST)


def bits_of(axis):
    return int(math.log2(lax.axis_size(axis)))


def groups_of(axis, first, width):
    bits = list(range(first, bits_of(axis)))
    return [(axis, tuple(bits[i:i + width])) for i in range(0, len(bits), width)]


def swap(values, axis, mask):
    return lax.ppermute(values, axis, [(i, i ^ mask) for i in range(lax.axis_size(axis))])


def side_of(axis, bit):
    return (lax.axis_index(axis) >> bit) & 1


def place_of(axis, bits):
    return sum(side_of(axis, bit) << i for i, bit in enumerate(bits))


def masks_of(bits):
    return [sum(((peer >> i) & 1) << bit for i, bit in enumerate(bits)) for peer in range(1 << len(bits))]


def pair_sum(parts):
    while len(parts) > 1:
        parts = [parts[i] + parts[i + 1] for i in range(0, len(parts), 2)]
    return parts[0]


def scatter_sum(values, group, dim):
    axis, bits = group
    peers = 1 << len(bits)
    extent = values.shape[dim] // peers
    place = place_of(axis, bits)
    parts = [lax.dynamic_slice_in_dim(values, (place ^ peer) * extent, extent, dim) for peer in range(peers)]
    return pair_sum([parts[0]] + [swap(parts[peer], axis, masks_of(bits)[peer]) for peer in range(1, peers)])


def whole_sum(values, group):
    axis, bits = group
    return pair_sum([values] + [swap(values, axis, mask) for mask in masks_of(bits)[1:]])


def gather(values, group, dim):
    axis, bits = group
    peers = 1 << len(bits)
    place = place_of(axis, bits)
    parts = [values] + [swap(values, axis, mask) for mask in masks_of(bits)[1:]]
    ordered = []
    for slot in range(peers):
        chosen = parts[slot]
        for here in range(1, peers):
            chosen = jnp.where(place == here, parts[slot ^ here], chosen)
        ordered.append(chosen)
    return jnp.concatenate(ordered, axis=dim)


def total_over_chips(values):
    for group in groups_of("cell", 1, 2):
        values = scatter_sum(values, group, 0)
    for group in groups_of("tm", 0, 2):
        values = whole_sum(values, group)
    for group in reversed(groups_of("cell", 1, 2)):
        values = gather(values, group, 0)
    return values


def split(values):
    top = values.astype(jnp.bfloat16)
    return top, (values - top.astype(jnp.float32)).astype(jnp.bfloat16)


def parts_dot(left, right, left_dim=1, right_dim=0):
    dims = (((left_dim,), (right_dim,)), ((), ()))
    pairs = ((left[0], right[0]), (left[0], right[1]), (left[1], right[0]))
    return sum(lax.dot_general(a, b, dims, preferred_element_type=jnp.float32) for a, b in pairs)


def call(kernel, out_shape, in_specs, out_specs, scratch=(), flops=0, limit=24):
    return pl.pallas_call(
        kernel,
        out_shape=out_shape,
        in_specs=in_specs,
        out_specs=out_specs,
        scratch_shapes=list(scratch),
        compiler_params=pltpu.CompilerParams(vmem_limit_bytes=limit * 1024 * 1024),
        cost_estimate=pl.CostEstimate(flops=flops, bytes_accessed=4 * 1024 * 1024, transcendentals=0),
    )


WHOLE = pl.BlockSpec(memory_space=pltpu.VMEM)
SCALAR = pl.BlockSpec(memory_space=pltpu.SMEM)
OUTSIDE = pl.BlockSpec(memory_space=pl.ANY)
TILES = 4


def float_shape(*shape):
    return jax.ShapeDtypeStruct(shape, jnp.float32)


def range_kernel(window_ref, test_ref, out_ref, held_ref, test_held_ref, top_ref, rest_ref, window_sem, test_sem):
    tile = held_ref.shape[1]
    test_copy = pltpu.make_async_copy(test_ref, test_held_ref, test_sem)
    test_copy.start()
    for i in range(TILES):
        pltpu.make_async_copy(window_ref.at[pl.ds(i * tile, tile)], held_ref.at[i], window_sem.at[i]).start()
    test_copy.wait()
    top_ref[...], rest_ref[...] = split(test_held_ref[...])

    def step(i, carry):
        start = pl.multiple_of(i * tile, tile)
        pltpu.make_async_copy(window_ref.at[pl.ds(start, tile)], held_ref.at[i], window_sem.at[i]).wait()
        out_ref[pl.ds(start, tile), :] = parts_dot(split(held_ref[i]), (top_ref[...], rest_ref[...]))
        return carry

    lax.fori_loop(0, TILES, step, 0)


def range_terms(window, range_test):
    rows, depth = window.shape
    k = range_test.shape[1]
    return call(
        range_kernel, float_shape(rows, k), [OUTSIDE, OUTSIDE], WHOLE,
        [
            pltpu.VMEM((TILES, rows // TILES, depth), jnp.float32), pltpu.VMEM((depth, k), jnp.float32),
            pltpu.VMEM((depth, k), jnp.bfloat16), pltpu.VMEM((depth, k), jnp.bfloat16),
            pltpu.SemaphoreType.DMA((TILES,)), pltpu.SemaphoreType.DMA,
        ],
        flops=6 * rows * depth * k,
    )(window, range_test)


def co_kernel(core_ref, window_ref, test_ref, sent_ref, kept_ref, top_ref, rest_ref):
    half = sent_ref.shape[1]
    tile = half // 2
    top_ref[...], rest_ref[...] = split(test_ref[...])
    for out_ref, side in ((sent_ref, 1 - core_ref[0]), (kept_ref, core_ref[0])):
        for i in range(2):
            start = pl.multiple_of(side * half + i * tile, tile)
            out_ref[:, i * tile:(i + 1) * tile] = parts_dot((top_ref[...], rest_ref[...]), split(window_ref[:, pl.ds(start, tile)]))


def co_terms(core, window, co_test):
    rows, cols = window.shape
    count = co_test.shape[0]
    return call(
        co_kernel, (float_shape(count, cols // 2),) * 2, [SCALAR, WHOLE, WHOLE], (WHOLE, WHOLE),
        [pltpu.VMEM((count, rows), jnp.bfloat16)] * 2,
        flops=6 * rows * cols * count,
    )(core, window, co_test)


def core_kernel(core_ref, window_ref, right_ref, left_ref, co_ref, range_ref, sent_ref, kept_ref, top_ref, rest_ref, z_ref, lt_ref, rt_ref):
    rows = window_ref.shape[0]
    tile = rows // TILES
    s_core, k = lt_ref.shape
    half = s_core // 2
    top_ref[...], rest_ref[...] = split(right_ref[...])
    z_ref[...] = jnp.zeros_like(z_ref)
    lt_ref[...] = jnp.zeros_like(lt_ref)
    rt_ref[...] = jnp.zeros_like(rt_ref)

    def step(i, carry):
        start = pl.multiple_of(i * tile, tile)
        image = split(parts_dot(split(window_ref[pl.ds(start, tile), :]), (top_ref[...], rest_ref[...]), 1, 1))
        left = split(left_ref[:, pl.ds(start, tile)])
        z_ref[...] += parts_dot(left, image)
        rt_ref[...] += parts_dot(split(co_ref[:, pl.ds(start, tile)]), image)
        lt_ref[...] += parts_dot(left, split(range_ref[pl.ds(start, tile), :]))
        return carry

    lax.fori_loop(0, TILES, step, 0)
    for first_ref, second_ref, core in ((kept_ref, sent_ref, 0), (sent_ref, kept_ref, 1)):
        @pl.when(core_ref[0] == core)
        def _():
            first_ref[:, :k] = lt_ref[...]
            first_ref[:, k:] = z_ref[:, :half]
            second_ref[:, :k] = rt_ref[...].T
            second_ref[:, k:] = z_ref[:, half:]


def core_terms(core, window, core_right, core_left, co_test, range_term):
    rows, cols = window.shape
    s_core, count, k = core_right.shape[0], co_test.shape[0], range_term.shape[1]
    return call(
        core_kernel, (float_shape(s_core, k + s_core // 2),) * 2, [SCALAR] + [WHOLE] * 5, (WHOLE, WHOLE),
        [pltpu.VMEM((s_core, cols), jnp.bfloat16)] * 2
        + [pltpu.VMEM((s_core, s_core), jnp.float32), pltpu.VMEM((s_core, k), jnp.float32), pltpu.VMEM((count, s_core), jnp.float32)],
        flops=18 * rows * cols * s_core,
    )(core, window, core_right, core_left, co_test, range_term)


def gram_kernel(scales, core_ref, range_ref, co_ref, sent_ref, kept_ref):
    gram_y = highest(range_ref[...], range_ref[...], 0, 0) / scales[0]
    gram_w = highest(co_ref[...], co_ref[...], 1, 1) / scales[1]
    first = core_ref[0] == 0
    kept_ref[...] = jnp.where(first, gram_y, gram_w)
    sent_ref[...] = jnp.where(first, gram_w, gram_y)


def gram_terms(core, range_piece, co_piece, scales):
    k = range_piece.shape[1]
    kernel = functools.partial(gram_kernel, scales)
    return call(kernel, (float_shape(k, k),) * 2, [SCALAR, WHOLE, WHOLE], (WHOLE, WHOLE), flops=12 * k * k * k * 2)(core, range_piece, co_piece)


def middle_kernel(core_ref, own_ref, other_ref, middle_ref, gram_ref):
    k = middle_ref.shape[0]
    first = core_ref[0] == 0
    own, other = own_ref[...], other_ref[...]
    left, right = jnp.where(first, own, other), jnp.where(first, other, own)
    gram_ref[...] = highest(own[:, :k], own[:, :k], 0, 0)
    halves = [highest(left[:, :k], side[:, k:], 0, 0) for side in (left, right)]
    middle_ref[...] = highest(jnp.concatenate(halves, axis=1), right[:, :k])


def middle_terms(core, own, other, k):
    return call(middle_kernel, (float_shape(k, k),) * 2, [SCALAR, WHOLE, WHOLE], (WHOLE, WHOLE), flops=12 * k * k * k * 8)(core, own, other)


def spread_lane(values, lane):
    return jnp.broadcast_to(values[:, lane:lane + 1], values.shape)


def spread_row(values, row):
    return jnp.broadcast_to(values[row:row + 1, :], values.shape)


def factor_blocks(blocks):
    count = len(blocks)
    groups = BASE // SUBLANES
    rows = [[x[SUBLANES * g:SUBLANES * (g + 1)] for g in range(groups)] for x in blocks]
    sub = lax.broadcasted_iota(jnp.int32, (SUBLANES, LANES), 0)
    pivots = [[] for _ in blocks]
    for p in range(groups):
        cols = [{g: [spread_lane(rows[b][g], SUBLANES * p + k) for k in range(SUBLANES)] for g in range(p, groups)} for b in range(count)]
        found = [jnp.zeros((SUBLANES, LANES), jnp.float32)] * count
        for k in range(SUBLANES):
            for b in range(count):
                held = cols[b]
                pivot = spread_row(held[p][k], k)
                found[b] = jnp.where(sub == k, pivot, found[b])
                scale = 1.0 / pivot
                pivot_row = spread_row(rows[b][p], k)
                heads = [spread_row(held[p][j], k) for j in range(k + 1, SUBLANES)]
                for g in range(p, groups):
                    weight = held[g][k] * scale
                    if g == p:
                        weight = jnp.where(sub > k, weight, 0.0)
                    rows[b][g] = rows[b][g] - weight * pivot_row
                    for j in range(k + 1, SUBLANES):
                        held[g][j] = held[g][j] - weight * heads[j - k - 1]
        for b in range(count):
            pivots[b].append(found[b])
    return [jnp.concatenate([rows[b][g] * lax.rsqrt(pivots[b][g]) for g in range(groups)], axis=0) for b in range(count)]


def factor_kernel(gram_ref, image_ref, out_ref, inverse_ref, upper_ref):
    count, n = inverse_ref.shape[0], inverse_ref.shape[1]
    every = range(count)
    inverse_ref[0] = gram_ref[...]
    inverse_ref[1] = image_ref[...]
    row_id = lax.broadcasted_iota(jnp.int32, (n, n), 0)
    col_id = lax.broadcasted_iota(jnp.int32, (n, n), 1)
    panel_col = lax.broadcasted_iota(jnp.int32, (BASE, n), 1)
    lane = lax.broadcasted_iota(jnp.int32, (BASE, LANES), 1)
    low = lax.broadcasted_iota(jnp.int32, (BASE, LANES), 0)

    def place(half, start):
        rest = [jnp.zeros((BASE, LANES), jnp.float32)] * (n // LANES - 1)
        return pltpu.roll(jnp.concatenate([jnp.where(lane < BASE, half, 0.0)] + rest, axis=1), start, 1)

    def step(t, carry):
        start = pl.multiple_of(t * BASE, BASE)
        back = jnp.where(t == 0, 0, n - start)
        panel = [inverse_ref[b, pl.ds(start, BASE), :] for b in every]
        whole = [inverse_ref[b] for b in every]
        block = [pltpu.roll(panel[b], back, 1)[:, :LANES] for b in every]
        block = [jnp.where(lane < BASE, block[b], jnp.where(lane - BASE == low, 1.0, 0.0)) for b in every]
        done = factor_blocks(block)
        inv = [pltpu.roll(done[b], LANES - BASE, 1) for b in every]
        inv_placed = [place(inv[b], start) for b in every]
        up_placed = place(done[0], start)
        inside = (panel_col >= start) & (panel_col < start + BASE)
        rows = [jnp.where(inside, inv_placed[b], highest(inv[b][:, :BASE], panel[b])) for b in every]
        below = [jnp.where(row_id[:, :BASE] >= start + BASE, highest(whole[b], inv_placed[b], 1, 1), 0.0) for b in every]
        spent = (row_id >= start + BASE) & (col_id >= start) & (col_id < start + BASE)
        left = [jnp.where(spent, 0.0, whole[b]) - highest(below[b], rows[b]) for b in every]
        for b in every:
            inverse_ref[b] = left[b]
        for b in every:
            inverse_ref[b, pl.ds(start, BASE), :] = rows[b]
        upper_ref[pl.ds(start, BASE), :] = jnp.where(inside, up_placed, jnp.where(panel_col >= start + BASE, rows[0], 0.0))
        return carry

    lax.fori_loop(0, n // BASE, step, 0)
    out_ref[0] = jnp.where(row_id >= col_id, inverse_ref[0], 0.0)
    upper = jnp.where(row_id <= col_id, upper_ref[...], 0.0)
    image = jnp.where(row_id >= col_id, inverse_ref[1], 0.0)
    out_ref[1] = highest(highest(upper, image, 1, 1), image)


def factor_grams(gram, image_gram):
    n = gram.shape[0]
    return call(
        factor_kernel, float_shape(2, n, n), [WHOLE, WHOLE], WHOLE,
        [pltpu.VMEM((2, n, n), jnp.float32), pltpu.VMEM((n, n), jnp.float32)],
        flops=n * n * n * 400,
    )(gram, image_gram)


def basis_kernel(spot, core_ref, own_ref, other_ref, middle_ref, range_ref, co_ref, range_out_ref, co_out_ref, core_out_ref, parts_ref, *, scale):
    first = core_ref[0] == 0

    @pl.when(pl.program_id(0) == 0)
    def _():
        for i in range(2):
            here = jnp.where((first if i == 0 else jnp.logical_not(first)), own_ref[0], other_ref[0])
            parts_ref[2 * i], parts_ref[2 * i + 1] = split(here)
        left = jnp.where(first, own_ref[1], other_ref[1])
        right = jnp.where(first, other_ref[1], own_ref[1])
        core_out_ref[...] = highest(highest(left, middle_ref[...]), right, 1, 1) * scale

    range_out_ref[...] = parts_dot(split(range_ref[...]), (parts_ref[0], parts_ref[1]), 1, 1)
    co_out_ref[...] = parts_dot((parts_ref[2], parts_ref[3]), split(co_ref[0]))


def bases(core, own, other, middle, range_full, co_all, spot, scale):
    rows, k = range_full.shape
    blocks, count, width = co_all.shape
    tile = rows // blocks
    fixed = pl.BlockSpec((2, k, k), lambda i: (0, 0, 0))
    square = pl.BlockSpec((k, k), lambda i: (0, 0))
    return pl.pallas_call(
        functools.partial(basis_kernel, spot, scale=scale),
        out_shape=(float_shape(rows, k), float_shape(count, blocks * width), float_shape(k, k)),
        grid=(blocks,),
        in_specs=[SCALAR, fixed, fixed, square, pl.BlockSpec((tile, k), lambda i: (i, 0)), pl.BlockSpec((1, count, width), lambda i: (i, 0, 0))],
        out_specs=(pl.BlockSpec((tile, k), lambda i: (i, 0)), pl.BlockSpec((count, width), lambda i: (0, spot(i))), square),
        scratch_shapes=[pltpu.VMEM((4, k, k), jnp.bfloat16)],
        compiler_params=pltpu.CompilerParams(vmem_limit_bytes=24 * 1024 * 1024),
        cost_estimate=pl.CostEstimate(flops=18 * rows * k * k, bytes_accessed=6 * 1024 * 1024, transcendentals=0),
    )(core, own, other, middle, range_full, co_all)


def per_device(window, range_test, co_test, core_left, core_right):
    rows_total = window.shape[0] * lax.axis_size("cell")
    cols_total = window.shape[1] * lax.axis_size("tm")
    k = range_test.shape[1]
    core = side_of("cell", 0).astype(jnp.int32).reshape(1)
    cell_groups = groups_of("cell", 1, 2)

    range_term = range_terms(window, range_test)
    range_piece = lax.psum_scatter(range_term, "tm", scatter_dimension=0, tiled=True)
    co_sent, co_kept = co_terms(core, window, co_test)
    co_piece = co_kept + swap(co_sent, "cell", 1)
    for group in cell_groups:
        co_piece = scatter_sum(co_piece, group, 1)
    fold_sent, fold_kept = core_terms(core, window, core_right, core_left, co_test, range_term)

    range_full = lax.all_gather(range_piece, "tm", axis=0, tiled=True)
    co_all = lax.all_gather(co_piece, "cell", axis=0)

    gram_sent, gram_kept = gram_terms(core, range_piece, co_piece, (rows_total, cols_total))
    gram = total_over_chips(gram_kept + swap(gram_sent, "cell", 1))

    fold = total_over_chips(fold_kept + swap(fold_sent, "cell", 1))
    middle, image_gram = middle_terms(core, fold, swap(fold, "cell", 1), k)

    own = factor_grams(gram, image_gram)

    def spot(device):
        block = device & 1
        for _, bits in cell_groups:
            block = block * (1 << len(bits)) + ((device >> bits[0]) & ((1 << len(bits)) - 1))
        return block

    return bases(core, own, swap(own, "cell", 1), middle, range_full, co_all, spot, math.sqrt(rows_total * cols_total))


def solution(mesh):
    return jax.shard_map(
        per_device,
        mesh=mesh,
        in_specs=(P("cell", "tm"), P("tm", None), P(None, "cell"), P(None, "cell"), P(None, "tm")),
        out_specs=(P("cell", None), P(None, "tm"), P()),
        check_vma=False,
    )
```

time: 211 us -> 198 us (0.938)
  matrix products: 46.3 us -> 0 us
  Pallas kernels: 29.4 us -> 48.4 us
  local copies, waits for them, and re-layouts: 5.55 us -> 20.1 us
  between operations: 1.15 us -> 13.9 us
  starting transfers between devices: 34.2 us -> 28.3 us
  waiting for transfers between devices: 86.3 us -> 80.6 us
    dot_general x20 -> x0, matrix products: 46.3 us -> none  [contract(): lax.dot_general(left, right, dims, precision=precision, preferred_element...]
    ppermute x30 -> x26, waiting for transfers between devices: 86.3 us -> 58.1 us  [swap(): lax.ppermute(values, axis, [(i, i ^ mask) for i in range(lax.axis_size(ax...]
    reduce_scatter x0 -> x1, waiting for transfers between devices: none -> 22.4 us  [per_device(): lax.psum_scatter(range_term, 'tm', scatter_dimension=0, tiled=True)]
    pallas_call x2 -> x7, Pallas kernels: 29.4 us -> 48.4 us  [the longest x1 15.1 us: factor_grams(): call(factor_kernel, float_shape(2, n, n), [WHOLE, WHOLE], WHOLE, [pltpu.V...]
    unnamed x10 -> x22, local copies, waits for them, and re-layouts: 0.03 us -> 18.4 us
    ppermute x30 -> x26, starting transfers between devices: 34.2 us -> 28.1 us  [swap(): lax.ppermute(values, axis, [(i, i ^ mask) for i in range(lax.axis_size(ax...]
    dynamic_slice x15 -> x3, local copies, waits for them, and re-layouts: 5.2 us -> 1.67 us  [scatter_sum(): lax.dynamic_slice_in_dim(values, (place ^ peer) * extent, extent, dim)]
    add x15 -> x8, other arithmetic: 4.94 us -> 6.05 us  [the longest x5 3.21 us: pair_sum(): parts = [parts[i] + parts[i + 1] for i in range(0, len(parts), 2)]]
  transfers between devices with their start and end apart: 30 -> 29, of which waited for: 13 -> 21; matrix products, arithmetic and copies ran while one was open for 21% -> 4% of each run, Pallas kernels for 7% -> 18%
where the time goes in v3:
time: 198 us
  waiting for transfers between devices  80.6 us (41%)
  Pallas kernels  48.4 us (24%)
  starting transfers between devices  28.3 us (14%)
  local copies, waits for them, and re-layouts  20.1 us (10%)
  between operations  13.9 us (7%)
  other arithmetic  6.32 us (3%)
    ppermute x26, waiting for transfers between devices, swap(): lax.ppermute(values, axis, [(i, i ^ mask) for i in range(lax.axis_size(ax...  58.1 us
    ppermute x26, starting transfers between devices, swap(): lax.ppermute(values, axis, [(i, i ^ mask) for i in range(lax.axis_size(ax...  28.1 us
    reduce_scatter x1, waiting for transfers between devices, per_device(): lax.psum_scatter(range_term, 'tm', scatter_dimension=0, tiled=True)  22.4 us
    unnamed x22, local copies, waits for them, and re-layouts  18.4 us
    pallas_call x1, Pallas kernels, factor_grams(): call(factor_kernel, float_shape(2, n, n), [WHOLE, WHOLE], WHOLE, [pltpu.V...  15.1 us
    pallas_call x1, Pallas kernels, core_terms(): call(core_kernel, (float_shape(s_core, k + s_core // 2),) * 2, [SCALAR] +...  14.6 us
    pallas_call x1, Pallas kernels, bases(): pl.pallas_call(functools.partial(basis_kernel, spot, scale=scale), out_sh...  5.99 us
    pallas_call x1, Pallas kernels, range_terms(): call(range_kernel, float_shape(rows, k), [OUTSIDE, OUTSIDE], WHOLE, [pltp...  5.93 us
  transfers between devices with their start and end apart: 29, of which 21 were waited for; matrix products, arithmetic and copies ran while one was open for 4% of the time, Pallas kernels for 18%

profile of v3, /device:TPU:0, one launch (start us, length us, event | category | flops | bytes accessed | tf_op | source)
XLA Modules:
  0.0 197.5 jit_solution(17266947685991437307)
XLA Ops:
  7.2 3.4 %copy-done.2 = f32[1024,2048]{1,0:T(8,128)S(1)} copy-done((f32[1024,2048]{1,0:T(8,128)S(1)}, f32[1024,2048]{1,0:T(8,128)}, u32[]{:S(2)}) %copy-start.2) | copy-done | bytes 8388632
  10.6 1.6 copy-done.6
  12.2 5.9 %shard_map.76.range_ref = f32[1024,256]{1,0:T(8,128)} custom-call(f32[1024,2048]{1,0:T(8,128)S(1)} %copy-done.2, f32[2048,256]{1,0:T(8,128)S(1)} %copy-done.6), custom_call_target="tpu_custom_call" | custom-call | flops 3221225472 | bytes 4194304 | tf_op jit(solution)/shard_map/pallas_call | solution.py:148
  18.2 3.4 %copy-done.3 = f32[1024,2048]{1,0:T(8,128)S(1)} copy-done((f32[1024,2048]{1,0:T(8,128)S(1)}, f32[1024,2048]{1,0:T(8,128)}, u32[]{:S(2)}) %copy-start.3) | copy-done | bytes 8388632
  21.6 3.7 %shard_map.77 = (f32[256,1024]{1,0:T(8,128)}, f32[256,1024]{1,0:T(8,128)S(1)}) custom-call(s32[1]{0:T(128)} %bitcast.core_ref, f32[1024,2048]{1,0:T(8,128)S(1)} %copy-done.3, f32[256,1024]{1,0:T(8,128)S(1)} %copy-done.9), custom_call_target="tpu_custom_call" | custom-call | flops 3221225472 | bytes 4194304 | tf_op jit(solution)/shard_map/pallas_call | solution.py:172
  25.3 0.5 collective-permute-start
  25.8 22.4 %reduce-scatter.2.cloned.1.call-done.range_ref = f32[256,256]{1,0:T(8,128)} async-done(((f32[1024,256]{1,0:T(8,128)}), f32[256,256]{1,0:T(8,128)}) %reduce-scatter.2.cloned.1.call-update) | async-done | bytes 262160 | tf_op jit(solution)/shard_map/reduce_scatter | solution.py:380
  48.2 3.4 %copy-done.4 = f32[1024,2048]{1,0:T(8,128)S(1)} copy-done((f32[1024,2048]{1,0:T(8,128)S(1)}, f32[1024,2048]{1,0:T(8,128)}, u32[]{:S(2)}) %copy-start.4) | copy-done | bytes 8388632
  51.6 2.2 %copy-done.5 = f32[512,2048]{1,0:T(8,128)S(1)} copy-done((f32[512,2048]{1,0:T(8,128)S(1)}, f32[512,2048]{1,0:T(8,128)}, u32[]{:S(2)}) %copy-start.5) | copy-done | bytes 4194328
  53.8 1.7 copy-done.7
  55.4 14.6 %shard_map.79 = (f32[512,512]{1,0:T(8,128)}, f32[512,512]{1,0:T(8,128)S(1)}) custom-call(s32[1]{0:T(128)} %bitcast.core_ref, f32[1024,2048]{1,0:T(8,128)S(1)} %copy-done.4, f32[512,2048]{1,0:T(8,128)S(1)} %copy-done.5, f32[512,1024]{1,0:T(8,128)S(1)} %copy-done.7, f32[256,1024]{1,0:T(8,128)S(1)} %copy-done.9, f32[1024,256]{1,0:T(8,128)} %shard_map.76.range_ref), custom_call_target="tpu_custom_call" | custom-call | flops 19327352832 | bytes 4194304 | tf_op jit(solution)/shard_map/pallas_call | solution.py:211
  70.0 1.4 add.100
  71.4 0.9 constant_dynamic-slice_fusion.8
  72.3 1.5 collective-permute-start.1
  73.8 1.5 collective-permute-start.3
  75.2 0.6 collective-permute-start.2
  75.8 1.4 add.119
  77.2 0.8 constant_dynamic-slice_fusion.2
  78.0 1.5 collective-permute-start.15
  79.5 1.5 collective-permute-start.17
  80.9 0.8 collective-permute-done.1
  81.7 1.5 collective-permute-start.16
  83.2 5.1 %collective-permute-done.3 = f32[256,256]{1,0:T(8,128)} collective-permute-done((f32[256,256]{1,0:T(8,128)}, f32[256,256]{1,0:T(8,128)}, u32[]{:S(2)}, u32[]{:S(2)}) %collective-permute-start.3) | collective-permute-done | bytes 262176 | tf_op jit(solution)/shard_map/ppermute | solution.py:35
  88.3 1.8 collective-permute-done.2
  90.1 1.9 add_add_fusion.2.co_ref
  92.0 0.9 collective-permute-done.15
  93.0 6.2 %collective-permute-done.17 = f32[128,512]{1,0:T(8,128)} collective-permute-done((f32[128,512]{1,0:T(8,128)S(1)}, f32[128,512]{1,0:T(8,128)}, u32[]{:S(2)}, u32[]{:S(2)}) %collective-permute-start.17) | collective-permute-done | bytes 262176 | tf_op jit(solution)/shard_map/ppermute | solution.py:35
  99.2 1.2 collective-permute-done.16
  100.4 1.2 add_add_fusion.1
  101.6 1.0 collective-permute-start.20
  102.7 3.4 %collective-permute-start.18 = (f32[128,512]{1,0:T(8,128)S(1)}, f32[128,512]{1,0:T(8,128)S(1)}, u32[]{:S(2)}, u32[]{:S(2)}) collective-permute-start(f32[128,512]{1,0:T(8,128)S(1)} %add_add_fusion.1), channel_id=1, source_target_pairs={{0,1},{1,0},{2,3},{3,2},{4,5},{5,4},{6,7},{7,6},{8,9},{9,8},{10,11... | collective-permute-start | bytes 786440 | tf_op jit(solution)/shard_map/ppermute | solution.py:35
  106.1 6.8 %collective-permute-done.20 = f32[128,512]{1,0:T(8,128)S(1)} collective-permute-done((f32[128,512]{1,0:T(8,128)S(1)}, f32[128,512]{1,0:T(8,128)S(1)}, u32[]{:S(2)}, u32[]{:S(2)}) %collective-permute-start.20) | collective-permute-done | bytes 262176 | tf_op jit(solution)/shard_map/ppermute | solution.py:35
  112.8 12.2 %collective-permute-done.19 = f32[128,512]{1,0:T(8,128)S(1)} collective-permute-done((f32[128,512]{1,0:T(8,128)S(1)}, f32[128,512]{1,0:T(8,128)S(1)}, u32[]{:S(2)}, u32[]{:S(2)}) %collective-permute-start.19) | collective-permute-done | bytes 262176 | tf_op jit(solution)/shard_map/ppermute | solution.py:35
  125.1 0.1 add_add_fusion
  125.2 1.5 collective-permute-start.23
  126.7 0.5 collective-permute-start.22
  127.2 1.5 collective-permute-start.21
  128.7 0.6 shard_map.78
  129.4 5.0 %collective-permute-done.23 = f32[128,512]{1,0:T(8,128)S(1)} collective-permute-done((f32[128,512]{1,0:T(8,128)S(1)}, f32[128,512]{1,0:T(8,128)S(1)}, u32[]{:S(2)}, u32[]{:S(2)}) %collective-permute-start.23) | collective-permute-done | bytes 262176 | tf_op jit(solution)/shard_map/ppermute | solution.py:35
  134.5 4.3 %collective-permute-done.22 = f32[128,512]{1,0:T(8,128)S(1)} collective-permute-done((f32[128,512]{1,0:T(8,128)S(1)}, f32[128,512]{1,0:T(8,128)S(1)}, u32[]{:S(2)}, u32[]{:S(2)}) %collective-permute-start.22) | collective-permute-done | bytes 262176 | tf_op jit(solution)/shard_map/ppermute | solution.py:35
  138.7 0.1 select_select_fusion.3
  139.1 0.6 collective-permute-start.5
  139.7 1.4 collective-permute-start.7
  141.2 1.5 collective-permute-start.6
  142.7 1.4 collective-permute-done.5
  144.1 1.1 collective-permute-done.7
  145.1 1.2 collective-permute-done.6
  146.4 3.2 %collective-permute-start.10 = (f32[64,256]{1,0:T(8,128)S(1)}, f32[64,256]{1,0:T(8,128)S(1)}, u32[]{:S(2)}, u32[]{:S(2)}) collective-permute-start(f32[64,256]{1,0:T(8,128)S(1)} %add_add_fusion.4), channel_id=1, source_target_pairs={{0,3},{1,2},{2,1},{3,0},{4,7},{5,6},{6,5},{7,4},{8,11},{9,10},{10,... | collective-permute-start | bytes 196616 | tf_op jit(solution)/shard_map/ppermute | solution.py:35
  149.6 1.2 collective-permute-start.8
  150.8 2.2 %collective-permute-done.10 = f32[64,256]{1,0:T(8,128)S(1)} collective-permute-done((f32[64,256]{1,0:T(8,128)S(1)}, f32[64,256]{1,0:T(8,128)S(1)}, u32[]{:S(2)}, u32[]{:S(2)}) %collective-permute-start.10) | collective-permute-done | bytes 65568 | tf_op jit(solution)/shard_map/ppermute | solution.py:35
  153.0 2.1 %collective-permute-done.9 = f32[64,256]{1,0:T(8,128)S(1)} collective-permute-done((f32[64,256]{1,0:T(8,128)S(1)}, f32[64,256]{1,0:T(8,128)S(1)}, u32[]{:S(2)}, u32[]{:S(2)}) %collective-permute-start.9) | collective-permute-done | bytes 65568 | tf_op jit(solution)/shard_map/ppermute | solution.py:35
  155.0 0.3 collective-permute-done.8
  155.4 1.5 collective-permute-start.13
  156.8 0.6 collective-permute-start.12
  157.4 1.5 collective-permute-start.11
  158.9 0.9 collective-permute-done.13
  159.9 1.4 collective-permute-done.12
  161.2 1.4 collective-permute-done.11
  162.7 2.4 %shard_map.80 = (f32[256,256]{1,0:T(8,128)S(1)}, f32[256,256]{1,0:T(8,128)S(1)}) custom-call(s32[1]{0:T(128)} %bitcast.core_ref, f32[512,512]{1,0:T(8,128)S(1)} %pad_maximum_fusion.own_ref, f32[512,512]{1,0:T(8,128)S(1)} %collective-permute-done.24.other_ref), custom_call_target="tpu_custom_call" | custom-call | flops 1610612736 | bytes 4194304 | tf_op jit(solution)/shard_map/pallas_call | solution.py:244
  165.1 15.1 %shard_map.81.own_ref = f32[2,256,256]{2,1,0:T(8,128)S(1)} custom-call(f32[256,256]{1,0:T(8,128)S(1)} %pad_maximum_fusion.1.gram_ref, f32[256,256]{1,0:T(8,128)S(1)} %get-tuple-element.17.image_ref), custom_call_target="tpu_custom_call" | custom-call | flops 6710886400 | bytes 4194304 | tf_op jit(solution)/shard_map/pallas_call | solution.py:331
  180.3 1.9 collective-permute-done.25.other_ref
  182.2 1.6 copy-done.8
  183.8 1.2 copy-done.10
  185.0 6.0 %shard_map.82 = (f32[1024,256]{1,0:T(8,128)}, f32[256,2048]{1,0:T(8,128)}, f32[256,256]{1,0:T(8,128)}) custom-call(s32[1]{0:T(128)} %bitcast.core_ref, f32[2,256,256]{2,1,0:T(8,128)S(1)} %shard_map.81.own_ref, f32[2,256,256]{2,1,0:T(8,128)S(1)} %collective-permute-done.25.other_ref, f32[256,256]{1,0:T(8,128)S(1)} %get-tuple-element.18.middle_ref, ...), custom_call_target="tpu_custom_call" | custom-call | flops 1207959552 | bytes 6291456 | tf_op jit(solution)/shard_map/pallas_call | solution.py:360
  (41 shorter events, 0.7 us)
Async XLA Ops:
  7.2 41.0 %reduce-scatter.2.cloned.1.call-start = ((), (), s32[]{:S(2)}) async-start(), calls=%async_computation.1 | async-start | bytes 1310720 | tf_op jit(solution)/shard_map/reduce_scatter | solution.py:380
  7.2 3.4 %copy-start.2 = (f32[1024,2048]{1,0:T(8,128)S(1)}, f32[1024,2048]{1,0:T(8,128)}, u32[]{:S(2)}) copy-start(f32[1024,2048]{1,0:T(8,128)} %window_ref.5) | copy-start | bytes 25165828
  10.6 1.6 copy-start.6
  12.2 6.0 %copy-start.9 = (f32[256,1024]{1,0:T(8,128)S(1)}, f32[256,1024]{1,0:T(8,128)}, u32[]{:S(2)}) copy-start(f32[256,1024]{1,0:T(8,128)} %co_ref.1) | copy-start | bytes 3145732
  18.2 164.0 %all-gather.4.cloned.1.call-start = ((), (), s32[]{:S(2)}) async-start(), calls=%async_computation.2 | async-start | bytes 1310720 | tf_op jit(solution)/shard_map/all_gather | solution.py:387
  18.2 3.4 %copy-start.3 = (f32[1024,2048]{1,0:T(8,128)S(1)}, f32[1024,2048]{1,0:T(8,128)}, u32[]{:S(2)}) copy-start(f32[1024,2048]{1,0:T(8,128)} %window_ref.5) | copy-start | bytes 25165828
  25.3 44.8 %collective-permute-start = (f32[256,1024]{1,0:T(8,128)}, f32[256,1024]{1,0:T(8,128)}, u32[]{:S(2)}, u32[]{:S(2)}) collective-permute-start(f32[256,1024]{1,0:T(8,128)} %get-tuple-element.12), channel_id=1, source_target_pairs={{0,4},{4,0},{8,12},{12,8},{16,20},{20,16},{24,28},{28,24},{1,5},{5... | collective-permute-start | bytes 3145736 | tf_op jit(solution)/shard_map/ppermute | solution.py:35
  48.2 134.0 %all-gather.6.cloned.1.call-start = ((), (), s32[]{:S(2)}) async-start(), calls=%async_computation.3 | async-start | bytes 2359296 | tf_op jit(solution)/shard_map/all_gather | solution.py:388
  48.2 3.4 %copy-start.4 = (f32[1024,2048]{1,0:T(8,128)S(1)}, f32[1024,2048]{1,0:T(8,128)}, u32[]{:S(2)}) copy-start(f32[1024,2048]{1,0:T(8,128)} %window_ref.5) | copy-start | bytes 25165828
  51.6 2.2 %copy-start.5 = (f32[512,2048]{1,0:T(8,128)S(1)}, f32[512,2048]{1,0:T(8,128)}, u32[]{:S(2)}) copy-start(f32[512,2048]{1,0:T(8,128)} %right_ref.1) | copy-start | bytes 12582916
  53.8 1.7 copy-start.7
  70.0 5.7 %collective-permute-start.14 = (f32[512,512]{1,0:T(8,128)}, f32[512,512]{1,0:T(8,128)}, u32[]{:S(2)}, u32[]{:S(2)}) collective-permute-start(f32[512,512]{1,0:T(8,128)} %get-tuple-element.16), channel_id=1, source_target_pairs={{0,4},{4,0},{8,12},{12,8},{16,20},{20,16},{24,28},{28,24},{1,5},{5... | collective-permute-start | bytes 3145736 | tf_op jit(solution)/shard_map/ppermute | solution.py:35
  72.3 9.4 %collective-permute-start.1 = (f32[256,256]{1,0:T(8,128)}, f32[256,256]{1,0:T(8,128)}, u32[]{:S(2)}, u32[]{:S(2)}) collective-permute-start(f32[256,256]{1,0:T(8,128)} %get-tuple-element.26), channel_id=1, source_target_pairs={{0,8},{4,12},{8,0},{12,4},{16,24},{20,28},{24,16},{28,20},{1,9},{5... | collective-permute-start | bytes 786440 | tf_op jit(solution)/shard_map/ppermute | solution.py:35
  73.8 14.5 %collective-permute-start.3 = (f32[256,256]{1,0:T(8,128)}, f32[256,256]{1,0:T(8,128)}, u32[]{:S(2)}, u32[]{:S(2)}) collective-permute-start(f32[256,256]{1,0:T(8,128)} %get-tuple-element.27), channel_id=1, source_target_pairs={{0,24},{4,28},{8,16},{12,20},{16,8},{20,12},{24,0},{28,4},{1,25},{... | collective-permute-start | bytes 786440 | tf_op jit(solution)/shard_map/ppermute | solution.py:35
  75.2 14.9 %collective-permute-start.2 = (f32[256,256]{1,0:T(8,128)S(1)}, f32[256,256]{1,0:T(8,128)}, u32[]{:S(2)}, u32[]{:S(2)}) collective-permute-start(f32[256,256]{1,0:T(8,128)S(1)} %get-tuple-element.28), channel_id=1, source_target_pairs={{0,16},{4,20},{8,24},{12,28},{16,0},{20,4},{24,8},{28,12},{1,17},{... | collective-permute-start | bytes 786440 | tf_op jit(solution)/shard_map/ppermute | solution.py:35
  78.0 15.0 %collective-permute-start.15 = (f32[128,512]{1,0:T(8,128)}, f32[128,512]{1,0:T(8,128)}, u32[]{:S(2)}, u32[]{:S(2)}) collective-permute-start(f32[128,512]{1,0:T(8,128)} %get-tuple-element.23), channel_id=1, source_target_pairs={{0,8},{4,12},{8,0},{12,4},{16,24},{20,28},{24,16},{28,20},{1,9},{5... | collective-permute-start | bytes 786440 | tf_op jit(solution)/shard_map/ppermute | solution.py:35
  79.5 19.8 %collective-permute-start.17 = (f32[128,512]{1,0:T(8,128)S(1)}, f32[128,512]{1,0:T(8,128)}, u32[]{:S(2)}, u32[]{:S(2)}) collective-permute-start(f32[128,512]{1,0:T(8,128)S(1)} %get-tuple-element.24), channel_id=1, source_target_pairs={{0,24},{4,28},{8,16},{12,20},{16,8},{20,12},{24,0},{28,4},{1,25},{... | collective-permute-start | bytes 786440 | tf_op jit(solution)/shard_map/ppermute | solution.py:35
  81.7 18.7 %collective-permute-start.16 = (f32[128,512]{1,0:T(8,128)S(1)}, f32[128,512]{1,0:T(8,128)}, u32[]{:S(2)}, u32[]{:S(2)}) collective-permute-start(f32[128,512]{1,0:T(8,128)S(1)} %get-tuple-element.25), channel_id=1, source_target_pairs={{0,16},{4,20},{8,24},{12,28},{16,0},{20,4},{24,8},{28,12},{1,17},{... | collective-permute-start | bytes 786440 | tf_op jit(solution)/shard_map/ppermute | solution.py:35
  83.2 45.5 %copy-start.1 = (f32[256,256]{1,0:T(8,128)S(1)}, f32[256,256]{1,0:T(8,128)}, u32[]{:S(2)}) copy-start(f32[256,256]{1,0:T(8,128)} %reduce-scatter.2.cloned.1.call-done.range_ref) | copy-start | bytes 786436
  92.0 36.7 %copy-start = (f32[256,256]{1,0:T(8,128)S(1)}, f32[256,256]{1,0:T(8,128)}, u32[]{:S(2)}) copy-start(f32[256,256]{1,0:T(8,128)} %add_add_fusion.2.co_ref) | copy-start | bytes 786436
  101.6 11.2 %collective-permute-start.20 = (f32[128,512]{1,0:T(8,128)S(1)}, f32[128,512]{1,0:T(8,128)S(1)}, u32[]{:S(2)}, u32[]{:S(2)}) collective-permute-start(f32[128,512]{1,0:T(8,128)S(1)} %add_add_fusion.1), channel_id=1, source_target_pairs={{0,3},{1,2},{2,1},{3,0},{4,7},{5,6},{6,5},{7,4},{8,11},{9,10},{10,... | collective-permute-start | bytes 786440 | tf_op jit(solution)/shard_map/ppermute | solution.py:35
  102.6 22.4 %collective-permute-start.19 = (f32[128,512]{1,0:T(8,128)S(1)}, f32[128,512]{1,0:T(8,128)S(1)}, u32[]{:S(2)}, u32[]{:S(2)}) collective-permute-start(f32[128,512]{1,0:T(8,128)S(1)} %add_add_fusion.1), channel_id=1, source_target_pairs={{0,2},{1,3},{2,0},{3,1},{4,6},{5,7},{6,4},{7,5},{8,10},{9,11},{10,... | collective-permute-start | bytes 786440 | tf_op jit(solution)/shard_map/ppermute | solution.py:35
  102.7 22.4 %collective-permute-start.18 = (f32[128,512]{1,0:T(8,128)S(1)}, f32[128,512]{1,0:T(8,128)S(1)}, u32[]{:S(2)}, u32[]{:S(2)}) collective-permute-start(f32[128,512]{1,0:T(8,128)S(1)} %add_add_fusion.1), channel_id=1, source_target_pairs={{0,1},{1,0},{2,3},{3,2},{4,5},{5,4},{6,7},{7,6},{8,9},{9,8},{10,11... | collective-permute-start | bytes 786440 | tf_op jit(solution)/shard_map/ppermute | solution.py:35
  125.2 9.3 %collective-permute-start.23 = (f32[128,512]{1,0:T(8,128)S(1)}, f32[128,512]{1,0:T(8,128)S(1)}, u32[]{:S(2)}, u32[]{:S(2)}) collective-permute-start(f32[128,512]{1,0:T(8,128)S(1)} %add_add_fusion), channel_id=1, source_target_pairs={{0,8},{4,12},{8,0},{12,4},{16,24},{20,28},{24,16},{28,20},{1,9},{5... | collective-permute-start | bytes 786440 | tf_op jit(solution)/shard_map/ppermute | solution.py:35
  126.7 12.0 %collective-permute-start.22 = (f32[128,512]{1,0:T(8,128)S(1)}, f32[128,512]{1,0:T(8,128)S(1)}, u32[]{:S(2)}, u32[]{:S(2)}) collective-permute-start(f32[128,512]{1,0:T(8,128)S(1)} %add_add_fusion), channel_id=1, source_target_pairs={{0,16},{4,20},{8,24},{12,28},{16,0},{20,4},{24,8},{28,12},{1,17},{... | collective-permute-start | bytes 786440 | tf_op jit(solution)/shard_map/ppermute | solution.py:35
  127.2 11.5 %collective-permute-start.21 = (f32[128,512]{1,0:T(8,128)S(1)}, f32[128,512]{1,0:T(8,128)S(1)}, u32[]{:S(2)}, u32[]{:S(2)}) collective-permute-start(f32[128,512]{1,0:T(8,128)S(1)} %add_add_fusion), channel_id=1, source_target_pairs={{0,24},{4,28},{8,16},{12,20},{16,8},{20,12},{24,0},{28,4},{1,25},{... | collective-permute-start | bytes 786440 | tf_op jit(solution)/shard_map/ppermute | solution.py:35
  129.4 9.7 %collective-permute-start.4 = (f32[256,256]{1,0:T(8,128)S(1)}, f32[256,256]{1,0:T(8,128)S(1)}, u32[]{:S(2)}, u32[]{:S(2)}) collective-permute-start(f32[256,256]{1,0:T(8,128)S(1)} %get-tuple-element.14), channel_id=1, source_target_pairs={{0,4},{4,0},{8,12},{12,8},{16,20},{20,16},{24,28},{28,24},{1,5},{5... | collective-permute-start | bytes 786440 | tf_op jit(solution)/shard_map/ppermute | solution.py:35
  139.0 23.7 %collective-permute-start.24 = (f32[512,512]{1,0:T(8,128)S(1)}, f32[512,512]{1,0:T(8,128)S(1)}, u32[]{:S(2)}, u32[]{:S(2)}) collective-permute-start(f32[512,512]{1,0:T(8,128)S(1)} %pad_maximum_fusion.own_ref), channel_id=1, source_target_pairs={{0,4},{4,0},{8,12},{12,8},{16,20},{20,16},{24,28},{28,24},{1,5},{5... | collective-permute-start | bytes 3145736 | tf_op jit(solution)/shard_map/ppermute | solution.py:35
  139.1 5.0 %collective-permute-start.5 = (f32[64,256]{1,0:T(8,128)S(1)}, f32[64,256]{1,0:T(8,128)S(1)}, u32[]{:S(2)}, u32[]{:S(2)}) collective-permute-start(f32[64,256]{1,0:T(8,128)S(1)} %get-tuple-element.33), channel_id=1, source_target_pairs={{0,8},{4,12},{8,0},{12,4},{16,24},{20,28},{24,16},{28,20},{1,9},{5... | collective-permute-start | bytes 196616 | tf_op jit(solution)/shard_map/ppermute | solution.py:35
  139.7 5.4 %collective-permute-start.7 = (f32[64,256]{1,0:T(8,128)S(1)}, f32[64,256]{1,0:T(8,128)S(1)}, u32[]{:S(2)}, u32[]{:S(2)}) collective-permute-start(f32[64,256]{1,0:T(8,128)S(1)} %get-tuple-element.34), channel_id=1, source_target_pairs={{0,24},{4,28},{8,16},{12,20},{16,8},{20,12},{24,0},{28,4},{1,25},{... | collective-permute-start | bytes 196616 | tf_op jit(solution)/shard_map/ppermute | solution.py:35
  141.2 5.2 %collective-permute-start.6 = (f32[64,256]{1,0:T(8,128)S(1)}, f32[64,256]{1,0:T(8,128)S(1)}, u32[]{:S(2)}, u32[]{:S(2)}) collective-permute-start(f32[64,256]{1,0:T(8,128)S(1)} %get-tuple-element.35), channel_id=1, source_target_pairs={{0,16},{4,20},{8,24},{12,28},{16,0},{20,4},{24,8},{28,12},{1,17},{... | collective-permute-start | bytes 196616 | tf_op jit(solution)/shard_map/ppermute | solution.py:35
  146.4 6.6 %collective-permute-start.10 = (f32[64,256]{1,0:T(8,128)S(1)}, f32[64,256]{1,0:T(8,128)S(1)}, u32[]{:S(2)}, u32[]{:S(2)}) collective-permute-start(f32[64,256]{1,0:T(8,128)S(1)} %add_add_fusion.4), channel_id=1, source_target_pairs={{0,3},{1,2},{2,1},{3,0},{4,7},{5,6},{6,5},{7,4},{8,11},{9,10},{10,... | collective-permute-start | bytes 196616 | tf_op jit(solution)/shard_map/ppermute | solution.py:35
  149.6 5.4 %collective-permute-start.9 = (f32[64,256]{1,0:T(8,128)S(1)}, f32[64,256]{1,0:T(8,128)S(1)}, u32[]{:S(2)}, u32[]{:S(2)}) collective-permute-start(f32[64,256]{1,0:T(8,128)S(1)} %add_add_fusion.4), channel_id=1, source_target_pairs={{0,2},{1,3},{2,0},{3,1},{4,6},{5,7},{6,4},{7,5},{8,10},{9,11},{10,... | collective-permute-start | bytes 196616 | tf_op jit(solution)/shard_map/ppermute | solution.py:35
  149.6 5.7 %collective-permute-start.8 = (f32[64,256]{1,0:T(8,128)S(1)}, f32[64,256]{1,0:T(8,128)S(1)}, u32[]{:S(2)}, u32[]{:S(2)}) collective-permute-start(f32[64,256]{1,0:T(8,128)S(1)} %add_add_fusion.4), channel_id=1, source_target_pairs={{0,1},{1,0},{2,3},{3,2},{4,5},{5,4},{6,7},{7,6},{8,9},{9,8},{10,11... | collective-permute-start | bytes 196616 | tf_op jit(solution)/shard_map/ppermute | solution.py:35
  155.4 4.5 %collective-permute-start.13 = (f32[64,256]{1,0:T(8,128)S(1)}, f32[64,256]{1,0:T(8,128)S(1)}, u32[]{:S(2)}, u32[]{:S(2)}) collective-permute-start(f32[64,256]{1,0:T(8,128)S(1)} %add_add_fusion.3), channel_id=1, source_target_pairs={{0,8},{4,12},{8,0},{12,4},{16,24},{20,28},{24,16},{28,20},{1,9},{5... | collective-permute-start | bytes 196616 | tf_op jit(solution)/shard_map/ppermute | solution.py:35
  156.8 4.4 %collective-permute-start.12 = (f32[64,256]{1,0:T(8,128)S(1)}, f32[64,256]{1,0:T(8,128)S(1)}, u32[]{:S(2)}, u32[]{:S(2)}) collective-permute-start(f32[64,256]{1,0:T(8,128)S(1)} %add_add_fusion.3), channel_id=1, source_target_pairs={{0,16},{4,20},{8,24},{12,28},{16,0},{20,4},{24,8},{28,12},{1,17},{... | collective-permute-start | bytes 196616 | tf_op jit(solution)/shard_map/ppermute | solution.py:35
  157.4 5.2 %collective-permute-start.11 = (f32[64,256]{1,0:T(8,128)S(1)}, f32[64,256]{1,0:T(8,128)S(1)}, u32[]{:S(2)}, u32[]{:S(2)}) collective-permute-start(f32[64,256]{1,0:T(8,128)S(1)} %add_add_fusion.3), channel_id=1, source_target_pairs={{0,24},{4,28},{8,16},{12,20},{16,8},{20,12},{24,0},{28,4},{1,25},{... | collective-permute-start | bytes 196616 | tf_op jit(solution)/shard_map/ppermute | solution.py:35
  180.2 2.0 %collective-permute-start.25 = (f32[2,256,256]{2,1,0:T(8,128)S(1)}, f32[2,256,256]{2,1,0:T(8,128)S(1)}, u32[]{:S(2)}, u32[]{:S(2)}) collective-permute-start(f32[2,256,256]{2,1,0:T(8,128)S(1)} %shard_map.81.own_ref), channel_id=1, source_target_pairs={{0,4},{4,0},{8,12},{12,8},{16,20},{20,16},{24,28},{28,24},{1,5},{5... | collective-permute-start | bytes 1572872 | tf_op jit(solution)/shard_map/ppermute | solution.py:35
  182.2 1.6 copy-start.8
  183.8 1.2 copy-start.10
Sparse Core Ops, SparseCore 0:
  18.3 29.8 reduce-scatter.1
  49.8 26.5 all-gather.3
  92.2 25.5 all-gather.5

commit v4 on v1

v4 whole, which is shorter than its diff:
```python
import functools
import math

import jax
import jax.numpy as jnp
from jax import lax
from jax.experimental import pallas as pl
from jax.experimental.pallas import tpu as pltpu
from jax.sharding import PartitionSpec as P

BASE = 64
LANES = 128
SUBLANES = 8
TILES = 4
WHOLE = pl.BlockSpec(memory_space=pltpu.VMEM)
SCALAR = pl.BlockSpec(memory_space=pltpu.SMEM)
OUTSIDE = pl.BlockSpec(memory_space=pl.ANY)


def highest(left, right, left_dim=1, right_dim=0):
    dims = (((left_dim,), (right_dim,)), ((), ()))
    return lax.dot_general(left, right, dims, precision=lax.Precision.HIGHEST, preferred_element_type=jnp.float32)


def split(values):
    top = values.astype(jnp.bfloat16)
    return top, (values - top.astype(jnp.float32)).astype(jnp.bfloat16)


def parts_dot(left, right, left_dim=1, right_dim=0):
    dims = (((left_dim,), (right_dim,)), ((), ()))
    pairs = ((left[0], right[0]), (left[0], right[1]), (left[1], right[0]))
    return sum(lax.dot_general(a, b, dims, preferred_element_type=jnp.float32) for a, b in pairs)


def float_shape(*shape):
    return jax.ShapeDtypeStruct(shape, jnp.float32)


def call(kernel, out_shape, in_specs, out_specs, scratch=(), flops=0, limit=24):
    return pl.pallas_call(
        kernel,
        out_shape=out_shape,
        in_specs=in_specs,
        out_specs=out_specs,
        scratch_shapes=list(scratch),
        compiler_params=pltpu.CompilerParams(vmem_limit_bytes=limit * 1024 * 1024),
        cost_estimate=pl.CostEstimate(flops=flops, bytes_accessed=4 * 1024 * 1024, transcendentals=0),
    )


def bits_of(axis):
    return int(math.log2(lax.axis_size(axis)))


def groups_of(axis, first, width):
    bits = list(range(first, bits_of(axis)))
    return [(axis, tuple(bits[i:i + width])) for i in range(0, len(bits), width)]


def place_of(groups, index):
    place = 0
    for _, bits in groups:
        place = (place << len(bits)) + sum(((index >> bit) & 1) << i for i, bit in enumerate(bits))
    return place


def swap(values, axis, mask):
    return lax.ppermute(values, axis, [(i, i ^ mask) for i in range(lax.axis_size(axis))])


def masks_of(bits):
    return [sum(((peer >> i) & 1) << bit for i, bit in enumerate(bits)) for peer in range(1 << len(bits))]


def pair_sum(parts):
    while len(parts) > 1:
        parts = [parts[i] + parts[i + 1] for i in range(0, len(parts), 2)]
    return parts[0]


def scatter_sum(blocks, groups):
    for axis, bits in groups:
        count = blocks.shape[0] >> len(bits)
        parts = [blocks[peer * count:(peer + 1) * count] for peer in range(1 << len(bits))]
        blocks = pair_sum([parts[0]] + [swap(part, axis, mask) for part, mask in zip(parts[1:], masks_of(bits)[1:])])
    return blocks


def gather(blocks, groups):
    parts = [blocks]
    for axis, bits in reversed(groups):
        blocks = jnp.concatenate(parts) if len(parts) > 1 else parts[0]
        parts = [blocks] + [swap(blocks, axis, mask) for mask in masks_of(bits)[1:]]
    return parts


def whole_sum(values, axis):
    for bit in range(bits_of(axis)):
        values = values + swap(values, axis, 1 << bit)
    return values


def after(values, *earlier):
    return lax.optimization_barrier((values,) + earlier)[0]


def block_start(place, block, extent):
    return pl.multiple_of((place ^ block) * extent, extent)


def put_blocks(refs, out_ref, place):
    count, extent = refs[0].shape[0], refs[0].shape[1]
    for i, ref in enumerate(refs):
        for j in range(count):
            out_ref[pl.ds(block_start(place, i * count + j, extent), extent), :] = ref[j]


def take_blocks(ref, out_ref, place, base=0):
    count, extent = out_ref.shape[0], out_ref.shape[1]
    for i in range(count):
        out_ref[i] = ref[pl.ds(pl.multiple_of(base + (place ^ i) * extent, extent), extent), :]


def pack_width(count, width, k):
    return count * width // k


def sketch_kernel(spot_ref, window_ref, test_ref, co_ref, left_ref, right_ref, r3_ref, r2_ref, r1_ref, r0_ref, sent_ref, kept_ref, held_ref, test_held_ref, co_held_ref, left_held_ref, right_held_ref, top_ref, rest_ref, co_done_ref, lt_ref, rt_ref, window_sem, sem):
    core, place, line = spot_ref[0], spot_ref[1], spot_ref[2]
    tile = held_ref.shape[1]
    chips, _, k = kept_ref.shape
    count, cols = co_done_ref.shape
    width = cols // (2 * chips)
    packed = pack_width(count, width, k)
    small = [(test_ref, test_held_ref), (co_ref, co_held_ref), (left_ref, left_held_ref), (right_ref, right_held_ref)]
    small = [pltpu.make_async_copy(a, b, sem.at[i]) for i, (a, b) in enumerate(small)]

    def window_copy(i):
        return pltpu.make_async_copy(window_ref.at[pl.ds(block_start(line, TILES - 1 - i, tile), tile)], held_ref.at[i], window_sem.at[i])

    small[0].start()
    window_copy(0).start()
    small[1].start()
    small[2].start()
    for i in range(1, TILES):
        window_copy(i).start()
    small[3].start()
    co_done_ref[...] = jnp.zeros_like(co_done_ref)
    lt_ref[...] = jnp.zeros_like(lt_ref)
    small[0].wait()
    top_ref[...], rest_ref[...] = split(test_held_ref[...])
    small[1].wait()
    small[2].wait()

    def step(i, carry):
        window_copy(i).wait()
        rows = split(held_ref[i])
        spot = pl.ds(block_start(line, TILES - 1 - i, tile), tile)
        done = parts_dot(rows, (top_ref[...], rest_ref[...]))
        co_done_ref[...] += parts_dot(split(co_held_ref[:, spot]), rows)
        lt_ref[...] += parts_dot(split(left_held_ref[:, spot]), split(done))
        for block, ref in enumerate((r3_ref, r2_ref, r1_ref, r0_ref)):
            @pl.when(i == block)
            def _():
                ref[...] = done

        return carry

    lax.fori_loop(0, TILES, step, 0)
    small[3].wait()
    rt_ref[...] = parts_dot(split(right_held_ref[...]), split(co_done_ref[...]), 1, 1)
    for ref, side in ((sent_ref, 1 - core), (kept_ref, core)):
        for i in range(chips):
            start = pl.multiple_of((side * chips + (place ^ i)) * width, width)
            for j in range(count // packed):
                ref[i, :packed, j * width:(j + 1) * width] = co_done_ref[j * packed:(j + 1) * packed, pl.ds(start, width)]
    for owner, left_out, right_out in ((0, kept_ref, sent_ref), (1, sent_ref, kept_ref)):
        @pl.when(core == owner)
        def _():
            take_blocks(lt_ref, left_out.at[:, packed:], place)
            take_blocks(rt_ref, right_out.at[:, packed:], place)


def sketch_terms(spot, chips, window, range_test, co_test, core_left, core_right):
    rows, cols = window.shape
    count, k, s_core = co_test.shape[0], range_test.shape[1], core_left.shape[0]
    block = pack_width(count, cols // (2 * chips), k) + s_core // chips
    return call(
        sketch_kernel, (float_shape(rows // TILES, k),) * 4 + (float_shape(chips, block, k),) * 2,
        [SCALAR] + [OUTSIDE] * 5, (WHOLE,) * 6,
        [
            pltpu.VMEM((TILES, rows // TILES, cols), jnp.float32), pltpu.VMEM((cols, k), jnp.float32), pltpu.VMEM((count, rows), jnp.float32),
            pltpu.VMEM((s_core, rows), jnp.float32), pltpu.VMEM((s_core, cols), jnp.float32),
            pltpu.VMEM((cols, k), jnp.bfloat16), pltpu.VMEM((cols, k), jnp.bfloat16),
            pltpu.VMEM((count, cols), jnp.float32), pltpu.VMEM((s_core, k), jnp.float32), pltpu.VMEM((s_core, k), jnp.float32),
            pltpu.SemaphoreType.DMA((TILES,)), pltpu.SemaphoreType.DMA((4,)),
        ],
        flops=12 * rows * cols * count, limit=56,
    )(spot, window, range_test, co_test, core_left, core_right)


def core_kernel(spot_ref, window_ref, right_ref, left_ref, z_ref, held_ref, right_held_ref, left_held_ref, image_ref, window_sem, right_sem, left_sem):
    width = held_ref.shape[2]
    tile = window_ref.shape[0] // TILES
    left_copy = pltpu.make_async_copy(left_ref, left_held_ref, left_sem)

    def copies(i):
        start = pl.multiple_of(i * width, width)
        return (
            pltpu.make_async_copy(right_ref.at[:, pl.ds(start, width)], right_held_ref.at[i], right_sem.at[i]),
            pltpu.make_async_copy(window_ref.at[:, pl.ds(start, width)], held_ref.at[i], window_sem.at[i]),
        )

    for i in range(TILES):
        for copy in copies(i):
            copy.start()
    left_copy.start()
    image_ref[...] = jnp.zeros_like(image_ref)

    def step(i, carry):
        for copy in copies(i):
            copy.wait()
        image_ref[...] += parts_dot(split(held_ref[i]), split(right_held_ref[i]), 1, 1)
        return carry

    lax.fori_loop(0, TILES, step, 0)
    left_copy.wait()
    z_ref[...] = jnp.zeros_like(z_ref)

    def fold(i, carry):
        start = pl.multiple_of(i * tile, tile)
        z_ref[...] += parts_dot(split(left_held_ref[:, pl.ds(start, tile)]), split(image_ref[pl.ds(start, tile), :]))
        return carry

    lax.fori_loop(0, TILES, fold, 0)


def core_terms(spot, window, core_right, core_left):
    rows, cols = window.shape
    s_core = core_right.shape[0]
    return call(
        core_kernel, float_shape(s_core, s_core), [SCALAR] + [OUTSIDE] * 3, WHOLE,
        [
            pltpu.VMEM((TILES, rows, cols // TILES), jnp.float32), pltpu.VMEM((TILES, s_core, cols // TILES), jnp.float32),
            pltpu.VMEM((s_core, rows), jnp.float32), pltpu.VMEM((rows, s_core), jnp.float32),
            pltpu.SemaphoreType.DMA((TILES,)), pltpu.SemaphoreType.DMA((TILES,)), pltpu.SemaphoreType.DMA,
        ],
        flops=9 * rows * cols * s_core, limit=56,
    )(spot, window, core_right, core_left)


def gram_kernel(scales, spot_ref, range_ref, co_ref, sent_ref, kept_ref, y_ref, w_ref):
    y_ref[...] = highest(range_ref[...], range_ref[...], 0, 0) / scales[0]
    w_ref[...] = highest(co_ref[...], co_ref[...], 1, 1) / scales[1]
    for owner, y_out, w_out in ((0, kept_ref, sent_ref), (1, sent_ref, kept_ref)):
        @pl.when(spot_ref[0] == owner)
        def _():
            take_blocks(y_ref, y_out, spot_ref[1])
            take_blocks(w_ref, w_out, spot_ref[1])


def gram_terms(spot, chips, range_piece, co_piece, scales):
    k = range_piece.shape[1]
    square = pltpu.VMEM((k, k), jnp.float32)
    return call(
        functools.partial(gram_kernel, scales), (float_shape(chips, k // chips, k),) * 2, [SCALAR, WHOLE, WHOLE], (WHOLE, WHOLE),
        [square, square], flops=24 * k * k * k,
    )(spot, range_piece, co_piece)


def middle_kernel(spot_ref, z_ref, own_ref, other_ref, sent_ref, kept_ref, gram_ref, left_ref, right_ref, middle_ref):
    core, place = spot_ref[0], spot_ref[1]
    for owner, left_in, right_in in ((0, own_ref, other_ref), (1, other_ref, own_ref)):
        @pl.when(core == owner)
        def _():
            put_blocks([left_in], left_ref, place)
            put_blocks([right_in], right_ref, place)

    first = core == 0
    own = jnp.where(first, left_ref[...], right_ref[...])
    gram_ref[...] = highest(own, own, 0, 0)
    middle_ref[...] = parts_dot(split(parts_dot(split(left_ref[...]), split(z_ref[...]), 0, 0)), split(right_ref[...]))
    half = middle_ref.shape[0] // 2
    take_blocks(middle_ref, kept_ref, place, core * half)
    take_blocks(middle_ref, sent_ref, place, (1 - core) * half)


def middle_terms(spot, chips, sketch_z, own, other):
    s_core, k = sketch_z.shape[0], own.shape[2]
    return call(
        middle_kernel, (float_shape(chips, k // (2 * chips), k),) * 2 + (float_shape(k, k),), [SCALAR] + [WHOLE] * 3, (WHOLE,) * 3,
        [pltpu.VMEM((s_core, k), jnp.float32), pltpu.VMEM((s_core, k), jnp.float32), pltpu.VMEM((k, k), jnp.float32)],
        flops=6 * k * s_core * s_core,
    )(spot, sketch_z, own, other)


def spread_lane(values, lane):
    return jnp.broadcast_to(values[:, lane:lane + 1], values.shape)


def spread_row(values, row):
    return jnp.broadcast_to(values[row:row + 1, :], values.shape)


def factor_blocks(blocks):
    count = len(blocks)
    groups = BASE // SUBLANES
    rows = [[x[SUBLANES * g:SUBLANES * (g + 1)] for g in range(groups)] for x in blocks]
    sub = lax.broadcasted_iota(jnp.int32, (SUBLANES, LANES), 0)
    pivots = [[] for _ in blocks]
    for p in range(groups):
        cols = [{g: [spread_lane(rows[b][g], SUBLANES * p + k) for k in range(SUBLANES)] for g in range(p, groups)} for b in range(count)]
        found = [jnp.zeros((SUBLANES, LANES), jnp.float32)] * count
        for k in range(SUBLANES):
            for b in range(count):
                held = cols[b]
                pivot = spread_row(held[p][k], k)
                found[b] = jnp.where(sub == k, pivot, found[b])
                scale = 1.0 / pivot
                pivot_row = spread_row(rows[b][p], k)
                heads = [spread_row(held[p][j], k) for j in range(k + 1, SUBLANES)]
                for g in range(p, groups):
                    weight = held[g][k] * scale
                    if g == p:
                        weight = jnp.where(sub > k, weight, 0.0)
                    rows[b][g] = rows[b][g] - weight * pivot_row
                    for j in range(k + 1, SUBLANES):
                        held[g][j] = held[g][j] - weight * heads[j - k - 1]
        for b in range(count):
            pivots[b].append(found[b])
    return [jnp.concatenate([rows[b][g] * lax.rsqrt(pivots[b][g]) for g in range(groups)], axis=0) for b in range(count)]


def factor_kernel(peers, spot_ref, *refs):
    gram_refs, (image_ref, out_ref, inverse_ref, upper_ref) = refs[:peers], refs[peers:]
    count, n = inverse_ref.shape[0], inverse_ref.shape[1]
    every = range(count)
    put_blocks(gram_refs, inverse_ref.at[0], spot_ref[1])
    inverse_ref[1] = image_ref[...]
    row_id = lax.broadcasted_iota(jnp.int32, (n, n), 0)
    col_id = lax.broadcasted_iota(jnp.int32, (n, n), 1)
    panel_col = lax.broadcasted_iota(jnp.int32, (BASE, n), 1)
    lane = lax.broadcasted_iota(jnp.int32, (BASE, LANES), 1)
    low = lax.broadcasted_iota(jnp.int32, (BASE, LANES), 0)

    def place(half, start):
        rest = [jnp.zeros((BASE, LANES), jnp.float32)] * (n // LANES - 1)
        return pltpu.roll(jnp.concatenate([jnp.where(lane < BASE, half, 0.0)] + rest, axis=1), start, 1)

    def step(t, carry):
        start = pl.multiple_of(t * BASE, BASE)
        back = jnp.where(t == 0, 0, n - start)
        panel = [inverse_ref[b, pl.ds(start, BASE), :] for b in every]
        whole = [inverse_ref[b] for b in every]
        block = [pltpu.roll(panel[b], back, 1)[:, :LANES] for b in every]
        block = [jnp.where(lane < BASE, block[b], jnp.where(lane - BASE == low, 1.0, 0.0)) for b in every]
        done = factor_blocks(block)
        inv = [pltpu.roll(done[b], LANES - BASE, 1) for b in every]
        inv_placed = [place(inv[b], start) for b in every]
        up_placed = place(done[0], start)
        inside = (panel_col >= start) & (panel_col < start + BASE)
        rows = [jnp.where(inside, inv_placed[b], highest(inv[b][:, :BASE], panel[b])) for b in every]
        below = [jnp.where(row_id[:, :BASE] >= start + BASE, highest(whole[b], inv_placed[b], 1, 1), 0.0) for b in every]
        spent = (row_id >= start + BASE) & (col_id >= start) & (col_id < start + BASE)
        left = [jnp.where(spent, 0.0, whole[b]) - highest(below[b], rows[b]) for b in every]
        for b in every:
            inverse_ref[b] = left[b]
        for b in every:
            inverse_ref[b, pl.ds(start, BASE), :] = rows[b]
        upper_ref[pl.ds(start, BASE), :] = jnp.where(inside, up_placed, jnp.where(panel_col >= start + BASE, rows[0], 0.0))
        return carry

    lax.fori_loop(0, n // BASE, step, 0)
    out_ref[0] = jnp.where(row_id >= col_id, inverse_ref[0], 0.0)
    upper = jnp.where(row_id <= col_id, upper_ref[...], 0.0)
    image = jnp.where(row_id >= col_id, inverse_ref[1], 0.0)
    out_ref[1] = highest(highest(upper, image, 1, 1), image)


def factor_grams(spot, grams, image_gram):
    n = image_gram.shape[0]
    return call(
        functools.partial(factor_kernel, len(grams)), float_shape(2, n, n), [SCALAR] + [WHOLE] * (len(grams) + 1), WHOLE,
        [pltpu.VMEM((2, n, n), jnp.float32), pltpu.VMEM((n, n), jnp.float32)],
        flops=n * n * n * 400,
    )(spot, *grams, image_gram)


def basis_kernel(columns, lines_at, spot_ref, own_ref, other_ref, range_ref, co_ref, range_out_ref, co_out_ref, range_held_ref, co_held_ref, range_done_ref, co_done_ref, range_sem, co_sem, range_out_sem, co_out_sem):
    lines, rows, _ = range_held_ref.shape
    cells, _, width = co_held_ref.shape
    ranges = [pltpu.make_async_copy(range_ref.at[f], range_held_ref.at[f], range_sem.at[f]) for f in range(lines)]
    ranges_out = [pltpu.make_async_copy(range_done_ref.at[f], range_out_ref.at[pl.ds(lines_at[f] * rows, rows)], range_out_sem.at[f]) for f in range(lines)]
    cos = [pltpu.make_async_copy(co_ref.at[f], co_held_ref.at[f], co_sem.at[f]) for f in range(cells)]
    cos_out = [pltpu.make_async_copy(co_done_ref.at[f], co_out_ref.at[:, pl.ds(columns[f] * width, width)], co_out_sem.at[f]) for f in range(cells)]
    core = spot_ref[0]
    for copy in ranges + cos:
        copy.start()
    first = core == 0
    left = split(jnp.where(first, own_ref[0], other_ref[0]))
    right = split(jnp.where(first, other_ref[0], own_ref[0]))
    for f, copy in enumerate(ranges):
        copy.wait()
        range_done_ref[f] = parts_dot(split(range_held_ref[f]), left, 1, 1)
        ranges_out[f].start()
    for f, copy in enumerate(cos):
        copy.wait()
        co_done_ref[f] = parts_dot(right, split(co_held_ref[f]))
        cos_out[f].start()
    for copy in ranges_out + cos_out:
        copy.wait()


def bases(spot, own, other, range_all, co_all, columns, lines_at):
    lines, rows, k = range_all.shape
    cells, count, width = co_all.shape
    range_held, co_held = pltpu.VMEM(range_all.shape, jnp.float32), pltpu.VMEM(co_all.shape, jnp.float32)
    line_sem, cell_sem = pltpu.SemaphoreType.DMA((lines,)), pltpu.SemaphoreType.DMA((cells,))
    return call(
        functools.partial(basis_kernel, columns, lines_at), (float_shape(lines * rows, k), float_shape(count, cells * width)),
        [SCALAR, WHOLE, WHOLE, OUTSIDE, OUTSIDE], (OUTSIDE, OUTSIDE),
        [range_held, co_held, range_held, co_held, line_sem, cell_sem, line_sem, cell_sem],
        flops=18 * lines * rows * k * k, limit=56,
    )(spot, own, other, range_all, co_all)


def finish_kernel(scale, spot_ref, own_ref, other_ref, middle_own_ref, middle_other_ref, out_ref, middle_ref):
    core, place = spot_ref[0], spot_ref[1]
    half = middle_ref.shape[0] // 2
    chips, extent = middle_own_ref.shape[0], middle_own_ref.shape[1]
    for side, ref in ((core, middle_own_ref), (1 - core, middle_other_ref)):
        for i in range(chips):
            middle_ref[pl.ds(pl.multiple_of(side * half + (place ^ i) * extent, extent), extent), :] = ref[i]
    left = jnp.where(core == 0, own_ref[1], other_ref[1])
    right = jnp.where(core == 0, other_ref[1], own_ref[1])
    out_ref[...] = highest(highest(left, middle_ref[...]), right, 1, 1) * scale


def finish(spot, own, other, middle_own, middle_other, scale):
    k = own.shape[1]
    return call(
        functools.partial(finish_kernel, scale), float_shape(k, k), [SCALAR] + [WHOLE] * 4, WHOLE,
        [pltpu.VMEM((k, k), jnp.float32)], flops=24 * k * k * k,
    )(spot, own, other, middle_own, middle_other)


def per_device(window, range_test, co_test, core_left, core_right):
    rows_total = window.shape[0] * lax.axis_size("cell")
    cols_total = window.shape[1] * lax.axis_size("tm")
    k = range_test.shape[1]
    chips = lax.axis_size("cell") // 2
    groups = groups_of("cell", 1, 2)
    line_groups = groups_of("tm", 0, 2)
    spot = jnp.stack([lax.axis_index("cell") & 1, place_of(groups, lax.axis_index("cell")), place_of(line_groups[:1], lax.axis_index("tm"))]).astype(jnp.int32)
    columns = [(cell & 1) * chips + place_of(groups, cell) for cell in range(2 * chips)]

    lines_at = [place_of(line_groups, line) for line in range(lax.axis_size("tm"))]

    def core_swap(values):
        return swap(values, "cell", 1)

    r3, r2, r1, r0, sent, kept = sketch_terms(spot, chips, window, range_test, co_test, core_left, core_right)
    far = swap(r3, "tm", 1)
    near = swap(r1, "tm", 1)
    pack = kept + core_swap(sent)
    handed = r2 + far
    sketch_z = core_terms(after(spot, pack, handed), window, core_right, core_left)
    pack = scatter_sum(pack, groups)[0]
    handed, near, pack, sketch_z = lax.optimization_barrier((swap(handed, "tm", 2), near, pack, sketch_z))
    range_piece = (r0 + near + handed).reshape(lax.axis_size("tm") // 4, -1, r0.shape[1])
    if line_groups[1:]:
        rest = place_of(line_groups[1:], lax.axis_index("tm"))
        range_piece = jnp.stack([lax.dynamic_index_in_dim(range_piece, rest ^ f, 0, False) for f in range(range_piece.shape[0])])
    range_piece = scatter_sum(range_piece, line_groups[1:])[0]
    width = window.shape[1] // (2 * chips)
    packed = pack_width(co_test.shape[0], width, k)
    co_piece = pack[:packed].reshape(packed, -1, width).swapaxes(0, 1).reshape(-1, width)
    fold = pack[None, packed:]
    range_all = lax.all_gather(range_piece, "tm", axis=0)
    co_all = lax.all_gather(co_piece, "cell", axis=0)

    gram_sent, gram_kept = gram_terms(spot, chips, range_piece, co_piece, (rows_total, cols_total))
    gram = scatter_sum(gram_kept + core_swap(gram_sent), groups)
    gram = whole_sum(gram, "tm")
    grams = gather(gram, groups)

    fold = jnp.concatenate(gather(whole_sum(fold, "tm"), groups))
    middle_sent, middle_kept, image_gram = middle_terms(spot, chips, sketch_z, fold, core_swap(fold))
    middle = whole_sum(scatter_sum(middle_kept + core_swap(middle_sent), groups), "tm")
    middle = jnp.concatenate(gather(middle, groups))
    middle_other = core_swap(middle)

    own = factor_grams(spot, grams, image_gram)
    other = core_swap(own)
    range_basis, co_basis = bases(spot, own, other, range_all, co_all, columns, lines_at)
    core_out = finish(spot, own, other, middle, middle_other, math.sqrt(rows_total * cols_total))
    return (range_basis, co_basis, core_out)


def solution(mesh):
    return jax.shard_map(
        per_device,
        mesh=mesh,
        in_specs=(P("cell", "tm"), P("tm", None), P(None, "cell"), P(None, "cell"), P(None, "tm")),
        out_specs=(P("cell", None), P(None, "tm"), P()),
        check_vma=False,
    )
```

time: 211 us -> 170 us (0.81)
  matrix products: 46.3 us -> 0 us
  Pallas kernels: 29.4 us -> 60.1 us
  waiting for transfers between devices: 86.3 us -> 57.4 us
  between operations: 1.15 us -> 14.4 us
  starting transfers between devices: 34.2 us -> 30.9 us
  other arithmetic: 7.48 us -> 4.25 us
  local copies, waits for them, and re-layouts: 5.55 us -> 2.78 us
    dot_general x20 -> x0, matrix products: 46.3 us -> none  [contract(): lax.dot_general(left, right, dims, precision=precision, preferred_element...]
    pallas_call x2 -> x7, Pallas kernels: 29.4 us -> 60.1 us  [the longest x1 17.3 us: sketch_terms(): call(sketch_kernel, (float_shape(rows // TILES, k),) * 4 + (float_shape(c...]
    ppermute x30 -> x33, waiting for transfers between devices: 86.3 us -> 57.4 us  [swap(): lax.ppermute(values, axis, [(i, i ^ mask) for i in range(lax.axis_size(ax...]
    dynamic_slice x15 -> x0, local copies, waits for them, and re-layouts: 5.2 us -> none  [halve(): sent = lax.dynamic_slice_in_dim(values, (1 - side) * extent, extent, dim)]
    ppermute x30 -> x33, starting transfers between devices: 34.2 us -> 30.9 us  [swap(): lax.ppermute(values, axis, [(i, i ^ mask) for i in range(lax.axis_size(ax...]
    add x15 -> x13, other arithmetic: 4.94 us -> 3.5 us  [the longest x1 1.61 us: per_device(): pack = kept + core_swap(sent)]
  transfers between devices with their start and end apart: 30 -> 35, of which waited for: 13 -> 20; matrix products, arithmetic and copies ran while one was open for 21% -> 2% of each run, Pallas kernels for 7% -> 21%
where the time goes in v4:
time: 170 us
  Pallas kernels  60.1 us (35%)
  waiting for transfers between devices  57.4 us (34%)
  starting transfers between devices  30.9 us (18%)
  between operations  14.4 us (8%)
  other arithmetic  4.25 us (2%)
  local copies, waits for them, and re-layouts  2.78 us (2%)
    ppermute x33, waiting for transfers between devices, swap(): lax.ppermute(values, axis, [(i, i ^ mask) for i in range(lax.axis_size(ax...  57.4 us
    ppermute x33, starting transfers between devices, swap(): lax.ppermute(values, axis, [(i, i ^ mask) for i in range(lax.axis_size(ax...  30.9 us
    pallas_call x1, Pallas kernels, sketch_terms(): call(sketch_kernel, (float_shape(rows // TILES, k),) * 4 + (float_shape(c...  17.3 us
    pallas_call x1, Pallas kernels, factor_grams(): call(functools.partial(factor_kernel, len(grams)), float_shape(2, n, n),...  15.6 us
    pallas_call x1, Pallas kernels, core_terms(): call(core_kernel, float_shape(s_core, s_core), [SCALAR] + [OUTSIDE] * 3,...  13.4 us
    pallas_call x1, Pallas kernels, bases(): call(functools.partial(basis_kernel, columns, lines_at), (float_shape(lin...  7.78 us
  transfers between devices with their start and end apart: 35, of which 20 were waited for; matrix products, arithmetic and copies ran while one was open for 2% of the time, Pallas kernels for 21%

profile of v4, /device:TPU:0, one launch (start us, length us, event | category | flops | bytes accessed | tf_op | source)
XLA Modules:
  0.0 169.8 jit_solution(14653950472158999874)
XLA Ops:
  7.2 0.6 pad_add_fusion.spot_ref
  7.8 17.3 %shard_map.76 = (f32[256,256]{1,0:T(8,128)}, f32[256,256]{1,0:T(8,128)}, f32[256,256]{1,0:T(8,128)}, f32[256,256]{1,0:T(8,128)}, f32[4,384,256]{2,1,0:T(8,128)}, /*index=5*/f32[4,384,256]{2,1,0:T(8,128)}) custom-call(s32[3]{0:T(128)} %pad_add_fusion.spot_ref, f32[1024,2048]{1,0:T(8,128)} %window_ref.3, f32[2048,256]{1,0:T(8,128)} %test_ref.1, ...), custom_call_target="tpu_custom_call" | custom-call | flops 6442450944 | bytes 4194304 | tf_op jit(solution)/shard_map/pallas_call | solution.py:189
  25.1 0.5 collective-permute-start.3
  25.6 2.6 %collective-permute-start = (f32[256,256]{1,0:T(8,128)}, f32[256,256]{1,0:T(8,128)S(1)}, u32[]{:S(2)}, u32[]{:S(2)}) collective-permute-start(f32[256,256]{1,0:T(8,128)} %get-tuple-element.23), channel_id=1, source_target_pairs={{0,1},{1,0},{2,3},{3,2},{4,5},{5,4},{6,7},{7,6},{8,9},{9,8},{10,11... | collective-permute-start | bytes 786440 | tf_op jit(solution)/shard_map/ppermute | solution.py:69
  28.3 0.1 collective-permute-start.2
  28.3 7.3 %collective-permute-done = f32[256,256]{1,0:T(8,128)S(1)} collective-permute-done((f32[256,256]{1,0:T(8,128)}, f32[256,256]{1,0:T(8,128)S(1)}, u32[]{:S(2)}, u32[]{:S(2)}) %collective-permute-start) | collective-permute-done | bytes 262176 | tf_op jit(solution)/shard_map/ppermute | solution.py:69
  35.6 1.0 add.71
  36.6 3.0 %collective-permute-start.1 = (f32[256,256]{1,0:T(8,128)S(1)}, f32[256,256]{1,0:T(8,128)S(1)}, u32[]{:S(2)}, u32[]{:S(2)}) collective-permute-start(f32[256,256]{1,0:T(8,128)S(1)} %add.71), channel_id=1, source_target_pairs={{0,2},{1,3},{2,0},{3,1},{4,6},{5,7},{6,4},{7,5},{8,10},{9,11},{10,... | collective-permute-start | bytes 786440 | tf_op jit(solution)/shard_map/ppermute | solution.py:69
  39.6 1.6 add.72
  41.3 0.1 fusion.5
  41.3 2.5 %collective-permute-start.6 = (f32[1,384,256]{2,1,0:T(8,128)S(1)}, f32[1,384,256]{2,1,0:T(8,128)S(1)}, u32[]{:S(2)}, u32[]{:S(2)}) collective-permute-start(f32[1,384,256]{2,1,0:T(8,128)S(1)} %get-tuple-element.39), channel_id=1, source_target_pairs={{0,24},{4,28},{8,16},{12,20},{16,8},{20,12},{24,0},{28,4},{1,25},{... | collective-permute-start | bytes 1179656 | tf_op jit(solution)/shard_map/ppermute | solution.py:69
  43.9 0.5 collective-permute-start.5
  44.4 0.5 collective-permute-start.4
  44.9 13.4 %shard_map.77.z_ref = f32[512,512]{1,0:T(8,128)} custom-call(s32[3]{0:T(128)} %pad_add_fusion.spot_ref, f32[1024,2048]{1,0:T(8,128)} %window_ref.3, f32[512,2048]{1,0:T(8,128)} %right_ref.3, f32[512,1024]{1,0:T(8,128)} %left_ref.3), custom_call_target="tpu_custom_call" | custom-call | flops 9663676416 | bytes 4194304 | tf_op jit(solution)/shard_map/pallas_call | solution.py:242
  58.4 2.3 %collective-permute-done.5 = f32[1,384,256]{2,1,0:T(8,128)S(1)} collective-permute-done((f32[1,384,256]{2,1,0:T(8,128)S(1)}, f32[1,384,256]{2,1,0:T(8,128)S(1)}, u32[]{:S(2)}, u32[]{:S(2)}) %collective-permute-start.5) | collective-permute-done | bytes 393248 | tf_op jit(solution)/shard_map/ppermute | solution.py:69
  60.7 0.1 collective-permute-done.4
  60.8 0.1 fusion.1
  60.9 0.8 add_add_fusion.range_ref
  61.8 0.7 slice.46.co_ref
  62.6 1.6 collective-permute-start.16
  64.2 0.9 copy-done.1
  65.2 0.9 copy-done.2
  66.1 1.2 shard_map.78
  67.3 0.1 collective-permute-start.7
  67.4 0.5 collective-permute-done.16
  68.0 0.4 collective-permute-start.17
  68.4 16.5 %collective-permute-done.17 = f32[1,128,256]{2,1,0:T(8,128)S(1)} collective-permute-done((f32[1,128,256]{2,1,0:T(8,128)S(1)}, f32[1,128,256]{2,1,0:T(8,128)S(1)}, u32[]{:S(2)}, u32[]{:S(2)}) %collective-permute-start.17) | collective-permute-done | bytes 131104 | tf_op jit(solution)/shard_map/ppermute | solution.py:69
  84.9 1.7 %collective-permute-start.20 = (f32[1,128,256]{2,1,0:T(8,128)S(1)}, f32[1,128,256]{2,1,0:T(8,128)S(1)}, u32[]{:S(2)}, u32[]{:S(2)}) collective-permute-start(f32[1,128,256]{2,1,0:T(8,128)S(1)} %add.85), channel_id=1, source_target_pairs={{0,24},{4,28},{8,16},{12,20},{16,8},{20,12},{24,0},{28,4},{1,25},{... | collective-permute-start | bytes 393224 | tf_op jit(solution)/shard_map/ppermute | solution.py:69
  86.6 1.3 collective-permute-start.19
  87.9 0.5 collective-permute-start.18
  88.5 3.7 %collective-permute-done.20 = f32[1,128,256]{2,1,0:T(8,128)S(1)} collective-permute-done((f32[1,128,256]{2,1,0:T(8,128)S(1)}, f32[1,128,256]{2,1,0:T(8,128)S(1)}, u32[]{:S(2)}, u32[]{:S(2)}) %collective-permute-start.20) | collective-permute-done | bytes 131104 | tf_op jit(solution)/shard_map/ppermute | solution.py:69
  92.2 1.8 %collective-permute-done.19 = f32[1,128,256]{2,1,0:T(8,128)S(1)} collective-permute-done((f32[1,128,256]{2,1,0:T(8,128)S(1)}, f32[1,128,256]{2,1,0:T(8,128)S(1)}, u32[]{:S(2)}, u32[]{:S(2)}) %collective-permute-start.19) | collective-permute-done | bytes 131104 | tf_op jit(solution)/shard_map/ppermute | solution.py:69
  94.1 0.2 collective-permute-start.21
  94.3 1.6 collective-permute-start.10
  95.9 1.4 collective-permute-start.9
  97.3 0.5 collective-permute-start.8
  97.9 1.9 %collective-permute-done.10 = f32[1,64,256]{2,1,0:T(8,128)S(1)} collective-permute-done((f32[1,64,256]{2,1,0:T(8,128)S(1)}, f32[1,64,256]{2,1,0:T(8,128)S(1)}, u32[]{:S(2)}, u32[]{:S(2)}) %collective-permute-start.10) | collective-permute-done | bytes 65568 | tf_op jit(solution)/shard_map/ppermute | solution.py:69
  99.7 1.3 collective-permute-done.9
  101.0 0.5 collective-permute-done.8
  101.6 0.1 collective-permute-start.11
  101.7 2.5 %shard_map.79 = (f32[4,32,256]{2,1,0:T(8,128)S(1)}, f32[4,32,256]{2,1,0:T(8,128)S(1)}, f32[256,256]{1,0:T(8,128)S(1)}) custom-call(s32[3]{0:T(128)S(1)} %copy-done.5, f32[512,512]{1,0:T(8,128)S(1)} %copy-done, f32[4,128,256]{2,1,0:T(8,128)S(1)} %pad_maximum_fusion.own_ref, f32[4,128,256]{2,1,0:T(8,128)S(1)} %collective-permute-done.21.other_ref), custom_call_target="tpu_custom_call" | custom-call | flops 402653184 | bytes 4194304 | tf_op jit(solution)/shard_map/pallas_call | solution.py:291
  104.3 1.6 collective-permute-done.11
  106.0 5.9 %collective-permute-done.12 = f32[1,64,256]{2,1,0:T(8,128)S(1)} collective-permute-done((f32[1,64,256]{2,1,0:T(8,128)S(1)}, f32[1,64,256]{2,1,0:T(8,128)S(1)}, u32[]{:S(2)}, u32[]{:S(2)}) %collective-permute-start.12) | collective-permute-done | bytes 65568 | tf_op jit(solution)/shard_map/ppermute | solution.py:69
  111.9 1.3 collective-permute-start.15
  113.2 1.2 collective-permute-start.14
  114.4 1.0 collective-permute-start.13
  115.5 1.3 collective-permute-start.26
  116.8 1.2 collective-permute-start.25
  118.0 0.4 collective-permute-done.15.refs_3_
  118.5 1.1 collective-permute-start.24
  119.6 0.5 collective-permute-done.13.refs_1_
  120.1 15.6 %shard_map.80.own_ref = f32[2,256,256]{2,1,0:T(8,128)S(1)} custom-call(s32[3]{0:T(128)S(1)} %copy-done.5, f32[1,64,256]{2,1,0:T(8,128)S(1)} %add.83.refs_0_, f32[1,64,256]{2,1,0:T(8,128)S(1)} %collective-permute-done.13.refs_1_, f32[1,64,256]{2,1,0:T(8,128)S(1)} %collective-permute-done.14.refs_2_, f32[1,64,256]{2,1,0:T(8,128)S(1)} %collective-permute-done.15.refs_3_, ...), custom_call_target="tpu_custom_call" | custom-call | flops 6710886400 | bytes 4194304 | tf_op jit(solution)/shard_map/pallas_call | solution.py:383
  135.9 0.5 collective-permute-start.27
  136.4 3.5 %collective-permute-done.27 = f32[1,32,256]{2,1,0:T(8,128)S(1)} collective-permute-done((f32[1,32,256]{2,1,0:T(8,128)S(1)}, f32[1,32,256]{2,1,0:T(8,128)S(1)}, u32[]{:S(2)}, u32[]{:S(2)}) %collective-permute-start.27) | collective-permute-done | bytes 32800 | tf_op jit(solution)/shard_map/ppermute | solution.py:69
  139.9 5.0 %collective-permute-done.28 = f32[1,32,256]{2,1,0:T(8,128)S(1)} collective-permute-done((f32[1,32,256]{2,1,0:T(8,128)S(1)}, f32[1,32,256]{2,1,0:T(8,128)S(1)}, u32[]{:S(2)}, u32[]{:S(2)}) %collective-permute-start.28) | collective-permute-done | bytes 32800 | tf_op jit(solution)/shard_map/ppermute | solution.py:69
  144.9 1.8 %collective-permute-start.31 = (f32[1,32,256]{2,1,0:T(8,128)S(1)}, f32[1,32,256]{2,1,0:T(8,128)S(1)}, u32[]{:S(2)}, u32[]{:S(2)}) collective-permute-start(f32[1,32,256]{2,1,0:T(8,128)S(1)} %add.91), channel_id=1, source_target_pairs={{0,24},{4,28},{8,16},{12,20},{16,8},{20,12},{24,0},{28,4},{1,25},{... | collective-permute-start | bytes 98312 | tf_op jit(solution)/shard_map/ppermute | solution.py:69
  146.7 0.9 collective-permute-start.30
  147.6 0.8 collective-permute-start.29
  148.4 1.3 collective-permute-done.31
  149.7 0.9 collective-permute-done.30
  150.6 0.9 collective-permute-done.29
  151.6 1.3 collective-permute-done.32.middle_other_ref
  152.9 2.3 %shard_map.82 = f32[256,256]{1,0:T(8,128)} custom-call(s32[3]{0:T(128)S(1)} %copy-done.5, f32[2,256,256]{2,1,0:T(8,128)S(1)} %shard_map.80.own_ref, f32[2,256,256]{2,1,0:T(8,128)S(1)} %collective-permute-done.22.other_ref, f32[4,32,256]{2,1,0:T(8,128)S(1)} %pad_maximum_fusion.1.middle_own_ref, f32[4,32,256]{2,1,0:T(8,128)S(1)} %collective-permute-done.32.middle_other_ref), custom_call_target="tpu_custom_call" | custom-call | flops 402653184 | bytes 4194304 | tf_op jit(solution)/shard_map/pallas_call | solution.py:442
  155.2 7.8 %shard_map.81 = (f32[1024,256]{1,0:T(8,128)}, f32[256,2048]{1,0:T(8,128)}) custom-call(s32[3]{0:T(128)} %pad_add_fusion.spot_ref, f32[2,256,256]{2,1,0:T(8,128)} %copy-done.3, f32[2,256,256]{2,1,0:T(8,128)} %copy-done.4, f32[4,256,256]{2,1,0:T(8,128)} %bitcast.12, f32[8,256,256]{2,1,0:T(8,128)} %bitcast.11), custom_call_target="tpu_custom_call" | custom-call | flops 1207959552 | bytes 4194304 | tf_op jit(solution)/shard_map/pallas_call | solution.py:420
  (51 shorter events, 0.7 us)
Async XLA Ops:
  7.2 148.0 %all-gather.5.cloned.1.call-start = ((), (), s32[]{:S(2)}) async-start(), calls=%async_computation | async-start | bytes 1310720 | tf_op jit(solution)/shard_map/all_gather | solution.py:480
  25.1 14.6 %collective-permute-start.3 = (f32[4,384,256]{2,1,0:T(8,128)}, f32[4,384,256]{2,1,0:T(8,128)S(1)}, u32[]{:S(2)}, u32[]{:S(2)}) collective-permute-start(f32[4,384,256]{2,1,0:T(8,128)} %get-tuple-element.26), channel_id=1, source_target_pairs={{0,4},{4,0},{8,12},{12,8},{16,20},{20,16},{24,28},{28,24},{1,5},{5... | collective-permute-start | bytes 4718600 | tf_op jit(solution)/shard_map/ppermute | solution.py:69
  25.6 10.0 %collective-permute-start = (f32[256,256]{1,0:T(8,128)}, f32[256,256]{1,0:T(8,128)S(1)}, u32[]{:S(2)}, u32[]{:S(2)}) collective-permute-start(f32[256,256]{1,0:T(8,128)} %get-tuple-element.23), channel_id=1, source_target_pairs={{0,1},{1,0},{2,3},{3,2},{4,5},{5,4},{6,7},{7,6},{8,9},{9,8},{10,11... | collective-permute-start | bytes 786440 | tf_op jit(solution)/shard_map/ppermute | solution.py:69
  28.3 32.6 %collective-permute-start.2 = (f32[256,256]{1,0:T(8,128)}, f32[256,256]{1,0:T(8,128)S(1)}, u32[]{:S(2)}, u32[]{:S(2)}) collective-permute-start(f32[256,256]{1,0:T(8,128)} %get-tuple-element.24), channel_id=1, source_target_pairs={{0,1},{1,0},{2,3},{3,2},{4,5},{5,4},{6,7},{7,6},{8,9},{9,8},{10,11... | collective-permute-start | bytes 786440 | tf_op jit(solution)/shard_map/ppermute | solution.py:69
  36.6 24.3 %collective-permute-start.1 = (f32[256,256]{1,0:T(8,128)S(1)}, f32[256,256]{1,0:T(8,128)S(1)}, u32[]{:S(2)}, u32[]{:S(2)}) collective-permute-start(f32[256,256]{1,0:T(8,128)S(1)} %add.71), channel_id=1, source_target_pairs={{0,2},{1,3},{2,0},{3,1},{4,6},{5,7},{6,4},{7,5},{8,10},{9,11},{10,... | collective-permute-start | bytes 786440 | tf_op jit(solution)/shard_map/ppermute | solution.py:69
  41.3 17.0 %collective-permute-start.6 = (f32[1,384,256]{2,1,0:T(8,128)S(1)}, f32[1,384,256]{2,1,0:T(8,128)S(1)}, u32[]{:S(2)}, u32[]{:S(2)}) collective-permute-start(f32[1,384,256]{2,1,0:T(8,128)S(1)} %get-tuple-element.39), channel_id=1, source_target_pairs={{0,24},{4,28},{8,16},{12,20},{16,8},{20,12},{24,0},{28,4},{1,25},{... | collective-permute-start | bytes 1179656 | tf_op jit(solution)/shard_map/ppermute | solution.py:69
  43.9 16.8 %collective-permute-start.5 = (f32[1,384,256]{2,1,0:T(8,128)S(1)}, f32[1,384,256]{2,1,0:T(8,128)S(1)}, u32[]{:S(2)}, u32[]{:S(2)}) collective-permute-start(f32[1,384,256]{2,1,0:T(8,128)S(1)} %get-tuple-element.40), channel_id=1, source_target_pairs={{0,16},{4,20},{8,24},{12,28},{16,0},{20,4},{24,8},{28,12},{1,17},{... | collective-permute-start | bytes 1179656 | tf_op jit(solution)/shard_map/ppermute | solution.py:69
  44.4 16.4 %collective-permute-start.4 = (f32[1,384,256]{2,1,0:T(8,128)S(1)}, f32[1,384,256]{2,1,0:T(8,128)S(1)}, u32[]{:S(2)}, u32[]{:S(2)}) collective-permute-start(f32[1,384,256]{2,1,0:T(8,128)S(1)} %get-tuple-element.41), channel_id=1, source_target_pairs={{0,8},{4,12},{8,0},{12,4},{16,24},{20,28},{24,16},{28,20},{1,9},{5... | collective-permute-start | bytes 1179656 | tf_op jit(solution)/shard_map/ppermute | solution.py:69
  58.3 2.6 %copy-start.6 = (f32[256,256]{1,0:T(8,128)S(1)}, f32[256,256]{1,0:T(8,128)}, u32[]{:S(2)}) copy-start(f32[256,256]{1,0:T(8,128)} %get-tuple-element.21) | copy-start | bytes 786436
  58.3 5.9 %copy-start.5 = (s32[3]{0:T(128)S(1)}, s32[3]{0:T(128)}, u32[]{:S(2)}) copy-start(s32[3]{0:T(128)} %pad_add_fusion.spot_ref) | copy-start | bytes 40
  61.7 93.5 %all-gather.7.cloned.1.call-start = ((), (), s32[]{:S(2)}) async-start(), calls=%async_computation.1 | async-start | bytes 2359296 | tf_op jit(solution)/shard_map/all_gather | solution.py:481
  62.5 39.1 %copy-start = (f32[512,512]{1,0:T(8,128)S(1)}, f32[512,512]{1,0:T(8,128)}, u32[]{:S(2)}) copy-start(f32[512,512]{1,0:T(8,128)} %shard_map.77.z_ref) | copy-start | bytes 3145732
  62.6 5.4 %collective-permute-start.16 = (f32[1,128,256]{2,1,0:T(8,128)S(1)}, f32[1,128,256]{2,1,0:T(8,128)S(1)}, u32[]{:S(2)}, u32[]{:S(2)}) collective-permute-start(f32[1,128,256]{2,1,0:T(8,128)S(1)} %slice_bitcast_fusion), channel_id=1, source_target_pairs={{0,1},{1,0},{2,3},{3,2},{4,5},{5,4},{6,7},{7,6},{8,9},{9,8},{10,11... | collective-permute-start | bytes 393224 | tf_op jit(solution)/shard_map/ppermute | solution.py:69
  64.2 1.0 copy-start.1
  65.1 0.9 copy-start.2
  67.3 21.1 %collective-permute-start.7 = (f32[4,64,256]{2,1,0:T(8,128)S(1)}, f32[4,64,256]{2,1,0:T(8,128)S(1)}, u32[]{:S(2)}, u32[]{:S(2)}) collective-permute-start(f32[4,64,256]{2,1,0:T(8,128)S(1)} %get-tuple-element.32), channel_id=1, source_target_pairs={{0,4},{4,0},{8,12},{12,8},{16,20},{20,16},{24,28},{28,24},{1,5},{5... | collective-permute-start | bytes 786440 | tf_op jit(solution)/shard_map/ppermute | solution.py:69
  68.0 16.9 %collective-permute-start.17 = (f32[1,128,256]{2,1,0:T(8,128)S(1)}, f32[1,128,256]{2,1,0:T(8,128)S(1)}, u32[]{:S(2)}, u32[]{:S(2)}) collective-permute-start(f32[1,128,256]{2,1,0:T(8,128)S(1)} %fusion.4), channel_id=1, source_target_pairs={{0,2},{1,3},{2,0},{3,1},{4,6},{5,7},{6,4},{7,5},{8,10},{9,11},{10,... | collective-permute-start | bytes 393224 | tf_op jit(solution)/shard_map/ppermute | solution.py:69
  84.9 7.3 %collective-permute-start.20 = (f32[1,128,256]{2,1,0:T(8,128)S(1)}, f32[1,128,256]{2,1,0:T(8,128)S(1)}, u32[]{:S(2)}, u32[]{:S(2)}) collective-permute-start(f32[1,128,256]{2,1,0:T(8,128)S(1)} %add.85), channel_id=1, source_target_pairs={{0,24},{4,28},{8,16},{12,20},{16,8},{20,12},{24,0},{28,4},{1,25},{... | collective-permute-start | bytes 393224 | tf_op jit(solution)/shard_map/ppermute | solution.py:69
  86.6 7.4 %collective-permute-start.19 = (f32[1,128,256]{2,1,0:T(8,128)S(1)}, f32[1,128,256]{2,1,0:T(8,128)S(1)}, u32[]{:S(2)}, u32[]{:S(2)}) collective-permute-start(f32[1,128,256]{2,1,0:T(8,128)S(1)} %add.85), channel_id=1, source_target_pairs={{0,16},{4,20},{8,24},{12,28},{16,0},{20,4},{24,8},{28,12},{1,17},{... | collective-permute-start | bytes 393224 | tf_op jit(solution)/shard_map/ppermute | solution.py:69
  87.9 6.1 %collective-permute-start.18 = (f32[1,128,256]{2,1,0:T(8,128)S(1)}, f32[1,128,256]{2,1,0:T(8,128)S(1)}, u32[]{:S(2)}, u32[]{:S(2)}) collective-permute-start(f32[1,128,256]{2,1,0:T(8,128)S(1)} %add.85), channel_id=1, source_target_pairs={{0,8},{4,12},{8,0},{12,4},{16,24},{20,28},{24,16},{28,20},{1,9},{5... | collective-permute-start | bytes 393224 | tf_op jit(solution)/shard_map/ppermute | solution.py:69
  94.1 7.6 %collective-permute-start.21 = (f32[4,128,256]{2,1,0:T(8,128)S(1)}, f32[4,128,256]{2,1,0:T(8,128)S(1)}, u32[]{:S(2)}, u32[]{:S(2)}) collective-permute-start(f32[4,128,256]{2,1,0:T(8,128)S(1)} %pad_maximum_fusion.own_ref), channel_id=1, source_target_pairs={{0,4},{4,0},{8,12},{12,8},{16,20},{20,16},{24,28},{28,24},{1,5},{5... | collective-permute-start | bytes 1572872 | tf_op jit(solution)/shard_map/ppermute | solution.py:69
  94.3 5.5 %collective-permute-start.10 = (f32[1,64,256]{2,1,0:T(8,128)S(1)}, f32[1,64,256]{2,1,0:T(8,128)S(1)}, u32[]{:S(2)}, u32[]{:S(2)}) collective-permute-start(f32[1,64,256]{2,1,0:T(8,128)S(1)} %get-tuple-element.42), channel_id=1, source_target_pairs={{0,24},{4,28},{8,16},{12,20},{16,8},{20,12},{24,0},{28,4},{1,25},{... | collective-permute-start | bytes 196616 | tf_op jit(solution)/shard_map/ppermute | solution.py:69
  95.9 5.1 %collective-permute-start.9 = (f32[1,64,256]{2,1,0:T(8,128)S(1)}, f32[1,64,256]{2,1,0:T(8,128)S(1)}, u32[]{:S(2)}, u32[]{:S(2)}) collective-permute-start(f32[1,64,256]{2,1,0:T(8,128)S(1)} %get-tuple-element.43), channel_id=1, source_target_pairs={{0,16},{4,20},{8,24},{12,28},{16,0},{20,4},{24,8},{28,12},{1,17},{... | collective-permute-start | bytes 196616 | tf_op jit(solution)/shard_map/ppermute | solution.py:69
  97.3 4.3 %collective-permute-start.8 = (f32[1,64,256]{2,1,0:T(8,128)S(1)}, f32[1,64,256]{2,1,0:T(8,128)S(1)}, u32[]{:S(2)}, u32[]{:S(2)}) collective-permute-start(f32[1,64,256]{2,1,0:T(8,128)S(1)} %get-tuple-element.44), channel_id=1, source_target_pairs={{0,8},{4,12},{8,0},{12,4},{16,24},{20,28},{24,16},{28,20},{1,9},{5... | collective-permute-start | bytes 196616 | tf_op jit(solution)/shard_map/ppermute | solution.py:69
  101.6 4.3 %collective-permute-start.11 = (f32[1,64,256]{2,1,0:T(8,128)S(1)}, f32[1,64,256]{2,1,0:T(8,128)S(1)}, u32[]{:S(2)}, u32[]{:S(2)}) collective-permute-start(f32[1,64,256]{2,1,0:T(8,128)S(1)} %fusion.2), channel_id=1, source_target_pairs={{0,1},{1,0},{2,3},{3,2},{4,5},{5,4},{6,7},{7,6},{8,9},{9,8},{10,11... | collective-permute-start | bytes 196616 | tf_op jit(solution)/shard_map/ppermute | solution.py:69
  104.2 11.3 %collective-permute-start.23 = (f32[4,32,256]{2,1,0:T(8,128)S(1)}, f32[4,32,256]{2,1,0:T(8,128)S(1)}, u32[]{:S(2)}, u32[]{:S(2)}) collective-permute-start(f32[4,32,256]{2,1,0:T(8,128)S(1)} %get-tuple-element.38), channel_id=1, source_target_pairs={{0,4},{4,0},{8,12},{12,8},{16,20},{20,16},{24,28},{28,24},{1,5},{5... | collective-permute-start | bytes 393224 | tf_op jit(solution)/shard_map/ppermute | solution.py:69
  105.9 6.0 %collective-permute-start.12 = (f32[1,64,256]{2,1,0:T(8,128)S(1)}, f32[1,64,256]{2,1,0:T(8,128)S(1)}, u32[]{:S(2)}, u32[]{:S(2)}) collective-permute-start(f32[1,64,256]{2,1,0:T(8,128)S(1)} %add.82), channel_id=1, source_target_pairs={{0,2},{1,3},{2,0},{3,1},{4,6},{5,7},{6,4},{7,5},{8,10},{9,11},{10,... | collective-permute-start | bytes 196616 | tf_op jit(solution)/shard_map/ppermute | solution.py:69
  111.9 6.6 %collective-permute-start.15 = (f32[1,64,256]{2,1,0:T(8,128)S(1)}, f32[1,64,256]{2,1,0:T(8,128)S(1)}, u32[]{:S(2)}, u32[]{:S(2)}) collective-permute-start(f32[1,64,256]{2,1,0:T(8,128)S(1)} %add.83.refs_0_), channel_id=1, source_target_pairs={{0,24},{4,28},{8,16},{12,20},{16,8},{20,12},{24,0},{28,4},{1,25},{... | collective-permute-start | bytes 196616 | tf_op jit(solution)/shard_map/ppermute | solution.py:69
  113.2 6.4 %collective-permute-start.14 = (f32[1,64,256]{2,1,0:T(8,128)S(1)}, f32[1,64,256]{2,1,0:T(8,128)S(1)}, u32[]{:S(2)}, u32[]{:S(2)}) collective-permute-start(f32[1,64,256]{2,1,0:T(8,128)S(1)} %add.83.refs_0_), channel_id=1, source_target_pairs={{0,16},{4,20},{8,24},{12,28},{16,0},{20,4},{24,8},{28,12},{1,17},{... | collective-permute-start | bytes 196616 | tf_op jit(solution)/shard_map/ppermute | solution.py:69
  114.4 5.6 %collective-permute-start.13 = (f32[1,64,256]{2,1,0:T(8,128)S(1)}, f32[1,64,256]{2,1,0:T(8,128)S(1)}, u32[]{:S(2)}, u32[]{:S(2)}) collective-permute-start(f32[1,64,256]{2,1,0:T(8,128)S(1)} %add.83.refs_0_), channel_id=1, source_target_pairs={{0,8},{4,12},{8,0},{12,4},{16,24},{20,28},{24,16},{28,20},{1,9},{5... | collective-permute-start | bytes 196616 | tf_op jit(solution)/shard_map/ppermute | solution.py:69
  115.5 20.3 %collective-permute-start.26 = (f32[1,32,256]{2,1,0:T(8,128)S(1)}, f32[1,32,256]{2,1,0:T(8,128)S(1)}, u32[]{:S(2)}, u32[]{:S(2)}) collective-permute-start(f32[1,32,256]{2,1,0:T(8,128)S(1)} %get-tuple-element.45), channel_id=1, source_target_pairs={{0,24},{4,28},{8,16},{12,20},{16,8},{20,12},{24,0},{28,4},{1,25},{... | collective-permute-start | bytes 98312 | tf_op jit(solution)/shard_map/ppermute | solution.py:69
  116.8 19.0 %collective-permute-start.25 = (f32[1,32,256]{2,1,0:T(8,128)S(1)}, f32[1,32,256]{2,1,0:T(8,128)S(1)}, u32[]{:S(2)}, u32[]{:S(2)}) collective-permute-start(f32[1,32,256]{2,1,0:T(8,128)S(1)} %get-tuple-element.46), channel_id=1, source_target_pairs={{0,16},{4,20},{8,24},{12,28},{16,0},{20,4},{24,8},{28,12},{1,17},{... | collective-permute-start | bytes 98312 | tf_op jit(solution)/shard_map/ppermute | solution.py:69
  118.5 17.4 %collective-permute-start.24 = (f32[1,32,256]{2,1,0:T(8,128)S(1)}, f32[1,32,256]{2,1,0:T(8,128)S(1)}, u32[]{:S(2)}, u32[]{:S(2)}) collective-permute-start(f32[1,32,256]{2,1,0:T(8,128)S(1)} %get-tuple-element.47), channel_id=1, source_target_pairs={{0,8},{4,12},{8,0},{12,4},{16,24},{20,28},{24,16},{28,20},{1,9},{5... | collective-permute-start | bytes 98312 | tf_op jit(solution)/shard_map/ppermute | solution.py:69
  135.7 19.5 %copy-start.3 = (f32[2,256,256]{2,1,0:T(8,128)}, f32[2,256,256]{2,1,0:T(8,128)S(1)}, u32[]{:S(2)}) copy-start(f32[2,256,256]{2,1,0:T(8,128)S(1)} %shard_map.80.own_ref) | copy-start | bytes 1572868
  135.7 17.2 %collective-permute-start.22 = (f32[2,256,256]{2,1,0:T(8,128)S(1)}, f32[2,256,256]{2,1,0:T(8,128)S(1)}, u32[]{:S(2)}, u32[]{:S(2)}) collective-permute-start(f32[2,256,256]{2,1,0:T(8,128)S(1)} %shard_map.80.own_ref), channel_id=1, source_target_pairs={{0,4},{4,0},{8,12},{12,8},{16,20},{20,16},{24,28},{28,24},{1,5},{5... | collective-permute-start | bytes 1572872 | tf_op jit(solution)/shard_map/ppermute | solution.py:69
  135.9 4.0 %collective-permute-start.27 = (f32[1,32,256]{2,1,0:T(8,128)S(1)}, f32[1,32,256]{2,1,0:T(8,128)S(1)}, u32[]{:S(2)}, u32[]{:S(2)}) collective-permute-start(f32[1,32,256]{2,1,0:T(8,128)S(1)} %fusion.3), channel_id=1, source_target_pairs={{0,1},{1,0},{2,3},{3,2},{4,5},{5,4},{6,7},{7,6},{8,9},{9,8},{10,11... | collective-permute-start | bytes 98312 | tf_op jit(solution)/shard_map/ppermute | solution.py:69
  139.9 5.0 %collective-permute-start.28 = (f32[1,32,256]{2,1,0:T(8,128)S(1)}, f32[1,32,256]{2,1,0:T(8,128)S(1)}, u32[]{:S(2)}, u32[]{:S(2)}) collective-permute-start(f32[1,32,256]{2,1,0:T(8,128)S(1)} %add.90), channel_id=1, source_target_pairs={{0,2},{1,3},{2,0},{3,1},{4,6},{5,7},{6,4},{7,5},{8,10},{9,11},{10,... | collective-permute-start | bytes 98312 | tf_op jit(solution)/shard_map/ppermute | solution.py:69
  144.9 4.8 %collective-permute-start.31 = (f32[1,32,256]{2,1,0:T(8,128)S(1)}, f32[1,32,256]{2,1,0:T(8,128)S(1)}, u32[]{:S(2)}, u32[]{:S(2)}) collective-permute-start(f32[1,32,256]{2,1,0:T(8,128)S(1)} %add.91), channel_id=1, source_target_pairs={{0,24},{4,28},{8,16},{12,20},{16,8},{20,12},{24,0},{28,4},{1,25},{... | collective-permute-start | bytes 98312 | tf_op jit(solution)/shard_map/ppermute | solution.py:69
  146.7 3.9 %collective-permute-start.30 = (f32[1,32,256]{2,1,0:T(8,128)S(1)}, f32[1,32,256]{2,1,0:T(8,128)S(1)}, u32[]{:S(2)}, u32[]{:S(2)}) collective-permute-start(f32[1,32,256]{2,1,0:T(8,128)S(1)} %add.91), channel_id=1, source_target_pairs={{0,16},{4,20},{8,24},{12,28},{16,0},{20,4},{24,8},{28,12},{1,17},{... | collective-permute-start | bytes 98312 | tf_op jit(solution)/shard_map/ppermute | solution.py:69
  147.6 3.9 %collective-permute-start.29 = (f32[1,32,256]{2,1,0:T(8,128)S(1)}, f32[1,32,256]{2,1,0:T(8,128)S(1)}, u32[]{:S(2)}, u32[]{:S(2)}) collective-permute-start(f32[1,32,256]{2,1,0:T(8,128)S(1)} %add.91), channel_id=1, source_target_pairs={{0,8},{4,12},{8,0},{12,4},{16,24},{20,28},{24,16},{28,20},{1,9},{5... | collective-permute-start | bytes 98312 | tf_op jit(solution)/shard_map/ppermute | solution.py:69
  151.5 1.4 collective-permute-start.32
  152.9 2.3 %copy-start.4 = (f32[2,256,256]{2,1,0:T(8,128)}, f32[2,256,256]{2,1,0:T(8,128)S(1)}, u32[]{:S(2)}) copy-start(f32[2,256,256]{2,1,0:T(8,128)S(1)} %collective-permute-done.22.other_ref) | copy-start | bytes 1572868
Sparse Core Ops, SparseCore 0:
  61.8 32.5 all-gather.4
  96.3 28.5 all-gather.6

commit v5 on v4

--- a/solution.py
+++ b/solution.py
@@ -332,12 +332,9 @@
     return [jnp.concatenate([rows[b][g] * lax.rsqrt(pivots[b][g]) for g in range(groups)], axis=0) for b in range(count)]
 
 
-def factor_kernel(peers, spot_ref, *refs):
-    gram_refs, (image_ref, out_ref, inverse_ref, upper_ref) = refs[:peers], refs[peers:]
+def factor_steps(steps, inverse_ref, upper_ref):
     count, n = inverse_ref.shape[0], inverse_ref.shape[1]
     every = range(count)
-    put_blocks(gram_refs, inverse_ref.at[0], spot_ref[1])
-    inverse_ref[1] = image_ref[...]
     row_id = lax.broadcasted_iota(jnp.int32, (n, n), 0)
     col_id = lax.broadcasted_iota(jnp.int32, (n, n), 1)
     panel_col = lax.broadcasted_iota(jnp.int32, (BASE, n), 1)
@@ -371,58 +368,103 @@
         upper_ref[pl.ds(start, BASE), :] = jnp.where(inside, up_placed, jnp.where(panel_col >= start + BASE, rows[0], 0.0))
         return carry
 
-    lax.fori_loop(0, n // BASE, step, 0)
+    lax.fori_loop(steps[0], steps[1], step, 0)
+
+
+def factor_start_kernel(steps, peers, spot_ref, *refs):
+    gram_refs, (image_ref, inverse_ref, upper_ref) = refs[:peers], refs[peers:]
+    put_blocks(gram_refs, inverse_ref.at[0], spot_ref[1])
+    inverse_ref[1] = image_ref[...]
+    upper_ref[...] = jnp.zeros_like(upper_ref)
+    factor_steps(steps, inverse_ref, upper_ref)
+
+
+def factor_end_kernel(steps, begun_ref, begun_upper_ref, out_ref, inverse_ref, upper_ref):
+    n = upper_ref.shape[0]
+    inverse_ref[...] = begun_ref[...]
+    upper_ref[...] = begun_upper_ref[...]
+    factor_steps(steps, inverse_ref, upper_ref)
+    row_id = lax.broadcasted_iota(jnp.int32, (n, n), 0)
+    col_id = lax.broadcasted_iota(jnp.int32, (n, n), 1)
     out_ref[0] = jnp.where(row_id >= col_id, inverse_ref[0], 0.0)
     upper = jnp.where(row_id <= col_id, upper_ref[...], 0.0)
     image = jnp.where(row_id >= col_id, inverse_ref[1], 0.0)
     out_ref[1] = highest(highest(upper, image, 1, 1), image)
 
 
-def factor_grams(spot, grams, image_gram):
+def factor_start(spot, grams, image_gram):
     n = image_gram.shape[0]
     return call(
-        functools.partial(factor_kernel, len(grams)), float_shape(2, n, n), [SCALAR] + [WHOLE] * (len(grams) + 1), WHOLE,
-        [pltpu.VMEM((2, n, n), jnp.float32), pltpu.VMEM((n, n), jnp.float32)],
-        flops=n * n * n * 400,
+        functools.partial(factor_start_kernel, (0, n // BASE // 2), len(grams)), (float_shape(2, n, n), float_shape(n, n)),
+        [SCALAR] + [WHOLE] * (len(grams) + 1), (WHOLE, WHOLE), flops=n * n * n * 200,
     )(spot, *grams, image_gram)
 
 
-def basis_kernel(columns, lines_at, spot_ref, own_ref, other_ref, range_ref, co_ref, range_out_ref, co_out_ref, range_held_ref, co_held_ref, range_done_ref, co_done_ref, range_sem, co_sem, range_out_sem, co_out_sem):
+def factor_end(begun, upper):
+    n = upper.shape[0]
+    return call(
+        functools.partial(factor_end_kernel, (n // BASE // 2, n // BASE)), float_shape(2, n, n), [WHOLE, WHOLE], WHOLE,
+        [pltpu.VMEM((2, n, n), jnp.float32), pltpu.VMEM((n, n), jnp.float32)], flops=n * n * n * 200,
+    )(begun, upper)
+
+
+def basis_kernel(spot_ref, at_ref, own_ref, other_ref, range_ref, co_ref, range_out_ref, co_out_ref, range_held_ref, co_held_ref, range_done_ref, co_done_ref, side_ref, range_sem, co_sem, range_out_sem, co_out_sem):
     lines, rows, _ = range_held_ref.shape
     cells, _, width = co_held_ref.shape
-    ranges = [pltpu.make_async_copy(range_ref.at[f], range_held_ref.at[f], range_sem.at[f]) for f in range(lines)]
-    ranges_out = [pltpu.make_async_copy(range_done_ref.at[f], range_out_ref.at[pl.ds(lines_at[f] * rows, rows)], range_out_sem.at[f]) for f in range(lines)]
-    cos = [pltpu.make_async_copy(co_ref.at[f], co_held_ref.at[f], co_sem.at[f]) for f in range(cells)]
-    cos_out = [pltpu.make_async_copy(co_done_ref.at[f], co_out_ref.at[:, pl.ds(columns[f] * width, width)], co_out_sem.at[f]) for f in range(cells)]
-    core = spot_ref[0]
-    for copy in ranges + cos:
-        copy.start()
-    first = core == 0
-    left = split(jnp.where(first, own_ref[0], other_ref[0]))
-    right = split(jnp.where(first, other_ref[0], own_ref[0]))
-    for f, copy in enumerate(ranges):
-        copy.wait()
-        range_done_ref[f] = parts_dot(split(range_held_ref[f]), left, 1, 1)
-        ranges_out[f].start()
-    for f, copy in enumerate(cos):
-        copy.wait()
-        co_done_ref[f] = parts_dot(right, split(co_held_ref[f]))
-        cos_out[f].start()
-    for copy in ranges_out + cos_out:
-        copy.wait()
-
-
-def bases(spot, own, other, range_all, co_all, columns, lines_at):
+
+    def range_copy(f):
+        return pltpu.make_async_copy(range_ref.at[f], range_held_ref.at[f], range_sem.at[f])
+
+    def co_copy(f):
+        return pltpu.make_async_copy(co_ref.at[f], co_held_ref.at[f], co_sem.at[f])
+
+    def range_out(f):
+        start = pl.multiple_of(at_ref[f] * rows, rows)
+        return pltpu.make_async_copy(range_done_ref.at[f], range_out_ref.at[pl.ds(start, rows)], range_out_sem.at[f])
+
+    def co_out(f):
+        start = pl.multiple_of(at_ref[lines + f] * width, width)
+        return pltpu.make_async_copy(co_done_ref.at[f], co_out_ref.at[:, pl.ds(start, width)], co_out_sem.at[f])
+
+    for f in range(lines):
+        range_copy(f).start()
+    for f in range(cells):
+        co_copy(f).start()
+    first = spot_ref[0] == 0
+    side_ref[0], side_ref[1] = split(jnp.where(first, own_ref[0], other_ref[0]))
+    side_ref[2], side_ref[3] = split(jnp.where(first, other_ref[0], own_ref[0]))
+
+    def range_step(f, carry):
+        range_copy(f).wait()
+        range_done_ref[f] = parts_dot(split(range_held_ref[f]), (side_ref[0], side_ref[1]), 1, 1)
+        range_out(f).start()
+        return carry
+
+    def co_step(f, carry):
+        co_copy(f).wait()
+        co_done_ref[f] = parts_dot((side_ref[2], side_ref[3]), split(co_held_ref[f]))
+        co_out(f).start()
+        return carry
+
+    lax.fori_loop(0, lines, range_step, 0)
+    lax.fori_loop(0, cells, co_step, 0)
+    for f in range(lines):
+        range_out(f).wait()
+    for f in range(cells):
+        co_out(f).wait()
+
+
+def bases(spot, at, own, other, range_all, co_all):
     lines, rows, k = range_all.shape
     cells, count, width = co_all.shape
     range_held, co_held = pltpu.VMEM(range_all.shape, jnp.float32), pltpu.VMEM(co_all.shape, jnp.float32)
     line_sem, cell_sem = pltpu.SemaphoreType.DMA((lines,)), pltpu.SemaphoreType.DMA((cells,))
     return call(
-        functools.partial(basis_kernel, columns, lines_at), (float_shape(lines * rows, k), float_shape(count, cells * width)),
-        [SCALAR, WHOLE, WHOLE, OUTSIDE, OUTSIDE], (OUTSIDE, OUTSIDE),
-        [range_held, co_held, range_held, co_held, line_sem, cell_sem, line_sem, cell_sem],
+        basis_kernel, (float_shape(lines * rows, k), float_shape(count, cells * width)),
+        [SCALAR, SCALAR, WHOLE, WHOLE, OUTSIDE, OUTSIDE], (OUTSIDE, OUTSIDE),
+        [range_held, co_held, range_held, co_held, pltpu.VMEM((4, k, k), jnp.bfloat16), line_sem, cell_sem, line_sem, cell_sem],
         flops=18 * lines * rows * k * k, limit=56,
-    )(spot, own, other, range_all, co_all)
+    )(spot, at, own, other, range_all, co_all)
 
 
 def finish_kernel(scale, spot_ref, own_ref, other_ref, middle_own_ref, middle_other_ref, out_ref, middle_ref):
@@ -453,9 +495,8 @@
     groups = groups_of("cell", 1, 2)
     line_groups = groups_of("tm", 0, 2)
     spot = jnp.stack([lax.axis_index("cell") & 1, place_of(groups, lax.axis_index("cell")), place_of(line_groups[:1], lax.axis_index("tm"))]).astype(jnp.int32)
-    columns = [(cell & 1) * chips + place_of(groups, cell) for cell in range(2 * chips)]
-
-    lines_at = [place_of(line_groups, line) for line in range(lax.axis_size("tm"))]
+    at = [place_of(line_groups, line) for line in range(lax.axis_size("tm"))]
+    at = jnp.array(at + [(cell & 1) * chips + place_of(groups, cell) for cell in range(2 * chips)], jnp.int32)
 
     def core_swap(values):
         return swap(values, "cell", 1)
@@ -464,7 +505,7 @@
     far = swap(r3, "tm", 1)
     near = swap(r1, "tm", 1)
     pack = kept + core_swap(sent)
-    handed = r2 + far
+    handed = r2 + after(far, pack)
     sketch_z = core_terms(after(spot, pack, handed), window, core_right, core_left)
     pack = scatter_sum(pack, groups)[0]
     handed, near, pack, sketch_z = lax.optimization_barrier((swap(handed, "tm", 2), near, pack, sketch_z))
@@ -477,23 +518,29 @@
     packed = pack_width(co_test.shape[0], width, k)
     co_piece = pack[:packed].reshape(packed, -1, width).swapaxes(0, 1).reshape(-1, width)
     fold = pack[None, packed:]
-    range_all = lax.all_gather(range_piece, "tm", axis=0)
     co_all = lax.all_gather(co_piece, "cell", axis=0)
 
     gram_sent, gram_kept = gram_terms(spot, chips, range_piece, co_piece, (rows_total, cols_total))
-    gram = scatter_sum(gram_kept + core_swap(gram_sent), groups)
-    gram = whole_sum(gram, "tm")
+    gram = whole_sum(scatter_sum(gram_kept + core_swap(gram_sent), groups), "tm")
+    fold = whole_sum(fold, "tm")
+    range_all = lax.all_gather(after(range_piece, gram, fold), "tm", axis=0)
     grams = gather(gram, groups)
-
-    fold = jnp.concatenate(gather(whole_sum(fold, "tm"), groups))
+    fold = jnp.concatenate(gather(fold, groups))
     middle_sent, middle_kept, image_gram = middle_terms(spot, chips, sketch_z, fold, core_swap(fold))
-    middle = whole_sum(scatter_sum(middle_kept + core_swap(middle_sent), groups), "tm")
+    middle = scatter_sum(middle_kept + core_swap(middle_sent), groups)
+
+    image_gram, middle = lax.optimization_barrier((image_gram, middle))
+    begun, upper = factor_start(spot, grams, image_gram)
+    for bit in range(bits_of("tm")):
+        middle = middle + swap(middle, "tm", 1 << bit)
+        if bit == 0:
+            middle, begun, upper = lax.optimization_barrier((middle, begun, upper))
+    own = factor_end(begun, upper)
+    middle, own = lax.optimization_barrier((middle, own))
     middle = jnp.concatenate(gather(middle, groups))
     middle_other = core_swap(middle)
-
-    own = factor_grams(spot, grams, image_gram)
     other = core_swap(own)
-    range_basis, co_basis = bases(spot, own, other, range_all, co_all, columns, lines_at)
+    range_basis, co_basis = bases(spot, at, own, other, range_all, co_all)
     core_out = finish(spot, own, other, middle, middle_other, math.sqrt(rows_total * cols_total))
     return (range_basis, co_basis, core_out)
 

time: 170 us -> 151 us (0.89)
  waiting for transfers between devices: 57.4 us -> 37.5 us
  starting transfers between devices: 30.9 us -> 37.4 us
  local copies, waits for them, and re-layouts: 2.78 us -> 0.18 us
    ppermute x33, waiting for transfers between devices: 57.4 us -> 31.7 us  [swap(): lax.ppermute(values, axis, [(i, i ^ mask) for i in range(lax.axis_size(ax...]
    ppermute x33, starting transfers between devices: 30.9 us -> 37.3 us  [swap(): lax.ppermute(values, axis, [(i, i ^ mask) for i in range(lax.axis_size(ax...]
    all_gather x1, waiting for transfers between devices: 0.01 us -> 5.06 us  [per_device(): co_all = lax.all_gather(co_piece, 'cell', axis=0)]
    unnamed x14 -> x19, local copies, waits for them, and re-layouts: 1.92 us -> 0.05 us
    pallas_call x2 -> x3, Pallas kernels: 23.4 us -> 22.5 us  [the longest x1 8.1 us: factor_end(): call(functools.partial(factor_end_kernel, (n // BASE // 2, n // BASE)), f...]
  transfers between devices with their start and end apart: 35 -> 35, of which waited for: 20 -> 20; matrix products, arithmetic and copies ran while one was open for 2% -> 1% of each run, Pallas kernels for 21% -> 22%
where the time goes in v5:
time: 151 us
  Pallas kernels  59.1 us (39%)
  waiting for transfers between devices  37.5 us (25%)
  starting transfers between devices  37.4 us (25%)
  between operations  14.4 us (10%)
  other arithmetic  2.65 us (2%)
    ppermute x33, starting transfers between devices, swap(): lax.ppermute(values, axis, [(i, i ^ mask) for i in range(lax.axis_size(ax...  37.3 us
    ppermute x33, waiting for transfers between devices, swap(): lax.ppermute(values, axis, [(i, i ^ mask) for i in range(lax.axis_size(ax...  31.7 us
    pallas_call x1, Pallas kernels, sketch_terms(): call(sketch_kernel, (float_shape(rows // TILES, k),) * 4 + (float_shape(c...  17.3 us
    pallas_call x1, Pallas kernels, core_terms(): call(core_kernel, float_shape(s_core, s_core), [SCALAR] + [OUTSIDE] * 3,...  13.4 us
    pallas_call x1, Pallas kernels, factor_end(): call(functools.partial(factor_end_kernel, (n // BASE // 2, n // BASE)), f...  8.1 us
    pallas_call x1, Pallas kernels, factor_start(): call(functools.partial(factor_start_kernel, (0, n // BASE // 2), len(gram...  7.59 us
    pallas_call x1, Pallas kernels, bases(): call(basis_kernel, (float_shape(lines * rows, k), float_shape(count, cell...  6.78 us
    all_gather x1, waiting for transfers between devices, per_device(): co_all = lax.all_gather(co_piece, 'cell', axis=0)  5.06 us
  transfers between devices with their start and end apart: 35, of which 20 were waited for; matrix products, arithmetic and copies ran while one was open for 1% of the time, Pallas kernels for 22%

profile of v5, /device:TPU:0, one launch (start us, length us, event | category | flops | bytes accessed | tf_op | source)
XLA Modules:
  0.0 151.2 jit_solution(11690516390445524355)
XLA Ops:
  7.2 0.7 pad_add_fusion.spot_ref
  7.9 17.3 %shard_map.85 = (f32[256,256]{1,0:T(8,128)}, f32[256,256]{1,0:T(8,128)}, f32[256,256]{1,0:T(8,128)}, f32[256,256]{1,0:T(8,128)}, f32[4,384,256]{2,1,0:T(8,128)}, /*index=5*/f32[4,384,256]{2,1,0:T(8,128)}) custom-call(s32[3]{0:T(128)} %pad_add_fusion.spot_ref, f32[1024,2048]{1,0:T(8,128)} %window_ref.3, f32[2048,256]{1,0:T(8,128)} %test_ref.1, ...), custom_call_target="tpu_custom_call" | custom-call | flops 6442450944 | bytes 4194304 | tf_op jit(solution)/shard_map/pallas_call | solution.py:189
  25.1 0.5 collective-permute-start.1
  25.7 2.6 %collective-permute-start = (f32[256,256]{1,0:T(8,128)}, f32[256,256]{1,0:T(8,128)S(1)}, u32[]{:S(2)}, u32[]{:S(2)}) collective-permute-start(f32[256,256]{1,0:T(8,128)} %get-tuple-element.33), channel_id=1, source_target_pairs={{0,1},{1,0},{2,3},{3,2},{4,5},{5,4},{6,7},{7,6},{8,9},{9,8},{10,11... | collective-permute-start | bytes 786440 | tf_op jit(solution)/shard_map/ppermute | solution.py:69
  28.3 0.1 collective-permute-start.3
  28.4 0.5 collective-permute-done.1
  28.9 1.6 %add.71 = f32[4,384,256]{2,1,0:T(8,128)S(1)} add(f32[4,384,256]{2,1,0:T(8,128)} %get-tuple-element.34, f32[4,384,256]{2,1,0:T(8,128)S(1)} %collective-permute-done.1) | non-fusion elementwise | flops 393216 | bytes 4718592 | tf_op jit(solution)/shard_map/add | solution.py:507
  30.6 0.1 fusion.5
  30.6 5.0 %collective-permute-done = f32[256,256]{1,0:T(8,128)S(1)} collective-permute-done((f32[256,256]{1,0:T(8,128)}, f32[256,256]{1,0:T(8,128)S(1)}, u32[]{:S(2)}, u32[]{:S(2)}) %collective-permute-start) | collective-permute-done | bytes 262176 | tf_op jit(solution)/shard_map/ppermute | solution.py:69
  35.7 3.0 %collective-permute-start.2 = (f32[256,256]{1,0:T(8,128)S(1)}, f32[256,256]{1,0:T(8,128)S(1)}, u32[]{:S(2)}, u32[]{:S(2)}) collective-permute-start(f32[256,256]{1,0:T(8,128)S(1)} %add.72), channel_id=1, source_target_pairs={{0,2},{1,3},{2,0},{3,1},{4,6},{5,7},{6,4},{7,5},{8,10},{9,11},{10,... | collective-permute-start | bytes 786440 | tf_op jit(solution)/shard_map/ppermute | solution.py:69
  38.8 1.5 collective-permute-start.4
  40.2 1.5 %collective-permute-start.5 = (f32[1,384,256]{2,1,0:T(8,128)S(1)}, f32[1,384,256]{2,1,0:T(8,128)S(1)}, u32[]{:S(2)}, u32[]{:S(2)}) collective-permute-start(f32[1,384,256]{2,1,0:T(8,128)S(1)} %get-tuple-element.62), channel_id=1, source_target_pairs={{0,16},{4,20},{8,24},{12,28},{16,0},{20,4},{24,8},{28,12},{1,17},{... | collective-permute-start | bytes 1179656 | tf_op jit(solution)/shard_map/ppermute | solution.py:69
  41.8 0.5 collective-permute-start.6
  42.2 13.4 %shard_map.86.z_ref = f32[512,512]{1,0:T(8,128)} custom-call(s32[3]{0:T(128)} %pad_add_fusion.spot_ref, f32[1024,2048]{1,0:T(8,128)} %window_ref.3, f32[512,2048]{1,0:T(8,128)} %right_ref.3, f32[512,1024]{1,0:T(8,128)} %left_ref.3), custom_call_target="tpu_custom_call" | custom-call | flops 9663676416 | bytes 4194304 | tf_op jit(solution)/shard_map/pallas_call | solution.py:242
  55.7 2.6 %collective-permute-done.5 = f32[1,384,256]{2,1,0:T(8,128)S(1)} collective-permute-done((f32[1,384,256]{2,1,0:T(8,128)S(1)}, f32[1,384,256]{2,1,0:T(8,128)S(1)}, u32[]{:S(2)}, u32[]{:S(2)}) %collective-permute-start.5) | collective-permute-done | bytes 393248 | tf_op jit(solution)/shard_map/ppermute | solution.py:69
  58.3 0.1 fusion.1
  58.6 1.2 shard_map.88
  59.8 0.1 collective-permute-start.18
  59.9 1.6 %collective-permute-start.7 = (f32[1,128,256]{2,1,0:T(8,128)S(1)}, f32[1,128,256]{2,1,0:T(8,128)S(1)}, u32[]{:S(2)}, u32[]{:S(2)}) collective-permute-start(f32[1,128,256]{2,1,0:T(8,128)S(1)} %slice_bitcast_fusion), channel_id=1, source_target_pairs={{0,1},{1,0},{2,3},{3,2},{4,5},{5,4},{6,7},{7,6},{8,9},{9,8},{10,11... | collective-permute-start | bytes 393224 | tf_op jit(solution)/shard_map/ppermute | solution.py:69
  61.6 1.3 collective-permute-start.19
  62.9 0.8 collective-permute-start.20
  63.7 1.4 collective-permute-start.21
  65.2 0.7 collective-permute-done.7
  65.9 0.4 collective-permute-start.8
  66.3 1.6 %collective-permute-done.20 = f32[1,64,256]{2,1,0:T(8,128)S(1)} collective-permute-done((f32[1,64,256]{2,1,0:T(8,128)S(1)}, f32[1,64,256]{2,1,0:T(8,128)S(1)}, u32[]{:S(2)}, u32[]{:S(2)}) %collective-permute-start.20) | collective-permute-done | bytes 65568 | tf_op jit(solution)/shard_map/ppermute | solution.py:69
  67.9 1.0 collective-permute-done.21
  68.9 1.5 collective-permute-start.22
  70.4 3.1 %collective-permute-done.22 = f32[1,64,256]{2,1,0:T(8,128)S(1)} collective-permute-done((f32[1,64,256]{2,1,0:T(8,128)S(1)}, f32[1,64,256]{2,1,0:T(8,128)S(1)}, u32[]{:S(2)}, u32[]{:S(2)}) %collective-permute-start.22) | collective-permute-done | bytes 65568 | tf_op jit(solution)/shard_map/ppermute | solution.py:69
  73.6 2.1 %collective-permute-start.23 = (f32[1,64,256]{2,1,0:T(8,128)S(1)}, f32[1,64,256]{2,1,0:T(8,128)S(1)}, u32[]{:S(2)}, u32[]{:S(2)}) collective-permute-start(f32[1,64,256]{2,1,0:T(8,128)S(1)} %add.89), channel_id=1, source_target_pairs={{0,2},{1,3},{2,0},{3,1},{4,6},{5,7},{6,4},{7,5},{8,10},{9,11},{10,... | collective-permute-start | bytes 196616 | tf_op jit(solution)/shard_map/ppermute | solution.py:69
  75.7 3.1 %collective-permute-done.23 = f32[1,64,256]{2,1,0:T(8,128)S(1)} collective-permute-done((f32[1,64,256]{2,1,0:T(8,128)S(1)}, f32[1,64,256]{2,1,0:T(8,128)S(1)}, u32[]{:S(2)}, u32[]{:S(2)}) %collective-permute-start.23) | collective-permute-done | bytes 65568 | tf_op jit(solution)/shard_map/ppermute | solution.py:69
  78.9 0.7 all-gather.7.cloned.1.call-update
  79.6 1.5 %collective-permute-start.11 = (f32[1,128,256]{2,1,0:T(8,128)S(1)}, f32[1,128,256]{2,1,0:T(8,128)S(1)}, u32[]{:S(2)}, u32[]{:S(2)}) collective-permute-start(f32[1,128,256]{2,1,0:T(8,128)S(1)} %add.77), channel_id=1, source_target_pairs={{0,24},{4,28},{8,16},{12,20},{16,8},{20,12},{24,0},{28,4},{1,25},{... | collective-permute-start | bytes 393224 | tf_op jit(solution)/shard_map/ppermute | solution.py:69
  81.1 1.4 collective-permute-start.10
  82.5 0.7 collective-permute-start.9
  83.2 2.5 %collective-permute-done.11 = f32[1,128,256]{2,1,0:T(8,128)S(1)} collective-permute-done((f32[1,128,256]{2,1,0:T(8,128)S(1)}, f32[1,128,256]{2,1,0:T(8,128)S(1)}, u32[]{:S(2)}, u32[]{:S(2)}) %collective-permute-start.11) | collective-permute-done | bytes 131104 | tf_op jit(solution)/shard_map/ppermute | solution.py:69
  85.6 1.3 collective-permute-done.10
  87.0 0.5 collective-permute-done.9
  87.5 0.1 collective-permute-start.12
  87.6 1.9 %collective-permute-done.12.other_ref = f32[4,128,256]{2,1,0:T(8,128)S(1)} collective-permute-done((f32[4,128,256]{2,1,0:T(8,128)S(1)}, f32[4,128,256]{2,1,0:T(8,128)S(1)}, u32[]{:S(2)}, u32[]{:S(2)}) %collective-permute-start.12) | collective-permute-done | bytes 524320 | tf_op jit(solution)/shard_map/ppermute | solution.py:69
  89.5 2.5 %shard_map.87 = (f32[4,32,256]{2,1,0:T(8,128)S(1)}, f32[4,32,256]{2,1,0:T(8,128)S(1)}, f32[256,256]{1,0:T(8,128)S(1)}) custom-call(s32[3]{0:T(128)S(1)} %copy-done.5, f32[512,512]{1,0:T(8,128)S(1)} %copy-done, f32[4,128,256]{2,1,0:T(8,128)S(1)} %pad_maximum_fusion.own_ref, f32[4,128,256]{2,1,0:T(8,128)S(1)} %collective-permute-done.12.other_ref), custom_call_target="tpu_custom_call" | custom-call | flops 402653184 | bytes 4194304 | tf_op jit(solution)/shard_map/pallas_call | solution.py:291
  92.0 0.2 collective-permute-start.13
  92.2 1.2 collective-permute-done.13
  93.4 0.9 collective-permute-start.14
  94.3 1.2 collective-permute-start.15
  95.5 1.5 collective-permute-start.16
  97.0 0.8 collective-permute-start.24
  97.8 1.2 collective-permute-start.25
  99.0 1.5 collective-permute-start.26
  100.5 1.6 %collective-permute-start.17 = (f32[1,32,256]{2,1,0:T(8,128)S(1)}, f32[1,32,256]{2,1,0:T(8,128)S(1)}, u32[]{:S(2)}, u32[]{:S(2)}) collective-permute-start(f32[1,32,256]{2,1,0:T(8,128)S(1)} %fusion.3), channel_id=1, source_target_pairs={{0,1},{1,0},{2,3},{3,2},{4,5},{5,4},{6,7},{7,6},{8,9},{9,8},{10,11... | collective-permute-start | bytes 98312 | tf_op jit(solution)/shard_map/ppermute | solution.py:69
  102.1 0.6 collective-permute-done.25.refs_2_
  102.7 1.5 collective-permute-done.26.refs_3_
  104.2 7.6 %shard_map.89 = (f32[2,256,256]{2,1,0:T(8,128)S(1)}, f32[256,256]{1,0:T(8,128)S(1)}) custom-call(s32[3]{0:T(128)S(1)} %copy-done.5, f32[1,64,256]{2,1,0:T(8,128)S(1)} %add.90.refs_0_, f32[1,64,256]{2,1,0:T(8,128)S(1)} %collective-permute-done.24.refs_1_, f32[1,64,256]{2,1,0:T(8,128)S(1)} %collective-permute-done.25.refs_2_, ...), custom_call_target="tpu_custom_call" | custom-call | flops 3355443200 | bytes 4194304 | tf_op jit(solution)/shard_map/pallas_call | solution.py:397
  111.8 2.2 %collective-permute-start.27 = (f32[1,32,256]{2,1,0:T(8,128)S(1)}, f32[1,32,256]{2,1,0:T(8,128)S(1)}, u32[]{:S(2)}, u32[]{:S(2)}) collective-permute-start(f32[1,32,256]{2,1,0:T(8,128)S(1)} %add.82), channel_id=1, source_target_pairs={{0,2},{1,3},{2,0},{3,1},{4,6},{5,7},{6,4},{7,5},{8,10},{9,11},{10,... | collective-permute-start | bytes 98312 | tf_op jit(solution)/shard_map/ppermute | solution.py:69
  114.0 8.1 %shard_map.90.own_ref = f32[2,256,256]{2,1,0:T(8,128)S(1)} custom-call(f32[2,256,256]{2,1,0:T(8,128)S(1)} %get-tuple-element.54.begun_ref, f32[256,256]{1,0:T(8,128)S(1)} %get-tuple-element.55.begun_upper_ref), custom_call_target="tpu_custom_call" | custom-call | flops 3355443200 | bytes 4194304 | tf_op jit(solution)/shard_map/pallas_call | solution.py:405
  122.2 0.9 collective-permute-start.29
  123.1 0.9 collective-permute-start.30
  124.0 1.7 %collective-permute-start.31 = (f32[1,32,256]{2,1,0:T(8,128)S(1)}, f32[1,32,256]{2,1,0:T(8,128)S(1)}, u32[]{:S(2)}, u32[]{:S(2)}) collective-permute-start(f32[1,32,256]{2,1,0:T(8,128)S(1)} %add.91), channel_id=1, source_target_pairs={{0,24},{4,28},{8,16},{12,20},{16,8},{20,12},{24,0},{28,4},{1,25},{... | collective-permute-start | bytes 98312 | tf_op jit(solution)/shard_map/ppermute | solution.py:69
  125.8 0.4 collective-permute-done.29
  126.2 0.8 collective-permute-done.30
  127.0 1.8 %collective-permute-done.31 = f32[1,32,256]{2,1,0:T(8,128)S(1)} collective-permute-done((f32[1,32,256]{2,1,0:T(8,128)S(1)}, f32[1,32,256]{2,1,0:T(8,128)S(1)}, u32[]{:S(2)}, u32[]{:S(2)}) %collective-permute-start.31) | collective-permute-done | bytes 32800 | tf_op jit(solution)/shard_map/ppermute | solution.py:69
  128.9 1.3 collective-permute-done.32.middle_other_ref
  130.2 2.3 %shard_map.92 = f32[256,256]{1,0:T(8,128)} custom-call(s32[3]{0:T(128)S(1)} %copy-done.5, f32[2,256,256]{2,1,0:T(8,128)S(1)} %shard_map.90.own_ref, f32[2,256,256]{2,1,0:T(8,128)S(1)} %collective-permute-done.28.other_ref, f32[4,32,256]{2,1,0:T(8,128)S(1)} %constant_dynamic-update-slice_fusion.middle_own_ref, ...), custom_call_target="tpu_custom_call" | custom-call | flops 402653184 | bytes 4194304 | tf_op jit(solution)/shard_map/pallas_call | solution.py:484
  132.5 5.1 %all-gather.7.cloned.1.call-done = f32[2048,256]{1,0:T(8,128)} async-done(((f32[256,256]{1,0:T(8,128)}), f32[2048,256]{1,0:T(8,128)}) %all-gather.7.cloned.1.call-update) | async-done | bytes 2097168 | tf_op jit(solution)/shard_map/all_gather | solution.py:521
  137.6 6.8 %shard_map.91 = (f32[1024,256]{1,0:T(8,128)}, f32[256,2048]{1,0:T(8,128)}) custom-call(s32[3]{0:T(128)} %pad_add_fusion.spot_ref, s32[12]{0:T(128)} %constant.17.clone.at_ref, f32[2,256,256]{2,1,0:T(8,128)} %copy-done.3, f32[2,256,256]{2,1,0:T(8,128)} %copy-done.4, f32[4,256,256]{2,1,0:T(8,128)} %bitcast.12, f32[8,256,256]{2,1,0:T(8,128)} %bitcast.11), custom_call_target="tpu_custom_call" | custom-call | flops 1207959552 | bytes 4194304 | tf_op jit(solution)/shard_map/pallas_call | solution.py:462
  (57 shorter events, 0.6 us)
Async XLA Ops:
  7.2 125.3 %all-gather.5.cloned.1.call-start = ((), (), s32[]{:S(2)}) async-start(), calls=%async_computation | async-start | bytes 1310720 | tf_op jit(solution)/shard_map/all_gather | solution.py:526
  25.1 3.8 %collective-permute-start.1 = (f32[4,384,256]{2,1,0:T(8,128)}, f32[4,384,256]{2,1,0:T(8,128)S(1)}, u32[]{:S(2)}, u32[]{:S(2)}) collective-permute-start(f32[4,384,256]{2,1,0:T(8,128)} %get-tuple-element.35), channel_id=1, source_target_pairs={{0,4},{4,0},{8,12},{12,8},{16,20},{20,16},{24,28},{28,24},{1,5},{5... | collective-permute-start | bytes 4718600 | tf_op jit(solution)/shard_map/ppermute | solution.py:69
  25.7 10.0 %collective-permute-start = (f32[256,256]{1,0:T(8,128)}, f32[256,256]{1,0:T(8,128)S(1)}, u32[]{:S(2)}, u32[]{:S(2)}) collective-permute-start(f32[256,256]{1,0:T(8,128)} %get-tuple-element.33), channel_id=1, source_target_pairs={{0,1},{1,0},{2,3},{3,2},{4,5},{5,4},{6,7},{7,6},{8,9},{9,8},{10,11... | collective-permute-start | bytes 786440 | tf_op jit(solution)/shard_map/ppermute | solution.py:69
  28.3 30.1 %collective-permute-start.3 = (f32[256,256]{1,0:T(8,128)}, f32[256,256]{1,0:T(8,128)S(1)}, u32[]{:S(2)}, u32[]{:S(2)}) collective-permute-start(f32[256,256]{1,0:T(8,128)} %get-tuple-element.37), channel_id=1, source_target_pairs={{0,1},{1,0},{2,3},{3,2},{4,5},{5,4},{6,7},{7,6},{8,9},{9,8},{10,11... | collective-permute-start | bytes 786440 | tf_op jit(solution)/shard_map/ppermute | solution.py:69
  30.5 5.1 %copy-start.6 = (f32[256,256]{1,0:T(8,128)S(1)}, f32[256,256]{1,0:T(8,128)}, u32[]{:S(2)}) copy-start(f32[256,256]{1,0:T(8,128)} %get-tuple-element.32) | copy-start | bytes 786436
  35.7 22.7 %collective-permute-start.2 = (f32[256,256]{1,0:T(8,128)S(1)}, f32[256,256]{1,0:T(8,128)S(1)}, u32[]{:S(2)}, u32[]{:S(2)}) collective-permute-start(f32[256,256]{1,0:T(8,128)S(1)} %add.72), channel_id=1, source_target_pairs={{0,2},{1,3},{2,0},{3,1},{4,6},{5,7},{6,4},{7,5},{8,10},{9,11},{10,... | collective-permute-start | bytes 786440 | tf_op jit(solution)/shard_map/ppermute | solution.py:69
  38.8 16.9 %collective-permute-start.4 = (f32[1,384,256]{2,1,0:T(8,128)S(1)}, f32[1,384,256]{2,1,0:T(8,128)S(1)}, u32[]{:S(2)}, u32[]{:S(2)}) collective-permute-start(f32[1,384,256]{2,1,0:T(8,128)S(1)} %get-tuple-element.63), channel_id=1, source_target_pairs={{0,8},{4,12},{8,0},{12,4},{16,24},{20,28},{24,16},{28,20},{1,9},{5... | collective-permute-start | bytes 1179656 | tf_op jit(solution)/shard_map/ppermute | solution.py:69
  40.2 18.1 %collective-permute-start.5 = (f32[1,384,256]{2,1,0:T(8,128)S(1)}, f32[1,384,256]{2,1,0:T(8,128)S(1)}, u32[]{:S(2)}, u32[]{:S(2)}) collective-permute-start(f32[1,384,256]{2,1,0:T(8,128)S(1)} %get-tuple-element.62), channel_id=1, source_target_pairs={{0,16},{4,20},{8,24},{12,28},{16,0},{20,4},{24,8},{28,12},{1,17},{... | collective-permute-start | bytes 1179656 | tf_op jit(solution)/shard_map/ppermute | solution.py:69
  41.8 16.6 %collective-permute-start.6 = (f32[1,384,256]{2,1,0:T(8,128)S(1)}, f32[1,384,256]{2,1,0:T(8,128)S(1)}, u32[]{:S(2)}, u32[]{:S(2)}) collective-permute-start(f32[1,384,256]{2,1,0:T(8,128)S(1)} %get-tuple-element.61), channel_id=1, source_target_pairs={{0,24},{4,28},{8,16},{12,20},{16,8},{20,12},{24,0},{28,4},{1,25},{... | collective-permute-start | bytes 1179656 | tf_op jit(solution)/shard_map/ppermute | solution.py:69
  55.7 2.8 %copy-start.7 = (f32[256,256]{1,0:T(8,128)S(1)}, f32[256,256]{1,0:T(8,128)}, u32[]{:S(2)}) copy-start(f32[256,256]{1,0:T(8,128)} %get-tuple-element.45) | copy-start | bytes 786436
  55.7 2.9 %copy-start.5 = (s32[3]{0:T(128)S(1)}, s32[3]{0:T(128)}, u32[]{:S(2)}) copy-start(s32[3]{0:T(128)} %pad_add_fusion.spot_ref) | copy-start | bytes 40
  58.5 7.4 %copy-start.1 = (f32[256,256]{1,0:T(8,128)}, f32[256,256]{1,0:T(8,128)S(1)}, u32[]{:S(2)}) copy-start(f32[256,256]{1,0:T(8,128)S(1)} %slice.51.co_ref) | copy-start | bytes 786436
  58.6 17.1 %copy-start.2 = (f32[256,256]{1,0:T(8,128)}, f32[256,256]{1,0:T(8,128)S(1)}, u32[]{:S(2)}) copy-start(f32[256,256]{1,0:T(8,128)S(1)} %add_add_fusion.range_ref) | copy-start | bytes 786436
  59.8 1.7 %collective-permute-start.18 = (f32[4,64,256]{2,1,0:T(8,128)S(1)}, f32[4,64,256]{2,1,0:T(8,128)S(1)}, u32[]{:S(2)}, u32[]{:S(2)}) collective-permute-start(f32[4,64,256]{2,1,0:T(8,128)S(1)} %get-tuple-element.49), channel_id=1, source_target_pairs={{0,4},{4,0},{8,12},{12,8},{16,20},{20,16},{24,28},{28,24},{1,5},{5... | collective-permute-start | bytes 786440 | tf_op jit(solution)/shard_map/ppermute | solution.py:69
  59.9 6.0 %collective-permute-start.7 = (f32[1,128,256]{2,1,0:T(8,128)S(1)}, f32[1,128,256]{2,1,0:T(8,128)S(1)}, u32[]{:S(2)}, u32[]{:S(2)}) collective-permute-start(f32[1,128,256]{2,1,0:T(8,128)S(1)} %slice_bitcast_fusion), channel_id=1, source_target_pairs={{0,1},{1,0},{2,3},{3,2},{4,5},{5,4},{6,7},{7,6},{8,9},{9,8},{10,11... | collective-permute-start | bytes 393224 | tf_op jit(solution)/shard_map/ppermute | solution.py:69
  61.6 27.9 %copy-start = (f32[512,512]{1,0:T(8,128)S(1)}, f32[512,512]{1,0:T(8,128)}, u32[]{:S(2)}) copy-start(f32[512,512]{1,0:T(8,128)} %shard_map.86.z_ref) | copy-start | bytes 3145732
  61.6 4.7 %collective-permute-start.19 = (f32[1,64,256]{2,1,0:T(8,128)S(1)}, f32[1,64,256]{2,1,0:T(8,128)S(1)}, u32[]{:S(2)}, u32[]{:S(2)}) collective-permute-start(f32[1,64,256]{2,1,0:T(8,128)S(1)} %get-tuple-element.66), channel_id=1, source_target_pairs={{0,8},{4,12},{8,0},{12,4},{16,24},{20,28},{24,16},{28,20},{1,9},{5... | collective-permute-start | bytes 196616 | tf_op jit(solution)/shard_map/ppermute | solution.py:69
  62.9 5.0 %collective-permute-start.20 = (f32[1,64,256]{2,1,0:T(8,128)S(1)}, f32[1,64,256]{2,1,0:T(8,128)S(1)}, u32[]{:S(2)}, u32[]{:S(2)}) collective-permute-start(f32[1,64,256]{2,1,0:T(8,128)S(1)} %get-tuple-element.65), channel_id=1, source_target_pairs={{0,16},{4,20},{8,24},{12,28},{16,0},{20,4},{24,8},{28,12},{1,17},{... | collective-permute-start | bytes 196616 | tf_op jit(solution)/shard_map/ppermute | solution.py:69
  63.7 5.2 %collective-permute-start.21 = (f32[1,64,256]{2,1,0:T(8,128)S(1)}, f32[1,64,256]{2,1,0:T(8,128)S(1)}, u32[]{:S(2)}, u32[]{:S(2)}) collective-permute-start(f32[1,64,256]{2,1,0:T(8,128)S(1)} %get-tuple-element.64), channel_id=1, source_target_pairs={{0,24},{4,28},{8,16},{12,20},{16,8},{20,12},{24,0},{28,4},{1,25},{... | collective-permute-start | bytes 196616 | tf_op jit(solution)/shard_map/ppermute | solution.py:69
  65.9 9.7 %collective-permute-start.8 = (f32[1,128,256]{2,1,0:T(8,128)S(1)}, f32[1,128,256]{2,1,0:T(8,128)S(1)}, u32[]{:S(2)}, u32[]{:S(2)}) collective-permute-start(f32[1,128,256]{2,1,0:T(8,128)S(1)} %fusion.4), channel_id=1, source_target_pairs={{0,2},{1,3},{2,0},{3,1},{4,6},{5,7},{6,4},{7,5},{8,10},{9,11},{10,... | collective-permute-start | bytes 393224 | tf_op jit(solution)/shard_map/ppermute | solution.py:69
  68.9 4.7 %collective-permute-start.22 = (f32[1,64,256]{2,1,0:T(8,128)S(1)}, f32[1,64,256]{2,1,0:T(8,128)S(1)}, u32[]{:S(2)}, u32[]{:S(2)}) collective-permute-start(f32[1,64,256]{2,1,0:T(8,128)S(1)} %fusion.2), channel_id=1, source_target_pairs={{0,1},{1,0},{2,3},{3,2},{4,5},{5,4},{6,7},{7,6},{8,9},{9,8},{10,11... | collective-permute-start | bytes 196616 | tf_op jit(solution)/shard_map/ppermute | solution.py:69
  73.6 5.2 %collective-permute-start.23 = (f32[1,64,256]{2,1,0:T(8,128)S(1)}, f32[1,64,256]{2,1,0:T(8,128)S(1)}, u32[]{:S(2)}, u32[]{:S(2)}) collective-permute-start(f32[1,64,256]{2,1,0:T(8,128)S(1)} %add.89), channel_id=1, source_target_pairs={{0,2},{1,3},{2,0},{3,1},{4,6},{5,7},{6,4},{7,5},{8,10},{9,11},{10,... | collective-permute-start | bytes 196616 | tf_op jit(solution)/shard_map/ppermute | solution.py:69
  78.9 58.7 %all-gather.7.cloned.1.call-start = ((), (), s32[]{:S(2)}) async-start(), calls=%async_computation.1 | async-start | bytes 2359296 | tf_op jit(solution)/shard_map/all_gather | solution.py:521
  79.6 6.0 %collective-permute-start.11 = (f32[1,128,256]{2,1,0:T(8,128)S(1)}, f32[1,128,256]{2,1,0:T(8,128)S(1)}, u32[]{:S(2)}, u32[]{:S(2)}) collective-permute-start(f32[1,128,256]{2,1,0:T(8,128)S(1)} %add.77), channel_id=1, source_target_pairs={{0,24},{4,28},{8,16},{12,20},{16,8},{20,12},{24,0},{28,4},{1,25},{... | collective-permute-start | bytes 393224 | tf_op jit(solution)/shard_map/ppermute | solution.py:69
  81.1 5.8 %collective-permute-start.10 = (f32[1,128,256]{2,1,0:T(8,128)S(1)}, f32[1,128,256]{2,1,0:T(8,128)S(1)}, u32[]{:S(2)}, u32[]{:S(2)}) collective-permute-start(f32[1,128,256]{2,1,0:T(8,128)S(1)} %add.77), channel_id=1, source_target_pairs={{0,16},{4,20},{8,24},{12,28},{16,0},{20,4},{24,8},{28,12},{1,17},{... | collective-permute-start | bytes 393224 | tf_op jit(solution)/shard_map/ppermute | solution.py:69
  82.5 5.0 %collective-permute-start.9 = (f32[1,128,256]{2,1,0:T(8,128)S(1)}, f32[1,128,256]{2,1,0:T(8,128)S(1)}, u32[]{:S(2)}, u32[]{:S(2)}) collective-permute-start(f32[1,128,256]{2,1,0:T(8,128)S(1)} %add.77), channel_id=1, source_target_pairs={{0,8},{4,12},{8,0},{12,4},{16,24},{20,28},{24,16},{28,20},{1,9},{5... | collective-permute-start | bytes 393224 | tf_op jit(solution)/shard_map/ppermute | solution.py:69
  87.5 2.0 %collective-permute-start.12 = (f32[4,128,256]{2,1,0:T(8,128)S(1)}, f32[4,128,256]{2,1,0:T(8,128)S(1)}, u32[]{:S(2)}, u32[]{:S(2)}) collective-permute-start(f32[4,128,256]{2,1,0:T(8,128)S(1)} %pad_maximum_fusion.own_ref), channel_id=1, source_target_pairs={{0,4},{4,0},{8,12},{12,8},{16,20},{20,16},{24,28},{28,24},{1,5},{5... | collective-permute-start | bytes 1572872 | tf_op jit(solution)/shard_map/ppermute | solution.py:69
  92.0 1.4 collective-permute-start.13
  93.4 5.6 %collective-permute-start.14 = (f32[1,32,256]{2,1,0:T(8,128)S(1)}, f32[1,32,256]{2,1,0:T(8,128)S(1)}, u32[]{:S(2)}, u32[]{:S(2)}) collective-permute-start(f32[1,32,256]{2,1,0:T(8,128)S(1)} %get-tuple-element.69), channel_id=1, source_target_pairs={{0,8},{4,12},{8,0},{12,4},{16,24},{20,28},{24,16},{28,20},{1,9},{5... | collective-permute-start | bytes 98312 | tf_op jit(solution)/shard_map/ppermute | solution.py:69
  94.3 6.1 %collective-permute-start.15 = (f32[1,32,256]{2,1,0:T(8,128)S(1)}, f32[1,32,256]{2,1,0:T(8,128)S(1)}, u32[]{:S(2)}, u32[]{:S(2)}) collective-permute-start(f32[1,32,256]{2,1,0:T(8,128)S(1)} %get-tuple-element.68), channel_id=1, source_target_pairs={{0,16},{4,20},{8,24},{12,28},{16,0},{20,4},{24,8},{28,12},{1,17},{... | collective-permute-start | bytes 98312 | tf_op jit(solution)/shard_map/ppermute | solution.py:69
  95.5 5.0 %collective-permute-start.16 = (f32[1,32,256]{2,1,0:T(8,128)S(1)}, f32[1,32,256]{2,1,0:T(8,128)S(1)}, u32[]{:S(2)}, u32[]{:S(2)}) collective-permute-start(f32[1,32,256]{2,1,0:T(8,128)S(1)} %get-tuple-element.67), channel_id=1, source_target_pairs={{0,24},{4,28},{8,16},{12,20},{16,8},{20,12},{24,0},{28,4},{1,25},{... | collective-permute-start | bytes 98312 | tf_op jit(solution)/shard_map/ppermute | solution.py:69
  97.0 5.1 %collective-permute-start.24 = (f32[1,64,256]{2,1,0:T(8,128)S(1)}, f32[1,64,256]{2,1,0:T(8,128)S(1)}, u32[]{:S(2)}, u32[]{:S(2)}) collective-permute-start(f32[1,64,256]{2,1,0:T(8,128)S(1)} %add.90.refs_0_), channel_id=1, source_target_pairs={{0,8},{4,12},{8,0},{12,4},{16,24},{20,28},{24,16},{28,20},{1,9},{5... | collective-permute-start | bytes 196616 | tf_op jit(solution)/shard_map/ppermute | solution.py:69
  97.8 4.9 %collective-permute-start.25 = (f32[1,64,256]{2,1,0:T(8,128)S(1)}, f32[1,64,256]{2,1,0:T(8,128)S(1)}, u32[]{:S(2)}, u32[]{:S(2)}) collective-permute-start(f32[1,64,256]{2,1,0:T(8,128)S(1)} %add.90.refs_0_), channel_id=1, source_target_pairs={{0,16},{4,20},{8,24},{12,28},{16,0},{20,4},{24,8},{28,12},{1,17},{... | collective-permute-start | bytes 196616 | tf_op jit(solution)/shard_map/ppermute | solution.py:69
  99.0 5.2 %collective-permute-start.26 = (f32[1,64,256]{2,1,0:T(8,128)S(1)}, f32[1,64,256]{2,1,0:T(8,128)S(1)}, u32[]{:S(2)}, u32[]{:S(2)}) collective-permute-start(f32[1,64,256]{2,1,0:T(8,128)S(1)} %add.90.refs_0_), channel_id=1, source_target_pairs={{0,24},{4,28},{8,16},{12,20},{16,8},{20,12},{24,0},{28,4},{1,25},{... | collective-permute-start | bytes 196616 | tf_op jit(solution)/shard_map/ppermute | solution.py:69
  100.5 11.3 %collective-permute-start.17 = (f32[1,32,256]{2,1,0:T(8,128)S(1)}, f32[1,32,256]{2,1,0:T(8,128)S(1)}, u32[]{:S(2)}, u32[]{:S(2)}) collective-permute-start(f32[1,32,256]{2,1,0:T(8,128)S(1)} %fusion.3), channel_id=1, source_target_pairs={{0,1},{1,0},{2,3},{3,2},{4,5},{5,4},{6,7},{7,6},{8,9},{9,8},{10,11... | collective-permute-start | bytes 98312 | tf_op jit(solution)/shard_map/ppermute | solution.py:69
  111.8 10.3 %collective-permute-start.27 = (f32[1,32,256]{2,1,0:T(8,128)S(1)}, f32[1,32,256]{2,1,0:T(8,128)S(1)}, u32[]{:S(2)}, u32[]{:S(2)}) collective-permute-start(f32[1,32,256]{2,1,0:T(8,128)S(1)} %add.82), channel_id=1, source_target_pairs={{0,2},{1,3},{2,0},{3,1},{4,6},{5,7},{6,4},{7,5},{8,10},{9,11},{10,... | collective-permute-start | bytes 98312 | tf_op jit(solution)/shard_map/ppermute | solution.py:69
  122.1 15.4 %copy-start.3 = (f32[2,256,256]{2,1,0:T(8,128)}, f32[2,256,256]{2,1,0:T(8,128)S(1)}, u32[]{:S(2)}) copy-start(f32[2,256,256]{2,1,0:T(8,128)S(1)} %shard_map.90.own_ref) | copy-start | bytes 1572868
  122.1 8.1 %collective-permute-start.28 = (f32[2,256,256]{2,1,0:T(8,128)S(1)}, f32[2,256,256]{2,1,0:T(8,128)S(1)}, u32[]{:S(2)}, u32[]{:S(2)}) collective-permute-start(f32[2,256,256]{2,1,0:T(8,128)S(1)} %shard_map.90.own_ref), channel_id=1, source_target_pairs={{0,4},{4,0},{8,12},{12,8},{16,20},{20,16},{24,28},{28,24},{1,5},{5... | collective-permute-start | bytes 1572872 | tf_op jit(solution)/shard_map/ppermute | solution.py:69
  122.2 4.0 %collective-permute-start.29 = (f32[1,32,256]{2,1,0:T(8,128)S(1)}, f32[1,32,256]{2,1,0:T(8,128)S(1)}, u32[]{:S(2)}, u32[]{:S(2)}) collective-permute-start(f32[1,32,256]{2,1,0:T(8,128)S(1)} %add.91), channel_id=1, source_target_pairs={{0,8},{4,12},{8,0},{12,4},{16,24},{20,28},{24,16},{28,20},{1,9},{5... | collective-permute-start | bytes 98312 | tf_op jit(solution)/shard_map/ppermute | solution.py:69
  123.1 3.9 %collective-permute-start.30 = (f32[1,32,256]{2,1,0:T(8,128)S(1)}, f32[1,32,256]{2,1,0:T(8,128)S(1)}, u32[]{:S(2)}, u32[]{:S(2)}) collective-permute-start(f32[1,32,256]{2,1,0:T(8,128)S(1)} %add.91), channel_id=1, source_target_pairs={{0,16},{4,20},{8,24},{12,28},{16,0},{20,4},{24,8},{28,12},{1,17},{... | collective-permute-start | bytes 98312 | tf_op jit(solution)/shard_map/ppermute | solution.py:69
  124.0 4.8 %collective-permute-start.31 = (f32[1,32,256]{2,1,0:T(8,128)S(1)}, f32[1,32,256]{2,1,0:T(8,128)S(1)}, u32[]{:S(2)}, u32[]{:S(2)}) collective-permute-start(f32[1,32,256]{2,1,0:T(8,128)S(1)} %add.91), channel_id=1, source_target_pairs={{0,24},{4,28},{8,16},{12,20},{16,8},{20,12},{24,0},{28,4},{1,25},{... | collective-permute-start | bytes 98312 | tf_op jit(solution)/shard_map/ppermute | solution.py:69
  128.9 1.3 collective-permute-start.32
  130.2 7.3 %copy-start.4 = (f32[2,256,256]{2,1,0:T(8,128)}, f32[2,256,256]{2,1,0:T(8,128)S(1)}, u32[]{:S(2)}) copy-start(f32[2,256,256]{2,1,0:T(8,128)S(1)} %collective-permute-done.28.other_ref) | copy-start | bytes 1572868
Sparse Core Ops, SparseCore 0:
  79.0 28.7 all-gather.4
  109.7 27.8 all-gather.6

commit v6 on v5

--- a/solution.py
+++ b/solution.py
@@ -269,7 +269,7 @@
     )(spot, range_piece, co_piece)
 
 
-def middle_kernel(spot_ref, z_ref, own_ref, other_ref, sent_ref, kept_ref, gram_ref, left_ref, right_ref, middle_ref):
+def middle_kernel(spot_ref, z_ref, own_ref, other_ref, blocks_ref, left_ref, right_ref, middle_ref):
     core, place = spot_ref[0], spot_ref[1]
     for owner, left_in, right_in in ((0, own_ref, other_ref), (1, other_ref, own_ref)):
         @pl.when(core == owner)
@@ -277,19 +277,14 @@
             put_blocks([left_in], left_ref, place)
             put_blocks([right_in], right_ref, place)
 
-    first = core == 0
-    own = jnp.where(first, left_ref[...], right_ref[...])
-    gram_ref[...] = highest(own, own, 0, 0)
     middle_ref[...] = parts_dot(split(parts_dot(split(left_ref[...]), split(z_ref[...]), 0, 0)), split(right_ref[...]))
-    half = middle_ref.shape[0] // 2
-    take_blocks(middle_ref, kept_ref, place, core * half)
-    take_blocks(middle_ref, sent_ref, place, (1 - core) * half)
+    take_blocks(middle_ref, blocks_ref, place)
 
 
 def middle_terms(spot, chips, sketch_z, own, other):
     s_core, k = sketch_z.shape[0], own.shape[2]
     return call(
-        middle_kernel, (float_shape(chips, k // (2 * chips), k),) * 2 + (float_shape(k, k),), [SCALAR] + [WHOLE] * 3, (WHOLE,) * 3,
+        middle_kernel, float_shape(chips, k // chips, k), [SCALAR] + [WHOLE] * 3, WHOLE,
         [pltpu.VMEM((s_core, k), jnp.float32), pltpu.VMEM((s_core, k), jnp.float32), pltpu.VMEM((k, k), jnp.float32)],
         flops=6 * k * s_core * s_core,
     )(spot, sketch_z, own, other)
@@ -372,10 +367,24 @@
 
 
 def factor_start_kernel(steps, peers, spot_ref, *refs):
-    gram_refs, (image_ref, inverse_ref, upper_ref) = refs[:peers], refs[peers:]
-    put_blocks(gram_refs, inverse_ref.at[0], spot_ref[1])
-    inverse_ref[1] = image_ref[...]
+    part_refs, (inverse_ref, upper_ref, fold_ref) = refs[:peers], refs[peers:]
+    n = upper_ref.shape[0]
+    inner = part_refs[0].shape[0]
+    rows = n // (peers * inner)
+    fold_rows = fold_ref.shape[0] // (peers * inner)
+    for i, ref in enumerate(part_refs):
+        for j in range(inner):
+            block = i * inner + j
+            inverse_ref[0, pl.ds(block_start(spot_ref[1], block, rows), rows), :] = ref[j, :rows]
+            fold_ref[block * fold_rows:(block + 1) * fold_rows, :] = ref[j, rows:]
+    inverse_ref[1] = highest(fold_ref[...], fold_ref[...], 0, 0)
     upper_ref[...] = jnp.zeros_like(upper_ref)
+    factor_steps(steps, inverse_ref, upper_ref)
+
+
+def factor_next_kernel(steps, begun_ref, begun_upper_ref, inverse_ref, upper_ref):
+    inverse_ref[...] = begun_ref[...]
+    upper_ref[...] = begun_upper_ref[...]
     factor_steps(steps, inverse_ref, upper_ref)
 
 
@@ -392,39 +401,55 @@
     out_ref[1] = highest(highest(upper, image, 1, 1), image)
 
 
-def factor_start(spot, grams, image_gram):
-    n = image_gram.shape[0]
-    return call(
-        functools.partial(factor_start_kernel, (0, n // BASE // 2), len(grams)), (float_shape(2, n, n), float_shape(n, n)),
-        [SCALAR] + [WHOLE] * (len(grams) + 1), (WHOLE, WHOLE), flops=n * n * n * 200,
-    )(spot, *grams, image_gram)
+def factor_start(spot, parts):
+    n = parts[0].shape[2]
+    blocks = len(parts) * parts[0].shape[0]
+    return call(
+        functools.partial(factor_start_kernel, (0, 1), len(parts)), (float_shape(2, n, n), float_shape(n, n)),
+        [SCALAR] + [WHOLE] * len(parts), (WHOLE, WHOLE), [pltpu.VMEM((blocks * parts[0].shape[1] - n, n), jnp.float32)], flops=n * n * n * 100,
+    )(spot, *parts)
+
+
+def factor_next(steps, begun, upper):
+    n = upper.shape[0]
+    return call(
+        functools.partial(factor_next_kernel, steps), (float_shape(2, n, n), float_shape(n, n)), [WHOLE, WHOLE], (WHOLE, WHOLE), flops=n * n * n * 100,
+    )(begun, upper)
 
 
 def factor_end(begun, upper):
     n = upper.shape[0]
     return call(
-        functools.partial(factor_end_kernel, (n // BASE // 2, n // BASE)), float_shape(2, n, n), [WHOLE, WHOLE], WHOLE,
-        [pltpu.VMEM((2, n, n), jnp.float32), pltpu.VMEM((n, n), jnp.float32)], flops=n * n * n * 200,
+        functools.partial(factor_end_kernel, (n // BASE - 1, n // BASE)), float_shape(2, n, n), [WHOLE, WHOLE], WHOLE,
+        [pltpu.VMEM((2, n, n), jnp.float32), pltpu.VMEM((n, n), jnp.float32)], flops=n * n * n * 100,
     )(begun, upper)
 
 
-def basis_kernel(spot_ref, at_ref, own_ref, other_ref, range_ref, co_ref, range_out_ref, co_out_ref, range_held_ref, co_held_ref, range_done_ref, co_done_ref, side_ref, range_sem, co_sem, range_out_sem, co_out_sem):
+def basis_kernel(peers, spot_ref, own_ref, other_ref, *refs):
+    range_refs, (co_own_ref, co_other_ref, range_out_ref, co_out_ref, range_held_ref, co_held_ref, range_done_ref, co_done_ref, side_ref, range_sem, co_sem, range_out_sem, co_out_sem) = refs[:peers], refs[peers:]
+    core, place, line = spot_ref[0], spot_ref[1], spot_ref[3]
     lines, rows, _ = range_held_ref.shape
     cells, _, width = co_held_ref.shape
+    chips = cells // 2
 
     def range_copy(f):
-        return pltpu.make_async_copy(range_ref.at[f], range_held_ref.at[f], range_sem.at[f])
+        return pltpu.make_async_copy(range_refs[f // (lines // peers)].at[f % (lines // peers)], range_held_ref.at[f], range_sem.at[f])
 
     def co_copy(f):
-        return pltpu.make_async_copy(co_ref.at[f], co_held_ref.at[f], co_sem.at[f])
+        return pltpu.make_async_copy((co_own_ref, co_other_ref)[f // chips].at[f % chips], co_held_ref.at[f], co_sem.at[f])
+
+    def range_wait(f):
+        pltpu.make_async_copy(range_refs[0].at[0], range_held_ref.at[f], range_sem.at[f]).wait()
+
+    def co_wait(f):
+        pltpu.make_async_copy(co_own_ref.at[0], co_held_ref.at[f], co_sem.at[f]).wait()
 
     def range_out(f):
-        start = pl.multiple_of(at_ref[f] * rows, rows)
-        return pltpu.make_async_copy(range_done_ref.at[f], range_out_ref.at[pl.ds(start, rows)], range_out_sem.at[f])
+        return pltpu.make_async_copy(range_done_ref.at[f], range_out_ref.at[pl.ds(block_start(line, f, rows), rows)], range_out_sem.at[f])
 
     def co_out(f):
-        start = pl.multiple_of(at_ref[lines + f] * width, width)
-        return pltpu.make_async_copy(co_done_ref.at[f], co_out_ref.at[:, pl.ds(start, width)], co_out_sem.at[f])
+        column = jnp.where(f < chips, core, 1 - core) * chips + (place ^ (f % chips))
+        return pltpu.make_async_copy(co_done_ref.at[f], co_out_ref.at[:, pl.ds(pl.multiple_of(column * width, width), width)], co_out_sem.at[f])
 
     for f in range(lines):
         range_copy(f).start()
@@ -435,13 +460,13 @@
     side_ref[2], side_ref[3] = split(jnp.where(first, other_ref[0], own_ref[0]))
 
     def range_step(f, carry):
-        range_copy(f).wait()
+        range_wait(f)
         range_done_ref[f] = parts_dot(split(range_held_ref[f]), (side_ref[0], side_ref[1]), 1, 1)
         range_out(f).start()
         return carry
 
     def co_step(f, carry):
-        co_copy(f).wait()
+        co_wait(f)
         co_done_ref[f] = parts_dot((side_ref[2], side_ref[3]), split(co_held_ref[f]))
         co_out(f).start()
         return carry
@@ -454,26 +479,25 @@
         co_out(f).wait()
 
 
-def bases(spot, at, own, other, range_all, co_all):
-    lines, rows, k = range_all.shape
-    cells, count, width = co_all.shape
-    range_held, co_held = pltpu.VMEM(range_all.shape, jnp.float32), pltpu.VMEM(co_all.shape, jnp.float32)
+def bases(spot, own, other, ranges, co_own, co_other):
+    inner, rows, k = ranges[0].shape
+    chips, count, width = co_own.shape
+    lines, cells = inner * len(ranges), 2 * chips
+    range_held, co_held = pltpu.VMEM((lines, rows, k), jnp.float32), pltpu.VMEM((cells, count, width), jnp.float32)
     line_sem, cell_sem = pltpu.SemaphoreType.DMA((lines,)), pltpu.SemaphoreType.DMA((cells,))
     return call(
-        basis_kernel, (float_shape(lines * rows, k), float_shape(count, cells * width)),
-        [SCALAR, SCALAR, WHOLE, WHOLE, OUTSIDE, OUTSIDE], (OUTSIDE, OUTSIDE),
+        functools.partial(basis_kernel, len(ranges)), (float_shape(lines * rows, k), float_shape(count, cells * width)),
+        [SCALAR, WHOLE, WHOLE] + [OUTSIDE] * (len(ranges) + 2), (OUTSIDE, OUTSIDE),
         [range_held, co_held, range_held, co_held, pltpu.VMEM((4, k, k), jnp.bfloat16), line_sem, cell_sem, line_sem, cell_sem],
         flops=18 * lines * rows * k * k, limit=56,
-    )(spot, at, own, other, range_all, co_all)
+    )(spot, own, other, *ranges, co_own, co_other)
 
 
 def finish_kernel(scale, spot_ref, own_ref, other_ref, middle_own_ref, middle_other_ref, out_ref, middle_ref):
     core, place = spot_ref[0], spot_ref[1]
-    half = middle_ref.shape[0] // 2
     chips, extent = middle_own_ref.shape[0], middle_own_ref.shape[1]
-    for side, ref in ((core, middle_own_ref), (1 - core, middle_other_ref)):
-        for i in range(chips):
-            middle_ref[pl.ds(pl.multiple_of(side * half + (place ^ i) * extent, extent), extent), :] = ref[i]
+    for i in range(chips):
+        middle_ref[pl.ds(block_start(place, i, extent), extent), :] = middle_own_ref[i] + middle_other_ref[i]
     left = jnp.where(core == 0, own_ref[1], other_ref[1])
     right = jnp.where(core == 0, other_ref[1], own_ref[1])
     out_ref[...] = highest(highest(left, middle_ref[...]), right, 1, 1) * scale
@@ -493,55 +517,61 @@
     k = range_test.shape[1]
     chips = lax.axis_size("cell") // 2
     groups = groups_of("cell", 1, 2)
-    line_groups = groups_of("tm", 0, 2)
-    spot = jnp.stack([lax.axis_index("cell") & 1, place_of(groups, lax.axis_index("cell")), place_of(line_groups[:1], lax.axis_index("tm"))]).astype(jnp.int32)
-    at = [place_of(line_groups, line) for line in range(lax.axis_size("tm"))]
-    at = jnp.array(at + [(cell & 1) * chips + place_of(groups, cell) for cell in range(2 * chips)], jnp.int32)
+    lines = [("tm", (bit,)) for bit in range(bits_of("tm"))]
+    cell, line = lax.axis_index("cell"), lax.axis_index("tm")
+    spot = jnp.stack([cell & 1, place_of(groups, cell), place_of(lines[:2], line), place_of(lines, line)]).astype(jnp.int32)
 
     def core_swap(values):
         return swap(values, "cell", 1)
 
     r3, r2, r1, r0, sent, kept = sketch_terms(spot, chips, window, range_test, co_test, core_left, core_right)
     far = swap(r3, "tm", 1)
-    near = swap(r1, "tm", 1)
     pack = kept + core_swap(sent)
-    handed = r2 + after(far, pack)
+    handed = r1 + after(far, pack)
+    near = swap(after(r2, handed), "tm", 1)
     sketch_z = core_terms(after(spot, pack, handed), window, core_right, core_left)
     pack = scatter_sum(pack, groups)[0]
     handed, near, pack, sketch_z = lax.optimization_barrier((swap(handed, "tm", 2), near, pack, sketch_z))
     range_piece = (r0 + near + handed).reshape(lax.axis_size("tm") // 4, -1, r0.shape[1])
-    if line_groups[1:]:
-        rest = place_of(line_groups[1:], lax.axis_index("tm"))
+    if lines[2:]:
+        rest = place_of(lines[2:], line)
         range_piece = jnp.stack([lax.dynamic_index_in_dim(range_piece, rest ^ f, 0, False) for f in range(range_piece.shape[0])])
-    range_piece = scatter_sum(range_piece, line_groups[1:])[0]
+    range_piece = scatter_sum(range_piece, lines[2:])
     width = window.shape[1] // (2 * chips)
     packed = pack_width(co_test.shape[0], width, k)
     co_piece = pack[:packed].reshape(packed, -1, width).swapaxes(0, 1).reshape(-1, width)
     fold = pack[None, packed:]
-    co_all = lax.all_gather(co_piece, "cell", axis=0)
-
-    gram_sent, gram_kept = gram_terms(spot, chips, range_piece, co_piece, (rows_total, cols_total))
-    gram = whole_sum(scatter_sum(gram_kept + core_swap(gram_sent), groups), "tm")
+
+    gram_sent, gram_kept = gram_terms(spot, chips, range_piece[0], co_piece, (rows_total, cols_total))
     fold = whole_sum(fold, "tm")
-    range_all = lax.all_gather(after(range_piece, gram, fold), "tm", axis=0)
-    grams = gather(gram, groups)
-    fold = jnp.concatenate(gather(fold, groups))
-    middle_sent, middle_kept, image_gram = middle_terms(spot, chips, sketch_z, fold, core_swap(fold))
-    middle = scatter_sum(middle_kept + core_swap(middle_sent), groups)
-
-    image_gram, middle = lax.optimization_barrier((image_gram, middle))
-    begun, upper = factor_start(spot, grams, image_gram)
+    gram = scatter_sum(gram_kept + core_swap(gram_sent), groups)
+    co_parts = gather(after(co_piece[None], gram), groups)
+    gram, co_parts = lax.optimization_barrier((whole_sum(gram, "tm"), co_parts))
+    rows = gram.shape[1]
+    parts = gather(jnp.concatenate([gram, fold], axis=1), groups)
+    co_own = jnp.concatenate(co_parts)
+    fold = jnp.concatenate([part[:, rows:] for part in parts])
+
+    range_parts = gather(after(range_piece, gram, fold), lines[1:])
+    co_other, fold_other = core_swap(co_own), core_swap(fold)
+    state = factor_start(spot, parts)
+    state, fold_other = lax.optimization_barrier((state, fold_other))
+    middle = middle_terms(spot, chips, sketch_z, fold, fold_other)
+    middle = scatter_sum(middle, groups)
+    state = factor_next((1, 2), *state)
+    state, middle, range_parts = lax.optimization_barrier((state, middle, range_parts))
+    range_all = gather(jnp.concatenate(range_parts), lines[:1])
     for bit in range(bits_of("tm")):
         middle = middle + swap(middle, "tm", 1 << bit)
         if bit == 0:
-            middle, begun, upper = lax.optimization_barrier((middle, begun, upper))
-    own = factor_end(begun, upper)
-    middle, own = lax.optimization_barrier((middle, own))
+            state = factor_next((2, state[1].shape[0] // BASE - 1), *state)
+            state, middle = lax.optimization_barrier((state, middle))
+    own = factor_end(*state)
+    own, middle = lax.optimization_barrier((own, middle))
+    other = core_swap(own)
     middle = jnp.concatenate(gather(middle, groups))
-    middle_other = core_swap(middle)
-    other = core_swap(own)
-    range_basis, co_basis = bases(spot, at, own, other, range_all, co_all)
-    core_out = finish(spot, own, other, middle, middle_other, math.sqrt(rows_total * cols_total))
+    range_basis, co_basis = bases(spot, own, other, range_all, co_own, co_other)
+    core_out = finish(spot, own, other, middle, core_swap(middle), math.sqrt(rows_total * cols_total))
     return (range_basis, co_basis, core_out)
 
 

time: 151 us -> 139 us (0.921)
  between operations: 14.4 us -> 1.31 us
  waiting for transfers between devices: 37.5 us -> 33.6 us
  starting transfers between devices: 37.4 us -> 39.4 us
  local copies, waits for them, and re-layouts: 0.18 us -> 2.07 us
    all_gather x2 -> x0, waiting for transfers between devices: 5.06 us -> none  [the longest x1 5.06 us: per_device(): co_all = lax.all_gather(co_piece, 'cell', axis=0)]
    ppermute x33 -> x35, starting transfers between devices: 37.3 us -> 39.4 us  [swap(): lax.ppermute(values, axis, [(i, i ^ mask) for i in range(lax.axis_size(ax...]
    ppermute x33 -> x35, waiting for transfers between devices: 31.7 us -> 33.6 us  [swap(): lax.ppermute(values, axis, [(i, i ^ mask) for i in range(lax.axis_size(ax...]
    unnamed x19 -> x29, local copies, waits for them, and re-layouts: 0.05 us -> 1.88 us
    pallas_call x4 -> x6, Pallas kernels: 24.9 us -> 25.2 us  [the longest x2 6.84 us: factor_next(): call(functools.partial(factor_next_kernel, steps), (float_shape(2, n, n),...]
  transfers between devices with their start and end apart: 35 -> 35, of which waited for: 20 -> 18; matrix products, arithmetic and copies ran while one was open for 1% -> 2% of each run, Pallas kernels for 22% -> 25%
where the time goes in v6:
time: 139 us
  Pallas kernels  59.6 us (43%)
  starting transfers between devices  39.4 us (28%)
  waiting for transfers between devices  33.6 us (24%)
  other arithmetic  2.63 us (2%)
  local copies, waits for them, and re-layouts  2.07 us (1%)
    ppermute x35, starting transfers between devices, swap(): lax.ppermute(values, axis, [(i, i ^ mask) for i in range(lax.axis_size(ax...  39.4 us
    ppermute x35, waiting for transfers between devices, swap(): lax.ppermute(values, axis, [(i, i ^ mask) for i in range(lax.axis_size(ax...  33.6 us
    pallas_call x1, Pallas kernels, sketch_terms(): call(sketch_kernel, (float_shape(rows // TILES, k),) * 4 + (float_shape(c...  17.3 us
    pallas_call x1, Pallas kernels, core_terms(): call(core_kernel, float_shape(s_core, s_core), [SCALAR] + [OUTSIDE] * 3,...  13.4 us
    pallas_call x2, Pallas kernels, factor_next(): call(functools.partial(factor_next_kernel, steps), (float_shape(2, n, n),...  6.84 us
    pallas_call x1, Pallas kernels, bases(): call(functools.partial(basis_kernel, len(ranges)), (float_shape(lines * r...  6.78 us
    pallas_call x1, Pallas kernels, factor_start(): call(functools.partial(factor_start_kernel, (0, 1), len(parts)), (float_s...  5.16 us
    pallas_call x1, Pallas kernels, factor_end(): call(functools.partial(factor_end_kernel, (n // BASE - 1, n // BASE)), fl...  4.38 us
  transfers between devices with their start and end apart: 35, of which 18 were waited for; matrix products, arithmetic and copies ran while one was open for 2% of the time, Pallas kernels for 25%

profile of v6, /device:TPU:0, one launch (start us, length us, event | category | flops | bytes accessed | tf_op | source)
XLA Modules:
  0.0 138.6 jit_solution(1686760660178479912)
XLA Ops:
  0.6 0.6 pad_add_fusion.spot_ref
  1.3 17.3 %shard_map.76 = (f32[256,256]{1,0:T(8,128)}, f32[256,256]{1,0:T(8,128)}, f32[256,256]{1,0:T(8,128)}, f32[256,256]{1,0:T(8,128)}, f32[4,384,256]{2,1,0:T(8,128)}, /*index=5*/f32[4,384,256]{2,1,0:T(8,128)}) custom-call(s32[4]{0:T(128)} %pad_add_fusion.spot_ref, f32[1024,2048]{1,0:T(8,128)} %window_ref.3, f32[2048,256]{1,0:T(8,128)} %test_ref.1, ...), custom_call_target="tpu_custom_call" | custom-call | flops 6442450944 | bytes 4194304 | tf_op jit(solution)/shard_map/pallas_call | solution.py:189
  18.5 0.5 collective-permute-start.1
  19.1 2.6 %collective-permute-start = (f32[256,256]{1,0:T(8,128)}, f32[256,256]{1,0:T(8,128)S(1)}, u32[]{:S(2)}, u32[]{:S(2)}) collective-permute-start(f32[256,256]{1,0:T(8,128)} %get-tuple-element.48), channel_id=1, source_target_pairs={{0,1},{1,0},{2,3},{3,2},{4,5},{5,4},{6,7},{7,6},{8,9},{9,8},{10,11... | collective-permute-start | bytes 786440 | tf_op jit(solution)/shard_map/ppermute | solution.py:69
  21.7 0.6 collective-permute-done.1
  22.3 1.6 %add.69 = f32[4,384,256]{2,1,0:T(8,128)S(1)} add(f32[4,384,256]{2,1,0:T(8,128)} %get-tuple-element.49, f32[4,384,256]{2,1,0:T(8,128)S(1)} %collective-permute-done.1) | non-fusion elementwise | flops 393216 | bytes 4718592 | tf_op jit(solution)/shard_map/add | solution.py:529
  23.9 0.1 fusion.5
  24.0 4.8 %collective-permute-done = f32[256,256]{1,0:T(8,128)S(1)} collective-permute-done((f32[256,256]{1,0:T(8,128)}, f32[256,256]{1,0:T(8,128)S(1)}, u32[]{:S(2)}, u32[]{:S(2)}) %collective-permute-start) | collective-permute-done | bytes 262176 | tf_op jit(solution)/shard_map/ppermute | solution.py:69
  28.8 2.8 %collective-permute-start.2 = (f32[256,256]{1,0:T(8,128)S(1)}, f32[256,256]{1,0:T(8,128)S(1)}, u32[]{:S(2)}, u32[]{:S(2)}) collective-permute-start(f32[256,256]{1,0:T(8,128)S(1)} %add.70), channel_id=1, source_target_pairs={{0,2},{1,3},{2,0},{3,1},{4,6},{5,7},{6,4},{7,5},{8,10},{9,11},{10,... | collective-permute-start | bytes 786440 | tf_op jit(solution)/shard_map/ppermute | solution.py:69
  31.7 1.6 %collective-permute-start.3 = (f32[256,256]{1,0:T(8,128)S(1)}, f32[256,256]{1,0:T(8,128)S(1)}, u32[]{:S(2)}, u32[]{:S(2)}) collective-permute-start(f32[256,256]{1,0:T(8,128)S(1)} %copy-done.10), channel_id=1, source_target_pairs={{0,1},{1,0},{2,3},{3,2},{4,5},{5,4},{6,7},{7,6},{8,9},{9,8},{10,11... | collective-permute-start | bytes 786440 | tf_op jit(solution)/shard_map/ppermute | solution.py:69
  33.3 1.5 %collective-permute-start.4 = (f32[1,384,256]{2,1,0:T(8,128)S(1)}, f32[1,384,256]{2,1,0:T(8,128)S(1)}, u32[]{:S(2)}, u32[]{:S(2)}) collective-permute-start(f32[1,384,256]{2,1,0:T(8,128)S(1)} %get-tuple-element.91), channel_id=1, source_target_pairs={{0,8},{4,12},{8,0},{12,4},{16,24},{20,28},{24,16},{28,20},{1,9},{5... | collective-permute-start | bytes 1179656 | tf_op jit(solution)/shard_map/ppermute | solution.py:69
  34.7 1.5 %collective-permute-start.5 = (f32[1,384,256]{2,1,0:T(8,128)S(1)}, f32[1,384,256]{2,1,0:T(8,128)S(1)}, u32[]{:S(2)}, u32[]{:S(2)}) collective-permute-start(f32[1,384,256]{2,1,0:T(8,128)S(1)} %get-tuple-element.90), channel_id=1, source_target_pairs={{0,16},{4,20},{8,24},{12,28},{16,0},{20,4},{24,8},{28,12},{1,17},{... | collective-permute-start | bytes 1179656 | tf_op jit(solution)/shard_map/ppermute | solution.py:69
  36.3 0.5 collective-permute-start.6
  36.7 13.4 %shard_map.77.z_ref = f32[512,512]{1,0:T(8,128)} custom-call(s32[4]{0:T(128)} %pad_add_fusion.spot_ref, f32[1024,2048]{1,0:T(8,128)} %window_ref.3, f32[512,2048]{1,0:T(8,128)} %right_ref.3, f32[512,1024]{1,0:T(8,128)} %left_ref.3), custom_call_target="tpu_custom_call" | custom-call | flops 9663676416 | bytes 4194304 | tf_op jit(solution)/shard_map/pallas_call | solution.py:242
  50.2 2.8 %collective-permute-done.5 = f32[1,384,256]{2,1,0:T(8,128)S(1)} collective-permute-done((f32[1,384,256]{2,1,0:T(8,128)S(1)}, f32[1,384,256]{2,1,0:T(8,128)S(1)}, u32[]{:S(2)}, u32[]{:S(2)}) %collective-permute-start.5) | collective-permute-done | bytes 393248 | tf_op jit(solution)/shard_map/ppermute | solution.py:69
  53.0 0.1 fusion.1
  53.2 1.4 %shard_map.78 = (f32[4,64,256]{2,1,0:T(8,128)S(1)}, f32[4,64,256]{2,1,0:T(8,128)S(1)}) custom-call(s32[4]{0:T(128)S(1)} %copy-done.3, f32[256,256]{1,0:T(8,128)S(1)} %get-tuple-element.100.range_ref, f32[256,256]{1,0:T(8,128)S(1)} %get-tuple-element.93.co_ref), custom_call_target="tpu_custom_call" | custom-call | flops 402653184 | bytes 4194304 | tf_op jit(solution)/shard_map/pallas_call | solution.py:266
  54.7 1.5 %collective-permute-done.7 = f32[4,64,256]{2,1,0:T(8,128)S(1)} collective-permute-done((f32[4,64,256]{2,1,0:T(8,128)S(1)}, f32[4,64,256]{2,1,0:T(8,128)S(1)}, u32[]{:S(2)}, u32[]{:S(2)}) %collective-permute-start.7) | collective-permute-done | bytes 262176 | tf_op jit(solution)/shard_map/ppermute | solution.py:69
  56.3 1.3 collective-permute-start.8
  57.6 0.8 collective-permute-start.9
  58.4 1.4 %collective-permute-start.10 = (f32[1,64,256]{2,1,0:T(8,128)S(1)}, f32[1,64,256]{2,1,0:T(8,128)S(1)}, u32[]{:S(2)}, u32[]{:S(2)}) collective-permute-start(f32[1,64,256]{2,1,0:T(8,128)S(1)} %get-tuple-element.97), channel_id=1, source_target_pairs={{0,24},{4,28},{8,16},{12,20},{16,8},{20,12},{24,0},{28,4},{1,25},{... | collective-permute-start | bytes 196616 | tf_op jit(solution)/shard_map/ppermute | solution.py:69
  59.9 0.5 collective-permute-start.16
  60.4 0.2 collective-permute-done.8
  60.6 1.9 %collective-permute-done.9 = f32[1,64,256]{2,1,0:T(8,128)S(1)} collective-permute-done((f32[1,64,256]{2,1,0:T(8,128)S(1)}, f32[1,64,256]{2,1,0:T(8,128)S(1)}, u32[]{:S(2)}, u32[]{:S(2)}) %collective-permute-start.9) | collective-permute-done | bytes 65568 | tf_op jit(solution)/shard_map/ppermute | solution.py:69
  62.6 1.0 collective-permute-done.10
  63.6 1.6 %collective-permute-start.13 = (f32[1,256,256]{2,1,0:T(8,128)S(1)}, f32[1,256,256]{2,1,0:T(8,128)S(1)}, u32[]{:S(2)}, u32[]{:S(2)}) collective-permute-start(f32[1,256,256]{2,1,0:T(8,128)S(1)} %get-tuple-element.82), channel_id=1, source_target_pairs={{0,8},{4,12},{8,0},{12,4},{16,24},{20,28},{24,16},{28,20},{1,9},{5... | collective-permute-start | bytes 786440 | tf_op jit(solution)/shard_map/ppermute | solution.py:69
  65.2 0.5 collective-permute-start.14
  65.7 1.5 %collective-permute-start.15 = (f32[1,256,256]{2,1,0:T(8,128)S(1)}, f32[1,256,256]{2,1,0:T(8,128)S(1)}, u32[]{:S(2)}, u32[]{:S(2)}) collective-permute-start(f32[1,256,256]{2,1,0:T(8,128)S(1)} %get-tuple-element.82), channel_id=1, source_target_pairs={{0,24},{4,28},{8,16},{12,20},{16,8},{20,12},{24,0},{28,4},{1,25},{... | collective-permute-start | bytes 786440 | tf_op jit(solution)/shard_map/ppermute | solution.py:69
  67.2 0.4 collective-permute-start.17
  67.6 0.4 collective-permute-start.11
  68.1 3.8 %collective-permute-done.11 = f32[1,64,256]{2,1,0:T(8,128)S(1)} collective-permute-done((f32[1,64,256]{2,1,0:T(8,128)S(1)}, f32[1,64,256]{2,1,0:T(8,128)S(1)}, u32[]{:S(2)}, u32[]{:S(2)}) %collective-permute-start.11) | collective-permute-done | bytes 65568 | tf_op jit(solution)/shard_map/ppermute | solution.py:69
  71.9 3.3 %collective-permute-start.12 = (f32[1,64,256]{2,1,0:T(8,128)S(1)}, f32[1,64,256]{2,1,0:T(8,128)S(1)}, u32[]{:S(2)}, u32[]{:S(2)}) collective-permute-start(f32[1,64,256]{2,1,0:T(8,128)S(1)} %add.80), channel_id=1, source_target_pairs={{0,2},{1,3},{2,0},{3,1},{4,6},{5,7},{6,4},{7,5},{8,10},{9,11},{10,... | collective-permute-start | bytes 196616 | tf_op jit(solution)/shard_map/ppermute | solution.py:69
  75.2 0.6 collective-permute-done.17
  75.8 2.3 %collective-permute-done.12 = f32[1,64,256]{2,1,0:T(8,128)S(1)} collective-permute-done((f32[1,64,256]{2,1,0:T(8,128)S(1)}, f32[1,64,256]{2,1,0:T(8,128)S(1)}, u32[]{:S(2)}, u32[]{:S(2)}) %collective-permute-start.12) | collective-permute-done | bytes 65568 | tf_op jit(solution)/shard_map/ppermute | solution.py:69
  78.2 1.5 %collective-permute-start.20 = (f32[1,192,256]{2,1,0:T(8,128)S(1)}, f32[1,192,256]{2,1,0:T(8,128)S(1)}, u32[]{:S(2)}, u32[]{:S(2)}) collective-permute-start(f32[1,192,256]{2,1,0:T(8,128)S(1)} %pad_maximum_fusion.1.refs_0_), channel_id=1, source_target_pairs={{0,24},{4,28},{8,16},{12,20},{16,8},{20,12},{24,0},{28,4},{1,25},{... | collective-permute-start | bytes 589832 | tf_op jit(solution)/shard_map/ppermute | solution.py:69
  79.7 0.7 collective-permute-start.19
  80.5 1.3 collective-permute-start.18
  81.8 3.6 %collective-permute-done.20.refs_3_ = f32[1,192,256]{2,1,0:T(8,128)S(1)} collective-permute-done((f32[1,192,256]{2,1,0:T(8,128)S(1)}, f32[1,192,256]{2,1,0:T(8,128)S(1)}, u32[]{:S(2)}, u32[]{:S(2)}) %collective-permute-start.20) | collective-permute-done | bytes 196640 | tf_op jit(solution)/shard_map/ppermute | solution.py:69
  85.4 2.0 %collective-permute-done.19.refs_2_ = f32[1,192,256]{2,1,0:T(8,128)S(1)} collective-permute-done((f32[1,192,256]{2,1,0:T(8,128)S(1)}, f32[1,192,256]{2,1,0:T(8,128)S(1)}, u32[]{:S(2)}, u32[]{:S(2)}) %collective-permute-start.19) | collective-permute-done | bytes 196640 | tf_op jit(solution)/shard_map/ppermute | solution.py:69
  87.6 0.6 collective-permute-start.30
  88.2 1.8 %collective-permute-start.25 = (f32[1,256,256]{2,1,0:T(8,128)S(1)}, f32[1,256,256]{2,1,0:T(8,128)S(1)}, u32[]{:S(2)}, u32[]{:S(2)}) collective-permute-start(f32[1,256,256]{2,1,0:T(8,128)S(1)} %bitcast.12), channel_id=1, source_target_pairs={{0,2},{1,3},{2,0},{3,1},{4,6},{5,7},{6,4},{7,5},{8,10},{9,11},{10,... | collective-permute-start | bytes 786440 | tf_op jit(solution)/shard_map/ppermute | solution.py:69
  90.0 5.2 %shard_map.79 = (f32[2,256,256]{2,1,0:T(8,128)S(1)}, f32[256,256]{1,0:T(8,128)S(1)}) custom-call(s32[4]{0:T(128)S(1)} %copy-done.3, f32[1,192,256]{2,1,0:T(8,128)S(1)} %pad_maximum_fusion.1.refs_0_, f32[1,192,256]{2,1,0:T(8,128)S(1)} %collective-permute-done.18.refs_1_, f32[1,192,256]{2,1,0:T(8,128)S(1)} %collective-permute-done.19.refs_2_, ...), custom_call_target="tpu_custom_call" | custom-call | flops 1677721600 | bytes 4194304 | tf_op jit(solution)/shard_map/pallas_call | solution.py:407
  95.2 2.1 %shard_map.81 = f32[4,64,256]{2,1,0:T(8,128)S(1)} custom-call(s32[4]{0:T(128)S(1)} %copy-done.3, f32[512,512]{1,0:T(8,128)S(1)} %copy-done, f32[4,128,256]{2,1,0:T(8,128)S(1)} %pad_maximum_fusion.own_ref, f32[4,128,256]{2,1,0:T(8,128)S(1)} %collective-permute-done.21.other_ref), custom_call_target="tpu_custom_call" | custom-call | flops 402653184 | bytes 4194304 | tf_op jit(solution)/shard_map/pallas_call | solution.py:286
  97.3 1.5 %collective-permute-start.22 = (f32[1,64,256]{2,1,0:T(8,128)S(1)}, f32[1,64,256]{2,1,0:T(8,128)S(1)}, u32[]{:S(2)}, u32[]{:S(2)}) collective-permute-start(f32[1,64,256]{2,1,0:T(8,128)S(1)} %get-tuple-element.96), channel_id=1, source_target_pairs={{0,8},{4,12},{8,0},{12,4},{16,24},{20,28},{24,16},{28,20},{1,9},{5... | collective-permute-start | bytes 196616 | tf_op jit(solution)/shard_map/ppermute | solution.py:69
  98.8 0.6 collective-permute-start.23
  99.4 1.4 %collective-permute-start.24 = (f32[1,64,256]{2,1,0:T(8,128)S(1)}, f32[1,64,256]{2,1,0:T(8,128)S(1)}, u32[]{:S(2)}, u32[]{:S(2)}) collective-permute-start(f32[1,64,256]{2,1,0:T(8,128)S(1)} %get-tuple-element.94), channel_id=1, source_target_pairs={{0,24},{4,28},{8,16},{12,20},{16,8},{20,12},{24,0},{28,4},{1,25},{... | collective-permute-start | bytes 196616 | tf_op jit(solution)/shard_map/ppermute | solution.py:69
  100.9 3.5 %shard_map.80 = (f32[2,256,256]{2,1,0:T(8,128)S(1)}, f32[256,256]{1,0:T(8,128)S(1)}) custom-call(f32[2,256,256]{2,1,0:T(8,128)S(1)} %get-tuple-element.64.begun_ref, f32[256,256]{1,0:T(8,128)S(1)} %get-tuple-element.65.begun_upper_ref), custom_call_target="tpu_custom_call" | custom-call | flops 1677721600 | bytes 4194304 | tf_op jit(solution)/shard_map/pallas_call | solution.py:415
  104.4 0.2 collective-permute-done.24
  104.8 2.1 %collective-permute-start.29 = (f32[2,256,256]{2,1,0:T(8,128)S(1)}, f32[2,256,256]{2,1,0:T(8,128)S(1)}, u32[]{:S(2)}, u32[]{:S(2)}) collective-permute-start(f32[2,256,256]{2,1,0:T(8,128)S(1)} %constant_dynamic-update-slice_fusion.refs_0_), channel_id=1, source_target_pairs={{0,1},{1,0},{2,3},{3,2},{4,5},{5,4},{6,7},{7,6},{8,9},{9,8},{10,11... | collective-permute-start | bytes 1572872 | tf_op jit(solution)/shard_map/ppermute | solution.py:69
  106.8 3.4 %shard_map.82 = (f32[2,256,256]{2,1,0:T(8,128)S(1)}, f32[256,256]{1,0:T(8,128)S(1)}) custom-call(f32[2,256,256]{2,1,0:T(8,128)S(1)} %get-tuple-element.71.begun_ref, f32[256,256]{1,0:T(8,128)S(1)} %get-tuple-element.72.begun_upper_ref), custom_call_target="tpu_custom_call" | custom-call | flops 1677721600 | bytes 4194304 | tf_op jit(solution)/shard_map/pallas_call | solution.py:415
  110.2 1.2 collective-permute-start.27
  111.4 4.4 %shard_map.83.own_ref = f32[2,256,256]{2,1,0:T(8,128)S(1)} custom-call(f32[2,256,256]{2,1,0:T(8,128)S(1)} %get-tuple-element.76.begun_ref, f32[256,256]{1,0:T(8,128)S(1)} %get-tuple-element.77.begun_upper_ref), custom_call_target="tpu_custom_call" | custom-call | flops 1677721600 | bytes 4194304 | tf_op jit(solution)/shard_map/pallas_call | solution.py:422
  115.8 2.9 %collective-permute-done.27 = f32[1,64,256]{2,1,0:T(8,128)S(1)} collective-permute-done((f32[1,64,256]{2,1,0:T(8,128)S(1)}, f32[1,64,256]{2,1,0:T(8,128)S(1)}, u32[]{:S(2)}, u32[]{:S(2)}) %collective-permute-start.27) | collective-permute-done | bytes 65568 | tf_op jit(solution)/shard_map/ppermute | solution.py:69
  118.8 1.5 %collective-permute-start.31 = (f32[1,64,256]{2,1,0:T(8,128)S(1)}, f32[1,64,256]{2,1,0:T(8,128)S(1)}, u32[]{:S(2)}, u32[]{:S(2)}) collective-permute-start(f32[1,64,256]{2,1,0:T(8,128)S(1)} %add.88), channel_id=1, source_target_pairs={{0,8},{4,12},{8,0},{12,4},{16,24},{20,28},{24,16},{28,20},{1,9},{5... | collective-permute-start | bytes 196616 | tf_op jit(solution)/shard_map/ppermute | solution.py:69
  120.3 0.6 collective-permute-start.32
  120.9 1.4 %collective-permute-start.33 = (f32[1,64,256]{2,1,0:T(8,128)S(1)}, f32[1,64,256]{2,1,0:T(8,128)S(1)}, u32[]{:S(2)}, u32[]{:S(2)}) collective-permute-start(f32[1,64,256]{2,1,0:T(8,128)S(1)} %add.88), channel_id=1, source_target_pairs={{0,24},{4,28},{8,16},{12,20},{16,8},{20,12},{24,0},{28,4},{1,25},{... | collective-permute-start | bytes 196616 | tf_op jit(solution)/shard_map/ppermute | solution.py:69
  122.3 1.3 collective-permute-done.31
  123.7 0.9 collective-permute-done.32
  124.6 1.5 %collective-permute-done.33 = f32[1,64,256]{2,1,0:T(8,128)S(1)} collective-permute-done((f32[1,64,256]{2,1,0:T(8,128)S(1)}, f32[1,64,256]{2,1,0:T(8,128)S(1)}, u32[]{:S(2)}, u32[]{:S(2)}) %collective-permute-start.33) | collective-permute-done | bytes 65568 | tf_op jit(solution)/shard_map/ppermute | solution.py:69
  126.1 1.5 %collective-permute-done.34.middle_other_ref = f32[4,64,256]{2,1,0:T(8,128)S(1)} collective-permute-done((f32[4,64,256]{2,1,0:T(8,128)S(1)}, f32[4,64,256]{2,1,0:T(8,128)S(1)}, u32[]{:S(2)}, u32[]{:S(2)}) %collective-permute-start.34) | collective-permute-done | bytes 262176 | tf_op jit(solution)/shard_map/ppermute | solution.py:69
  127.6 2.3 %shard_map.85 = f32[256,256]{1,0:T(8,128)} custom-call(s32[4]{0:T(128)S(1)} %copy-done.3, f32[2,256,256]{2,1,0:T(8,128)S(1)} %shard_map.83.own_ref, f32[2,256,256]{2,1,0:T(8,128)S(1)} %collective-permute-done.28.other_ref, f32[4,64,256]{2,1,0:T(8,128)S(1)} %constant_dynamic-update-slice_fusion.6.middle_own_ref, ...), custom_call_target="tpu_custom_call" | custom-call | flops 402653184 | bytes 4194304 | tf_op jit(solution)/shard_map/pallas_call | solution.py:508
  129.9 0.9 copy-done.8
  130.9 0.8 copy-done.9
  131.7 6.8 %shard_map.84 = (f32[1024,256]{1,0:T(8,128)}, f32[256,2048]{1,0:T(8,128)}) custom-call(s32[4]{0:T(128)} %pad_add_fusion.spot_ref, f32[2,256,256]{2,1,0:T(8,128)} %copy-done.1, f32[2,256,256]{2,1,0:T(8,128)} %copy-done.2, f32[2,256,256]{2,1,0:T(8,128)} %copy-done.6, f32[2,256,256]{2,1,0:T(8,128)} %copy-done.9, f32[4,256,256]{2,1,0:T(8,128)} %copy-done.7, ...), custom_call_target="tpu_custom_call" | custom-call | flops 1207959552 | bytes 4194304 | tf_op jit(solution)/shard_map/pallas_call | solution.py:488
  (71 shorter events, 0.8 us)
Async XLA Ops:
  18.5 3.8 %collective-permute-start.1 = (f32[4,384,256]{2,1,0:T(8,128)}, f32[4,384,256]{2,1,0:T(8,128)S(1)}, u32[]{:S(2)}, u32[]{:S(2)}) collective-permute-start(f32[4,384,256]{2,1,0:T(8,128)} %get-tuple-element.50), channel_id=1, source_target_pairs={{0,4},{4,0},{8,12},{12,8},{16,20},{20,16},{24,28},{28,24},{1,5},{5... | collective-permute-start | bytes 4718600 | tf_op jit(solution)/shard_map/ppermute | solution.py:69
  19.1 9.7 %collective-permute-start = (f32[256,256]{1,0:T(8,128)}, f32[256,256]{1,0:T(8,128)S(1)}, u32[]{:S(2)}, u32[]{:S(2)}) collective-permute-start(f32[256,256]{1,0:T(8,128)} %get-tuple-element.48), channel_id=1, source_target_pairs={{0,1},{1,0},{2,3},{3,2},{4,5},{5,4},{6,7},{7,6},{8,9},{9,8},{10,11... | collective-permute-start | bytes 786440 | tf_op jit(solution)/shard_map/ppermute | solution.py:69
  23.9 4.9 %copy-start.5 = (f32[256,256]{1,0:T(8,128)S(1)}, f32[256,256]{1,0:T(8,128)}, u32[]{:S(2)}) copy-start(f32[256,256]{1,0:T(8,128)} %get-tuple-element.47) | copy-start | bytes 786436
  23.9 7.8 %copy-start.10 = (f32[256,256]{1,0:T(8,128)S(1)}, f32[256,256]{1,0:T(8,128)}, u32[]{:S(2)}) copy-start(f32[256,256]{1,0:T(8,128)} %get-tuple-element.53) | copy-start | bytes 786436
  28.8 24.3 %collective-permute-start.2 = (f32[256,256]{1,0:T(8,128)S(1)}, f32[256,256]{1,0:T(8,128)S(1)}, u32[]{:S(2)}, u32[]{:S(2)}) collective-permute-start(f32[256,256]{1,0:T(8,128)S(1)} %add.70), channel_id=1, source_target_pairs={{0,2},{1,3},{2,0},{3,1},{4,6},{5,7},{6,4},{7,5},{8,10},{9,11},{10,... | collective-permute-start | bytes 786440 | tf_op jit(solution)/shard_map/ppermute | solution.py:69
  31.7 21.5 %collective-permute-start.3 = (f32[256,256]{1,0:T(8,128)S(1)}, f32[256,256]{1,0:T(8,128)S(1)}, u32[]{:S(2)}, u32[]{:S(2)}) collective-permute-start(f32[256,256]{1,0:T(8,128)S(1)} %copy-done.10), channel_id=1, source_target_pairs={{0,1},{1,0},{2,3},{3,2},{4,5},{5,4},{6,7},{7,6},{8,9},{9,8},{10,11... | collective-permute-start | bytes 786440 | tf_op jit(solution)/shard_map/ppermute | solution.py:69
  33.3 16.9 %collective-permute-start.4 = (f32[1,384,256]{2,1,0:T(8,128)S(1)}, f32[1,384,256]{2,1,0:T(8,128)S(1)}, u32[]{:S(2)}, u32[]{:S(2)}) collective-permute-start(f32[1,384,256]{2,1,0:T(8,128)S(1)} %get-tuple-element.91), channel_id=1, source_target_pairs={{0,8},{4,12},{8,0},{12,4},{16,24},{20,28},{24,16},{28,20},{1,9},{5... | collective-permute-start | bytes 1179656 | tf_op jit(solution)/shard_map/ppermute | solution.py:69
  34.7 18.3 %collective-permute-start.5 = (f32[1,384,256]{2,1,0:T(8,128)S(1)}, f32[1,384,256]{2,1,0:T(8,128)S(1)}, u32[]{:S(2)}, u32[]{:S(2)}) collective-permute-start(f32[1,384,256]{2,1,0:T(8,128)S(1)} %get-tuple-element.90), channel_id=1, source_target_pairs={{0,16},{4,20},{8,24},{12,28},{16,0},{20,4},{24,8},{28,12},{1,17},{... | collective-permute-start | bytes 1179656 | tf_op jit(solution)/shard_map/ppermute | solution.py:69
  36.3 16.7 %collective-permute-start.6 = (f32[1,384,256]{2,1,0:T(8,128)S(1)}, f32[1,384,256]{2,1,0:T(8,128)S(1)}, u32[]{:S(2)}, u32[]{:S(2)}) collective-permute-start(f32[1,384,256]{2,1,0:T(8,128)S(1)} %get-tuple-element.89), channel_id=1, source_target_pairs={{0,24},{4,28},{8,16},{12,20},{16,8},{20,12},{24,0},{28,4},{1,25},{... | collective-permute-start | bytes 1179656 | tf_op jit(solution)/shard_map/ppermute | solution.py:69
  50.2 3.0 %copy-start.4 = (f32[256,256]{1,0:T(8,128)S(1)}, f32[256,256]{1,0:T(8,128)}, u32[]{:S(2)}) copy-start(f32[256,256]{1,0:T(8,128)} %get-tuple-element.46) | copy-start | bytes 786436
  50.2 3.0 %copy-start.3 = (s32[4]{0:T(128)S(1)}, s32[4]{0:T(128)}, u32[]{:S(2)}) copy-start(s32[4]{0:T(128)} %pad_add_fusion.spot_ref) | copy-start | bytes 52
  54.7 1.6 %collective-permute-start.7 = (f32[4,64,256]{2,1,0:T(8,128)S(1)}, f32[4,64,256]{2,1,0:T(8,128)S(1)}, u32[]{:S(2)}, u32[]{:S(2)}) collective-permute-start(f32[4,64,256]{2,1,0:T(8,128)S(1)} %get-tuple-element.59), channel_id=1, source_target_pairs={{0,4},{4,0},{8,12},{12,8},{16,20},{20,16},{24,28},{28,24},{1,5},{5... | collective-permute-start | bytes 786440 | tf_op jit(solution)/shard_map/ppermute | solution.py:69
  56.3 4.3 %collective-permute-start.8 = (f32[1,64,256]{2,1,0:T(8,128)S(1)}, f32[1,64,256]{2,1,0:T(8,128)S(1)}, u32[]{:S(2)}, u32[]{:S(2)}) collective-permute-start(f32[1,64,256]{2,1,0:T(8,128)S(1)} %get-tuple-element.99), channel_id=1, source_target_pairs={{0,8},{4,12},{8,0},{12,4},{16,24},{20,28},{24,16},{28,20},{1,9},{5... | collective-permute-start | bytes 196616 | tf_op jit(solution)/shard_map/ppermute | solution.py:69
  57.6 5.0 %collective-permute-start.9 = (f32[1,64,256]{2,1,0:T(8,128)S(1)}, f32[1,64,256]{2,1,0:T(8,128)S(1)}, u32[]{:S(2)}, u32[]{:S(2)}) collective-permute-start(f32[1,64,256]{2,1,0:T(8,128)S(1)} %get-tuple-element.98), channel_id=1, source_target_pairs={{0,16},{4,20},{8,24},{12,28},{16,0},{20,4},{24,8},{28,12},{1,17},{... | collective-permute-start | bytes 196616 | tf_op jit(solution)/shard_map/ppermute | solution.py:69
  58.4 5.2 %collective-permute-start.10 = (f32[1,64,256]{2,1,0:T(8,128)S(1)}, f32[1,64,256]{2,1,0:T(8,128)S(1)}, u32[]{:S(2)}, u32[]{:S(2)}) collective-permute-start(f32[1,64,256]{2,1,0:T(8,128)S(1)} %get-tuple-element.97), channel_id=1, source_target_pairs={{0,24},{4,28},{8,16},{12,20},{16,8},{20,12},{24,0},{28,4},{1,25},{... | collective-permute-start | bytes 196616 | tf_op jit(solution)/shard_map/ppermute | solution.py:69
  59.9 7.3 %collective-permute-start.16 = (f32[1,128,256]{2,1,0:T(8,128)S(1)}, f32[1,128,256]{2,1,0:T(8,128)S(1)}, u32[]{:S(2)}, u32[]{:S(2)}) collective-permute-start(f32[1,128,256]{2,1,0:T(8,128)S(1)} %slice_bitcast_fusion), channel_id=1, source_target_pairs={{0,1},{1,0},{2,3},{3,2},{4,5},{5,4},{6,7},{7,6},{8,9},{9,8},{10,11... | collective-permute-start | bytes 393224 | tf_op jit(solution)/shard_map/ppermute | solution.py:69
  63.6 14.5 %collective-permute-start.13 = (f32[1,256,256]{2,1,0:T(8,128)S(1)}, f32[1,256,256]{2,1,0:T(8,128)S(1)}, u32[]{:S(2)}, u32[]{:S(2)}) collective-permute-start(f32[1,256,256]{2,1,0:T(8,128)S(1)} %get-tuple-element.82), channel_id=1, source_target_pairs={{0,8},{4,12},{8,0},{12,4},{16,24},{20,28},{24,16},{28,20},{1,9},{5... | collective-permute-start | bytes 786440 | tf_op jit(solution)/shard_map/ppermute | solution.py:69
  65.2 13.0 %collective-permute-start.14 = (f32[1,256,256]{2,1,0:T(8,128)S(1)}, f32[1,256,256]{2,1,0:T(8,128)S(1)}, u32[]{:S(2)}, u32[]{:S(2)}) collective-permute-start(f32[1,256,256]{2,1,0:T(8,128)S(1)} %get-tuple-element.82), channel_id=1, source_target_pairs={{0,16},{4,20},{8,24},{12,28},{16,0},{20,4},{24,8},{28,12},{1,17},{... | collective-permute-start | bytes 786440 | tf_op jit(solution)/shard_map/ppermute | solution.py:69
  65.7 12.5 %collective-permute-start.15 = (f32[1,256,256]{2,1,0:T(8,128)S(1)}, f32[1,256,256]{2,1,0:T(8,128)S(1)}, u32[]{:S(2)}, u32[]{:S(2)}) collective-permute-start(f32[1,256,256]{2,1,0:T(8,128)S(1)} %get-tuple-element.82), channel_id=1, source_target_pairs={{0,24},{4,28},{8,16},{12,20},{16,8},{20,12},{24,0},{28,4},{1,25},{... | collective-permute-start | bytes 786440 | tf_op jit(solution)/shard_map/ppermute | solution.py:69
  67.2 8.6 %collective-permute-start.17 = (f32[1,128,256]{2,1,0:T(8,128)S(1)}, f32[1,128,256]{2,1,0:T(8,128)S(1)}, u32[]{:S(2)}, u32[]{:S(2)}) collective-permute-start(f32[1,128,256]{2,1,0:T(8,128)S(1)} %fusion.4), channel_id=1, source_target_pairs={{0,2},{1,3},{2,0},{3,1},{4,6},{5,7},{6,4},{7,5},{8,10},{9,11},{10,... | collective-permute-start | bytes 393224 | tf_op jit(solution)/shard_map/ppermute | solution.py:69
  67.6 4.3 %collective-permute-start.11 = (f32[1,64,256]{2,1,0:T(8,128)S(1)}, f32[1,64,256]{2,1,0:T(8,128)S(1)}, u32[]{:S(2)}, u32[]{:S(2)}) collective-permute-start(f32[1,64,256]{2,1,0:T(8,128)S(1)} %fusion.3), channel_id=1, source_target_pairs={{0,1},{1,0},{2,3},{3,2},{4,5},{5,4},{6,7},{7,6},{8,9},{9,8},{10,11... | collective-permute-start | bytes 196616 | tf_op jit(solution)/shard_map/ppermute | solution.py:69
  71.9 6.2 %collective-permute-start.12 = (f32[1,64,256]{2,1,0:T(8,128)S(1)}, f32[1,64,256]{2,1,0:T(8,128)S(1)}, u32[]{:S(2)}, u32[]{:S(2)}) collective-permute-start(f32[1,64,256]{2,1,0:T(8,128)S(1)} %add.80), channel_id=1, source_target_pairs={{0,2},{1,3},{2,0},{3,1},{4,6},{5,7},{6,4},{7,5},{8,10},{9,11},{10,... | collective-permute-start | bytes 196616 | tf_op jit(solution)/shard_map/ppermute | solution.py:69
  78.2 7.2 %collective-permute-start.20 = (f32[1,192,256]{2,1,0:T(8,128)S(1)}, f32[1,192,256]{2,1,0:T(8,128)S(1)}, u32[]{:S(2)}, u32[]{:S(2)}) collective-permute-start(f32[1,192,256]{2,1,0:T(8,128)S(1)} %pad_maximum_fusion.1.refs_0_), channel_id=1, source_target_pairs={{0,24},{4,28},{8,16},{12,20},{16,8},{20,12},{24,0},{28,4},{1,25},{... | collective-permute-start | bytes 589832 | tf_op jit(solution)/shard_map/ppermute | solution.py:69
  79.7 7.6 %collective-permute-start.19 = (f32[1,192,256]{2,1,0:T(8,128)S(1)}, f32[1,192,256]{2,1,0:T(8,128)S(1)}, u32[]{:S(2)}, u32[]{:S(2)}) collective-permute-start(f32[1,192,256]{2,1,0:T(8,128)S(1)} %pad_maximum_fusion.1.refs_0_), channel_id=1, source_target_pairs={{0,16},{4,20},{8,24},{12,28},{16,0},{20,4},{24,8},{28,12},{1,17},{... | collective-permute-start | bytes 589832 | tf_op jit(solution)/shard_map/ppermute | solution.py:69
  80.5 6.9 %collective-permute-start.18 = (f32[1,192,256]{2,1,0:T(8,128)S(1)}, f32[1,192,256]{2,1,0:T(8,128)S(1)}, u32[]{:S(2)}, u32[]{:S(2)}) collective-permute-start(f32[1,192,256]{2,1,0:T(8,128)S(1)} %pad_maximum_fusion.1.refs_0_), channel_id=1, source_target_pairs={{0,8},{4,12},{8,0},{12,4},{16,24},{20,28},{24,16},{28,20},{1,9},{5... | collective-permute-start | bytes 589832 | tf_op jit(solution)/shard_map/ppermute | solution.py:69
  87.4 7.8 %collective-permute-start.21 = (f32[4,128,256]{2,1,0:T(8,128)S(1)}, f32[4,128,256]{2,1,0:T(8,128)S(1)}, u32[]{:S(2)}, u32[]{:S(2)}) collective-permute-start(f32[4,128,256]{2,1,0:T(8,128)S(1)} %pad_maximum_fusion.own_ref), channel_id=1, source_target_pairs={{0,4},{4,0},{8,12},{12,8},{16,20},{20,16},{24,28},{28,24},{1,5},{5... | collective-permute-start | bytes 1572872 | tf_op jit(solution)/shard_map/ppermute | solution.py:69
  87.6 7.6 %copy-start.7 = (f32[4,256,256]{2,1,0:T(8,128)}, f32[4,256,256]{2,1,0:T(8,128)S(1)}, u32[]{:S(2)}) copy-start(f32[4,256,256]{2,1,0:T(8,128)S(1)} %constant_dynamic-update-slice_fusion.2.refs_2_) | copy-start | bytes 3145732
  87.6 42.3 %collective-permute-start.30 = (f32[4,256,256]{2,1,0:T(8,128)S(1)}, f32[4,256,256]{2,1,0:T(8,128)S(1)}, u32[]{:S(2)}, u32[]{:S(2)}) collective-permute-start(f32[4,256,256]{2,1,0:T(8,128)S(1)} %constant_dynamic-update-slice_fusion.2.refs_2_), channel_id=1, source_target_pairs={{0,4},{4,0},{8,12},{12,8},{16,20},{20,16},{24,28},{28,24},{1,5},{5... | collective-permute-start | bytes 3145736 | tf_op jit(solution)/shard_map/ppermute | solution.py:69
  88.2 7.0 %copy-start = (f32[512,512]{1,0:T(8,128)S(1)}, f32[512,512]{1,0:T(8,128)}, u32[]{:S(2)}) copy-start(f32[512,512]{1,0:T(8,128)} %shard_map.77.z_ref) | copy-start | bytes 3145732
  88.2 16.4 %collective-permute-start.25 = (f32[1,256,256]{2,1,0:T(8,128)S(1)}, f32[1,256,256]{2,1,0:T(8,128)S(1)}, u32[]{:S(2)}, u32[]{:S(2)}) collective-permute-start(f32[1,256,256]{2,1,0:T(8,128)S(1)} %bitcast.12), channel_id=1, source_target_pairs={{0,2},{1,3},{2,0},{3,1},{4,6},{5,7},{6,4},{7,5},{8,10},{9,11},{10,... | collective-permute-start | bytes 786440 | tf_op jit(solution)/shard_map/ppermute | solution.py:69
  97.3 7.0 %collective-permute-start.22 = (f32[1,64,256]{2,1,0:T(8,128)S(1)}, f32[1,64,256]{2,1,0:T(8,128)S(1)}, u32[]{:S(2)}, u32[]{:S(2)}) collective-permute-start(f32[1,64,256]{2,1,0:T(8,128)S(1)} %get-tuple-element.96), channel_id=1, source_target_pairs={{0,8},{4,12},{8,0},{12,4},{16,24},{20,28},{24,16},{28,20},{1,9},{5... | collective-permute-start | bytes 196616 | tf_op jit(solution)/shard_map/ppermute | solution.py:69
  98.8 5.5 %collective-permute-start.23 = (f32[1,64,256]{2,1,0:T(8,128)S(1)}, f32[1,64,256]{2,1,0:T(8,128)S(1)}, u32[]{:S(2)}, u32[]{:S(2)}) collective-permute-start(f32[1,64,256]{2,1,0:T(8,128)S(1)} %get-tuple-element.95), channel_id=1, source_target_pairs={{0,16},{4,20},{8,24},{12,28},{16,0},{20,4},{24,8},{28,12},{1,17},{... | collective-permute-start | bytes 196616 | tf_op jit(solution)/shard_map/ppermute | solution.py:69
  99.4 5.2 %collective-permute-start.24 = (f32[1,64,256]{2,1,0:T(8,128)S(1)}, f32[1,64,256]{2,1,0:T(8,128)S(1)}, u32[]{:S(2)}, u32[]{:S(2)}) collective-permute-start(f32[1,64,256]{2,1,0:T(8,128)S(1)} %get-tuple-element.94), channel_id=1, source_target_pairs={{0,24},{4,28},{8,16},{12,20},{16,8},{20,12},{24,0},{28,4},{1,25},{... | collective-permute-start | bytes 196616 | tf_op jit(solution)/shard_map/ppermute | solution.py:69
  104.6 5.6 %collective-permute-start.26 = (f32[1,64,256]{2,1,0:T(8,128)S(1)}, f32[1,64,256]{2,1,0:T(8,128)S(1)}, u32[]{:S(2)}, u32[]{:S(2)}) collective-permute-start(f32[1,64,256]{2,1,0:T(8,128)S(1)} %fusion.2), channel_id=1, source_target_pairs={{0,1},{1,0},{2,3},{3,2},{4,5},{5,4},{6,7},{7,6},{8,9},{9,8},{10,11... | collective-permute-start | bytes 196616 | tf_op jit(solution)/shard_map/ppermute | solution.py:69
  104.7 5.5 %copy-start.6 = (f32[2,256,256]{2,1,0:T(8,128)}, f32[2,256,256]{2,1,0:T(8,128)S(1)}, u32[]{:S(2)}) copy-start(f32[2,256,256]{2,1,0:T(8,128)S(1)} %constant_dynamic-update-slice_fusion.refs_0_) | copy-start | bytes 1572868
  104.8 25.2 %collective-permute-start.29 = (f32[2,256,256]{2,1,0:T(8,128)S(1)}, f32[2,256,256]{2,1,0:T(8,128)S(1)}, u32[]{:S(2)}, u32[]{:S(2)}) collective-permute-start(f32[2,256,256]{2,1,0:T(8,128)S(1)} %constant_dynamic-update-slice_fusion.refs_0_), channel_id=1, source_target_pairs={{0,1},{1,0},{2,3},{3,2},{4,5},{5,4},{6,7},{7,6},{8,9},{9,8},{10,11... | collective-permute-start | bytes 1572872 | tf_op jit(solution)/shard_map/ppermute | solution.py:69
  110.2 8.5 %collective-permute-start.27 = (f32[1,64,256]{2,1,0:T(8,128)S(1)}, f32[1,64,256]{2,1,0:T(8,128)S(1)}, u32[]{:S(2)}, u32[]{:S(2)}) collective-permute-start(f32[1,64,256]{2,1,0:T(8,128)S(1)} %add.87), channel_id=1, source_target_pairs={{0,2},{1,3},{2,0},{3,1},{4,6},{5,7},{6,4},{7,5},{8,10},{9,11},{10,... | collective-permute-start | bytes 196616 | tf_op jit(solution)/shard_map/ppermute | solution.py:69
  115.8 14.1 %copy-start.1 = (f32[2,256,256]{2,1,0:T(8,128)}, f32[2,256,256]{2,1,0:T(8,128)S(1)}, u32[]{:S(2)}) copy-start(f32[2,256,256]{2,1,0:T(8,128)S(1)} %shard_map.83.own_ref) | copy-start | bytes 1572868
  118.8 4.9 %collective-permute-start.31 = (f32[1,64,256]{2,1,0:T(8,128)S(1)}, f32[1,64,256]{2,1,0:T(8,128)S(1)}, u32[]{:S(2)}, u32[]{:S(2)}) collective-permute-start(f32[1,64,256]{2,1,0:T(8,128)S(1)} %add.88), channel_id=1, source_target_pairs={{0,8},{4,12},{8,0},{12,4},{16,24},{20,28},{24,16},{28,20},{1,9},{5... | collective-permute-start | bytes 196616 | tf_op jit(solution)/shard_map/ppermute | solution.py:69
  120.3 4.3 %collective-permute-start.32 = (f32[1,64,256]{2,1,0:T(8,128)S(1)}, f32[1,64,256]{2,1,0:T(8,128)S(1)}, u32[]{:S(2)}, u32[]{:S(2)}) collective-permute-start(f32[1,64,256]{2,1,0:T(8,128)S(1)} %add.88), channel_id=1, source_target_pairs={{0,16},{4,20},{8,24},{12,28},{16,0},{20,4},{24,8},{28,12},{1,17},{... | collective-permute-start | bytes 196616 | tf_op jit(solution)/shard_map/ppermute | solution.py:69
  120.9 5.2 %collective-permute-start.33 = (f32[1,64,256]{2,1,0:T(8,128)S(1)}, f32[1,64,256]{2,1,0:T(8,128)S(1)}, u32[]{:S(2)}, u32[]{:S(2)}) collective-permute-start(f32[1,64,256]{2,1,0:T(8,128)S(1)} %add.88), channel_id=1, source_target_pairs={{0,24},{4,28},{8,16},{12,20},{16,8},{20,12},{24,0},{28,4},{1,25},{... | collective-permute-start | bytes 196616 | tf_op jit(solution)/shard_map/ppermute | solution.py:69
  123.7 3.9 %collective-permute-start.28 = (f32[2,256,256]{2,1,0:T(8,128)S(1)}, f32[2,256,256]{2,1,0:T(8,128)S(1)}, u32[]{:S(2)}, u32[]{:S(2)}) collective-permute-start(f32[2,256,256]{2,1,0:T(8,128)S(1)} %shard_map.83.own_ref), channel_id=1, source_target_pairs={{0,4},{4,0},{8,12},{12,8},{16,20},{20,16},{24,28},{28,24},{1,5},{5... | collective-permute-start | bytes 1572872 | tf_op jit(solution)/shard_map/ppermute | solution.py:69
  126.1 1.5 %collective-permute-start.34 = (f32[4,64,256]{2,1,0:T(8,128)S(1)}, f32[4,64,256]{2,1,0:T(8,128)S(1)}, u32[]{:S(2)}, u32[]{:S(2)}) collective-permute-start(f32[4,64,256]{2,1,0:T(8,128)S(1)} %constant_dynamic-update-slice_fusion.6.middle_own_ref), channel_id=1, source_target_pairs={{0,4},{4,0},{8,12},{12,8},{16,20},{20,16},{24,28},{28,24},{1,5},{5... | collective-permute-start | bytes 786440 | tf_op jit(solution)/shard_map/ppermute | solution.py:69
  127.6 2.3 %copy-start.2 = (f32[2,256,256]{2,1,0:T(8,128)}, f32[2,256,256]{2,1,0:T(8,128)S(1)}, u32[]{:S(2)}) copy-start(f32[2,256,256]{2,1,0:T(8,128)S(1)} %collective-permute-done.28.other_ref) | copy-start | bytes 1572868
  129.9 1.0 copy-start.8
  130.9 0.8 copy-start.9

commit v7 on v6

--- a/solution.py
+++ b/solution.py
@@ -126,13 +126,14 @@
     return count * width // k
 
 
-def sketch_kernel(spot_ref, window_ref, test_ref, co_ref, left_ref, right_ref, r3_ref, r2_ref, r1_ref, r0_ref, sent_ref, kept_ref, held_ref, test_held_ref, co_held_ref, left_held_ref, right_held_ref, top_ref, rest_ref, co_done_ref, lt_ref, rt_ref, window_sem, sem):
+def sketch_kernel(spot_ref, window_ref, test_ref, co_ref, left_ref, right_ref, r3_ref, r2_ref, r1_ref, r0_ref, sent_ref, kept_ref, held_ref, test_held_ref, co_held_ref, left_held_ref, right_held_ref, top_ref, rest_ref, range_done_ref, co_done_ref, lt_ref, rt_ref, fold_ref, window_sem, sem, range_sem, co_sem, fold_sem):
     core, place, line = spot_ref[0], spot_ref[1], spot_ref[2]
     tile = held_ref.shape[1]
     chips, _, k = kept_ref.shape
     count, cols = co_done_ref.shape
     width = cols // (2 * chips)
     packed = pack_width(count, width, k)
+    extent = lt_ref.shape[0] // chips
     small = [(test_ref, test_held_ref), (co_ref, co_held_ref), (left_ref, left_held_ref), (right_ref, right_held_ref)]
     small = [pltpu.make_async_copy(a, b, sem.at[i]) for i, (a, b) in enumerate(small)]
 
@@ -142,59 +143,80 @@
     small[0].start()
     window_copy(0).start()
     small[1].start()
-    small[2].start()
-    for i in range(1, TILES):
-        window_copy(i).start()
-    small[3].start()
     co_done_ref[...] = jnp.zeros_like(co_done_ref)
     lt_ref[...] = jnp.zeros_like(lt_ref)
     small[0].wait()
+    window_copy(1).start()
+    small[2].start()
+    for i in range(2, TILES):
+        window_copy(i).start()
+    small[3].start()
     top_ref[...], rest_ref[...] = split(test_held_ref[...])
+    range_outs = [pltpu.make_async_copy(range_done_ref.at[i], ref, range_sem.at[i]) for i, ref in enumerate((r3_ref, r2_ref, r1_ref, r0_ref))]
     small[1].wait()
-    small[2].wait()
 
     def step(i, carry):
         window_copy(i).wait()
         rows = split(held_ref[i])
         spot = pl.ds(block_start(line, TILES - 1 - i, tile), tile)
         done = parts_dot(rows, (top_ref[...], rest_ref[...]))
-        co_done_ref[...] += parts_dot(split(co_held_ref[:, spot]), rows)
-        lt_ref[...] += parts_dot(split(left_held_ref[:, spot]), split(done))
-        for block, ref in enumerate((r3_ref, r2_ref, r1_ref, r0_ref)):
+        range_done_ref[i] = done
+        for block, copy in enumerate(range_outs):
             @pl.when(i == block)
             def _():
-                ref[...] = done
-
+                copy.start()
+
+        co_done_ref[...] += parts_dot(split(co_held_ref[:, spot]), rows)
+
+        @pl.when(i == 0)
+        def _():
+            small[2].wait()
+
+        lt_ref[...] += parts_dot(split(left_held_ref[:, spot]), split(done))
         return carry
 
     lax.fori_loop(0, TILES, step, 0)
+    co_outs = []
+    for out_ref, side in ((sent_ref, 1 - core), (kept_ref, core)):
+        for i in range(chips):
+            for j in range(count // packed):
+                start = pl.multiple_of((side * chips + (place ^ i)) * width, width)
+                part = co_done_ref.at[j * packed:(j + 1) * packed, pl.ds(start, width)]
+                co_outs.append(pltpu.make_async_copy(part, out_ref.at[i, :packed, j * width:(j + 1) * width], co_sem.at[len(co_outs)]))
+    for copy in co_outs:
+        copy.start()
     small[3].wait()
     rt_ref[...] = parts_dot(split(right_held_ref[...]), split(co_done_ref[...]), 1, 1)
-    for ref, side in ((sent_ref, 1 - core), (kept_ref, core)):
+    first = core == 0
+    fold_ref[0] = jnp.where(first, rt_ref[...], lt_ref[...])
+    fold_ref[1] = jnp.where(first, lt_ref[...], rt_ref[...])
+    fold_outs = []
+    for side, out_ref in enumerate((sent_ref, kept_ref)):
         for i in range(chips):
-            start = pl.multiple_of((side * chips + (place ^ i)) * width, width)
-            for j in range(count // packed):
-                ref[i, :packed, j * width:(j + 1) * width] = co_done_ref[j * packed:(j + 1) * packed, pl.ds(start, width)]
-    for owner, left_out, right_out in ((0, kept_ref, sent_ref), (1, sent_ref, kept_ref)):
-        @pl.when(core == owner)
-        def _():
-            take_blocks(lt_ref, left_out.at[:, packed:], place)
-            take_blocks(rt_ref, right_out.at[:, packed:], place)
+            part = fold_ref.at[side, pl.ds(block_start(place, i, extent), extent)]
+            fold_outs.append(pltpu.make_async_copy(part, out_ref.at[i, packed:], fold_sem.at[len(fold_outs)]))
+    for copy in fold_outs:
+        copy.start()
+    for copy in range_outs + co_outs + fold_outs:
+        copy.wait()
 
 
 def sketch_terms(spot, chips, window, range_test, co_test, core_left, core_right):
     rows, cols = window.shape
     count, k, s_core = co_test.shape[0], range_test.shape[1], core_left.shape[0]
-    block = pack_width(count, cols // (2 * chips), k) + s_core // chips
+    width = cols // (2 * chips)
+    block = pack_width(count, width, k) + s_core // chips
     return call(
         sketch_kernel, (float_shape(rows // TILES, k),) * 4 + (float_shape(chips, block, k),) * 2,
-        [SCALAR] + [OUTSIDE] * 5, (WHOLE,) * 6,
+        [SCALAR] + [OUTSIDE] * 5, (OUTSIDE,) * 6,
         [
             pltpu.VMEM((TILES, rows // TILES, cols), jnp.float32), pltpu.VMEM((cols, k), jnp.float32), pltpu.VMEM((count, rows), jnp.float32),
             pltpu.VMEM((s_core, rows), jnp.float32), pltpu.VMEM((s_core, cols), jnp.float32),
             pltpu.VMEM((cols, k), jnp.bfloat16), pltpu.VMEM((cols, k), jnp.bfloat16),
-            pltpu.VMEM((count, cols), jnp.float32), pltpu.VMEM((s_core, k), jnp.float32), pltpu.VMEM((s_core, k), jnp.float32),
-            pltpu.SemaphoreType.DMA((TILES,)), pltpu.SemaphoreType.DMA((4,)),
+            pltpu.VMEM((TILES, rows // TILES, k), jnp.float32), pltpu.VMEM((count, cols), jnp.float32),
+            pltpu.VMEM((s_core, k), jnp.float32), pltpu.VMEM((s_core, k), jnp.float32), pltpu.VMEM((2, s_core, k), jnp.float32),
+            pltpu.SemaphoreType.DMA((TILES,)), pltpu.SemaphoreType.DMA((4,)), pltpu.SemaphoreType.DMA((TILES,)),
+            pltpu.SemaphoreType.DMA((2 * cols // width,)), pltpu.SemaphoreType.DMA((2 * chips,)),
         ],
         flops=12 * rows * cols * count, limit=56,
     )(spot, window, range_test, co_test, core_left, core_right)
@@ -426,56 +448,40 @@
 
 
 def basis_kernel(peers, spot_ref, own_ref, other_ref, *refs):
-    range_refs, (co_own_ref, co_other_ref, range_out_ref, co_out_ref, range_held_ref, co_held_ref, range_done_ref, co_done_ref, side_ref, range_sem, co_sem, range_out_sem, co_out_sem) = refs[:peers], refs[peers:]
+    range_refs, (co_own_ref, co_other_ref, range_out_ref, co_out_ref, range_done_ref, co_done_ref, side_ref, range_sem, co_sem) = refs[:peers], refs[peers:]
     core, place, line = spot_ref[0], spot_ref[1], spot_ref[3]
-    lines, rows, _ = range_held_ref.shape
-    cells, _, width = co_held_ref.shape
-    chips = cells // 2
-
-    def range_copy(f):
-        return pltpu.make_async_copy(range_refs[f // (lines // peers)].at[f % (lines // peers)], range_held_ref.at[f], range_sem.at[f])
-
-    def co_copy(f):
-        return pltpu.make_async_copy((co_own_ref, co_other_ref)[f // chips].at[f % chips], co_held_ref.at[f], co_sem.at[f])
-
-    def range_wait(f):
-        pltpu.make_async_copy(range_refs[0].at[0], range_held_ref.at[f], range_sem.at[f]).wait()
-
-    def co_wait(f):
-        pltpu.make_async_copy(co_own_ref.at[0], co_held_ref.at[f], co_sem.at[f]).wait()
+    inner, rows, _ = range_refs[0].shape
+    chips, _, width = co_own_ref.shape
+    first = core == 0
+    side_ref[0], side_ref[1] = split(jnp.where(first, own_ref[0], other_ref[0]))
+    side_ref[2], side_ref[3] = split(jnp.where(first, other_ref[0], own_ref[0]))
 
     def range_out(f):
-        return pltpu.make_async_copy(range_done_ref.at[f], range_out_ref.at[pl.ds(block_start(line, f, rows), rows)], range_out_sem.at[f])
+        return pltpu.make_async_copy(range_done_ref.at[f], range_out_ref.at[pl.ds(block_start(line, f, rows), rows)], range_sem.at[f])
 
     def co_out(f):
         column = jnp.where(f < chips, core, 1 - core) * chips + (place ^ (f % chips))
-        return pltpu.make_async_copy(co_done_ref.at[f], co_out_ref.at[:, pl.ds(pl.multiple_of(column * width, width), width)], co_out_sem.at[f])
-
-    for f in range(lines):
-        range_copy(f).start()
-    for f in range(cells):
-        co_copy(f).start()
-    first = spot_ref[0] == 0
-    side_ref[0], side_ref[1] = split(jnp.where(first, own_ref[0], other_ref[0]))
-    side_ref[2], side_ref[3] = split(jnp.where(first, other_ref[0], own_ref[0]))
-
-    def range_step(f, carry):
-        range_wait(f)
-        range_done_ref[f] = parts_dot(split(range_held_ref[f]), (side_ref[0], side_ref[1]), 1, 1)
-        range_out(f).start()
-        return carry
-
-    def co_step(f, carry):
-        co_wait(f)
-        co_done_ref[f] = parts_dot((side_ref[2], side_ref[3]), split(co_held_ref[f]))
-        co_out(f).start()
-        return carry
-
-    lax.fori_loop(0, lines, range_step, 0)
-    lax.fori_loop(0, cells, co_step, 0)
-    for f in range(lines):
+        return pltpu.make_async_copy(co_done_ref.at[f], co_out_ref.at[:, pl.ds(pl.multiple_of(column * width, width), width)], co_sem.at[f])
+
+    for i, ref in enumerate(range_refs):
+        def range_step(j, carry, i=i, ref=ref):
+            f = i * inner + j
+            range_done_ref[f] = parts_dot(split(ref[j]), (side_ref[0], side_ref[1]), 1, 1)
+            range_out(f).start()
+            return carry
+
+        lax.fori_loop(0, inner, range_step, 0)
+    for i, ref in enumerate((co_own_ref, co_other_ref)):
+        def co_step(j, carry, i=i, ref=ref):
+            f = i * chips + j
+            co_done_ref[f] = parts_dot((side_ref[2], side_ref[3]), split(ref[j]))
+            co_out(f).start()
+            return carry
+
+        lax.fori_loop(0, chips, co_step, 0)
+    for f in range(peers * inner):
         range_out(f).wait()
-    for f in range(cells):
+    for f in range(2 * chips):
         co_out(f).wait()
 
 
@@ -483,13 +489,14 @@
     inner, rows, k = ranges[0].shape
     chips, count, width = co_own.shape
     lines, cells = inner * len(ranges), 2 * chips
-    range_held, co_held = pltpu.VMEM((lines, rows, k), jnp.float32), pltpu.VMEM((cells, count, width), jnp.float32)
-    line_sem, cell_sem = pltpu.SemaphoreType.DMA((lines,)), pltpu.SemaphoreType.DMA((cells,))
     return call(
         functools.partial(basis_kernel, len(ranges)), (float_shape(lines * rows, k), float_shape(count, cells * width)),
-        [SCALAR, WHOLE, WHOLE] + [OUTSIDE] * (len(ranges) + 2), (OUTSIDE, OUTSIDE),
-        [range_held, co_held, range_held, co_held, pltpu.VMEM((4, k, k), jnp.bfloat16), line_sem, cell_sem, line_sem, cell_sem],
-        flops=18 * lines * rows * k * k, limit=56,
+        [SCALAR] + [WHOLE] * (len(ranges) + 4), (OUTSIDE, OUTSIDE),
+        [
+            pltpu.VMEM((lines, rows, k), jnp.float32), pltpu.VMEM((cells, count, width), jnp.float32), pltpu.VMEM((4, k, k), jnp.bfloat16),
+            pltpu.SemaphoreType.DMA((lines,)), pltpu.SemaphoreType.DMA((cells,)),
+        ],
+        flops=18 * lines * rows * k * k, limit=24,
     )(spot, own, other, *ranges, co_own, co_other)
 
 
@@ -526,12 +533,12 @@
 
     r3, r2, r1, r0, sent, kept = sketch_terms(spot, chips, window, range_test, co_test, core_left, core_right)
     far = swap(r3, "tm", 1)
+    near = swap(r2, "tm", 1)
     pack = kept + core_swap(sent)
-    handed = r1 + after(far, pack)
-    near = swap(after(r2, handed), "tm", 1)
-    sketch_z = core_terms(after(spot, pack, handed), window, core_right, core_left)
+    sketch_z = core_terms(after(spot, pack), window, core_right, core_left)
+    handed = swap(r1 + after(far, pack), "tm", 2)
     pack = scatter_sum(pack, groups)[0]
-    handed, near, pack, sketch_z = lax.optimization_barrier((swap(handed, "tm", 2), near, pack, sketch_z))
+    handed, near, pack, sketch_z = lax.optimization_barrier((handed, near, pack, sketch_z))
     range_piece = (r0 + near + handed).reshape(lax.axis_size("tm") // 4, -1, r0.shape[1])
     if lines[2:]:
         rest = place_of(lines[2:], line)
@@ -560,17 +567,19 @@
     middle = scatter_sum(middle, groups)
     state = factor_next((1, 2), *state)
     state, middle, range_parts = lax.optimization_barrier((state, middle, range_parts))
-    range_all = gather(jnp.concatenate(range_parts), lines[:1])
+    range_all = jnp.concatenate(range_parts)
     for bit in range(bits_of("tm")):
         middle = middle + swap(middle, "tm", 1 << bit)
         if bit == 0:
             state = factor_next((2, state[1].shape[0] // BASE - 1), *state)
-            state, middle = lax.optimization_barrier((state, middle))
+            state, middle, range_all = lax.optimization_barrier((state, middle, range_all))
+    range_all = gather(range_all, lines[:1])
     own = factor_end(*state)
     own, middle = lax.optimization_barrier((own, middle))
     other = core_swap(own)
-    middle = jnp.concatenate(gather(middle, groups))
     range_basis, co_basis = bases(spot, own, other, range_all, co_own, co_other)
+    middle, range_basis, co_basis = lax.optimization_barrier((gather(middle, groups), range_basis, co_basis))
+    middle = jnp.concatenate(middle)
     core_out = finish(spot, own, other, middle, core_swap(middle), math.sqrt(rows_total * cols_total))
     return (range_basis, co_basis, core_out)
 

time: 139 us -> 126 us (0.906)
  waiting for transfers between devices: 33.6 us -> 23.6 us
  Pallas kernels: 59.6 us -> 56 us
  starting transfers between devices: 39.4 us -> 41.7 us
  local copies, waits for them, and re-layouts: 2.07 us -> 0.42 us
    ppermute x35, waiting for transfers between devices: 33.6 us -> 23.6 us  [swap(): lax.ppermute(values, axis, [(i, i ^ mask) for i in range(lax.axis_size(ax...]
    ppermute x35, starting transfers between devices: 39.4 us -> 41.7 us  [swap(): lax.ppermute(values, axis, [(i, i ^ mask) for i in range(lax.axis_size(ax...]
    pallas_call x1, Pallas kernels: 6.78 us -> 4.87 us  [bases(): call(functools.partial(basis_kernel, len(ranges)), (float_shape(lines * r...]
    pallas_call x1, Pallas kernels: 17.3 us -> 15.5 us  [sketch_terms(): call(sketch_kernel, (float_shape(rows // TILES, k),) * 4 + (float_shape(c...]
    unnamed x29 -> x14, local copies, waits for them, and re-layouts: 1.88 us -> 0.25 us
  transfers between devices with their start and end apart: 35 -> 35, of which waited for: 18 -> 13; matrix products, arithmetic and copies ran while one was open for 2% -> 2% of each run, Pallas kernels for 25% -> 29%
where the time goes in v7:
time: 126 us; the launch traced here: 125 us
  Pallas kernels  56 us (44%)
  starting transfers between devices  41.7 us (33%)
  waiting for transfers between devices  23.6 us (19%)
  other arithmetic  2.64 us (2%)
    ppermute x35, starting transfers between devices, swap(): lax.ppermute(values, axis, [(i, i ^ mask) for i in range(lax.axis_size(ax...  41.7 us
    ppermute x35, waiting for transfers between devices, swap(): lax.ppermute(values, axis, [(i, i ^ mask) for i in range(lax.axis_size(ax...  23.6 us
    pallas_call x1, Pallas kernels, sketch_terms(): call(sketch_kernel, (float_shape(rows // TILES, k),) * 4 + (float_shape(c...  15.5 us
    pallas_call x1, Pallas kernels, core_terms(): call(core_kernel, float_shape(s_core, s_core), [SCALAR] + [OUTSIDE] * 3,...  13.4 us
    pallas_call x2, Pallas kernels, factor_next(): call(functools.partial(factor_next_kernel, steps), (float_shape(2, n, n),...  6.85 us
    pallas_call x1, Pallas kernels, factor_start(): call(functools.partial(factor_start_kernel, (0, 1), len(parts)), (float_s...  5.16 us
    pallas_call x1, Pallas kernels, bases(): call(functools.partial(basis_kernel, len(ranges)), (float_shape(lines * r...  4.87 us
    pallas_call x1, Pallas kernels, factor_end(): call(functools.partial(factor_end_kernel, (n // BASE - 1, n // BASE)), fl...  4.38 us
  transfers between devices with their start and end apart: 35, of which 13 were waited for; matrix products, arithmetic and copies ran while one was open for 2% of the time, Pallas kernels for 29%

profile of v7, /device:TPU:0, one launch (start us, length us, event | category | flops | bytes accessed | tf_op | source)
XLA Modules:
  0.0 125.5 jit_solution(15986979953730243389)
XLA Ops:
  0.6 0.6 pad_add_fusion.spot_ref
  1.2 15.5 %shard_map.76 = (f32[256,256]{1,0:T(8,128)}, f32[256,256]{1,0:T(8,128)}, f32[256,256]{1,0:T(8,128)}, f32[256,256]{1,0:T(8,128)}, f32[4,384,256]{2,1,0:T(8,128)}, /*index=5*/f32[4,384,256]{2,1,0:T(8,128)}) custom-call(s32[4]{0:T(128)} %pad_add_fusion.spot_ref, f32[1024,2048]{1,0:T(8,128)} %window_ref.3, f32[2048,256]{1,0:T(8,128)} %test_ref.1, ...), custom_call_target="tpu_custom_call" | custom-call | flops 6442450944 | bytes 4194304 | tf_op jit(solution)/shard_map/pallas_call | solution.py:209
  16.8 0.5 collective-permute-start.1
  17.3 2.6 %collective-permute-start = (f32[256,256]{1,0:T(8,128)}, f32[256,256]{1,0:T(8,128)S(1)}, u32[]{:S(2)}, u32[]{:S(2)}) collective-permute-start(f32[256,256]{1,0:T(8,128)} %get-tuple-element.54), channel_id=1, source_target_pairs={{0,1},{1,0},{2,3},{3,2},{4,5},{5,4},{6,7},{7,6},{8,9},{9,8},{10,11... | collective-permute-start | bytes 786440 | tf_op jit(solution)/shard_map/ppermute | solution.py:69
  19.9 0.1 collective-permute-start.3
  20.0 0.5 collective-permute-done.1
  20.5 1.6 %add.69 = f32[4,384,256]{2,1,0:T(8,128)S(1)} add(f32[4,384,256]{2,1,0:T(8,128)} %get-tuple-element.55, f32[4,384,256]{2,1,0:T(8,128)S(1)} %collective-permute-done.1) | non-fusion elementwise | flops 393216 | bytes 4718592 | tf_op jit(solution)/shard_map/add | solution.py:537
  22.2 0.1 fusion.5
  22.3 2.9 %collective-permute-start.4 = (f32[1,384,256]{2,1,0:T(8,128)S(1)}, f32[1,384,256]{2,1,0:T(8,128)S(1)}, u32[]{:S(2)}, u32[]{:S(2)}) collective-permute-start(f32[1,384,256]{2,1,0:T(8,128)S(1)} %get-tuple-element.103), channel_id=1, source_target_pairs={{0,8},{4,12},{8,0},{12,4},{16,24},{20,28},{24,16},{28,20},{1,9},{5... | collective-permute-start | bytes 1179656 | tf_op jit(solution)/shard_map/ppermute | solution.py:69
  25.2 1.5 %collective-permute-start.5 = (f32[1,384,256]{2,1,0:T(8,128)S(1)}, f32[1,384,256]{2,1,0:T(8,128)S(1)}, u32[]{:S(2)}, u32[]{:S(2)}) collective-permute-start(f32[1,384,256]{2,1,0:T(8,128)S(1)} %get-tuple-element.102), channel_id=1, source_target_pairs={{0,16},{4,20},{8,24},{12,28},{16,0},{20,4},{24,8},{28,12},{1,17},{... | collective-permute-start | bytes 1179656 | tf_op jit(solution)/shard_map/ppermute | solution.py:69
  26.7 0.0 collective-permute-start.6
  26.7 0.6 collective-permute-done
  27.4 3.0 %collective-permute-start.2 = (f32[256,256]{1,0:T(8,128)S(1)}, f32[256,256]{1,0:T(8,128)S(1)}, u32[]{:S(2)}, u32[]{:S(2)}) collective-permute-start(f32[256,256]{1,0:T(8,128)S(1)} %add.70), channel_id=1, source_target_pairs={{0,2},{1,3},{2,0},{3,1},{4,6},{5,7},{6,4},{7,5},{8,10},{9,11},{10,... | collective-permute-start | bytes 786440 | tf_op jit(solution)/shard_map/ppermute | solution.py:69
  30.4 13.4 %shard_map.77.z_ref = f32[512,512]{1,0:T(8,128)} custom-call(s32[4]{0:T(128)} %pad_add_fusion.spot_ref, f32[1024,2048]{1,0:T(8,128)} %window_ref.3, f32[512,2048]{1,0:T(8,128)} %right_ref.3, f32[512,1024]{1,0:T(8,128)} %left_ref.3), custom_call_target="tpu_custom_call" | custom-call | flops 9663676416 | bytes 4194304 | tf_op jit(solution)/shard_map/pallas_call | solution.py:264
  43.8 0.6 collective-permute-done.5
  44.5 0.1 fusion.1
  44.6 0.2 copy-done.2
  44.8 0.1 slice_bitcast_fusion.1
  44.9 1.4 %shard_map.78 = (f32[4,64,256]{2,1,0:T(8,128)S(1)}, f32[4,64,256]{2,1,0:T(8,128)S(1)}) custom-call(s32[4]{0:T(128)S(1)} %copy-done.1, f32[256,256]{1,0:T(8,128)S(1)} %get-tuple-element.112.range_ref, f32[256,256]{1,0:T(8,128)S(1)} %get-tuple-element.105.co_ref), custom_call_target="tpu_custom_call" | custom-call | flops 402653184 | bytes 4194304 | tf_op jit(solution)/shard_map/pallas_call | solution.py:288
  46.3 0.1 collective-permute-start.7
  46.3 1.5 %collective-permute-done.7 = f32[4,64,256]{2,1,0:T(8,128)S(1)} collective-permute-done((f32[4,64,256]{2,1,0:T(8,128)S(1)}, f32[4,64,256]{2,1,0:T(8,128)S(1)}, u32[]{:S(2)}, u32[]{:S(2)}) %collective-permute-start.7) | collective-permute-done | bytes 262176 | tf_op jit(solution)/shard_map/ppermute | solution.py:69
  47.9 2.5 %collective-permute-start.10 = (f32[1,64,256]{2,1,0:T(8,128)S(1)}, f32[1,64,256]{2,1,0:T(8,128)S(1)}, u32[]{:S(2)}, u32[]{:S(2)}) collective-permute-start(f32[1,64,256]{2,1,0:T(8,128)S(1)} %get-tuple-element.109), channel_id=1, source_target_pairs={{0,24},{4,28},{8,16},{12,20},{16,8},{20,12},{24,0},{28,4},{1,25},{... | collective-permute-start | bytes 196616 | tf_op jit(solution)/shard_map/ppermute | solution.py:69
  50.4 0.5 collective-permute-start.8
  51.0 0.5 collective-permute-start.9
  51.5 1.6 %collective-permute-start.16 = (f32[1,128,256]{2,1,0:T(8,128)S(1)}, f32[1,128,256]{2,1,0:T(8,128)S(1)}, u32[]{:S(2)}, u32[]{:S(2)}) collective-permute-start(f32[1,128,256]{2,1,0:T(8,128)S(1)} %slice_bitcast_fusion), channel_id=1, source_target_pairs={{0,1},{1,0},{2,3},{3,2},{4,5},{5,4},{6,7},{7,6},{8,9},{9,8},{10,11... | collective-permute-start | bytes 393224 | tf_op jit(solution)/shard_map/ppermute | solution.py:69
  53.1 0.4 collective-permute-done.10
  53.6 1.1 collective-permute-done.8
  54.7 0.5 collective-permute-done.9
  55.3 1.6 %collective-permute-start.13 = (f32[1,256,256]{2,1,0:T(8,128)S(1)}, f32[1,256,256]{2,1,0:T(8,128)S(1)}, u32[]{:S(2)}, u32[]{:S(2)}) collective-permute-start(f32[1,256,256]{2,1,0:T(8,128)S(1)} %get-tuple-element.89), channel_id=1, source_target_pairs={{0,8},{4,12},{8,0},{12,4},{16,24},{20,28},{24,16},{28,20},{1,9},{5... | collective-permute-start | bytes 786440 | tf_op jit(solution)/shard_map/ppermute | solution.py:69
  56.8 0.7 collective-permute-start.14
  57.5 1.3 %collective-permute-start.15 = (f32[1,256,256]{2,1,0:T(8,128)S(1)}, f32[1,256,256]{2,1,0:T(8,128)S(1)}, u32[]{:S(2)}, u32[]{:S(2)}) collective-permute-start(f32[1,256,256]{2,1,0:T(8,128)S(1)} %get-tuple-element.89), channel_id=1, source_target_pairs={{0,24},{4,28},{8,16},{12,20},{16,8},{20,12},{24,0},{28,4},{1,25},{... | collective-permute-start | bytes 786440 | tf_op jit(solution)/shard_map/ppermute | solution.py:69
  58.8 2.5 %collective-permute-start.17 = (f32[1,128,256]{2,1,0:T(8,128)S(1)}, f32[1,128,256]{2,1,0:T(8,128)S(1)}, u32[]{:S(2)}, u32[]{:S(2)}) collective-permute-start(f32[1,128,256]{2,1,0:T(8,128)S(1)} %fusion.4), channel_id=1, source_target_pairs={{0,2},{1,3},{2,0},{3,1},{4,6},{5,7},{6,4},{7,5},{8,10},{9,11},{10,... | collective-permute-start | bytes 393224 | tf_op jit(solution)/shard_map/ppermute | solution.py:69
  61.4 1.6 %collective-permute-start.11 = (f32[1,64,256]{2,1,0:T(8,128)S(1)}, f32[1,64,256]{2,1,0:T(8,128)S(1)}, u32[]{:S(2)}, u32[]{:S(2)}) collective-permute-start(f32[1,64,256]{2,1,0:T(8,128)S(1)} %fusion.3), channel_id=1, source_target_pairs={{0,1},{1,0},{2,3},{3,2},{4,5},{5,4},{6,7},{7,6},{8,9},{9,8},{10,11... | collective-permute-start | bytes 196616 | tf_op jit(solution)/shard_map/ppermute | solution.py:69
  62.9 2.7 %collective-permute-done.11 = f32[1,64,256]{2,1,0:T(8,128)S(1)} collective-permute-done((f32[1,64,256]{2,1,0:T(8,128)S(1)}, f32[1,64,256]{2,1,0:T(8,128)S(1)}, u32[]{:S(2)}, u32[]{:S(2)}) %collective-permute-start.11) | collective-permute-done | bytes 65568 | tf_op jit(solution)/shard_map/ppermute | solution.py:69
  65.6 1.5 %collective-permute-start.12 = (f32[1,64,256]{2,1,0:T(8,128)S(1)}, f32[1,64,256]{2,1,0:T(8,128)S(1)}, u32[]{:S(2)}, u32[]{:S(2)}) collective-permute-start(f32[1,64,256]{2,1,0:T(8,128)S(1)} %add.80), channel_id=1, source_target_pairs={{0,2},{1,3},{2,0},{3,1},{4,6},{5,7},{6,4},{7,5},{8,10},{9,11},{10,... | collective-permute-start | bytes 196616 | tf_op jit(solution)/shard_map/ppermute | solution.py:69
  67.2 3.7 %collective-permute-done.12 = f32[1,64,256]{2,1,0:T(8,128)S(1)} collective-permute-done((f32[1,64,256]{2,1,0:T(8,128)S(1)}, f32[1,64,256]{2,1,0:T(8,128)S(1)}, u32[]{:S(2)}, u32[]{:S(2)}) %collective-permute-start.12) | collective-permute-done | bytes 65568 | tf_op jit(solution)/shard_map/ppermute | solution.py:69
  70.9 1.8 %collective-permute-start.18 = (f32[1,192,256]{2,1,0:T(8,128)S(1)}, f32[1,192,256]{2,1,0:T(8,128)S(1)}, u32[]{:S(2)}, u32[]{:S(2)}) collective-permute-start(f32[1,192,256]{2,1,0:T(8,128)S(1)} %pad_maximum_fusion.2.refs_0_), channel_id=1, source_target_pairs={{0,8},{4,12},{8,0},{12,4},{16,24},{20,28},{24,16},{28,20},{1,9},{5... | collective-permute-start | bytes 589832 | tf_op jit(solution)/shard_map/ppermute | solution.py:69
  72.8 0.0 collective-permute-start.19
  72.8 1.7 %collective-permute-start.20 = (f32[1,192,256]{2,1,0:T(8,128)S(1)}, f32[1,192,256]{2,1,0:T(8,128)S(1)}, u32[]{:S(2)}, u32[]{:S(2)}) collective-permute-start(f32[1,192,256]{2,1,0:T(8,128)S(1)} %pad_maximum_fusion.2.refs_0_), channel_id=1, source_target_pairs={{0,24},{4,28},{8,16},{12,20},{16,8},{20,12},{24,0},{28,4},{1,25},{... | collective-permute-start | bytes 589832 | tf_op jit(solution)/shard_map/ppermute | solution.py:69
  74.5 2.7 %collective-permute-done.18.refs_1_ = f32[1,192,256]{2,1,0:T(8,128)S(1)} collective-permute-done((f32[1,192,256]{2,1,0:T(8,128)S(1)}, f32[1,192,256]{2,1,0:T(8,128)S(1)}, u32[]{:S(2)}, u32[]{:S(2)}) %collective-permute-start.18) | collective-permute-done | bytes 196640 | tf_op jit(solution)/shard_map/ppermute | solution.py:69
  77.1 3.4 %collective-permute-done.19.refs_2_ = f32[1,192,256]{2,1,0:T(8,128)S(1)} collective-permute-done((f32[1,192,256]{2,1,0:T(8,128)S(1)}, f32[1,192,256]{2,1,0:T(8,128)S(1)}, u32[]{:S(2)}, u32[]{:S(2)}) %collective-permute-start.19) | collective-permute-done | bytes 196640 | tf_op jit(solution)/shard_map/ppermute | solution.py:69
  80.6 0.1 collective-permute-start.21
  80.8 0.6 collective-permute-start.33
  81.4 1.2 collective-permute-start.25
  82.6 5.2 %shard_map.79 = (f32[2,256,256]{2,1,0:T(8,128)S(1)}, f32[256,256]{1,0:T(8,128)S(1)}) custom-call(s32[4]{0:T(128)S(1)} %copy-done.1, f32[1,192,256]{2,1,0:T(8,128)S(1)} %pad_maximum_fusion.2.refs_0_, f32[1,192,256]{2,1,0:T(8,128)S(1)} %collective-permute-done.18.refs_1_, f32[1,192,256]{2,1,0:T(8,128)S(1)} %collective-permute-done.19.refs_2_, ...), custom_call_target="tpu_custom_call" | custom-call | flops 1677721600 | bytes 4194304 | tf_op jit(solution)/shard_map/pallas_call | solution.py:429
  87.8 2.1 %shard_map.81 = f32[4,64,256]{2,1,0:T(8,128)S(1)} custom-call(s32[4]{0:T(128)S(1)} %copy-done.1, f32[512,512]{1,0:T(8,128)S(1)} %copy-done, f32[4,128,256]{2,1,0:T(8,128)S(1)} %pad_maximum_fusion.own_ref, f32[4,128,256]{2,1,0:T(8,128)S(1)} %collective-permute-done.21.other_ref), custom_call_target="tpu_custom_call" | custom-call | flops 402653184 | bytes 4194304 | tf_op jit(solution)/shard_map/pallas_call | solution.py:308
  89.9 0.7 collective-permute-start.22
  90.6 0.8 collective-permute-start.23
  91.4 2.1 %collective-permute-start.24 = (f32[1,64,256]{2,1,0:T(8,128)S(1)}, f32[1,64,256]{2,1,0:T(8,128)S(1)}, u32[]{:S(2)}, u32[]{:S(2)}) collective-permute-start(f32[1,64,256]{2,1,0:T(8,128)S(1)} %get-tuple-element.106), channel_id=1, source_target_pairs={{0,24},{4,28},{8,16},{12,20},{16,8},{20,12},{24,0},{28,4},{1,25},{... | collective-permute-start | bytes 196616 | tf_op jit(solution)/shard_map/ppermute | solution.py:69
  93.4 3.5 %shard_map.80 = (f32[2,256,256]{2,1,0:T(8,128)S(1)}, f32[256,256]{1,0:T(8,128)S(1)}) custom-call(f32[2,256,256]{2,1,0:T(8,128)S(1)} %get-tuple-element.69.begun_ref, f32[256,256]{1,0:T(8,128)S(1)} %get-tuple-element.70.begun_upper_ref), custom_call_target="tpu_custom_call" | custom-call | flops 1677721600 | bytes 4194304 | tf_op jit(solution)/shard_map/pallas_call | solution.py:437
  97.0 1.7 %collective-permute-start.26 = (f32[1,64,256]{2,1,0:T(8,128)S(1)}, f32[1,64,256]{2,1,0:T(8,128)S(1)}, u32[]{:S(2)}, u32[]{:S(2)}) collective-permute-start(f32[1,64,256]{2,1,0:T(8,128)S(1)} %fusion.2), channel_id=1, source_target_pairs={{0,1},{1,0},{2,3},{3,2},{4,5},{5,4},{6,7},{7,6},{8,9},{9,8},{10,11... | collective-permute-start | bytes 196616 | tf_op jit(solution)/shard_map/ppermute | solution.py:69
  98.6 3.4 %shard_map.82 = (f32[2,256,256]{2,1,0:T(8,128)S(1)}, f32[256,256]{1,0:T(8,128)S(1)}) custom-call(f32[2,256,256]{2,1,0:T(8,128)S(1)} %get-tuple-element.76.begun_ref, f32[256,256]{1,0:T(8,128)S(1)} %get-tuple-element.77.begun_upper_ref), custom_call_target="tpu_custom_call" | custom-call | flops 1677721600 | bytes 4194304 | tf_op jit(solution)/shard_map/pallas_call | solution.py:437
  102.1 1.2 collective-permute-start.27
  103.3 1.0 collective-permute-start.32
  104.3 4.4 %shard_map.83.own_ref = f32[2,256,256]{2,1,0:T(8,128)S(1)} custom-call(f32[2,256,256]{2,1,0:T(8,128)S(1)} %get-tuple-element.83.begun_ref, f32[256,256]{1,0:T(8,128)S(1)} %get-tuple-element.84.begun_upper_ref), custom_call_target="tpu_custom_call" | custom-call | flops 1677721600 | bytes 4194304 | tf_op jit(solution)/shard_map/pallas_call | solution.py:444
  108.7 0.1 collective-permute-start.31
  108.8 1.0 collective-permute-start.28
  109.8 1.2 collective-permute-start.29
  111.0 1.3 %collective-permute-start.30 = (f32[1,64,256]{2,1,0:T(8,128)S(1)}, f32[1,64,256]{2,1,0:T(8,128)S(1)}, u32[]{:S(2)}, u32[]{:S(2)}) collective-permute-start(f32[1,64,256]{2,1,0:T(8,128)S(1)} %add.88), channel_id=1, source_target_pairs={{0,24},{4,28},{8,16},{12,20},{16,8},{20,12},{24,0},{28,4},{1,25},{... | collective-permute-start | bytes 196616 | tf_op jit(solution)/shard_map/ppermute | solution.py:69
  112.3 4.3 %collective-permute-done.32.refs_1_ = f32[2,256,256]{2,1,0:T(8,128)S(1)} collective-permute-done((f32[2,256,256]{2,1,0:T(8,128)S(1)}, f32[2,256,256]{2,1,0:T(8,128)S(1)}, u32[]{:S(2)}, u32[]{:S(2)}) %collective-permute-start.32) | collective-permute-done | bytes 524320 | tf_op jit(solution)/shard_map/ppermute | solution.py:69
  116.6 4.9 %shard_map.84 = (f32[1024,256]{1,0:T(8,128)}, f32[256,2048]{1,0:T(8,128)}) custom-call(s32[4]{0:T(128)S(1)} %copy-done.1, f32[2,256,256]{2,1,0:T(8,128)S(1)} %shard_map.83.own_ref, f32[2,256,256]{2,1,0:T(8,128)S(1)} %collective-permute-done.31.other_ref, f32[2,256,256]{2,1,0:T(8,128)S(1)} %pad_maximum_fusion.1.refs_0_, ...), custom_call_target="tpu_custom_call" | custom-call | flops 1207959552 | bytes 4194304 | tf_op jit(solution)/shard_map/pallas_call | solution.py:492
  121.6 0.1 collective-permute-start.34
  121.7 1.5 %collective-permute-done.34.middle_other_ref = f32[4,64,256]{2,1,0:T(8,128)S(1)} collective-permute-done((f32[4,64,256]{2,1,0:T(8,128)S(1)}, f32[4,64,256]{2,1,0:T(8,128)S(1)}, u32[]{:S(2)}, u32[]{:S(2)}) %collective-permute-start.34) | collective-permute-done | bytes 262176 | tf_op jit(solution)/shard_map/ppermute | solution.py:69
  123.2 2.3 %shard_map.85 = f32[256,256]{1,0:T(8,128)} custom-call(s32[4]{0:T(128)S(1)} %copy-done.1, f32[2,256,256]{2,1,0:T(8,128)S(1)} %shard_map.83.own_ref, f32[2,256,256]{2,1,0:T(8,128)S(1)} %collective-permute-done.31.other_ref, f32[4,64,256]{2,1,0:T(8,128)S(1)} %constant_dynamic-update-slice_fusion.4.middle_own_ref, ...), custom_call_target="tpu_custom_call" | custom-call | flops 402653184 | bytes 4194304 | tf_op jit(solution)/shard_map/pallas_call | solution.py:515
  (56 shorter events, 0.5 us)
Async XLA Ops:
  16.8 3.8 %collective-permute-start.1 = (f32[4,384,256]{2,1,0:T(8,128)}, f32[4,384,256]{2,1,0:T(8,128)S(1)}, u32[]{:S(2)}, u32[]{:S(2)}) collective-permute-start(f32[4,384,256]{2,1,0:T(8,128)} %get-tuple-element.56), channel_id=1, source_target_pairs={{0,4},{4,0},{8,12},{12,8},{16,20},{20,16},{24,28},{28,24},{1,5},{5... | collective-permute-start | bytes 4718600 | tf_op jit(solution)/shard_map/ppermute | solution.py:69
  17.3 10.0 %collective-permute-start = (f32[256,256]{1,0:T(8,128)}, f32[256,256]{1,0:T(8,128)S(1)}, u32[]{:S(2)}, u32[]{:S(2)}) collective-permute-start(f32[256,256]{1,0:T(8,128)} %get-tuple-element.54), channel_id=1, source_target_pairs={{0,1},{1,0},{2,3},{3,2},{4,5},{5,4},{6,7},{7,6},{8,9},{9,8},{10,11... | collective-permute-start | bytes 786440 | tf_op jit(solution)/shard_map/ppermute | solution.py:69
  19.9 24.7 %collective-permute-start.3 = (f32[256,256]{1,0:T(8,128)}, f32[256,256]{1,0:T(8,128)S(1)}, u32[]{:S(2)}, u32[]{:S(2)}) collective-permute-start(f32[256,256]{1,0:T(8,128)} %get-tuple-element.58), channel_id=1, source_target_pairs={{0,1},{1,0},{2,3},{3,2},{4,5},{5,4},{6,7},{7,6},{8,9},{9,8},{10,11... | collective-permute-start | bytes 786440 | tf_op jit(solution)/shard_map/ppermute | solution.py:69
  22.2 5.2 %copy-start.3 = (f32[256,256]{1,0:T(8,128)S(1)}, f32[256,256]{1,0:T(8,128)}, u32[]{:S(2)}) copy-start(f32[256,256]{1,0:T(8,128)} %get-tuple-element.53) | copy-start | bytes 786436
  22.3 21.6 %collective-permute-start.4 = (f32[1,384,256]{2,1,0:T(8,128)S(1)}, f32[1,384,256]{2,1,0:T(8,128)S(1)}, u32[]{:S(2)}, u32[]{:S(2)}) collective-permute-start(f32[1,384,256]{2,1,0:T(8,128)S(1)} %get-tuple-element.103), channel_id=1, source_target_pairs={{0,8},{4,12},{8,0},{12,4},{16,24},{20,28},{24,16},{28,20},{1,9},{5... | collective-permute-start | bytes 1179656 | tf_op jit(solution)/shard_map/ppermute | solution.py:69
  25.2 19.3 %collective-permute-start.5 = (f32[1,384,256]{2,1,0:T(8,128)S(1)}, f32[1,384,256]{2,1,0:T(8,128)S(1)}, u32[]{:S(2)}, u32[]{:S(2)}) collective-permute-start(f32[1,384,256]{2,1,0:T(8,128)S(1)} %get-tuple-element.102), channel_id=1, source_target_pairs={{0,16},{4,20},{8,24},{12,28},{16,0},{20,4},{24,8},{28,12},{1,17},{... | collective-permute-start | bytes 1179656 | tf_op jit(solution)/shard_map/ppermute | solution.py:69
  26.7 17.8 %collective-permute-start.6 = (f32[1,384,256]{2,1,0:T(8,128)S(1)}, f32[1,384,256]{2,1,0:T(8,128)S(1)}, u32[]{:S(2)}, u32[]{:S(2)}) collective-permute-start(f32[1,384,256]{2,1,0:T(8,128)S(1)} %get-tuple-element.101), channel_id=1, source_target_pairs={{0,24},{4,28},{8,16},{12,20},{16,8},{20,12},{24,0},{28,4},{1,25},{... | collective-permute-start | bytes 1179656 | tf_op jit(solution)/shard_map/ppermute | solution.py:69
  27.4 17.3 %collective-permute-start.2 = (f32[256,256]{1,0:T(8,128)S(1)}, f32[256,256]{1,0:T(8,128)S(1)}, u32[]{:S(2)}, u32[]{:S(2)}) collective-permute-start(f32[256,256]{1,0:T(8,128)S(1)} %add.70), channel_id=1, source_target_pairs={{0,2},{1,3},{2,0},{3,1},{4,6},{5,7},{6,4},{7,5},{8,10},{9,11},{10,... | collective-permute-start | bytes 786440 | tf_op jit(solution)/shard_map/ppermute | solution.py:69
  43.8 1.0 copy-start.2
  43.8 1.0 copy-start.1
  46.3 1.6 %collective-permute-start.7 = (f32[4,64,256]{2,1,0:T(8,128)S(1)}, f32[4,64,256]{2,1,0:T(8,128)S(1)}, u32[]{:S(2)}, u32[]{:S(2)}) collective-permute-start(f32[4,64,256]{2,1,0:T(8,128)S(1)} %get-tuple-element.64), channel_id=1, source_target_pairs={{0,4},{4,0},{8,12},{12,8},{16,20},{20,16},{24,28},{28,24},{1,5},{5... | collective-permute-start | bytes 786440 | tf_op jit(solution)/shard_map/ppermute | solution.py:69
  47.9 5.6 %collective-permute-start.10 = (f32[1,64,256]{2,1,0:T(8,128)S(1)}, f32[1,64,256]{2,1,0:T(8,128)S(1)}, u32[]{:S(2)}, u32[]{:S(2)}) collective-permute-start(f32[1,64,256]{2,1,0:T(8,128)S(1)} %get-tuple-element.109), channel_id=1, source_target_pairs={{0,24},{4,28},{8,16},{12,20},{16,8},{20,12},{24,0},{28,4},{1,25},{... | collective-permute-start | bytes 196616 | tf_op jit(solution)/shard_map/ppermute | solution.py:69
  50.4 4.3 %collective-permute-start.8 = (f32[1,64,256]{2,1,0:T(8,128)S(1)}, f32[1,64,256]{2,1,0:T(8,128)S(1)}, u32[]{:S(2)}, u32[]{:S(2)}) collective-permute-start(f32[1,64,256]{2,1,0:T(8,128)S(1)} %get-tuple-element.111), channel_id=1, source_target_pairs={{0,8},{4,12},{8,0},{12,4},{16,24},{20,28},{24,16},{28,20},{1,9},{5... | collective-permute-start | bytes 196616 | tf_op jit(solution)/shard_map/ppermute | solution.py:69
  51.0 4.3 %collective-permute-start.9 = (f32[1,64,256]{2,1,0:T(8,128)S(1)}, f32[1,64,256]{2,1,0:T(8,128)S(1)}, u32[]{:S(2)}, u32[]{:S(2)}) collective-permute-start(f32[1,64,256]{2,1,0:T(8,128)S(1)} %get-tuple-element.110), channel_id=1, source_target_pairs={{0,16},{4,20},{8,24},{12,28},{16,0},{20,4},{24,8},{28,12},{1,17},{... | collective-permute-start | bytes 196616 | tf_op jit(solution)/shard_map/ppermute | solution.py:69
  51.5 7.3 %collective-permute-start.16 = (f32[1,128,256]{2,1,0:T(8,128)S(1)}, f32[1,128,256]{2,1,0:T(8,128)S(1)}, u32[]{:S(2)}, u32[]{:S(2)}) collective-permute-start(f32[1,128,256]{2,1,0:T(8,128)S(1)} %slice_bitcast_fusion), channel_id=1, source_target_pairs={{0,1},{1,0},{2,3},{3,2},{4,5},{5,4},{6,7},{7,6},{8,9},{9,8},{10,11... | collective-permute-start | bytes 393224 | tf_op jit(solution)/shard_map/ppermute | solution.py:69
  55.3 15.6 %collective-permute-start.13 = (f32[1,256,256]{2,1,0:T(8,128)S(1)}, f32[1,256,256]{2,1,0:T(8,128)S(1)}, u32[]{:S(2)}, u32[]{:S(2)}) collective-permute-start(f32[1,256,256]{2,1,0:T(8,128)S(1)} %get-tuple-element.89), channel_id=1, source_target_pairs={{0,8},{4,12},{8,0},{12,4},{16,24},{20,28},{24,16},{28,20},{1,9},{5... | collective-permute-start | bytes 786440 | tf_op jit(solution)/shard_map/ppermute | solution.py:69
  56.8 14.1 %collective-permute-start.14 = (f32[1,256,256]{2,1,0:T(8,128)S(1)}, f32[1,256,256]{2,1,0:T(8,128)S(1)}, u32[]{:S(2)}, u32[]{:S(2)}) collective-permute-start(f32[1,256,256]{2,1,0:T(8,128)S(1)} %get-tuple-element.89), channel_id=1, source_target_pairs={{0,16},{4,20},{8,24},{12,28},{16,0},{20,4},{24,8},{28,12},{1,17},{... | collective-permute-start | bytes 786440 | tf_op jit(solution)/shard_map/ppermute | solution.py:69
  57.5 13.4 %collective-permute-start.15 = (f32[1,256,256]{2,1,0:T(8,128)S(1)}, f32[1,256,256]{2,1,0:T(8,128)S(1)}, u32[]{:S(2)}, u32[]{:S(2)}) collective-permute-start(f32[1,256,256]{2,1,0:T(8,128)S(1)} %get-tuple-element.89), channel_id=1, source_target_pairs={{0,24},{4,28},{8,16},{12,20},{16,8},{20,12},{24,0},{28,4},{1,25},{... | collective-permute-start | bytes 786440 | tf_op jit(solution)/shard_map/ppermute | solution.py:69
  58.8 8.3 %collective-permute-start.17 = (f32[1,128,256]{2,1,0:T(8,128)S(1)}, f32[1,128,256]{2,1,0:T(8,128)S(1)}, u32[]{:S(2)}, u32[]{:S(2)}) collective-permute-start(f32[1,128,256]{2,1,0:T(8,128)S(1)} %fusion.4), channel_id=1, source_target_pairs={{0,2},{1,3},{2,0},{3,1},{4,6},{5,7},{6,4},{7,5},{8,10},{9,11},{10,... | collective-permute-start | bytes 393224 | tf_op jit(solution)/shard_map/ppermute | solution.py:69
  61.4 4.3 %collective-permute-start.11 = (f32[1,64,256]{2,1,0:T(8,128)S(1)}, f32[1,64,256]{2,1,0:T(8,128)S(1)}, u32[]{:S(2)}, u32[]{:S(2)}) collective-permute-start(f32[1,64,256]{2,1,0:T(8,128)S(1)} %fusion.3), channel_id=1, source_target_pairs={{0,1},{1,0},{2,3},{3,2},{4,5},{5,4},{6,7},{7,6},{8,9},{9,8},{10,11... | collective-permute-start | bytes 196616 | tf_op jit(solution)/shard_map/ppermute | solution.py:69
  65.6 5.2 %collective-permute-start.12 = (f32[1,64,256]{2,1,0:T(8,128)S(1)}, f32[1,64,256]{2,1,0:T(8,128)S(1)}, u32[]{:S(2)}, u32[]{:S(2)}) collective-permute-start(f32[1,64,256]{2,1,0:T(8,128)S(1)} %add.80), channel_id=1, source_target_pairs={{0,2},{1,3},{2,0},{3,1},{4,6},{5,7},{6,4},{7,5},{8,10},{9,11},{10,... | collective-permute-start | bytes 196616 | tf_op jit(solution)/shard_map/ppermute | solution.py:69
  70.9 6.2 %collective-permute-start.18 = (f32[1,192,256]{2,1,0:T(8,128)S(1)}, f32[1,192,256]{2,1,0:T(8,128)S(1)}, u32[]{:S(2)}, u32[]{:S(2)}) collective-permute-start(f32[1,192,256]{2,1,0:T(8,128)S(1)} %pad_maximum_fusion.2.refs_0_), channel_id=1, source_target_pairs={{0,8},{4,12},{8,0},{12,4},{16,24},{20,28},{24,16},{28,20},{1,9},{5... | collective-permute-start | bytes 589832 | tf_op jit(solution)/shard_map/ppermute | solution.py:69
  72.8 7.8 %collective-permute-start.19 = (f32[1,192,256]{2,1,0:T(8,128)S(1)}, f32[1,192,256]{2,1,0:T(8,128)S(1)}, u32[]{:S(2)}, u32[]{:S(2)}) collective-permute-start(f32[1,192,256]{2,1,0:T(8,128)S(1)} %pad_maximum_fusion.2.refs_0_), channel_id=1, source_target_pairs={{0,16},{4,20},{8,24},{12,28},{16,0},{20,4},{24,8},{28,12},{1,17},{... | collective-permute-start | bytes 589832 | tf_op jit(solution)/shard_map/ppermute | solution.py:69
  72.8 7.8 %collective-permute-start.20 = (f32[1,192,256]{2,1,0:T(8,128)S(1)}, f32[1,192,256]{2,1,0:T(8,128)S(1)}, u32[]{:S(2)}, u32[]{:S(2)}) collective-permute-start(f32[1,192,256]{2,1,0:T(8,128)S(1)} %pad_maximum_fusion.2.refs_0_), channel_id=1, source_target_pairs={{0,24},{4,28},{8,16},{12,20},{16,8},{20,12},{24,0},{28,4},{1,25},{... | collective-permute-start | bytes 589832 | tf_op jit(solution)/shard_map/ppermute | solution.py:69
  80.6 7.1 %collective-permute-start.21 = (f32[4,128,256]{2,1,0:T(8,128)S(1)}, f32[4,128,256]{2,1,0:T(8,128)S(1)}, u32[]{:S(2)}, u32[]{:S(2)}) collective-permute-start(f32[4,128,256]{2,1,0:T(8,128)S(1)} %pad_maximum_fusion.own_ref), channel_id=1, source_target_pairs={{0,4},{4,0},{8,12},{12,8},{16,20},{20,16},{24,28},{28,24},{1,5},{5... | collective-permute-start | bytes 1572872 | tf_op jit(solution)/shard_map/ppermute | solution.py:69
  80.8 30.2 %collective-permute-start.33 = (f32[4,256,256]{2,1,0:T(8,128)S(1)}, f32[4,256,256]{2,1,0:T(8,128)S(1)}, u32[]{:S(2)}, u32[]{:S(2)}) collective-permute-start(f32[4,256,256]{2,1,0:T(8,128)S(1)} %constant_dynamic-update-slice_fusion.refs_2_), channel_id=1, source_target_pairs={{0,4},{4,0},{8,12},{12,8},{16,20},{20,16},{24,28},{28,24},{1,5},{5... | collective-permute-start | bytes 3145736 | tf_op jit(solution)/shard_map/ppermute | solution.py:69
  81.4 6.4 %copy-start = (f32[512,512]{1,0:T(8,128)S(1)}, f32[512,512]{1,0:T(8,128)}, u32[]{:S(2)}) copy-start(f32[512,512]{1,0:T(8,128)} %shard_map.77.z_ref) | copy-start | bytes 3145732
  81.4 15.6 %collective-permute-start.25 = (f32[1,256,256]{2,1,0:T(8,128)S(1)}, f32[1,256,256]{2,1,0:T(8,128)S(1)}, u32[]{:S(2)}, u32[]{:S(2)}) collective-permute-start(f32[1,256,256]{2,1,0:T(8,128)S(1)} %bitcast.12), channel_id=1, source_target_pairs={{0,2},{1,3},{2,0},{3,1},{4,6},{5,7},{6,4},{7,5},{8,10},{9,11},{10,... | collective-permute-start | bytes 786440 | tf_op jit(solution)/shard_map/ppermute | solution.py:69
  89.9 7.0 %collective-permute-start.22 = (f32[1,64,256]{2,1,0:T(8,128)S(1)}, f32[1,64,256]{2,1,0:T(8,128)S(1)}, u32[]{:S(2)}, u32[]{:S(2)}) collective-permute-start(f32[1,64,256]{2,1,0:T(8,128)S(1)} %get-tuple-element.108), channel_id=1, source_target_pairs={{0,8},{4,12},{8,0},{12,4},{16,24},{20,28},{24,16},{28,20},{1,9},{5... | collective-permute-start | bytes 196616 | tf_op jit(solution)/shard_map/ppermute | solution.py:69
  90.6 6.4 %collective-permute-start.23 = (f32[1,64,256]{2,1,0:T(8,128)S(1)}, f32[1,64,256]{2,1,0:T(8,128)S(1)}, u32[]{:S(2)}, u32[]{:S(2)}) collective-permute-start(f32[1,64,256]{2,1,0:T(8,128)S(1)} %get-tuple-element.107), channel_id=1, source_target_pairs={{0,16},{4,20},{8,24},{12,28},{16,0},{20,4},{24,8},{28,12},{1,17},{... | collective-permute-start | bytes 196616 | tf_op jit(solution)/shard_map/ppermute | solution.py:69
  91.4 5.6 %collective-permute-start.24 = (f32[1,64,256]{2,1,0:T(8,128)S(1)}, f32[1,64,256]{2,1,0:T(8,128)S(1)}, u32[]{:S(2)}, u32[]{:S(2)}) collective-permute-start(f32[1,64,256]{2,1,0:T(8,128)S(1)} %get-tuple-element.106), channel_id=1, source_target_pairs={{0,24},{4,28},{8,16},{12,20},{16,8},{20,12},{24,0},{28,4},{1,25},{... | collective-permute-start | bytes 196616 | tf_op jit(solution)/shard_map/ppermute | solution.py:69
  97.0 5.1 %collective-permute-start.26 = (f32[1,64,256]{2,1,0:T(8,128)S(1)}, f32[1,64,256]{2,1,0:T(8,128)S(1)}, u32[]{:S(2)}, u32[]{:S(2)}) collective-permute-start(f32[1,64,256]{2,1,0:T(8,128)S(1)} %fusion.2), channel_id=1, source_target_pairs={{0,1},{1,0},{2,3},{3,2},{4,5},{5,4},{6,7},{7,6},{8,9},{9,8},{10,11... | collective-permute-start | bytes 196616 | tf_op jit(solution)/shard_map/ppermute | solution.py:69
  102.1 6.6 %collective-permute-start.27 = (f32[1,64,256]{2,1,0:T(8,128)S(1)}, f32[1,64,256]{2,1,0:T(8,128)S(1)}, u32[]{:S(2)}, u32[]{:S(2)}) collective-permute-start(f32[1,64,256]{2,1,0:T(8,128)S(1)} %add.87), channel_id=1, source_target_pairs={{0,2},{1,3},{2,0},{3,1},{4,6},{5,7},{6,4},{7,5},{8,10},{9,11},{10,... | collective-permute-start | bytes 196616 | tf_op jit(solution)/shard_map/ppermute | solution.py:69
  103.3 13.3 %collective-permute-start.32 = (f32[2,256,256]{2,1,0:T(8,128)S(1)}, f32[2,256,256]{2,1,0:T(8,128)S(1)}, u32[]{:S(2)}, u32[]{:S(2)}) collective-permute-start(f32[2,256,256]{2,1,0:T(8,128)S(1)} %pad_maximum_fusion.1.refs_0_), channel_id=1, source_target_pairs={{0,1},{1,0},{2,3},{3,2},{4,5},{5,4},{6,7},{7,6},{8,9},{9,8},{10,11... | collective-permute-start | bytes 1572872 | tf_op jit(solution)/shard_map/ppermute | solution.py:69
  108.7 7.9 %collective-permute-start.31 = (f32[2,256,256]{2,1,0:T(8,128)S(1)}, f32[2,256,256]{2,1,0:T(8,128)S(1)}, u32[]{:S(2)}, u32[]{:S(2)}) collective-permute-start(f32[2,256,256]{2,1,0:T(8,128)S(1)} %shard_map.83.own_ref), channel_id=1, source_target_pairs={{0,4},{4,0},{8,12},{12,8},{16,20},{20,16},{24,28},{28,24},{1,5},{5... | collective-permute-start | bytes 1572872 | tf_op jit(solution)/shard_map/ppermute | solution.py:69
  108.8 12.7 %collective-permute-start.28 = (f32[1,64,256]{2,1,0:T(8,128)S(1)}, f32[1,64,256]{2,1,0:T(8,128)S(1)}, u32[]{:S(2)}, u32[]{:S(2)}) collective-permute-start(f32[1,64,256]{2,1,0:T(8,128)S(1)} %add.88), channel_id=1, source_target_pairs={{0,8},{4,12},{8,0},{12,4},{16,24},{20,28},{24,16},{28,20},{1,9},{5... | collective-permute-start | bytes 196616 | tf_op jit(solution)/shard_map/ppermute | solution.py:69
  109.8 11.7 %collective-permute-start.29 = (f32[1,64,256]{2,1,0:T(8,128)S(1)}, f32[1,64,256]{2,1,0:T(8,128)S(1)}, u32[]{:S(2)}, u32[]{:S(2)}) collective-permute-start(f32[1,64,256]{2,1,0:T(8,128)S(1)} %add.88), channel_id=1, source_target_pairs={{0,16},{4,20},{8,24},{12,28},{16,0},{20,4},{24,8},{28,12},{1,17},{... | collective-permute-start | bytes 196616 | tf_op jit(solution)/shard_map/ppermute | solution.py:69
  111.0 10.5 %collective-permute-start.30 = (f32[1,64,256]{2,1,0:T(8,128)S(1)}, f32[1,64,256]{2,1,0:T(8,128)S(1)}, u32[]{:S(2)}, u32[]{:S(2)}) collective-permute-start(f32[1,64,256]{2,1,0:T(8,128)S(1)} %add.88), channel_id=1, source_target_pairs={{0,24},{4,28},{8,16},{12,20},{16,8},{20,12},{24,0},{28,4},{1,25},{... | collective-permute-start | bytes 196616 | tf_op jit(solution)/shard_map/ppermute | solution.py:69
  121.6 1.6 %collective-permute-start.34 = (f32[4,64,256]{2,1,0:T(8,128)S(1)}, f32[4,64,256]{2,1,0:T(8,128)S(1)}, u32[]{:S(2)}, u32[]{:S(2)}) collective-permute-start(f32[4,64,256]{2,1,0:T(8,128)S(1)} %constant_dynamic-update-slice_fusion.4.middle_own_ref), channel_id=1, source_target_pairs={{0,4},{4,0},{8,12},{12,8},{16,20},{20,16},{24,28},{28,24},{1,5},{5... | collective-permute-start | bytes 786440 | tf_op jit(solution)/shard_map/ppermute | solution.py:69

commit v8 on v7

--- a/solution.py
+++ b/solution.py
@@ -375,14 +375,14 @@
         up_placed = place(done[0], start)
         inside = (panel_col >= start) & (panel_col < start + BASE)
         rows = [jnp.where(inside, inv_placed[b], highest(inv[b][:, :BASE], panel[b])) for b in every]
-        below = [jnp.where(row_id[:, :BASE] >= start + BASE, highest(whole[b], inv_placed[b], 1, 1), 0.0) for b in every]
+        right = [jnp.where(panel_col >= start + BASE, rows[b], 0.0) for b in every]
         spent = (row_id >= start + BASE) & (col_id >= start) & (col_id < start + BASE)
-        left = [jnp.where(spent, 0.0, whole[b]) - highest(below[b], rows[b]) for b in every]
+        left = [jnp.where(spent, 0.0, whole[b]) - highest(right[b], rows[b], 0, 0) for b in every]
         for b in every:
             inverse_ref[b] = left[b]
         for b in every:
             inverse_ref[b, pl.ds(start, BASE), :] = rows[b]
-        upper_ref[pl.ds(start, BASE), :] = jnp.where(inside, up_placed, jnp.where(panel_col >= start + BASE, rows[0], 0.0))
+        upper_ref[pl.ds(start, BASE), :] = jnp.where(inside, up_placed, right[0])
         return carry
 
     lax.fori_loop(steps[0], steps[1], step, 0)
@@ -560,22 +560,23 @@
     fold = jnp.concatenate([part[:, rows:] for part in parts])
 
     range_parts = gather(after(range_piece, gram, fold), lines[1:])
+    range_near = swap(range_parts[0], "tm", 1)
     co_other, fold_other = core_swap(co_own), core_swap(fold)
     state = factor_start(spot, parts)
     state, fold_other = lax.optimization_barrier((state, fold_other))
     middle = middle_terms(spot, chips, sketch_z, fold, fold_other)
     middle = scatter_sum(middle, groups)
     state = factor_next((1, 2), *state)
-    state, middle, range_parts = lax.optimization_barrier((state, middle, range_parts))
-    range_all = jnp.concatenate(range_parts)
+    state, middle, range_parts, range_near = lax.optimization_barrier((state, middle, range_parts, range_near))
     for bit in range(bits_of("tm")):
         middle = middle + swap(middle, "tm", 1 << bit)
         if bit == 0:
             state = factor_next((2, state[1].shape[0] // BASE - 1), *state)
-            state, middle, range_all = lax.optimization_barrier((state, middle, range_all))
-    range_all = gather(range_all, lines[:1])
+            state, middle, range_parts = lax.optimization_barrier((state, middle, range_parts))
+    corners = [swap(part, "tm", 1) for part in range_parts[1:]]
     own = factor_end(*state)
-    own, middle = lax.optimization_barrier((own, middle))
+    own, middle, corners = lax.optimization_barrier((own, middle, corners))
+    range_all = range_parts + [range_near] + corners
     other = core_swap(own)
     range_basis, co_basis = bases(spot, own, other, range_all, co_own, co_other)
     middle, range_basis, co_basis = lax.optimization_barrier((gather(middle, groups), range_basis, co_basis))

time: 126 us -> 123 us (0.976)
  Pallas kernels: 56 us -> 53.8 us
    ppermute x35 -> x36, starting transfers between devices: 41.7 us -> 40.9 us  [swap(): lax.ppermute(values, axis, [(i, i ^ mask) for i in range(lax.axis_size(ax...]
    ppermute x35 -> x36, waiting for transfers between devices: 23.6 us -> 23.6 us  [swap(): lax.ppermute(values, axis, [(i, i ^ mask) for i in range(lax.axis_size(ax...]
  transfers between devices with their start and end apart: 35 -> 36, of which waited for: 13 -> 16; matrix products, arithmetic and copies ran while one was open for 2% -> 2% of each run, Pallas kernels for 29% -> 28%
where the time goes in v8:
time: 123 us
  Pallas kernels  53.8 us (44%)
  starting transfers between devices  40.9 us (33%)
  waiting for transfers between devices  23.6 us (19%)
  other arithmetic  2.66 us (2%)
    ppermute x36, starting transfers between devices, swap(): lax.ppermute(values, axis, [(i, i ^ mask) for i in range(lax.axis_size(ax...  40.9 us
    ppermute x36, waiting for transfers between devices, swap(): lax.ppermute(values, axis, [(i, i ^ mask) for i in range(lax.axis_size(ax...  23.6 us
    pallas_call x1, Pallas kernels, sketch_terms(): call(sketch_kernel, (float_shape(rows // TILES, k),) * 4 + (float_shape(c...  15.5 us
    pallas_call x1, Pallas kernels, core_terms(): call(core_kernel, float_shape(s_core, s_core), [SCALAR] + [OUTSIDE] * 3,...  13.4 us
    pallas_call x2, Pallas kernels, factor_next(): call(functools.partial(factor_next_kernel, steps), (float_shape(2, n, n),...  6.16 us
    pallas_call x1, Pallas kernels, factor_start(): call(functools.partial(factor_start_kernel, (0, 1), len(parts)), (float_s...  4.82 us
    pallas_call x1, Pallas kernels, bases(): call(functools.partial(basis_kernel, len(ranges)), (float_shape(lines * r...  4.29 us
    pallas_call x1, Pallas kernels, factor_end(): call(functools.partial(factor_end_kernel, (n // BASE - 1, n // BASE)), fl...  4.08 us
  transfers between devices with their start and end apart: 36, of which 16 were waited for; matrix products, arithmetic and copies ran while one was open for 2% of the time, Pallas kernels for 28%

profile of v8, /device:TPU:0, one launch (start us, length us, event | category | flops | bytes accessed | tf_op | source)
XLA Modules:
  0.0 122.5 jit_solution(14502041935992127800)
XLA Ops:
  0.6 0.6 pad_add_fusion.spot_ref
  1.3 15.5 %shard_map.76 = (f32[256,256]{1,0:T(8,128)}, f32[256,256]{1,0:T(8,128)}, f32[256,256]{1,0:T(8,128)}, f32[256,256]{1,0:T(8,128)}, f32[4,384,256]{2,1,0:T(8,128)}, /*index=5*/f32[4,384,256]{2,1,0:T(8,128)}) custom-call(s32[4]{0:T(128)} %pad_add_fusion.spot_ref, f32[1024,2048]{1,0:T(8,128)} %window_ref.3, f32[2048,256]{1,0:T(8,128)} %test_ref.1, ...), custom_call_target="tpu_custom_call" | custom-call | flops 6442450944 | bytes 4194304 | tf_op jit(solution)/shard_map/pallas_call | solution.py:209
  16.8 0.5 collective-permute-start.1
  17.4 2.7 %collective-permute-start = (f32[256,256]{1,0:T(8,128)}, f32[256,256]{1,0:T(8,128)S(1)}, u32[]{:S(2)}, u32[]{:S(2)}) collective-permute-start(f32[256,256]{1,0:T(8,128)} %get-tuple-element.57), channel_id=1, source_target_pairs={{0,1},{1,0},{2,3},{3,2},{4,5},{5,4},{6,7},{7,6},{8,9},{9,8},{10,11... | collective-permute-start | bytes 786440 | tf_op jit(solution)/shard_map/ppermute | solution.py:69
  20.0 0.1 collective-permute-start.3
  20.1 0.5 collective-permute-done.1
  20.6 1.6 %add.69 = f32[4,384,256]{2,1,0:T(8,128)S(1)} add(f32[4,384,256]{2,1,0:T(8,128)} %get-tuple-element.58, f32[4,384,256]{2,1,0:T(8,128)S(1)} %collective-permute-done.1) | non-fusion elementwise | flops 393216 | bytes 4718592 | tf_op jit(solution)/shard_map/add | solution.py:537
  22.2 0.1 fusion.5
  22.3 2.9 %collective-permute-start.4 = (f32[1,384,256]{2,1,0:T(8,128)S(1)}, f32[1,384,256]{2,1,0:T(8,128)S(1)}, u32[]{:S(2)}, u32[]{:S(2)}) collective-permute-start(f32[1,384,256]{2,1,0:T(8,128)S(1)} %get-tuple-element.109), channel_id=1, source_target_pairs={{0,8},{4,12},{8,0},{12,4},{16,24},{20,28},{24,16},{28,20},{1,9},{5... | collective-permute-start | bytes 1179656 | tf_op jit(solution)/shard_map/ppermute | solution.py:69
  25.2 1.5 %collective-permute-start.5 = (f32[1,384,256]{2,1,0:T(8,128)S(1)}, f32[1,384,256]{2,1,0:T(8,128)S(1)}, u32[]{:S(2)}, u32[]{:S(2)}) collective-permute-start(f32[1,384,256]{2,1,0:T(8,128)S(1)} %get-tuple-element.108), channel_id=1, source_target_pairs={{0,16},{4,20},{8,24},{12,28},{16,0},{20,4},{24,8},{28,12},{1,17},{... | collective-permute-start | bytes 1179656 | tf_op jit(solution)/shard_map/ppermute | solution.py:69
  26.8 0.6 collective-permute-done
  27.4 3.0 %collective-permute-start.2 = (f32[256,256]{1,0:T(8,128)S(1)}, f32[256,256]{1,0:T(8,128)S(1)}, u32[]{:S(2)}, u32[]{:S(2)}) collective-permute-start(f32[256,256]{1,0:T(8,128)S(1)} %add.70), channel_id=1, source_target_pairs={{0,2},{1,3},{2,0},{3,1},{4,6},{5,7},{6,4},{7,5},{8,10},{9,11},{10,... | collective-permute-start | bytes 786440 | tf_op jit(solution)/shard_map/ppermute | solution.py:69
  30.4 13.4 %shard_map.77.z_ref = f32[512,512]{1,0:T(8,128)} custom-call(s32[4]{0:T(128)} %pad_add_fusion.spot_ref, f32[1024,2048]{1,0:T(8,128)} %window_ref.3, f32[512,2048]{1,0:T(8,128)} %right_ref.3, f32[512,1024]{1,0:T(8,128)} %left_ref.3), custom_call_target="tpu_custom_call" | custom-call | flops 9663676416 | bytes 4194304 | tf_op jit(solution)/shard_map/pallas_call | solution.py:264
  43.9 0.6 collective-permute-done.5
  44.5 0.1 fusion.1
  44.7 0.2 copy-done.2
  44.8 0.1 slice_bitcast_fusion.1
  44.9 1.4 %shard_map.78 = (f32[4,64,256]{2,1,0:T(8,128)S(1)}, f32[4,64,256]{2,1,0:T(8,128)S(1)}) custom-call(s32[4]{0:T(128)S(1)} %copy-done.1, f32[256,256]{1,0:T(8,128)S(1)} %get-tuple-element.118.range_ref, f32[256,256]{1,0:T(8,128)S(1)} %get-tuple-element.111.co_ref), custom_call_target="tpu_custom_call" | custom-call | flops 402653184 | bytes 4194304 | tf_op jit(solution)/shard_map/pallas_call | solution.py:288
  46.3 0.1 collective-permute-start.7
  46.4 1.5 %collective-permute-done.7 = f32[4,64,256]{2,1,0:T(8,128)S(1)} collective-permute-done((f32[4,64,256]{2,1,0:T(8,128)S(1)}, f32[4,64,256]{2,1,0:T(8,128)S(1)}, u32[]{:S(2)}, u32[]{:S(2)}) %collective-permute-start.7) | collective-permute-done | bytes 262176 | tf_op jit(solution)/shard_map/ppermute | solution.py:69
  48.0 2.5 %collective-permute-start.10 = (f32[1,64,256]{2,1,0:T(8,128)S(1)}, f32[1,64,256]{2,1,0:T(8,128)S(1)}, u32[]{:S(2)}, u32[]{:S(2)}) collective-permute-start(f32[1,64,256]{2,1,0:T(8,128)S(1)} %get-tuple-element.115), channel_id=1, source_target_pairs={{0,24},{4,28},{8,16},{12,20},{16,8},{20,12},{24,0},{28,4},{1,25},{... | collective-permute-start | bytes 196616 | tf_op jit(solution)/shard_map/ppermute | solution.py:69
  50.5 0.5 collective-permute-start.8
  51.0 0.5 collective-permute-start.9
  51.6 1.6 %collective-permute-start.16 = (f32[1,128,256]{2,1,0:T(8,128)S(1)}, f32[1,128,256]{2,1,0:T(8,128)S(1)}, u32[]{:S(2)}, u32[]{:S(2)}) collective-permute-start(f32[1,128,256]{2,1,0:T(8,128)S(1)} %slice_bitcast_fusion), channel_id=1, source_target_pairs={{0,1},{1,0},{2,3},{3,2},{4,5},{5,4},{6,7},{7,6},{8,9},{9,8},{10,11... | collective-permute-start | bytes 393224 | tf_op jit(solution)/shard_map/ppermute | solution.py:69
  53.2 0.4 collective-permute-done.10
  53.6 1.1 collective-permute-done.8
  54.8 0.5 collective-permute-done.9
  55.3 1.6 %collective-permute-start.13 = (f32[1,256,256]{2,1,0:T(8,128)S(1)}, f32[1,256,256]{2,1,0:T(8,128)S(1)}, u32[]{:S(2)}, u32[]{:S(2)}) collective-permute-start(f32[1,256,256]{2,1,0:T(8,128)S(1)} %get-tuple-element.95), channel_id=1, source_target_pairs={{0,8},{4,12},{8,0},{12,4},{16,24},{20,28},{24,16},{28,20},{1,9},{5... | collective-permute-start | bytes 786440 | tf_op jit(solution)/shard_map/ppermute | solution.py:69
  56.9 0.7 collective-permute-start.14
  57.6 1.3 %collective-permute-start.15 = (f32[1,256,256]{2,1,0:T(8,128)S(1)}, f32[1,256,256]{2,1,0:T(8,128)S(1)}, u32[]{:S(2)}, u32[]{:S(2)}) collective-permute-start(f32[1,256,256]{2,1,0:T(8,128)S(1)} %get-tuple-element.95), channel_id=1, source_target_pairs={{0,24},{4,28},{8,16},{12,20},{16,8},{20,12},{24,0},{28,4},{1,25},{... | collective-permute-start | bytes 786440 | tf_op jit(solution)/shard_map/ppermute | solution.py:69
  58.9 2.5 %collective-permute-start.17 = (f32[1,128,256]{2,1,0:T(8,128)S(1)}, f32[1,128,256]{2,1,0:T(8,128)S(1)}, u32[]{:S(2)}, u32[]{:S(2)}) collective-permute-start(f32[1,128,256]{2,1,0:T(8,128)S(1)} %fusion.4), channel_id=1, source_target_pairs={{0,2},{1,3},{2,0},{3,1},{4,6},{5,7},{6,4},{7,5},{8,10},{9,11},{10,... | collective-permute-start | bytes 393224 | tf_op jit(solution)/shard_map/ppermute | solution.py:69
  61.4 1.6 %collective-permute-start.11 = (f32[1,64,256]{2,1,0:T(8,128)S(1)}, f32[1,64,256]{2,1,0:T(8,128)S(1)}, u32[]{:S(2)}, u32[]{:S(2)}) collective-permute-start(f32[1,64,256]{2,1,0:T(8,128)S(1)} %fusion.3), channel_id=1, source_target_pairs={{0,1},{1,0},{2,3},{3,2},{4,5},{5,4},{6,7},{7,6},{8,9},{9,8},{10,11... | collective-permute-start | bytes 196616 | tf_op jit(solution)/shard_map/ppermute | solution.py:69
  63.0 2.7 %collective-permute-done.11 = f32[1,64,256]{2,1,0:T(8,128)S(1)} collective-permute-done((f32[1,64,256]{2,1,0:T(8,128)S(1)}, f32[1,64,256]{2,1,0:T(8,128)S(1)}, u32[]{:S(2)}, u32[]{:S(2)}) %collective-permute-start.11) | collective-permute-done | bytes 65568 | tf_op jit(solution)/shard_map/ppermute | solution.py:69
  65.7 1.5 %collective-permute-start.12 = (f32[1,64,256]{2,1,0:T(8,128)S(1)}, f32[1,64,256]{2,1,0:T(8,128)S(1)}, u32[]{:S(2)}, u32[]{:S(2)}) collective-permute-start(f32[1,64,256]{2,1,0:T(8,128)S(1)} %add.80), channel_id=1, source_target_pairs={{0,2},{1,3},{2,0},{3,1},{4,6},{5,7},{6,4},{7,5},{8,10},{9,11},{10,... | collective-permute-start | bytes 196616 | tf_op jit(solution)/shard_map/ppermute | solution.py:69
  67.3 3.7 %collective-permute-done.12 = f32[1,64,256]{2,1,0:T(8,128)S(1)} collective-permute-done((f32[1,64,256]{2,1,0:T(8,128)S(1)}, f32[1,64,256]{2,1,0:T(8,128)S(1)}, u32[]{:S(2)}, u32[]{:S(2)}) %collective-permute-start.12) | collective-permute-done | bytes 65568 | tf_op jit(solution)/shard_map/ppermute | solution.py:69
  71.0 1.8 %collective-permute-start.18 = (f32[1,192,256]{2,1,0:T(8,128)S(1)}, f32[1,192,256]{2,1,0:T(8,128)S(1)}, u32[]{:S(2)}, u32[]{:S(2)}) collective-permute-start(f32[1,192,256]{2,1,0:T(8,128)S(1)} %pad_maximum_fusion.1.refs_0_), channel_id=1, source_target_pairs={{0,8},{4,12},{8,0},{12,4},{16,24},{20,28},{24,16},{28,20},{1,9},{5... | collective-permute-start | bytes 589832 | tf_op jit(solution)/shard_map/ppermute | solution.py:69
  72.8 1.7 %collective-permute-start.20 = (f32[1,192,256]{2,1,0:T(8,128)S(1)}, f32[1,192,256]{2,1,0:T(8,128)S(1)}, u32[]{:S(2)}, u32[]{:S(2)}) collective-permute-start(f32[1,192,256]{2,1,0:T(8,128)S(1)} %pad_maximum_fusion.1.refs_0_), channel_id=1, source_target_pairs={{0,24},{4,28},{8,16},{12,20},{16,8},{20,12},{24,0},{28,4},{1,25},{... | collective-permute-start | bytes 589832 | tf_op jit(solution)/shard_map/ppermute | solution.py:69
  74.5 2.7 %collective-permute-done.18.refs_1_ = f32[1,192,256]{2,1,0:T(8,128)S(1)} collective-permute-done((f32[1,192,256]{2,1,0:T(8,128)S(1)}, f32[1,192,256]{2,1,0:T(8,128)S(1)}, u32[]{:S(2)}, u32[]{:S(2)}) %collective-permute-start.18) | collective-permute-done | bytes 196640 | tf_op jit(solution)/shard_map/ppermute | solution.py:69
  77.2 3.4 %collective-permute-done.19.refs_2_ = f32[1,192,256]{2,1,0:T(8,128)S(1)} collective-permute-done((f32[1,192,256]{2,1,0:T(8,128)S(1)}, f32[1,192,256]{2,1,0:T(8,128)S(1)}, u32[]{:S(2)}, u32[]{:S(2)}) %collective-permute-start.19) | collective-permute-done | bytes 196640 | tf_op jit(solution)/shard_map/ppermute | solution.py:69
  80.7 0.1 collective-permute-start.21
  80.9 1.3 %collective-permute-start.25 = (f32[1,256,256]{2,1,0:T(8,128)S(1)}, f32[1,256,256]{2,1,0:T(8,128)S(1)}, u32[]{:S(2)}, u32[]{:S(2)}) collective-permute-start(f32[1,256,256]{2,1,0:T(8,128)S(1)} %bitcast.12), channel_id=1, source_target_pairs={{0,2},{1,3},{2,0},{3,1},{4,6},{5,7},{6,4},{7,5},{8,10},{9,11},{10,... | collective-permute-start | bytes 786440 | tf_op jit(solution)/shard_map/ppermute | solution.py:69
  82.2 1.2 %collective-permute-start.26 = (f32[1,256,256]{2,1,0:T(8,128)S(1)}, f32[1,256,256]{2,1,0:T(8,128)S(1)}, u32[]{:S(2)}, u32[]{:S(2)}) collective-permute-start(f32[1,256,256]{2,1,0:T(8,128)S(1)} %bitcast.13), channel_id=1, source_target_pairs={{0,1},{1,0},{2,3},{3,2},{4,5},{5,4},{6,7},{7,6},{8,9},{9,8},{10,11... | collective-permute-start | bytes 786440 | tf_op jit(solution)/shard_map/ppermute | solution.py:69
  83.4 4.8 %shard_map.79 = (f32[2,256,256]{2,1,0:T(8,128)S(1)}, f32[256,256]{1,0:T(8,128)S(1)}) custom-call(s32[4]{0:T(128)S(1)} %copy-done.1, f32[1,192,256]{2,1,0:T(8,128)S(1)} %pad_maximum_fusion.1.refs_0_, f32[1,192,256]{2,1,0:T(8,128)S(1)} %collective-permute-done.18.refs_1_, f32[1,192,256]{2,1,0:T(8,128)S(1)} %collective-permute-done.19.refs_2_, ...), custom_call_target="tpu_custom_call" | custom-call | flops 1677721600 | bytes 4194304 | tf_op jit(solution)/shard_map/pallas_call | solution.py:429
  88.2 1.8 %shard_map.81 = f32[4,64,256]{2,1,0:T(8,128)S(1)} custom-call(s32[4]{0:T(128)S(1)} %copy-done.1, f32[512,512]{1,0:T(8,128)S(1)} %copy-done, f32[4,128,256]{2,1,0:T(8,128)S(1)} %pad_maximum_fusion.own_ref, f32[4,128,256]{2,1,0:T(8,128)S(1)} %collective-permute-done.21.other_ref), custom_call_target="tpu_custom_call" | custom-call | flops 402653184 | bytes 4194304 | tf_op jit(solution)/shard_map/pallas_call | solution.py:308
  90.1 1.5 %collective-permute-start.22 = (f32[1,64,256]{2,1,0:T(8,128)S(1)}, f32[1,64,256]{2,1,0:T(8,128)S(1)}, u32[]{:S(2)}, u32[]{:S(2)}) collective-permute-start(f32[1,64,256]{2,1,0:T(8,128)S(1)} %get-tuple-element.114), channel_id=1, source_target_pairs={{0,8},{4,12},{8,0},{12,4},{16,24},{20,28},{24,16},{28,20},{1,9},{5... | collective-permute-start | bytes 196616 | tf_op jit(solution)/shard_map/ppermute | solution.py:69
  91.6 0.8 collective-permute-start.23
  92.4 1.3 %collective-permute-start.24 = (f32[1,64,256]{2,1,0:T(8,128)S(1)}, f32[1,64,256]{2,1,0:T(8,128)S(1)}, u32[]{:S(2)}, u32[]{:S(2)}) collective-permute-start(f32[1,64,256]{2,1,0:T(8,128)S(1)} %get-tuple-element.112), channel_id=1, source_target_pairs={{0,24},{4,28},{8,16},{12,20},{16,8},{20,12},{24,0},{28,4},{1,25},{... | collective-permute-start | bytes 196616 | tf_op jit(solution)/shard_map/ppermute | solution.py:69
  93.7 3.1 %shard_map.80 = (f32[2,256,256]{2,1,0:T(8,128)S(1)}, f32[256,256]{1,0:T(8,128)S(1)}) custom-call(f32[2,256,256]{2,1,0:T(8,128)S(1)} %get-tuple-element.72.begun_ref, f32[256,256]{1,0:T(8,128)S(1)} %get-tuple-element.73.begun_upper_ref), custom_call_target="tpu_custom_call" | custom-call | flops 1677721600 | bytes 4194304 | tf_op jit(solution)/shard_map/pallas_call | solution.py:437
  96.9 0.6 collective-permute-done.24
  97.6 0.2 collective-permute-start.27
  97.8 3.0 %shard_map.82 = (f32[2,256,256]{2,1,0:T(8,128)S(1)}, f32[256,256]{1,0:T(8,128)S(1)}) custom-call(f32[2,256,256]{2,1,0:T(8,128)S(1)} %get-tuple-element.79.begun_ref, f32[256,256]{1,0:T(8,128)S(1)} %get-tuple-element.80.begun_upper_ref), custom_call_target="tpu_custom_call" | custom-call | flops 1677721600 | bytes 4194304 | tf_op jit(solution)/shard_map/pallas_call | solution.py:437
  100.9 1.1 collective-permute-done.27
  101.9 0.9 collective-permute-start.29
  102.8 1.3 %collective-permute-start.28 = (f32[1,64,256]{2,1,0:T(8,128)S(1)}, f32[1,64,256]{2,1,0:T(8,128)S(1)}, u32[]{:S(2)}, u32[]{:S(2)}) collective-permute-start(f32[1,64,256]{2,1,0:T(8,128)S(1)} %add.87), channel_id=1, source_target_pairs={{0,2},{1,3},{2,0},{3,1},{4,6},{5,7},{6,4},{7,5},{8,10},{9,11},{10,... | collective-permute-start | bytes 196616 | tf_op jit(solution)/shard_map/ppermute | solution.py:69
  104.1 4.1 %shard_map.83.own_ref = f32[2,256,256]{2,1,0:T(8,128)S(1)} custom-call(f32[2,256,256]{2,1,0:T(8,128)S(1)} %get-tuple-element.86.begun_ref, f32[256,256]{1,0:T(8,128)S(1)} %get-tuple-element.87.begun_upper_ref), custom_call_target="tpu_custom_call" | custom-call | flops 1677721600 | bytes 4194304 | tf_op jit(solution)/shard_map/pallas_call | solution.py:444
  108.2 1.3 %collective-permute-done.28 = f32[1,64,256]{2,1,0:T(8,128)S(1)} collective-permute-done((f32[1,64,256]{2,1,0:T(8,128)S(1)}, f32[1,64,256]{2,1,0:T(8,128)S(1)}, u32[]{:S(2)}, u32[]{:S(2)}) %collective-permute-start.28) | collective-permute-done | bytes 65568 | tf_op jit(solution)/shard_map/ppermute | solution.py:69
  109.5 1.2 collective-permute-done.29.refs_3_
  110.8 1.6 %collective-permute-start.30 = (f32[1,64,256]{2,1,0:T(8,128)S(1)}, f32[1,64,256]{2,1,0:T(8,128)S(1)}, u32[]{:S(2)}, u32[]{:S(2)}) collective-permute-start(f32[1,64,256]{2,1,0:T(8,128)S(1)} %add.88), channel_id=1, source_target_pairs={{0,8},{4,12},{8,0},{12,4},{16,24},{20,28},{24,16},{28,20},{1,9},{5... | collective-permute-start | bytes 196616 | tf_op jit(solution)/shard_map/ppermute | solution.py:69
  112.3 0.2 collective-permute-start.31
  112.5 1.7 %collective-permute-start.32 = (f32[1,64,256]{2,1,0:T(8,128)S(1)}, f32[1,64,256]{2,1,0:T(8,128)S(1)}, u32[]{:S(2)}, u32[]{:S(2)}) collective-permute-start(f32[1,64,256]{2,1,0:T(8,128)S(1)} %add.88), channel_id=1, source_target_pairs={{0,24},{4,28},{8,16},{12,20},{16,8},{20,12},{24,0},{28,4},{1,25},{... | collective-permute-start | bytes 196616 | tf_op jit(solution)/shard_map/ppermute | solution.py:69
  114.3 4.3 %shard_map.84 = (f32[1024,256]{1,0:T(8,128)}, f32[256,2048]{1,0:T(8,128)}) custom-call(s32[4]{0:T(128)S(1)} %copy-done.1, f32[2,256,256]{2,1,0:T(8,128)S(1)} %shard_map.83.own_ref, f32[2,256,256]{2,1,0:T(8,128)S(1)} %collective-permute-done.33.other_ref, f32[1,256,256]{2,1,0:T(8,128)S(1)} %bitcast.14, f32[1,256,256]{2,1,0:T(8,128)S(1)} %collective-permute-done.25.refs_1_, ...), custom_call_target="tpu_custom_call" | custom-call | flops 1207959552 | bytes 4194304 | tf_op jit(solution)/shard_map/pallas_call | solution.py:492
  118.7 0.1 collective-permute-start.35
  118.7 1.5 %collective-permute-done.35.middle_other_ref = f32[4,64,256]{2,1,0:T(8,128)S(1)} collective-permute-done((f32[4,64,256]{2,1,0:T(8,128)S(1)}, f32[4,64,256]{2,1,0:T(8,128)S(1)}, u32[]{:S(2)}, u32[]{:S(2)}) %collective-permute-start.35) | collective-permute-done | bytes 262176 | tf_op jit(solution)/shard_map/ppermute | solution.py:69
  120.3 2.3 %shard_map.85 = f32[256,256]{1,0:T(8,128)} custom-call(s32[4]{0:T(128)S(1)} %copy-done.1, f32[2,256,256]{2,1,0:T(8,128)S(1)} %shard_map.83.own_ref, f32[2,256,256]{2,1,0:T(8,128)S(1)} %collective-permute-done.33.other_ref, f32[4,64,256]{2,1,0:T(8,128)S(1)} %constant_dynamic-update-slice_fusion.4.middle_own_ref, ...), custom_call_target="tpu_custom_call" | custom-call | flops 402653184 | bytes 4194304 | tf_op jit(solution)/shard_map/pallas_call | solution.py:515
  (57 shorter events, 0.6 us)
Async XLA Ops:
  16.8 3.8 %collective-permute-start.1 = (f32[4,384,256]{2,1,0:T(8,128)}, f32[4,384,256]{2,1,0:T(8,128)S(1)}, u32[]{:S(2)}, u32[]{:S(2)}) collective-permute-start(f32[4,384,256]{2,1,0:T(8,128)} %get-tuple-element.59), channel_id=1, source_target_pairs={{0,4},{4,0},{8,12},{12,8},{16,20},{20,16},{24,28},{28,24},{1,5},{5... | collective-permute-start | bytes 4718600 | tf_op jit(solution)/shard_map/ppermute | solution.py:69
  17.4 10.0 %collective-permute-start = (f32[256,256]{1,0:T(8,128)}, f32[256,256]{1,0:T(8,128)S(1)}, u32[]{:S(2)}, u32[]{:S(2)}) collective-permute-start(f32[256,256]{1,0:T(8,128)} %get-tuple-element.57), channel_id=1, source_target_pairs={{0,1},{1,0},{2,3},{3,2},{4,5},{5,4},{6,7},{7,6},{8,9},{9,8},{10,11... | collective-permute-start | bytes 786440 | tf_op jit(solution)/shard_map/ppermute | solution.py:69
  20.0 24.6 %collective-permute-start.3 = (f32[256,256]{1,0:T(8,128)}, f32[256,256]{1,0:T(8,128)S(1)}, u32[]{:S(2)}, u32[]{:S(2)}) collective-permute-start(f32[256,256]{1,0:T(8,128)} %get-tuple-element.61), channel_id=1, source_target_pairs={{0,1},{1,0},{2,3},{3,2},{4,5},{5,4},{6,7},{7,6},{8,9},{9,8},{10,11... | collective-permute-start | bytes 786440 | tf_op jit(solution)/shard_map/ppermute | solution.py:69
  22.2 5.2 %copy-start.3 = (f32[256,256]{1,0:T(8,128)S(1)}, f32[256,256]{1,0:T(8,128)}, u32[]{:S(2)}) copy-start(f32[256,256]{1,0:T(8,128)} %get-tuple-element.56) | copy-start | bytes 786436
  22.3 21.6 %collective-permute-start.4 = (f32[1,384,256]{2,1,0:T(8,128)S(1)}, f32[1,384,256]{2,1,0:T(8,128)S(1)}, u32[]{:S(2)}, u32[]{:S(2)}) collective-permute-start(f32[1,384,256]{2,1,0:T(8,128)S(1)} %get-tuple-element.109), channel_id=1, source_target_pairs={{0,8},{4,12},{8,0},{12,4},{16,24},{20,28},{24,16},{28,20},{1,9},{5... | collective-permute-start | bytes 1179656 | tf_op jit(solution)/shard_map/ppermute | solution.py:69
  25.2 19.3 %collective-permute-start.5 = (f32[1,384,256]{2,1,0:T(8,128)S(1)}, f32[1,384,256]{2,1,0:T(8,128)S(1)}, u32[]{:S(2)}, u32[]{:S(2)}) collective-permute-start(f32[1,384,256]{2,1,0:T(8,128)S(1)} %get-tuple-element.108), channel_id=1, source_target_pairs={{0,16},{4,20},{8,24},{12,28},{16,0},{20,4},{24,8},{28,12},{1,17},{... | collective-permute-start | bytes 1179656 | tf_op jit(solution)/shard_map/ppermute | solution.py:69
  26.8 17.8 %collective-permute-start.6 = (f32[1,384,256]{2,1,0:T(8,128)S(1)}, f32[1,384,256]{2,1,0:T(8,128)S(1)}, u32[]{:S(2)}, u32[]{:S(2)}) collective-permute-start(f32[1,384,256]{2,1,0:T(8,128)S(1)} %get-tuple-element.107), channel_id=1, source_target_pairs={{0,24},{4,28},{8,16},{12,20},{16,8},{20,12},{24,0},{28,4},{1,25},{... | collective-permute-start | bytes 1179656 | tf_op jit(solution)/shard_map/ppermute | solution.py:69
  27.4 17.2 %collective-permute-start.2 = (f32[256,256]{1,0:T(8,128)S(1)}, f32[256,256]{1,0:T(8,128)S(1)}, u32[]{:S(2)}, u32[]{:S(2)}) collective-permute-start(f32[256,256]{1,0:T(8,128)S(1)} %add.70), channel_id=1, source_target_pairs={{0,2},{1,3},{2,0},{3,1},{4,6},{5,7},{6,4},{7,5},{8,10},{9,11},{10,... | collective-permute-start | bytes 786440 | tf_op jit(solution)/shard_map/ppermute | solution.py:69
  43.9 1.0 copy-start.2
  43.9 1.0 copy-start.1
  46.3 1.6 %collective-permute-start.7 = (f32[4,64,256]{2,1,0:T(8,128)S(1)}, f32[4,64,256]{2,1,0:T(8,128)S(1)}, u32[]{:S(2)}, u32[]{:S(2)}) collective-permute-start(f32[4,64,256]{2,1,0:T(8,128)S(1)} %get-tuple-element.67), channel_id=1, source_target_pairs={{0,4},{4,0},{8,12},{12,8},{16,20},{20,16},{24,28},{28,24},{1,5},{5... | collective-permute-start | bytes 786440 | tf_op jit(solution)/shard_map/ppermute | solution.py:69
  48.0 5.6 %collective-permute-start.10 = (f32[1,64,256]{2,1,0:T(8,128)S(1)}, f32[1,64,256]{2,1,0:T(8,128)S(1)}, u32[]{:S(2)}, u32[]{:S(2)}) collective-permute-start(f32[1,64,256]{2,1,0:T(8,128)S(1)} %get-tuple-element.115), channel_id=1, source_target_pairs={{0,24},{4,28},{8,16},{12,20},{16,8},{20,12},{24,0},{28,4},{1,25},{... | collective-permute-start | bytes 196616 | tf_op jit(solution)/shard_map/ppermute | solution.py:69
  50.5 4.3 %collective-permute-start.8 = (f32[1,64,256]{2,1,0:T(8,128)S(1)}, f32[1,64,256]{2,1,0:T(8,128)S(1)}, u32[]{:S(2)}, u32[]{:S(2)}) collective-permute-start(f32[1,64,256]{2,1,0:T(8,128)S(1)} %get-tuple-element.117), channel_id=1, source_target_pairs={{0,8},{4,12},{8,0},{12,4},{16,24},{20,28},{24,16},{28,20},{1,9},{5... | collective-permute-start | bytes 196616 | tf_op jit(solution)/shard_map/ppermute | solution.py:69
  51.0 4.3 %collective-permute-start.9 = (f32[1,64,256]{2,1,0:T(8,128)S(1)}, f32[1,64,256]{2,1,0:T(8,128)S(1)}, u32[]{:S(2)}, u32[]{:S(2)}) collective-permute-start(f32[1,64,256]{2,1,0:T(8,128)S(1)} %get-tuple-element.116), channel_id=1, source_target_pairs={{0,16},{4,20},{8,24},{12,28},{16,0},{20,4},{24,8},{28,12},{1,17},{... | collective-permute-start | bytes 196616 | tf_op jit(solution)/shard_map/ppermute | solution.py:69
  51.6 7.3 %collective-permute-start.16 = (f32[1,128,256]{2,1,0:T(8,128)S(1)}, f32[1,128,256]{2,1,0:T(8,128)S(1)}, u32[]{:S(2)}, u32[]{:S(2)}) collective-permute-start(f32[1,128,256]{2,1,0:T(8,128)S(1)} %slice_bitcast_fusion), channel_id=1, source_target_pairs={{0,1},{1,0},{2,3},{3,2},{4,5},{5,4},{6,7},{7,6},{8,9},{9,8},{10,11... | collective-permute-start | bytes 393224 | tf_op jit(solution)/shard_map/ppermute | solution.py:69
  55.3 15.6 %collective-permute-start.13 = (f32[1,256,256]{2,1,0:T(8,128)S(1)}, f32[1,256,256]{2,1,0:T(8,128)S(1)}, u32[]{:S(2)}, u32[]{:S(2)}) collective-permute-start(f32[1,256,256]{2,1,0:T(8,128)S(1)} %get-tuple-element.95), channel_id=1, source_target_pairs={{0,8},{4,12},{8,0},{12,4},{16,24},{20,28},{24,16},{28,20},{1,9},{5... | collective-permute-start | bytes 786440 | tf_op jit(solution)/shard_map/ppermute | solution.py:69
  56.9 14.1 %collective-permute-start.14 = (f32[1,256,256]{2,1,0:T(8,128)S(1)}, f32[1,256,256]{2,1,0:T(8,128)S(1)}, u32[]{:S(2)}, u32[]{:S(2)}) collective-permute-start(f32[1,256,256]{2,1,0:T(8,128)S(1)} %get-tuple-element.95), channel_id=1, source_target_pairs={{0,16},{4,20},{8,24},{12,28},{16,0},{20,4},{24,8},{28,12},{1,17},{... | collective-permute-start | bytes 786440 | tf_op jit(solution)/shard_map/ppermute | solution.py:69
  57.6 13.4 %collective-permute-start.15 = (f32[1,256,256]{2,1,0:T(8,128)S(1)}, f32[1,256,256]{2,1,0:T(8,128)S(1)}, u32[]{:S(2)}, u32[]{:S(2)}) collective-permute-start(f32[1,256,256]{2,1,0:T(8,128)S(1)} %get-tuple-element.95), channel_id=1, source_target_pairs={{0,24},{4,28},{8,16},{12,20},{16,8},{20,12},{24,0},{28,4},{1,25},{... | collective-permute-start | bytes 786440 | tf_op jit(solution)/shard_map/ppermute | solution.py:69
  58.9 8.3 %collective-permute-start.17 = (f32[1,128,256]{2,1,0:T(8,128)S(1)}, f32[1,128,256]{2,1,0:T(8,128)S(1)}, u32[]{:S(2)}, u32[]{:S(2)}) collective-permute-start(f32[1,128,256]{2,1,0:T(8,128)S(1)} %fusion.4), channel_id=1, source_target_pairs={{0,2},{1,3},{2,0},{3,1},{4,6},{5,7},{6,4},{7,5},{8,10},{9,11},{10,... | collective-permute-start | bytes 393224 | tf_op jit(solution)/shard_map/ppermute | solution.py:69
  61.4 4.3 %collective-permute-start.11 = (f32[1,64,256]{2,1,0:T(8,128)S(1)}, f32[1,64,256]{2,1,0:T(8,128)S(1)}, u32[]{:S(2)}, u32[]{:S(2)}) collective-permute-start(f32[1,64,256]{2,1,0:T(8,128)S(1)} %fusion.3), channel_id=1, source_target_pairs={{0,1},{1,0},{2,3},{3,2},{4,5},{5,4},{6,7},{7,6},{8,9},{9,8},{10,11... | collective-permute-start | bytes 196616 | tf_op jit(solution)/shard_map/ppermute | solution.py:69
  65.7 5.2 %collective-permute-start.12 = (f32[1,64,256]{2,1,0:T(8,128)S(1)}, f32[1,64,256]{2,1,0:T(8,128)S(1)}, u32[]{:S(2)}, u32[]{:S(2)}) collective-permute-start(f32[1,64,256]{2,1,0:T(8,128)S(1)} %add.80), channel_id=1, source_target_pairs={{0,2},{1,3},{2,0},{3,1},{4,6},{5,7},{6,4},{7,5},{8,10},{9,11},{10,... | collective-permute-start | bytes 196616 | tf_op jit(solution)/shard_map/ppermute | solution.py:69
  71.0 6.2 %collective-permute-start.18 = (f32[1,192,256]{2,1,0:T(8,128)S(1)}, f32[1,192,256]{2,1,0:T(8,128)S(1)}, u32[]{:S(2)}, u32[]{:S(2)}) collective-permute-start(f32[1,192,256]{2,1,0:T(8,128)S(1)} %pad_maximum_fusion.1.refs_0_), channel_id=1, source_target_pairs={{0,8},{4,12},{8,0},{12,4},{16,24},{20,28},{24,16},{28,20},{1,9},{5... | collective-permute-start | bytes 589832 | tf_op jit(solution)/shard_map/ppermute | solution.py:69
  72.8 7.8 %collective-permute-start.19 = (f32[1,192,256]{2,1,0:T(8,128)S(1)}, f32[1,192,256]{2,1,0:T(8,128)S(1)}, u32[]{:S(2)}, u32[]{:S(2)}) collective-permute-start(f32[1,192,256]{2,1,0:T(8,128)S(1)} %pad_maximum_fusion.1.refs_0_), channel_id=1, source_target_pairs={{0,16},{4,20},{8,24},{12,28},{16,0},{20,4},{24,8},{28,12},{1,17},{... | collective-permute-start | bytes 589832 | tf_op jit(solution)/shard_map/ppermute | solution.py:69
  72.8 7.8 %collective-permute-start.20 = (f32[1,192,256]{2,1,0:T(8,128)S(1)}, f32[1,192,256]{2,1,0:T(8,128)S(1)}, u32[]{:S(2)}, u32[]{:S(2)}) collective-permute-start(f32[1,192,256]{2,1,0:T(8,128)S(1)} %pad_maximum_fusion.1.refs_0_), channel_id=1, source_target_pairs={{0,24},{4,28},{8,16},{12,20},{16,8},{20,12},{24,0},{28,4},{1,25},{... | collective-permute-start | bytes 589832 | tf_op jit(solution)/shard_map/ppermute | solution.py:69
  80.7 7.5 %collective-permute-start.21 = (f32[4,128,256]{2,1,0:T(8,128)S(1)}, f32[4,128,256]{2,1,0:T(8,128)S(1)}, u32[]{:S(2)}, u32[]{:S(2)}) collective-permute-start(f32[4,128,256]{2,1,0:T(8,128)S(1)} %pad_maximum_fusion.own_ref), channel_id=1, source_target_pairs={{0,4},{4,0},{8,12},{12,8},{16,20},{20,16},{24,28},{28,24},{1,5},{5... | collective-permute-start | bytes 1572872 | tf_op jit(solution)/shard_map/ppermute | solution.py:69
  80.9 7.4 %copy-start = (f32[512,512]{1,0:T(8,128)S(1)}, f32[512,512]{1,0:T(8,128)}, u32[]{:S(2)}) copy-start(f32[512,512]{1,0:T(8,128)} %shard_map.77.z_ref) | copy-start | bytes 3145732
  80.9 16.7 %collective-permute-start.25 = (f32[1,256,256]{2,1,0:T(8,128)S(1)}, f32[1,256,256]{2,1,0:T(8,128)S(1)}, u32[]{:S(2)}, u32[]{:S(2)}) collective-permute-start(f32[1,256,256]{2,1,0:T(8,128)S(1)} %bitcast.12), channel_id=1, source_target_pairs={{0,2},{1,3},{2,0},{3,1},{4,6},{5,7},{6,4},{7,5},{8,10},{9,11},{10,... | collective-permute-start | bytes 786440 | tf_op jit(solution)/shard_map/ppermute | solution.py:69
  82.2 15.4 %collective-permute-start.26 = (f32[1,256,256]{2,1,0:T(8,128)S(1)}, f32[1,256,256]{2,1,0:T(8,128)S(1)}, u32[]{:S(2)}, u32[]{:S(2)}) collective-permute-start(f32[1,256,256]{2,1,0:T(8,128)S(1)} %bitcast.13), channel_id=1, source_target_pairs={{0,1},{1,0},{2,3},{3,2},{4,5},{5,4},{6,7},{7,6},{8,9},{9,8},{10,11... | collective-permute-start | bytes 786440 | tf_op jit(solution)/shard_map/ppermute | solution.py:69
  90.1 6.7 %collective-permute-start.22 = (f32[1,64,256]{2,1,0:T(8,128)S(1)}, f32[1,64,256]{2,1,0:T(8,128)S(1)}, u32[]{:S(2)}, u32[]{:S(2)}) collective-permute-start(f32[1,64,256]{2,1,0:T(8,128)S(1)} %get-tuple-element.114), channel_id=1, source_target_pairs={{0,8},{4,12},{8,0},{12,4},{16,24},{20,28},{24,16},{28,20},{1,9},{5... | collective-permute-start | bytes 196616 | tf_op jit(solution)/shard_map/ppermute | solution.py:69
  91.6 5.3 %collective-permute-start.23 = (f32[1,64,256]{2,1,0:T(8,128)S(1)}, f32[1,64,256]{2,1,0:T(8,128)S(1)}, u32[]{:S(2)}, u32[]{:S(2)}) collective-permute-start(f32[1,64,256]{2,1,0:T(8,128)S(1)} %get-tuple-element.113), channel_id=1, source_target_pairs={{0,16},{4,20},{8,24},{12,28},{16,0},{20,4},{24,8},{28,12},{1,17},{... | collective-permute-start | bytes 196616 | tf_op jit(solution)/shard_map/ppermute | solution.py:69
  92.4 5.2 %collective-permute-start.24 = (f32[1,64,256]{2,1,0:T(8,128)S(1)}, f32[1,64,256]{2,1,0:T(8,128)S(1)}, u32[]{:S(2)}, u32[]{:S(2)}) collective-permute-start(f32[1,64,256]{2,1,0:T(8,128)S(1)} %get-tuple-element.112), channel_id=1, source_target_pairs={{0,24},{4,28},{8,16},{12,20},{16,8},{20,12},{24,0},{28,4},{1,25},{... | collective-permute-start | bytes 196616 | tf_op jit(solution)/shard_map/ppermute | solution.py:69
  96.8 17.4 %collective-permute-start.34 = (f32[4,256,256]{2,1,0:T(8,128)S(1)}, f32[4,256,256]{2,1,0:T(8,128)S(1)}, u32[]{:S(2)}, u32[]{:S(2)}) collective-permute-start(f32[4,256,256]{2,1,0:T(8,128)S(1)} %constant_dynamic-update-slice_fusion.refs_4_), channel_id=1, source_target_pairs={{0,4},{4,0},{8,12},{12,8},{16,20},{20,16},{24,28},{28,24},{1,5},{5... | collective-permute-start | bytes 3145736 | tf_op jit(solution)/shard_map/ppermute | solution.py:69
  97.6 4.3 %collective-permute-start.27 = (f32[1,64,256]{2,1,0:T(8,128)S(1)}, f32[1,64,256]{2,1,0:T(8,128)S(1)}, u32[]{:S(2)}, u32[]{:S(2)}) collective-permute-start(f32[1,64,256]{2,1,0:T(8,128)S(1)} %fusion.2), channel_id=1, source_target_pairs={{0,1},{1,0},{2,3},{3,2},{4,5},{5,4},{6,7},{7,6},{8,9},{9,8},{10,11... | collective-permute-start | bytes 196616 | tf_op jit(solution)/shard_map/ppermute | solution.py:69
  101.9 8.8 %collective-permute-start.29 = (f32[1,256,256]{2,1,0:T(8,128)S(1)}, f32[1,256,256]{2,1,0:T(8,128)S(1)}, u32[]{:S(2)}, u32[]{:S(2)}) collective-permute-start(f32[1,256,256]{2,1,0:T(8,128)S(1)} %collective-permute-done.25.refs_1_), channel_id=1, source_target_pairs={{0,1},{1,0},{2,3},{3,2},{4,5},{5,4},{6,7},{7,6},{8,9},{9,8},{10,11... | collective-permute-start | bytes 786440 | tf_op jit(solution)/shard_map/ppermute | solution.py:69
  102.8 6.7 %collective-permute-start.28 = (f32[1,64,256]{2,1,0:T(8,128)S(1)}, f32[1,64,256]{2,1,0:T(8,128)S(1)}, u32[]{:S(2)}, u32[]{:S(2)}) collective-permute-start(f32[1,64,256]{2,1,0:T(8,128)S(1)} %add.87), channel_id=1, source_target_pairs={{0,2},{1,3},{2,0},{3,1},{4,6},{5,7},{6,4},{7,5},{8,10},{9,11},{10,... | collective-permute-start | bytes 196616 | tf_op jit(solution)/shard_map/ppermute | solution.py:69
  110.8 3.5 %collective-permute-start.33 = (f32[2,256,256]{2,1,0:T(8,128)S(1)}, f32[2,256,256]{2,1,0:T(8,128)S(1)}, u32[]{:S(2)}, u32[]{:S(2)}) collective-permute-start(f32[2,256,256]{2,1,0:T(8,128)S(1)} %shard_map.83.own_ref), channel_id=1, source_target_pairs={{0,4},{4,0},{8,12},{12,8},{16,20},{20,16},{24,28},{28,24},{1,5},{5... | collective-permute-start | bytes 1572872 | tf_op jit(solution)/shard_map/ppermute | solution.py:69
  110.8 7.8 %collective-permute-start.30 = (f32[1,64,256]{2,1,0:T(8,128)S(1)}, f32[1,64,256]{2,1,0:T(8,128)S(1)}, u32[]{:S(2)}, u32[]{:S(2)}) collective-permute-start(f32[1,64,256]{2,1,0:T(8,128)S(1)} %add.88), channel_id=1, source_target_pairs={{0,8},{4,12},{8,0},{12,4},{16,24},{20,28},{24,16},{28,20},{1,9},{5... | collective-permute-start | bytes 196616 | tf_op jit(solution)/shard_map/ppermute | solution.py:69
  112.3 6.2 %collective-permute-start.31 = (f32[1,64,256]{2,1,0:T(8,128)S(1)}, f32[1,64,256]{2,1,0:T(8,128)S(1)}, u32[]{:S(2)}, u32[]{:S(2)}) collective-permute-start(f32[1,64,256]{2,1,0:T(8,128)S(1)} %add.88), channel_id=1, source_target_pairs={{0,16},{4,20},{8,24},{12,28},{16,0},{20,4},{24,8},{28,12},{1,17},{... | collective-permute-start | bytes 196616 | tf_op jit(solution)/shard_map/ppermute | solution.py:69
  112.5 6.0 %collective-permute-start.32 = (f32[1,64,256]{2,1,0:T(8,128)S(1)}, f32[1,64,256]{2,1,0:T(8,128)S(1)}, u32[]{:S(2)}, u32[]{:S(2)}) collective-permute-start(f32[1,64,256]{2,1,0:T(8,128)S(1)} %add.88), channel_id=1, source_target_pairs={{0,24},{4,28},{8,16},{12,20},{16,8},{20,12},{24,0},{28,4},{1,25},{... | collective-permute-start | bytes 196616 | tf_op jit(solution)/shard_map/ppermute | solution.py:69
  118.7 1.6 %collective-permute-start.35 = (f32[4,64,256]{2,1,0:T(8,128)S(1)}, f32[4,64,256]{2,1,0:T(8,128)S(1)}, u32[]{:S(2)}, u32[]{:S(2)}) collective-permute-start(f32[4,64,256]{2,1,0:T(8,128)S(1)} %constant_dynamic-update-slice_fusion.4.middle_own_ref), channel_id=1, source_target_pairs={{0,4},{4,0},{8,12},{12,8},{16,20},{20,16},{24,28},{28,24},{1,5},{5... | collective-permute-start | bytes 786440 | tf_op jit(solution)/shard_map/ppermute | solution.py:69

commit v9 on v8

--- a/solution.py
+++ b/solution.py
@@ -507,7 +507,7 @@
         middle_ref[pl.ds(block_start(place, i, extent), extent), :] = middle_own_ref[i] + middle_other_ref[i]
     left = jnp.where(core == 0, own_ref[1], other_ref[1])
     right = jnp.where(core == 0, other_ref[1], own_ref[1])
-    out_ref[...] = highest(highest(left, middle_ref[...]), right, 1, 1) * scale
+    out_ref[...] = parts_dot(split(parts_dot(split(left), split(middle_ref[...]))), split(right), 1, 1) * scale
 
 
 def finish(spot, own, other, middle_own, middle_other, scale):

time: 123 us -> 122 us (level)
  no operation moved by 1% of the time
where the time goes in v9:
time: 122 us
  Pallas kernels  53.4 us (44%)
  starting transfers between devices  40.9 us (34%)
  waiting for transfers between devices  23.6 us (19%)
  other arithmetic  2.66 us (2%)
    ppermute x36, starting transfers between devices, swap(): lax.ppermute(values, axis, [(i, i ^ mask) for i in range(lax.axis_size(ax...  40.9 us
    ppermute x36, waiting for transfers between devices, swap(): lax.ppermute(values, axis, [(i, i ^ mask) for i in range(lax.axis_size(ax...  23.6 us
    pallas_call x1, Pallas kernels, sketch_terms(): call(sketch_kernel, (float_shape(rows // TILES, k),) * 4 + (float_shape(c...  15.5 us
    pallas_call x1, Pallas kernels, core_terms(): call(core_kernel, float_shape(s_core, s_core), [SCALAR] + [OUTSIDE] * 3,...  13.4 us
    pallas_call x2, Pallas kernels, factor_next(): call(functools.partial(factor_next_kernel, steps), (float_shape(2, n, n),...  6.16 us
    pallas_call x1, Pallas kernels, factor_start(): call(functools.partial(factor_start_kernel, (0, 1), len(parts)), (float_s...  4.82 us
    pallas_call x1, Pallas kernels, bases(): call(functools.partial(basis_kernel, len(ranges)), (float_shape(lines * r...  4.29 us
    pallas_call x1, Pallas kernels, factor_end(): call(functools.partial(factor_end_kernel, (n // BASE - 1, n // BASE)), fl...  4.08 us
  transfers between devices with their start and end apart: 36, of which 16 were waited for; matrix products, arithmetic and copies ran while one was open for 2% of the time, Pallas kernels for 28%

profile of v9, /device:TPU:0, one launch (start us, length us, event | category | flops | bytes accessed | tf_op | source)
XLA Modules:
  0.0 122.1 jit_solution(10529708143146890467)
XLA Ops:
  0.6 0.6 pad_add_fusion.spot_ref
  1.3 15.5 %shard_map.76 = (f32[256,256]{1,0:T(8,128)}, f32[256,256]{1,0:T(8,128)}, f32[256,256]{1,0:T(8,128)}, f32[256,256]{1,0:T(8,128)}, f32[4,384,256]{2,1,0:T(8,128)}, /*index=5*/f32[4,384,256]{2,1,0:T(8,128)}) custom-call(s32[4]{0:T(128)} %pad_add_fusion.spot_ref, f32[1024,2048]{1,0:T(8,128)} %window_ref.3, f32[2048,256]{1,0:T(8,128)} %test_ref.1, ...), custom_call_target="tpu_custom_call" | custom-call | flops 6442450944 | bytes 4194304 | tf_op jit(solution)/shard_map/pallas_call | solution.py:209
  16.8 0.5 collective-permute-start.1
  17.4 2.7 %collective-permute-start = (f32[256,256]{1,0:T(8,128)}, f32[256,256]{1,0:T(8,128)S(1)}, u32[]{:S(2)}, u32[]{:S(2)}) collective-permute-start(f32[256,256]{1,0:T(8,128)} %get-tuple-element.57), channel_id=1, source_target_pairs={{0,1},{1,0},{2,3},{3,2},{4,5},{5,4},{6,7},{7,6},{8,9},{9,8},{10,11... | collective-permute-start | bytes 786440 | tf_op jit(solution)/shard_map/ppermute | solution.py:69
  20.0 0.1 collective-permute-start.3
  20.1 0.5 collective-permute-done.1
  20.6 1.6 %add.69 = f32[4,384,256]{2,1,0:T(8,128)S(1)} add(f32[4,384,256]{2,1,0:T(8,128)} %get-tuple-element.58, f32[4,384,256]{2,1,0:T(8,128)S(1)} %collective-permute-done.1) | non-fusion elementwise | flops 393216 | bytes 4718592 | tf_op jit(solution)/shard_map/add | solution.py:537
  22.2 0.1 fusion.5
  22.3 2.9 %collective-permute-start.4 = (f32[1,384,256]{2,1,0:T(8,128)S(1)}, f32[1,384,256]{2,1,0:T(8,128)S(1)}, u32[]{:S(2)}, u32[]{:S(2)}) collective-permute-start(f32[1,384,256]{2,1,0:T(8,128)S(1)} %get-tuple-element.109), channel_id=1, source_target_pairs={{0,8},{4,12},{8,0},{12,4},{16,24},{20,28},{24,16},{28,20},{1,9},{5... | collective-permute-start | bytes 1179656 | tf_op jit(solution)/shard_map/ppermute | solution.py:69
  25.2 1.5 %collective-permute-start.5 = (f32[1,384,256]{2,1,0:T(8,128)S(1)}, f32[1,384,256]{2,1,0:T(8,128)S(1)}, u32[]{:S(2)}, u32[]{:S(2)}) collective-permute-start(f32[1,384,256]{2,1,0:T(8,128)S(1)} %get-tuple-element.108), channel_id=1, source_target_pairs={{0,16},{4,20},{8,24},{12,28},{16,0},{20,4},{24,8},{28,12},{1,17},{... | collective-permute-start | bytes 1179656 | tf_op jit(solution)/shard_map/ppermute | solution.py:69
  26.8 0.6 collective-permute-done
  27.4 3.0 %collective-permute-start.2 = (f32[256,256]{1,0:T(8,128)S(1)}, f32[256,256]{1,0:T(8,128)S(1)}, u32[]{:S(2)}, u32[]{:S(2)}) collective-permute-start(f32[256,256]{1,0:T(8,128)S(1)} %add.70), channel_id=1, source_target_pairs={{0,2},{1,3},{2,0},{3,1},{4,6},{5,7},{6,4},{7,5},{8,10},{9,11},{10,... | collective-permute-start | bytes 786440 | tf_op jit(solution)/shard_map/ppermute | solution.py:69
  30.4 13.4 %shard_map.77.z_ref = f32[512,512]{1,0:T(8,128)} custom-call(s32[4]{0:T(128)} %pad_add_fusion.spot_ref, f32[1024,2048]{1,0:T(8,128)} %window_ref.3, f32[512,2048]{1,0:T(8,128)} %right_ref.3, f32[512,1024]{1,0:T(8,128)} %left_ref.3), custom_call_target="tpu_custom_call" | custom-call | flops 9663676416 | bytes 4194304 | tf_op jit(solution)/shard_map/pallas_call | solution.py:264
  43.9 0.6 collective-permute-done.5
  44.5 0.1 fusion.1
  44.7 0.2 copy-done.2
  44.8 0.1 slice_bitcast_fusion.1
  44.9 1.4 %shard_map.78 = (f32[4,64,256]{2,1,0:T(8,128)S(1)}, f32[4,64,256]{2,1,0:T(8,128)S(1)}) custom-call(s32[4]{0:T(128)S(1)} %copy-done.1, f32[256,256]{1,0:T(8,128)S(1)} %get-tuple-element.118.range_ref, f32[256,256]{1,0:T(8,128)S(1)} %get-tuple-element.111.co_ref), custom_call_target="tpu_custom_call" | custom-call | flops 402653184 | bytes 4194304 | tf_op jit(solution)/shard_map/pallas_call | solution.py:288
  46.3 0.1 collective-permute-start.7
  46.4 1.5 %collective-permute-done.7 = f32[4,64,256]{2,1,0:T(8,128)S(1)} collective-permute-done((f32[4,64,256]{2,1,0:T(8,128)S(1)}, f32[4,64,256]{2,1,0:T(8,128)S(1)}, u32[]{:S(2)}, u32[]{:S(2)}) %collective-permute-start.7) | collective-permute-done | bytes 262176 | tf_op jit(solution)/shard_map/ppermute | solution.py:69
  48.0 2.5 %collective-permute-start.10 = (f32[1,64,256]{2,1,0:T(8,128)S(1)}, f32[1,64,256]{2,1,0:T(8,128)S(1)}, u32[]{:S(2)}, u32[]{:S(2)}) collective-permute-start(f32[1,64,256]{2,1,0:T(8,128)S(1)} %get-tuple-element.115), channel_id=1, source_target_pairs={{0,24},{4,28},{8,16},{12,20},{16,8},{20,12},{24,0},{28,4},{1,25},{... | collective-permute-start | bytes 196616 | tf_op jit(solution)/shard_map/ppermute | solution.py:69
  50.5 0.5 collective-permute-start.8
  51.0 0.5 collective-permute-start.9
  51.6 1.6 %collective-permute-start.16 = (f32[1,128,256]{2,1,0:T(8,128)S(1)}, f32[1,128,256]{2,1,0:T(8,128)S(1)}, u32[]{:S(2)}, u32[]{:S(2)}) collective-permute-start(f32[1,128,256]{2,1,0:T(8,128)S(1)} %slice_bitcast_fusion), channel_id=1, source_target_pairs={{0,1},{1,0},{2,3},{3,2},{4,5},{5,4},{6,7},{7,6},{8,9},{9,8},{10,11... | collective-permute-start | bytes 393224 | tf_op jit(solution)/shard_map/ppermute | solution.py:69
  53.2 0.4 collective-permute-done.10
  53.6 1.1 collective-permute-done.8
  54.8 0.5 collective-permute-done.9
  55.3 1.6 %collective-permute-start.13 = (f32[1,256,256]{2,1,0:T(8,128)S(1)}, f32[1,256,256]{2,1,0:T(8,128)S(1)}, u32[]{:S(2)}, u32[]{:S(2)}) collective-permute-start(f32[1,256,256]{2,1,0:T(8,128)S(1)} %get-tuple-element.95), channel_id=1, source_target_pairs={{0,8},{4,12},{8,0},{12,4},{16,24},{20,28},{24,16},{28,20},{1,9},{5... | collective-permute-start | bytes 786440 | tf_op jit(solution)/shard_map/ppermute | solution.py:69
  56.9 0.7 collective-permute-start.14
  57.6 1.3 %collective-permute-start.15 = (f32[1,256,256]{2,1,0:T(8,128)S(1)}, f32[1,256,256]{2,1,0:T(8,128)S(1)}, u32[]{:S(2)}, u32[]{:S(2)}) collective-permute-start(f32[1,256,256]{2,1,0:T(8,128)S(1)} %get-tuple-element.95), channel_id=1, source_target_pairs={{0,24},{4,28},{8,16},{12,20},{16,8},{20,12},{24,0},{28,4},{1,25},{... | collective-permute-start | bytes 786440 | tf_op jit(solution)/shard_map/ppermute | solution.py:69
  58.9 2.5 %collective-permute-start.17 = (f32[1,128,256]{2,1,0:T(8,128)S(1)}, f32[1,128,256]{2,1,0:T(8,128)S(1)}, u32[]{:S(2)}, u32[]{:S(2)}) collective-permute-start(f32[1,128,256]{2,1,0:T(8,128)S(1)} %fusion.4), channel_id=1, source_target_pairs={{0,2},{1,3},{2,0},{3,1},{4,6},{5,7},{6,4},{7,5},{8,10},{9,11},{10,... | collective-permute-start | bytes 393224 | tf_op jit(solution)/shard_map/ppermute | solution.py:69
  61.4 1.6 %collective-permute-start.11 = (f32[1,64,256]{2,1,0:T(8,128)S(1)}, f32[1,64,256]{2,1,0:T(8,128)S(1)}, u32[]{:S(2)}, u32[]{:S(2)}) collective-permute-start(f32[1,64,256]{2,1,0:T(8,128)S(1)} %fusion.3), channel_id=1, source_target_pairs={{0,1},{1,0},{2,3},{3,2},{4,5},{5,4},{6,7},{7,6},{8,9},{9,8},{10,11... | collective-permute-start | bytes 196616 | tf_op jit(solution)/shard_map/ppermute | solution.py:69
  63.0 2.7 %collective-permute-done.11 = f32[1,64,256]{2,1,0:T(8,128)S(1)} collective-permute-done((f32[1,64,256]{2,1,0:T(8,128)S(1)}, f32[1,64,256]{2,1,0:T(8,128)S(1)}, u32[]{:S(2)}, u32[]{:S(2)}) %collective-permute-start.11) | collective-permute-done | bytes 65568 | tf_op jit(solution)/shard_map/ppermute | solution.py:69
  65.7 1.5 %collective-permute-start.12 = (f32[1,64,256]{2,1,0:T(8,128)S(1)}, f32[1,64,256]{2,1,0:T(8,128)S(1)}, u32[]{:S(2)}, u32[]{:S(2)}) collective-permute-start(f32[1,64,256]{2,1,0:T(8,128)S(1)} %add.80), channel_id=1, source_target_pairs={{0,2},{1,3},{2,0},{3,1},{4,6},{5,7},{6,4},{7,5},{8,10},{9,11},{10,... | collective-permute-start | bytes 196616 | tf_op jit(solution)/shard_map/ppermute | solution.py:69
  67.3 3.7 %collective-permute-done.12 = f32[1,64,256]{2,1,0:T(8,128)S(1)} collective-permute-done((f32[1,64,256]{2,1,0:T(8,128)S(1)}, f32[1,64,256]{2,1,0:T(8,128)S(1)}, u32[]{:S(2)}, u32[]{:S(2)}) %collective-permute-start.12) | collective-permute-done | bytes 65568 | tf_op jit(solution)/shard_map/ppermute | solution.py:69
  71.0 1.8 %collective-permute-start.18 = (f32[1,192,256]{2,1,0:T(8,128)S(1)}, f32[1,192,256]{2,1,0:T(8,128)S(1)}, u32[]{:S(2)}, u32[]{:S(2)}) collective-permute-start(f32[1,192,256]{2,1,0:T(8,128)S(1)} %pad_maximum_fusion.1.refs_0_), channel_id=1, source_target_pairs={{0,8},{4,12},{8,0},{12,4},{16,24},{20,28},{24,16},{28,20},{1,9},{5... | collective-permute-start | bytes 589832 | tf_op jit(solution)/shard_map/ppermute | solution.py:69
  72.8 1.7 %collective-permute-start.20 = (f32[1,192,256]{2,1,0:T(8,128)S(1)}, f32[1,192,256]{2,1,0:T(8,128)S(1)}, u32[]{:S(2)}, u32[]{:S(2)}) collective-permute-start(f32[1,192,256]{2,1,0:T(8,128)S(1)} %pad_maximum_fusion.1.refs_0_), channel_id=1, source_target_pairs={{0,24},{4,28},{8,16},{12,20},{16,8},{20,12},{24,0},{28,4},{1,25},{... | collective-permute-start | bytes 589832 | tf_op jit(solution)/shard_map/ppermute | solution.py:69
  74.5 2.7 %collective-permute-done.18.refs_1_ = f32[1,192,256]{2,1,0:T(8,128)S(1)} collective-permute-done((f32[1,192,256]{2,1,0:T(8,128)S(1)}, f32[1,192,256]{2,1,0:T(8,128)S(1)}, u32[]{:S(2)}, u32[]{:S(2)}) %collective-permute-start.18) | collective-permute-done | bytes 196640 | tf_op jit(solution)/shard_map/ppermute | solution.py:69
  77.2 3.4 %collective-permute-done.19.refs_2_ = f32[1,192,256]{2,1,0:T(8,128)S(1)} collective-permute-done((f32[1,192,256]{2,1,0:T(8,128)S(1)}, f32[1,192,256]{2,1,0:T(8,128)S(1)}, u32[]{:S(2)}, u32[]{:S(2)}) %collective-permute-start.19) | collective-permute-done | bytes 196640 | tf_op jit(solution)/shard_map/ppermute | solution.py:69
  80.7 0.1 collective-permute-start.21
  80.9 1.3 %collective-permute-start.25 = (f32[1,256,256]{2,1,0:T(8,128)S(1)}, f32[1,256,256]{2,1,0:T(8,128)S(1)}, u32[]{:S(2)}, u32[]{:S(2)}) collective-permute-start(f32[1,256,256]{2,1,0:T(8,128)S(1)} %bitcast.12), channel_id=1, source_target_pairs={{0,2},{1,3},{2,0},{3,1},{4,6},{5,7},{6,4},{7,5},{8,10},{9,11},{10,... | collective-permute-start | bytes 786440 | tf_op jit(solution)/shard_map/ppermute | solution.py:69
  82.2 1.2 %collective-permute-start.26 = (f32[1,256,256]{2,1,0:T(8,128)S(1)}, f32[1,256,256]{2,1,0:T(8,128)S(1)}, u32[]{:S(2)}, u32[]{:S(2)}) collective-permute-start(f32[1,256,256]{2,1,0:T(8,128)S(1)} %bitcast.13), channel_id=1, source_target_pairs={{0,1},{1,0},{2,3},{3,2},{4,5},{5,4},{6,7},{7,6},{8,9},{9,8},{10,11... | collective-permute-start | bytes 786440 | tf_op jit(solution)/shard_map/ppermute | solution.py:69
  83.4 4.8 %shard_map.79 = (f32[2,256,256]{2,1,0:T(8,128)S(1)}, f32[256,256]{1,0:T(8,128)S(1)}) custom-call(s32[4]{0:T(128)S(1)} %copy-done.1, f32[1,192,256]{2,1,0:T(8,128)S(1)} %pad_maximum_fusion.1.refs_0_, f32[1,192,256]{2,1,0:T(8,128)S(1)} %collective-permute-done.18.refs_1_, f32[1,192,256]{2,1,0:T(8,128)S(1)} %collective-permute-done.19.refs_2_, ...), custom_call_target="tpu_custom_call" | custom-call | flops 1677721600 | bytes 4194304 | tf_op jit(solution)/shard_map/pallas_call | solution.py:429
  88.2 1.8 %shard_map.81 = f32[4,64,256]{2,1,0:T(8,128)S(1)} custom-call(s32[4]{0:T(128)S(1)} %copy-done.1, f32[512,512]{1,0:T(8,128)S(1)} %copy-done, f32[4,128,256]{2,1,0:T(8,128)S(1)} %pad_maximum_fusion.own_ref, f32[4,128,256]{2,1,0:T(8,128)S(1)} %collective-permute-done.21.other_ref), custom_call_target="tpu_custom_call" | custom-call | flops 402653184 | bytes 4194304 | tf_op jit(solution)/shard_map/pallas_call | solution.py:308
  90.1 1.5 %collective-permute-start.22 = (f32[1,64,256]{2,1,0:T(8,128)S(1)}, f32[1,64,256]{2,1,0:T(8,128)S(1)}, u32[]{:S(2)}, u32[]{:S(2)}) collective-permute-start(f32[1,64,256]{2,1,0:T(8,128)S(1)} %get-tuple-element.114), channel_id=1, source_target_pairs={{0,8},{4,12},{8,0},{12,4},{16,24},{20,28},{24,16},{28,20},{1,9},{5... | collective-permute-start | bytes 196616 | tf_op jit(solution)/shard_map/ppermute | solution.py:69
  91.6 0.8 collective-permute-start.23
  92.4 1.3 %collective-permute-start.24 = (f32[1,64,256]{2,1,0:T(8,128)S(1)}, f32[1,64,256]{2,1,0:T(8,128)S(1)}, u32[]{:S(2)}, u32[]{:S(2)}) collective-permute-start(f32[1,64,256]{2,1,0:T(8,128)S(1)} %get-tuple-element.112), channel_id=1, source_target_pairs={{0,24},{4,28},{8,16},{12,20},{16,8},{20,12},{24,0},{28,4},{1,25},{... | collective-permute-start | bytes 196616 | tf_op jit(solution)/shard_map/ppermute | solution.py:69
  93.7 3.1 %shard_map.80 = (f32[2,256,256]{2,1,0:T(8,128)S(1)}, f32[256,256]{1,0:T(8,128)S(1)}) custom-call(f32[2,256,256]{2,1,0:T(8,128)S(1)} %get-tuple-element.72.begun_ref, f32[256,256]{1,0:T(8,128)S(1)} %get-tuple-element.73.begun_upper_ref), custom_call_target="tpu_custom_call" | custom-call | flops 1677721600 | bytes 4194304 | tf_op jit(solution)/shard_map/pallas_call | solution.py:437
  96.8 0.1 collective-permute-start.34
  96.9 0.6 collective-permute-done.24
  97.6 0.2 collective-permute-start.27
  97.8 3.0 %shard_map.82 = (f32[2,256,256]{2,1,0:T(8,128)S(1)}, f32[256,256]{1,0:T(8,128)S(1)}) custom-call(f32[2,256,256]{2,1,0:T(8,128)S(1)} %get-tuple-element.79.begun_ref, f32[256,256]{1,0:T(8,128)S(1)} %get-tuple-element.80.begun_upper_ref), custom_call_target="tpu_custom_call" | custom-call | flops 1677721600 | bytes 4194304 | tf_op jit(solution)/shard_map/pallas_call | solution.py:437
  100.9 1.1 collective-permute-done.27
  101.9 0.9 collective-permute-start.29
  102.8 1.3 %collective-permute-start.28 = (f32[1,64,256]{2,1,0:T(8,128)S(1)}, f32[1,64,256]{2,1,0:T(8,128)S(1)}, u32[]{:S(2)}, u32[]{:S(2)}) collective-permute-start(f32[1,64,256]{2,1,0:T(8,128)S(1)} %add.87), channel_id=1, source_target_pairs={{0,2},{1,3},{2,0},{3,1},{4,6},{5,7},{6,4},{7,5},{8,10},{9,11},{10,... | collective-permute-start | bytes 196616 | tf_op jit(solution)/shard_map/ppermute | solution.py:69
  104.1 4.1 %shard_map.83.own_ref = f32[2,256,256]{2,1,0:T(8,128)S(1)} custom-call(f32[2,256,256]{2,1,0:T(8,128)S(1)} %get-tuple-element.86.begun_ref, f32[256,256]{1,0:T(8,128)S(1)} %get-tuple-element.87.begun_upper_ref), custom_call_target="tpu_custom_call" | custom-call | flops 1677721600 | bytes 4194304 | tf_op jit(solution)/shard_map/pallas_call | solution.py:444
  108.2 1.3 %collective-permute-done.28 = f32[1,64,256]{2,1,0:T(8,128)S(1)} collective-permute-done((f32[1,64,256]{2,1,0:T(8,128)S(1)}, f32[1,64,256]{2,1,0:T(8,128)S(1)}, u32[]{:S(2)}, u32[]{:S(2)}) %collective-permute-start.28) | collective-permute-done | bytes 65568 | tf_op jit(solution)/shard_map/ppermute | solution.py:69
  109.5 1.2 %collective-permute-done.29.refs_3_ = f32[1,256,256]{2,1,0:T(8,128)S(1)} collective-permute-done((f32[1,256,256]{2,1,0:T(8,128)S(1)}, f32[1,256,256]{2,1,0:T(8,128)S(1)}, u32[]{:S(2)}, u32[]{:S(2)}) %collective-permute-start.29) | collective-permute-done | bytes 262176 | tf_op jit(solution)/shard_map/ppermute | solution.py:69
  110.8 1.6 %collective-permute-start.30 = (f32[1,64,256]{2,1,0:T(8,128)S(1)}, f32[1,64,256]{2,1,0:T(8,128)S(1)}, u32[]{:S(2)}, u32[]{:S(2)}) collective-permute-start(f32[1,64,256]{2,1,0:T(8,128)S(1)} %add.88), channel_id=1, source_target_pairs={{0,8},{4,12},{8,0},{12,4},{16,24},{20,28},{24,16},{28,20},{1,9},{5... | collective-permute-start | bytes 196616 | tf_op jit(solution)/shard_map/ppermute | solution.py:69
  112.3 0.2 collective-permute-start.31
  112.5 1.7 %collective-permute-start.32 = (f32[1,64,256]{2,1,0:T(8,128)S(1)}, f32[1,64,256]{2,1,0:T(8,128)S(1)}, u32[]{:S(2)}, u32[]{:S(2)}) collective-permute-start(f32[1,64,256]{2,1,0:T(8,128)S(1)} %add.88), channel_id=1, source_target_pairs={{0,24},{4,28},{8,16},{12,20},{16,8},{20,12},{24,0},{28,4},{1,25},{... | collective-permute-start | bytes 196616 | tf_op jit(solution)/shard_map/ppermute | solution.py:69
  114.3 4.3 %shard_map.84 = (f32[1024,256]{1,0:T(8,128)}, f32[256,2048]{1,0:T(8,128)}) custom-call(s32[4]{0:T(128)S(1)} %copy-done.1, f32[2,256,256]{2,1,0:T(8,128)S(1)} %shard_map.83.own_ref, f32[2,256,256]{2,1,0:T(8,128)S(1)} %collective-permute-done.33.other_ref, f32[1,256,256]{2,1,0:T(8,128)S(1)} %bitcast.14, f32[1,256,256]{2,1,0:T(8,128)S(1)} %collective-permute-done.25.refs_1_, ...), custom_call_target="tpu_custom_call" | custom-call | flops 1207959552 | bytes 4194304 | tf_op jit(solution)/shard_map/pallas_call | solution.py:492
  118.7 1.5 %collective-permute-done.35.middle_other_ref = f32[4,64,256]{2,1,0:T(8,128)S(1)} collective-permute-done((f32[4,64,256]{2,1,0:T(8,128)S(1)}, f32[4,64,256]{2,1,0:T(8,128)S(1)}, u32[]{:S(2)}, u32[]{:S(2)}) %collective-permute-start.35) | collective-permute-done | bytes 262176 | tf_op jit(solution)/shard_map/ppermute | solution.py:69
  120.3 1.9 %shard_map.85 = f32[256,256]{1,0:T(8,128)} custom-call(s32[4]{0:T(128)S(1)} %copy-done.1, f32[2,256,256]{2,1,0:T(8,128)S(1)} %shard_map.83.own_ref, f32[2,256,256]{2,1,0:T(8,128)S(1)} %collective-permute-done.33.other_ref, f32[4,64,256]{2,1,0:T(8,128)S(1)} %constant_dynamic-update-slice_fusion.4.middle_own_ref, ...), custom_call_target="tpu_custom_call" | custom-call | flops 402653184 | bytes 4194304 | tf_op jit(solution)/shard_map/pallas_call | solution.py:515
  (57 shorter events, 0.6 us)
Async XLA Ops:
  16.8 3.8 %collective-permute-start.1 = (f32[4,384,256]{2,1,0:T(8,128)}, f32[4,384,256]{2,1,0:T(8,128)S(1)}, u32[]{:S(2)}, u32[]{:S(2)}) collective-permute-start(f32[4,384,256]{2,1,0:T(8,128)} %get-tuple-element.59), channel_id=1, source_target_pairs={{0,4},{4,0},{8,12},{12,8},{16,20},{20,16},{24,28},{28,24},{1,5},{5... | collective-permute-start | bytes 4718600 | tf_op jit(solution)/shard_map/ppermute | solution.py:69
  17.4 10.0 %collective-permute-start = (f32[256,256]{1,0:T(8,128)}, f32[256,256]{1,0:T(8,128)S(1)}, u32[]{:S(2)}, u32[]{:S(2)}) collective-permute-start(f32[256,256]{1,0:T(8,128)} %get-tuple-element.57), channel_id=1, source_target_pairs={{0,1},{1,0},{2,3},{3,2},{4,5},{5,4},{6,7},{7,6},{8,9},{9,8},{10,11... | collective-permute-start | bytes 786440 | tf_op jit(solution)/shard_map/ppermute | solution.py:69
  20.0 24.6 %collective-permute-start.3 = (f32[256,256]{1,0:T(8,128)}, f32[256,256]{1,0:T(8,128)S(1)}, u32[]{:S(2)}, u32[]{:S(2)}) collective-permute-start(f32[256,256]{1,0:T(8,128)} %get-tuple-element.61), channel_id=1, source_target_pairs={{0,1},{1,0},{2,3},{3,2},{4,5},{5,4},{6,7},{7,6},{8,9},{9,8},{10,11... | collective-permute-start | bytes 786440 | tf_op jit(solution)/shard_map/ppermute | solution.py:69
  22.2 5.2 %copy-start.3 = (f32[256,256]{1,0:T(8,128)S(1)}, f32[256,256]{1,0:T(8,128)}, u32[]{:S(2)}) copy-start(f32[256,256]{1,0:T(8,128)} %get-tuple-element.56) | copy-start | bytes 786436
  22.3 21.6 %collective-permute-start.4 = (f32[1,384,256]{2,1,0:T(8,128)S(1)}, f32[1,384,256]{2,1,0:T(8,128)S(1)}, u32[]{:S(2)}, u32[]{:S(2)}) collective-permute-start(f32[1,384,256]{2,1,0:T(8,128)S(1)} %get-tuple-element.109), channel_id=1, source_target_pairs={{0,8},{4,12},{8,0},{12,4},{16,24},{20,28},{24,16},{28,20},{1,9},{5... | collective-permute-start | bytes 1179656 | tf_op jit(solution)/shard_map/ppermute | solution.py:69
  25.2 19.3 %collective-permute-start.5 = (f32[1,384,256]{2,1,0:T(8,128)S(1)}, f32[1,384,256]{2,1,0:T(8,128)S(1)}, u32[]{:S(2)}, u32[]{:S(2)}) collective-permute-start(f32[1,384,256]{2,1,0:T(8,128)S(1)} %get-tuple-element.108), channel_id=1, source_target_pairs={{0,16},{4,20},{8,24},{12,28},{16,0},{20,4},{24,8},{28,12},{1,17},{... | collective-permute-start | bytes 1179656 | tf_op jit(solution)/shard_map/ppermute | solution.py:69
  26.8 17.8 %collective-permute-start.6 = (f32[1,384,256]{2,1,0:T(8,128)S(1)}, f32[1,384,256]{2,1,0:T(8,128)S(1)}, u32[]{:S(2)}, u32[]{:S(2)}) collective-permute-start(f32[1,384,256]{2,1,0:T(8,128)S(1)} %get-tuple-element.107), channel_id=1, source_target_pairs={{0,24},{4,28},{8,16},{12,20},{16,8},{20,12},{24,0},{28,4},{1,25},{... | collective-permute-start | bytes 1179656 | tf_op jit(solution)/shard_map/ppermute | solution.py:69
  27.4 17.2 %collective-permute-start.2 = (f32[256,256]{1,0:T(8,128)S(1)}, f32[256,256]{1,0:T(8,128)S(1)}, u32[]{:S(2)}, u32[]{:S(2)}) collective-permute-start(f32[256,256]{1,0:T(8,128)S(1)} %add.70), channel_id=1, source_target_pairs={{0,2},{1,3},{2,0},{3,1},{4,6},{5,7},{6,4},{7,5},{8,10},{9,11},{10,... | collective-permute-start | bytes 786440 | tf_op jit(solution)/shard_map/ppermute | solution.py:69
  43.9 1.0 copy-start.2
  43.9 1.0 copy-start.1
  46.3 1.6 %collective-permute-start.7 = (f32[4,64,256]{2,1,0:T(8,128)S(1)}, f32[4,64,256]{2,1,0:T(8,128)S(1)}, u32[]{:S(2)}, u32[]{:S(2)}) collective-permute-start(f32[4,64,256]{2,1,0:T(8,128)S(1)} %get-tuple-element.67), channel_id=1, source_target_pairs={{0,4},{4,0},{8,12},{12,8},{16,20},{20,16},{24,28},{28,24},{1,5},{5... | collective-permute-start | bytes 786440 | tf_op jit(solution)/shard_map/ppermute | solution.py:69
  48.0 5.6 %collective-permute-start.10 = (f32[1,64,256]{2,1,0:T(8,128)S(1)}, f32[1,64,256]{2,1,0:T(8,128)S(1)}, u32[]{:S(2)}, u32[]{:S(2)}) collective-permute-start(f32[1,64,256]{2,1,0:T(8,128)S(1)} %get-tuple-element.115), channel_id=1, source_target_pairs={{0,24},{4,28},{8,16},{12,20},{16,8},{20,12},{24,0},{28,4},{1,25},{... | collective-permute-start | bytes 196616 | tf_op jit(solution)/shard_map/ppermute | solution.py:69
  50.5 4.3 %collective-permute-start.8 = (f32[1,64,256]{2,1,0:T(8,128)S(1)}, f32[1,64,256]{2,1,0:T(8,128)S(1)}, u32[]{:S(2)}, u32[]{:S(2)}) collective-permute-start(f32[1,64,256]{2,1,0:T(8,128)S(1)} %get-tuple-element.117), channel_id=1, source_target_pairs={{0,8},{4,12},{8,0},{12,4},{16,24},{20,28},{24,16},{28,20},{1,9},{5... | collective-permute-start | bytes 196616 | tf_op jit(solution)/shard_map/ppermute | solution.py:69
  51.0 4.3 %collective-permute-start.9 = (f32[1,64,256]{2,1,0:T(8,128)S(1)}, f32[1,64,256]{2,1,0:T(8,128)S(1)}, u32[]{:S(2)}, u32[]{:S(2)}) collective-permute-start(f32[1,64,256]{2,1,0:T(8,128)S(1)} %get-tuple-element.116), channel_id=1, source_target_pairs={{0,16},{4,20},{8,24},{12,28},{16,0},{20,4},{24,8},{28,12},{1,17},{... | collective-permute-start | bytes 196616 | tf_op jit(solution)/shard_map/ppermute | solution.py:69
  51.6 7.3 %collective-permute-start.16 = (f32[1,128,256]{2,1,0:T(8,128)S(1)}, f32[1,128,256]{2,1,0:T(8,128)S(1)}, u32[]{:S(2)}, u32[]{:S(2)}) collective-permute-start(f32[1,128,256]{2,1,0:T(8,128)S(1)} %slice_bitcast_fusion), channel_id=1, source_target_pairs={{0,1},{1,0},{2,3},{3,2},{4,5},{5,4},{6,7},{7,6},{8,9},{9,8},{10,11... | collective-permute-start | bytes 393224 | tf_op jit(solution)/shard_map/ppermute | solution.py:69
  55.3 15.6 %collective-permute-start.13 = (f32[1,256,256]{2,1,0:T(8,128)S(1)}, f32[1,256,256]{2,1,0:T(8,128)S(1)}, u32[]{:S(2)}, u32[]{:S(2)}) collective-permute-start(f32[1,256,256]{2,1,0:T(8,128)S(1)} %get-tuple-element.95), channel_id=1, source_target_pairs={{0,8},{4,12},{8,0},{12,4},{16,24},{20,28},{24,16},{28,20},{1,9},{5... | collective-permute-start | bytes 786440 | tf_op jit(solution)/shard_map/ppermute | solution.py:69
  56.9 14.1 %collective-permute-start.14 = (f32[1,256,256]{2,1,0:T(8,128)S(1)}, f32[1,256,256]{2,1,0:T(8,128)S(1)}, u32[]{:S(2)}, u32[]{:S(2)}) collective-permute-start(f32[1,256,256]{2,1,0:T(8,128)S(1)} %get-tuple-element.95), channel_id=1, source_target_pairs={{0,16},{4,20},{8,24},{12,28},{16,0},{20,4},{24,8},{28,12},{1,17},{... | collective-permute-start | bytes 786440 | tf_op jit(solution)/shard_map/ppermute | solution.py:69
  57.6 13.4 %collective-permute-start.15 = (f32[1,256,256]{2,1,0:T(8,128)S(1)}, f32[1,256,256]{2,1,0:T(8,128)S(1)}, u32[]{:S(2)}, u32[]{:S(2)}) collective-permute-start(f32[1,256,256]{2,1,0:T(8,128)S(1)} %get-tuple-element.95), channel_id=1, source_target_pairs={{0,24},{4,28},{8,16},{12,20},{16,8},{20,12},{24,0},{28,4},{1,25},{... | collective-permute-start | bytes 786440 | tf_op jit(solution)/shard_map/ppermute | solution.py:69
  58.9 8.3 %collective-permute-start.17 = (f32[1,128,256]{2,1,0:T(8,128)S(1)}, f32[1,128,256]{2,1,0:T(8,128)S(1)}, u32[]{:S(2)}, u32[]{:S(2)}) collective-permute-start(f32[1,128,256]{2,1,0:T(8,128)S(1)} %fusion.4), channel_id=1, source_target_pairs={{0,2},{1,3},{2,0},{3,1},{4,6},{5,7},{6,4},{7,5},{8,10},{9,11},{10,... | collective-permute-start | bytes 393224 | tf_op jit(solution)/shard_map/ppermute | solution.py:69
  61.4 4.3 %collective-permute-start.11 = (f32[1,64,256]{2,1,0:T(8,128)S(1)}, f32[1,64,256]{2,1,0:T(8,128)S(1)}, u32[]{:S(2)}, u32[]{:S(2)}) collective-permute-start(f32[1,64,256]{2,1,0:T(8,128)S(1)} %fusion.3), channel_id=1, source_target_pairs={{0,1},{1,0},{2,3},{3,2},{4,5},{5,4},{6,7},{7,6},{8,9},{9,8},{10,11... | collective-permute-start | bytes 196616 | tf_op jit(solution)/shard_map/ppermute | solution.py:69
  65.7 5.2 %collective-permute-start.12 = (f32[1,64,256]{2,1,0:T(8,128)S(1)}, f32[1,64,256]{2,1,0:T(8,128)S(1)}, u32[]{:S(2)}, u32[]{:S(2)}) collective-permute-start(f32[1,64,256]{2,1,0:T(8,128)S(1)} %add.80), channel_id=1, source_target_pairs={{0,2},{1,3},{2,0},{3,1},{4,6},{5,7},{6,4},{7,5},{8,10},{9,11},{10,... | collective-permute-start | bytes 196616 | tf_op jit(solution)/shard_map/ppermute | solution.py:69
  71.0 6.2 %collective-permute-start.18 = (f32[1,192,256]{2,1,0:T(8,128)S(1)}, f32[1,192,256]{2,1,0:T(8,128)S(1)}, u32[]{:S(2)}, u32[]{:S(2)}) collective-permute-start(f32[1,192,256]{2,1,0:T(8,128)S(1)} %pad_maximum_fusion.1.refs_0_), channel_id=1, source_target_pairs={{0,8},{4,12},{8,0},{12,4},{16,24},{20,28},{24,16},{28,20},{1,9},{5... | collective-permute-start | bytes 589832 | tf_op jit(solution)/shard_map/ppermute | solution.py:69
  72.8 7.8 %collective-permute-start.19 = (f32[1,192,256]{2,1,0:T(8,128)S(1)}, f32[1,192,256]{2,1,0:T(8,128)S(1)}, u32[]{:S(2)}, u32[]{:S(2)}) collective-permute-start(f32[1,192,256]{2,1,0:T(8,128)S(1)} %pad_maximum_fusion.1.refs_0_), channel_id=1, source_target_pairs={{0,16},{4,20},{8,24},{12,28},{16,0},{20,4},{24,8},{28,12},{1,17},{... | collective-permute-start | bytes 589832 | tf_op jit(solution)/shard_map/ppermute | solution.py:69
  72.8 7.8 %collective-permute-start.20 = (f32[1,192,256]{2,1,0:T(8,128)S(1)}, f32[1,192,256]{2,1,0:T(8,128)S(1)}, u32[]{:S(2)}, u32[]{:S(2)}) collective-permute-start(f32[1,192,256]{2,1,0:T(8,128)S(1)} %pad_maximum_fusion.1.refs_0_), channel_id=1, source_target_pairs={{0,24},{4,28},{8,16},{12,20},{16,8},{20,12},{24,0},{28,4},{1,25},{... | collective-permute-start | bytes 589832 | tf_op jit(solution)/shard_map/ppermute | solution.py:69
  80.7 7.5 %collective-permute-start.21 = (f32[4,128,256]{2,1,0:T(8,128)S(1)}, f32[4,128,256]{2,1,0:T(8,128)S(1)}, u32[]{:S(2)}, u32[]{:S(2)}) collective-permute-start(f32[4,128,256]{2,1,0:T(8,128)S(1)} %pad_maximum_fusion.own_ref), channel_id=1, source_target_pairs={{0,4},{4,0},{8,12},{12,8},{16,20},{20,16},{24,28},{28,24},{1,5},{5... | collective-permute-start | bytes 1572872 | tf_op jit(solution)/shard_map/ppermute | solution.py:69
  80.9 7.4 %copy-start = (f32[512,512]{1,0:T(8,128)S(1)}, f32[512,512]{1,0:T(8,128)}, u32[]{:S(2)}) copy-start(f32[512,512]{1,0:T(8,128)} %shard_map.77.z_ref) | copy-start | bytes 3145732
  80.9 16.7 %collective-permute-start.25 = (f32[1,256,256]{2,1,0:T(8,128)S(1)}, f32[1,256,256]{2,1,0:T(8,128)S(1)}, u32[]{:S(2)}, u32[]{:S(2)}) collective-permute-start(f32[1,256,256]{2,1,0:T(8,128)S(1)} %bitcast.12), channel_id=1, source_target_pairs={{0,2},{1,3},{2,0},{3,1},{4,6},{5,7},{6,4},{7,5},{8,10},{9,11},{10,... | collective-permute-start | bytes 786440 | tf_op jit(solution)/shard_map/ppermute | solution.py:69
  82.2 15.4 %collective-permute-start.26 = (f32[1,256,256]{2,1,0:T(8,128)S(1)}, f32[1,256,256]{2,1,0:T(8,128)S(1)}, u32[]{:S(2)}, u32[]{:S(2)}) collective-permute-start(f32[1,256,256]{2,1,0:T(8,128)S(1)} %bitcast.13), channel_id=1, source_target_pairs={{0,1},{1,0},{2,3},{3,2},{4,5},{5,4},{6,7},{7,6},{8,9},{9,8},{10,11... | collective-permute-start | bytes 786440 | tf_op jit(solution)/shard_map/ppermute | solution.py:69
  90.1 6.7 %collective-permute-start.22 = (f32[1,64,256]{2,1,0:T(8,128)S(1)}, f32[1,64,256]{2,1,0:T(8,128)S(1)}, u32[]{:S(2)}, u32[]{:S(2)}) collective-permute-start(f32[1,64,256]{2,1,0:T(8,128)S(1)} %get-tuple-element.114), channel_id=1, source_target_pairs={{0,8},{4,12},{8,0},{12,4},{16,24},{20,28},{24,16},{28,20},{1,9},{5... | collective-permute-start | bytes 196616 | tf_op jit(solution)/shard_map/ppermute | solution.py:69
  91.6 5.3 %collective-permute-start.23 = (f32[1,64,256]{2,1,0:T(8,128)S(1)}, f32[1,64,256]{2,1,0:T(8,128)S(1)}, u32[]{:S(2)}, u32[]{:S(2)}) collective-permute-start(f32[1,64,256]{2,1,0:T(8,128)S(1)} %get-tuple-element.113), channel_id=1, source_target_pairs={{0,16},{4,20},{8,24},{12,28},{16,0},{20,4},{24,8},{28,12},{1,17},{... | collective-permute-start | bytes 196616 | tf_op jit(solution)/shard_map/ppermute | solution.py:69
  92.4 5.2 %collective-permute-start.24 = (f32[1,64,256]{2,1,0:T(8,128)S(1)}, f32[1,64,256]{2,1,0:T(8,128)S(1)}, u32[]{:S(2)}, u32[]{:S(2)}) collective-permute-start(f32[1,64,256]{2,1,0:T(8,128)S(1)} %get-tuple-element.112), channel_id=1, source_target_pairs={{0,24},{4,28},{8,16},{12,20},{16,8},{20,12},{24,0},{28,4},{1,25},{... | collective-permute-start | bytes 196616 | tf_op jit(solution)/shard_map/ppermute | solution.py:69
  96.8 17.4 %collective-permute-start.34 = (f32[4,256,256]{2,1,0:T(8,128)S(1)}, f32[4,256,256]{2,1,0:T(8,128)S(1)}, u32[]{:S(2)}, u32[]{:S(2)}) collective-permute-start(f32[4,256,256]{2,1,0:T(8,128)S(1)} %constant_dynamic-update-slice_fusion.refs_4_), channel_id=1, source_target_pairs={{0,4},{4,0},{8,12},{12,8},{16,20},{20,16},{24,28},{28,24},{1,5},{5... | collective-permute-start | bytes 3145736 | tf_op jit(solution)/shard_map/ppermute | solution.py:69
  97.6 4.3 %collective-permute-start.27 = (f32[1,64,256]{2,1,0:T(8,128)S(1)}, f32[1,64,256]{2,1,0:T(8,128)S(1)}, u32[]{:S(2)}, u32[]{:S(2)}) collective-permute-start(f32[1,64,256]{2,1,0:T(8,128)S(1)} %fusion.2), channel_id=1, source_target_pairs={{0,1},{1,0},{2,3},{3,2},{4,5},{5,4},{6,7},{7,6},{8,9},{9,8},{10,11... | collective-permute-start | bytes 196616 | tf_op jit(solution)/shard_map/ppermute | solution.py:69
  101.9 8.8 %collective-permute-start.29 = (f32[1,256,256]{2,1,0:T(8,128)S(1)}, f32[1,256,256]{2,1,0:T(8,128)S(1)}, u32[]{:S(2)}, u32[]{:S(2)}) collective-permute-start(f32[1,256,256]{2,1,0:T(8,128)S(1)} %collective-permute-done.25.refs_1_), channel_id=1, source_target_pairs={{0,1},{1,0},{2,3},{3,2},{4,5},{5,4},{6,7},{7,6},{8,9},{9,8},{10,11... | collective-permute-start | bytes 786440 | tf_op jit(solution)/shard_map/ppermute | solution.py:69
  102.8 6.7 %collective-permute-start.28 = (f32[1,64,256]{2,1,0:T(8,128)S(1)}, f32[1,64,256]{2,1,0:T(8,128)S(1)}, u32[]{:S(2)}, u32[]{:S(2)}) collective-permute-start(f32[1,64,256]{2,1,0:T(8,128)S(1)} %add.87), channel_id=1, source_target_pairs={{0,2},{1,3},{2,0},{3,1},{4,6},{5,7},{6,4},{7,5},{8,10},{9,11},{10,... | collective-permute-start | bytes 196616 | tf_op jit(solution)/shard_map/ppermute | solution.py:69
  110.8 3.5 %collective-permute-start.33 = (f32[2,256,256]{2,1,0:T(8,128)S(1)}, f32[2,256,256]{2,1,0:T(8,128)S(1)}, u32[]{:S(2)}, u32[]{:S(2)}) collective-permute-start(f32[2,256,256]{2,1,0:T(8,128)S(1)} %shard_map.83.own_ref), channel_id=1, source_target_pairs={{0,4},{4,0},{8,12},{12,8},{16,20},{20,16},{24,28},{28,24},{1,5},{5... | collective-permute-start | bytes 1572872 | tf_op jit(solution)/shard_map/ppermute | solution.py:69
  110.8 7.8 %collective-permute-start.30 = (f32[1,64,256]{2,1,0:T(8,128)S(1)}, f32[1,64,256]{2,1,0:T(8,128)S(1)}, u32[]{:S(2)}, u32[]{:S(2)}) collective-permute-start(f32[1,64,256]{2,1,0:T(8,128)S(1)} %add.88), channel_id=1, source_target_pairs={{0,8},{4,12},{8,0},{12,4},{16,24},{20,28},{24,16},{28,20},{1,9},{5... | collective-permute-start | bytes 196616 | tf_op jit(solution)/shard_map/ppermute | solution.py:69
  112.3 6.2 %collective-permute-start.31 = (f32[1,64,256]{2,1,0:T(8,128)S(1)}, f32[1,64,256]{2,1,0:T(8,128)S(1)}, u32[]{:S(2)}, u32[]{:S(2)}) collective-permute-start(f32[1,64,256]{2,1,0:T(8,128)S(1)} %add.88), channel_id=1, source_target_pairs={{0,16},{4,20},{8,24},{12,28},{16,0},{20,4},{24,8},{28,12},{1,17},{... | collective-permute-start | bytes 196616 | tf_op jit(solution)/shard_map/ppermute | solution.py:69
  112.5 6.0 %collective-permute-start.32 = (f32[1,64,256]{2,1,0:T(8,128)S(1)}, f32[1,64,256]{2,1,0:T(8,128)S(1)}, u32[]{:S(2)}, u32[]{:S(2)}) collective-permute-start(f32[1,64,256]{2,1,0:T(8,128)S(1)} %add.88), channel_id=1, source_target_pairs={{0,24},{4,28},{8,16},{12,20},{16,8},{20,12},{24,0},{28,4},{1,25},{... | collective-permute-start | bytes 196616 | tf_op jit(solution)/shard_map/ppermute | solution.py:69
  118.7 1.6 %collective-permute-start.35 = (f32[4,64,256]{2,1,0:T(8,128)S(1)}, f32[4,64,256]{2,1,0:T(8,128)S(1)}, u32[]{:S(2)}, u32[]{:S(2)}) collective-permute-start(f32[4,64,256]{2,1,0:T(8,128)S(1)} %constant_dynamic-update-slice_fusion.4.middle_own_ref), channel_id=1, source_target_pairs={{0,4},{4,0},{8,12},{12,8},{16,20},{20,16},{24,28},{28,24},{1,5},{5... | collective-permute-start | bytes 786440 | tf_op jit(solution)/shard_map/ppermute | solution.py:69
